TPU v7x, 512 devices: a whole 4x4x16 slice. The times are simulated.
512 devices in a mesh: lat: 128 (over z, y, core), lon: 4 (over x).
Axes of the slice: x: 4, y: 4, z: 16, core: 2. Of those that a mesh axis runs over, the one named last changes fastest.
Arguments:
- grid: bfloat16 [256, 512, 384], P('lat', 'lon'), may hold values from -6 to 6
- cotangent: bfloat16 [256, 512, 384], P('lat', 'lon'), may hold values from -6 to 6
- spectral_weight: bfloat16 [2, 256, 384, 384], P(None, 'lat', None, 'lon'), may hold values from -0.21875 to 0.21875
- w_in: bfloat16 [384, 768], replicated, may hold values from -0.3125 to 0.3125
- w_out: bfloat16 [768, 384], replicated, may hold values from -0.21875 to 0.21875
Outputs:
- block_output: bfloat16 [256, 512, 384], P('lat', 'lon')
- grad_input: bfloat16 [256, 512, 384], P('lat', 'lon')
- grad_spectral: float32 [2, 256, 384, 384], P(None, 'lat', 'lon')
- grad_w_in: float32 [294912], P(('lat', 'lon'))
- grad_w_out: float32 [294912], P(('lat', 'lon'))
All inputs are finite; a program needn't handle non-finite values.
Results may differ from a plain program's by a relative error of at most 0.019.
Values may be sent and summed in bfloat16 or wider, within the bound.
No kernel may reach another device: no remote copies, remote signals or barrier semaphores. Data moves between devices by JAX's collectives and lax.ppermute only.
A program may use at most 64 MiB of HBM per device.

v0:
```python
import math

import jax
import jax.numpy as jnp
from jax import lax
from jax.sharding import PartitionSpec as P


def lat_geometry(nlat, nlon):
    rows = jnp.arange(nlat, dtype=jnp.float32)
    theta = math.pi * (rows + 0.5) / nlat
    sines = jnp.sin(theta)
    weights = math.pi / nlat * sines * (2.0 * math.pi / nlon)
    return (jnp.cos(theta), jnp.log(sines), weights)


def fourier_tables(nlon, modes):
    lon_ids = jnp.arange(nlon, dtype=jnp.int32)[:, None]
    mode_ids = jnp.arange(modes, dtype=jnp.int32)[None, :]
    phase = (lon_ids * mode_ids % nlon).astype(jnp.float32)
    angle = 2.0 * math.pi / nlon * phase
    cosine = jnp.cos(angle).astype(jnp.bfloat16)
    sine = jnp.sin(angle).astype(jnp.bfloat16)
    factor = jnp.where(mode_ids == 0, 1.0, 2.0).astype(jnp.float32)
    cos_syn = (cosine.astype(jnp.float32) * factor).astype(jnp.bfloat16)
    sin_syn = (sine.astype(jnp.float32) * factor).astype(jnp.bfloat16)
    return (cosine, sine, cos_syn, sin_syn)


def combine_steps(earlier, later):
    e11, e12, e21, e22, escale = earlier
    l11, l12, l21, l22, lscale = later
    m11 = l11 * e11 + l12 * e21
    m12 = l11 * e12 + l12 * e22
    m21 = l21 * e11 + l22 * e21
    m22 = l21 * e12 + l22 * e22
    largest = jnp.maximum(
        jnp.maximum(jnp.abs(m11), jnp.abs(m12)), jnp.maximum(jnp.abs(m21), jnp.abs(m22))
    )
    return (
        m11 / largest,
        m12 / largest,
        m21 / largest,
        m22 / largest,
        escale + lscale + jnp.log(largest),
    )


def legendre_rows(order, degrees, cosv, logsin, limit):
    level = degrees[:, None]
    active = level >= order + 2.0
    safe = jnp.where(active, level, order + 2.0)
    alpha = jnp.sqrt((4.0 * safe * safe - 1.0) / (safe * safe - order * order))
    beta = jnp.sqrt(
        ((safe - 1.0) * (safe - 1.0) - order * order) / (4.0 * (safe - 1.0) * (safe - 1.0) - 1.0)
    )
    ones = jnp.ones_like(level * cosv)
    zeros = jnp.zeros_like(ones)
    step11 = jnp.where(active, alpha * cosv, ones)
    step12 = jnp.where(active, -alpha * beta * ones, zeros)
    step21 = jnp.where(active, ones, zeros)
    step22 = jnp.where(active, zeros, ones)
    m11, m12, m21, m22, scale = lax.associative_scan(
        combine_steps, (step11, step12, step21, step22, zeros), axis=0
    )
    log_start = (
        0.5
        * (
            jnp.log((2.0 * order + 1.0) / (4.0 * math.pi))
            + lax.lgamma(2.0 * order + 1.0)
            - 2.0 * lax.lgamma(order + 1.0)
            - order * math.log(4.0)
        )
        + order * logsin
    )
    first = jnp.sqrt(2.0 * order + 3.0) * cosv
    value = (m11 * first + m12) * jnp.exp(scale + log_start)
    value = jnp.where(
        level >= order + 1.0, value, jnp.where(level == order, jnp.exp(log_start) * ones, zeros)
    )
    return jnp.where(level < limit, value, zeros)


def gelu_value(values):
    return 0.5 * values * (1.0 + lax.erf(values * (1.0 / math.sqrt(2.0))))


def gelu_slope(values):
    return 0.5 * (1.0 + lax.erf(values * (1.0 / math.sqrt(2.0)))) + values * jnp.exp(
        -0.5 * values * values
    ) * (1.0 / math.sqrt(2.0 * math.pi))


def reorder(values, axis, first, second):
    shape = values.shape
    split = shape[:axis] + (first, second) + shape[axis + 1 :]
    return jnp.swapaxes(values.reshape(split), axis, axis + 1).reshape(shape)


def regroup(values):
    return lax.all_to_all(values, "lat", split_axis=1, concat_axis=0, tiled=True)


def lon_split(values):
    return lax.all_to_all(values, "lon", split_axis=2, concat_axis=1, tiled=True)


def lon_merge(values):
    return lax.all_to_all(values, "lon", split_axis=1, concat_axis=2, tiled=True)


def mix_product(inputs, weights):
    return jnp.einsum("mkc,kcd->kmd", inputs, weights, preferred_element_type=jnp.float32)


def unmix_product(grads, weights):
    return jnp.einsum("mko,kio->kmi", grads, weights, preferred_element_type=jnp.float32)


def outer_product(inputs, grads):
    return jnp.einsum("mki,mko->kio", inputs, grads, preferred_element_type=jnp.float32)


def body(grid, cotangent, spectral_weight, w_in, w_out):
    lat_count = lax.axis_size("lat")
    lon_count = lax.axis_size("lon")
    lat_index = lax.axis_index("lat")
    per_device, lon_rows, width = grid.shape
    quarter = width // lon_count
    total_lat = per_device * lat_count
    total_lon = lon_rows * lon_count
    cosv, logsin, quad = lat_geometry(total_lat, total_lon)
    cosine, sine, cos_syn, sin_syn = fourier_tables(total_lon, total_lat)
    local_quad = lax.dynamic_slice_in_dim(quad, lat_index * per_device, per_device)[:, None, None]
    lat_float = lat_index.astype(jnp.float32)
    tables = []
    starts = []
    for block in range(per_device):
        order = lat_float + block * lat_count
        degrees = order + jnp.arange((per_device - block) * lat_count, dtype=jnp.float32)
        tables.append(legendre_rows(order, degrees, cosv, logsin, total_lat).astype(jnp.bfloat16))
        starts.append(order.astype(jnp.int32))

    def analyze(data):
        blocks = []
        for block in range(per_device):
            part = jnp.dot(tables[block], data[:, block], preferred_element_type=jnp.float32)
            padded = jnp.zeros((total_lat + lat_count, part.shape[1]), jnp.float32)
            part = lax.dynamic_update_slice_in_dim(padded, part, starts[block], 0)[:total_lat]
            blocks.append(part)
        return jnp.stack(blocks)

    def synthesize(coef):
        blocks = []
        for block in range(per_device):
            column = coef[:, block]
            padded = jnp.concatenate(
                [column, jnp.zeros((lat_count, column.shape[1]), column.dtype)], axis=0
            )
            column = lax.dynamic_slice_in_dim(padded, starts[block], tables[block].shape[0], 0)
            blocks.append(
                lax.dot_general(
                    tables[block],
                    column,
                    (((0,), (0,)), ((), ())),
                    preferred_element_type=jnp.float32,
                )
            )
        return jnp.stack(blocks)

    def to_orders(waves):
        waves = reorder(waves, 1, per_device, lat_count)
        return regroup(waves)

    def to_degrees(coef):
        got = regroup(coef)
        got = reorder(got, 0, lat_count, per_device)
        return got

    def from_degrees(coef):
        coef = reorder(coef, 1, per_device, lat_count)
        fields = synthesize(regroup(coef)).astype(jnp.bfloat16)
        back = regroup(fields)
        back = reorder(back, 0, lat_count, per_device)
        return back

    spread = lon_split(grid)
    four_re = (
        jnp.einsum("jkc,km->jmc", spread, cosine, preferred_element_type=jnp.float32) * local_quad
    )
    four_im = (
        jnp.einsum("jkc,km->jmc", spread, sine, preferred_element_type=jnp.float32) * local_quad
    )
    four = jnp.concatenate([four_re, -four_im], axis=2).astype(jnp.bfloat16)
    spectrum = to_degrees(analyze(to_orders(four)).astype(jnp.bfloat16))
    spec_four = spectrum.reshape(total_lat, per_device, 2, quarter)
    spec_re = spec_four[:, :, 0]
    spec_im = spec_four[:, :, 1]
    piece = lax.all_gather(spec_four, "lon", axis=3, tiled=True)
    weight_re = spectral_weight[0]
    weight_im = spectral_weight[1]
    part_re = piece[:, :, 0]
    part_im = piece[:, :, 1]
    total_re = mix_product(part_re, weight_re) - mix_product(part_im, weight_im)
    total_im = mix_product(part_re, weight_im) + mix_product(part_im, weight_re)
    mixed = jnp.concatenate([total_re, total_im], axis=2).astype(jnp.bfloat16)
    row_weights = lax.all_to_all(spectral_weight, "lon", split_axis=2, concat_axis=3, tiled=True)
    fields = from_degrees(mixed)
    wave = (
        jnp.einsum(
            "mjc,km->jkc", fields[:, :, :quarter], cos_syn, preferred_element_type=jnp.float32
        )
        - jnp.einsum(
            "mjc,km->jkc", fields[:, :, quarter:], sin_syn, preferred_element_type=jnp.float32
        )
    ).astype(jnp.bfloat16)
    wave_rows = lon_merge(wave)
    hidden = (grid.astype(jnp.float32) + wave_rows.astype(jnp.float32)).astype(jnp.bfloat16)
    flat_rows = hidden.reshape(-1, width)
    pre = jnp.dot(flat_rows, w_in, preferred_element_type=jnp.float32)
    act = gelu_value(pre).astype(jnp.bfloat16)
    block_output = (
        flat_rows.astype(jnp.float32) + jnp.dot(act, w_out, preferred_element_type=jnp.float32)
    ).astype(jnp.bfloat16)
    back = cotangent.reshape(-1, width)
    act_grad = jnp.dot(back, w_out.T, preferred_element_type=jnp.float32)
    pre_grad = (act_grad * gelu_slope(pre)).astype(jnp.bfloat16)
    hidden_grad = (
        back.astype(jnp.float32) + jnp.dot(pre_grad, w_in.T, preferred_element_type=jnp.float32)
    ).astype(jnp.bfloat16)
    out_part = jnp.dot(act.T, back, preferred_element_type=jnp.float32).reshape(-1)
    in_part = jnp.dot(flat_rows.T, pre_grad, preferred_element_type=jnp.float32).reshape(-1)
    grad_w_in, grad_w_out = (
        lax.psum_scatter(in_part, ("lat", "lon"), scatter_dimension=0, tiled=True),
        lax.psum_scatter(out_part, ("lat", "lon"), scatter_dimension=0, tiled=True),
    )
    grad_rows = hidden_grad.reshape(grid.shape)
    grad_spread = lon_split(grad_rows)
    field_re = jnp.einsum("jkc,km->jmc", grad_spread, cos_syn, preferred_element_type=jnp.float32)
    field_im = jnp.einsum("jkc,km->jmc", grad_spread, sin_syn, preferred_element_type=jnp.float32)
    field_grad = jnp.concatenate([field_re, -field_im], axis=2).astype(jnp.bfloat16)
    mixed_grad = to_degrees(analyze(to_orders(field_grad)).astype(jnp.bfloat16))
    grad_four = mixed_grad.reshape(total_lat, per_device, 2, quarter)
    piece = lax.all_gather(grad_four, "lon", axis=3, tiled=True)
    rows_re = row_weights[0]
    rows_im = row_weights[1]
    part_re = piece[:, :, 0]
    part_im = piece[:, :, 1]
    back_re = unmix_product(part_re, rows_re) + unmix_product(part_im, rows_im)
    back_im = unmix_product(part_im, rows_re) - unmix_product(part_re, rows_im)
    block_re = outer_product(spec_re, part_re) + outer_product(spec_im, part_im)
    block_im = outer_product(spec_re, part_im) - outer_product(spec_im, part_re)
    weight_re = block_re
    weight_im = block_im
    grad_spectral = jnp.stack([weight_re, weight_im])
    spectrum_grad = jnp.concatenate([back_re, back_im], axis=2).astype(jnp.bfloat16)
    four_grad = from_degrees(spectrum_grad)
    wave_back = (
        (
            jnp.einsum(
                "mjc,km->jkc", four_grad[:, :, :quarter], cosine, preferred_element_type=jnp.float32
            )
            - jnp.einsum(
                "mjc,km->jkc", four_grad[:, :, quarter:], sine, preferred_element_type=jnp.float32
            )
        )
        * local_quad
    ).astype(jnp.bfloat16)
    wave_grad = lon_merge(wave_back)
    grad_input = (grad_rows.astype(jnp.float32) + wave_grad.astype(jnp.float32)).astype(
        jnp.bfloat16
    )
    return (block_output.reshape(grid.shape), grad_input, grad_spectral, grad_w_in, grad_w_out)


def solution(mesh):
    in_specs = (P("lat", "lon", None), P("lat", "lon", None), P(None, "lat", None, "lon"), P(), P())
    out_specs = (
        P("lat", "lon", None),
        P("lat", "lon", None),
        P(None, "lat", "lon", None),
        P(("lat", "lon")),
        P(("lat", "lon")),
    )
    return jax.shard_map(body, mesh=mesh, in_specs=in_specs, out_specs=out_specs, check_vma=False)
```

profile of v0, /device:TPU:8, one launch (start us, length us, event | category | flops | bytes accessed | tf_op | source)
XLA Modules:
  0.0 914.7 jit_solution(8124220780295118554)
XLA Ops:
  7.2 1.8 copy.181
  9.0 4.3 all-to-all-start
  75.6 1.4 slice.1279
  77.0 1.4 slice.1278
  81.6 0.8 fusion.192
  104.2 2.1 fusion.44
  106.3 2.1 fusion.46
  108.9 1.7 pad_maximum_fusion.1
  110.6 19.5 %all-to-all-start.1 = ((bf16[2,256,192]{2,0,1:T(2,128)(2,1)}), bf16[2,256,192]{2,0,1:T(2,128)(2,1)S(1)}, u32[]{:S(2)}, u32[]{:S(2)}) async-start(bf16[2,256,192]{2,0,1:T(2,128)(2,1)} %bitcast.11), calls=%async_computation.1 | async-start | bytes 524288 | tf_op jit(solution)/shard_map/all_to_all | solution.py:101
  131.0 1.3 pad.566
  132.4 1.3 pad.567
  134.6 1.0 select_convert_fusion.1
  135.9 15.4 %all-to-all-done.1 = bf16[2,256,192]{2,0,1:T(2,128)(2,1)S(1)} async-done(((bf16[2,256,192]{2,0,1:T(2,128)(2,1)}), bf16[2,256,192]{2,0,1:T(2,128)(2,1)S(1)}, u32[]{:S(2)}, u32[]{:S(2)}) %all-to-all-start.1) | async-done | bytes 196640 | tf_op jit(solution)/shard_map/all_to_all | solution.py:101
  153.2 1.0 dynamic_update_slice.12
  154.4 28.6 %all_to_all.177 = bf16[2,256,192]{2,0,1:T(2,128)(2,1)S(1)} all-to-all(bf16[2,256,192]{2,0,1:T(2,128)(2,1)S(1)} %copy.189), channel_id=1, replica_groups=mesh['lat'=128,'lon'=4] {'lat'}, dimensions={1} | all-to-all | bytes 393216 | tf_op jit(solution)/shard_map/all_to_all | solution.py:101
  183.7 14.7 %all_gather.6 = bf16[256,2,2,384]{0,2,1,3:T(2,128)(2,1)S(1)} all-gather(bf16[256,2,2,96]{0,2,1,3:T(2,128)(2,1)S(1)} %copy.191), channel_id=1, replica_groups=mesh['lat'=128,'lon'=4] {'lon'}, dimensions={3}, use_global_device_ids=true | all-gather | bytes 983040 | tf_op jit(solution)/shard_map/all_gather | solution.py:199
  198.4 1.1 fusion.199
  202.9 28.7 %all_to_all.178 = bf16[2,256,192]{2,0,1:T(2,128)(2,1)S(1)} all-to-all(bf16[2,256,192]{2,0,1:T(2,128)(2,1)S(1)} %bitcast.245), channel_id=1, replica_groups=mesh['lat'=128,'lon'=4] {'lat'}, dimensions={1} | all-to-all | bytes 393216 | tf_op jit(solution)/shard_map/all_to_all | solution.py:101
  233.0 0.9 copy.199
  233.9 7.5 all-to-all-start.4
  241.4 21.2 %all-to-all-done.4 = bf16[2,256,192]{2,0,1:T(2,128)(2,1)S(1)} async-done(((bf16[2,256,192]{2,0,1:T(2,128)(2,1)}), bf16[2,256,192]{2,0,1:T(2,128)(2,1)S(1)}, u32[]{:S(2)}, u32[]{:S(2)}) %all-to-all-start.4) | async-done | bytes 196640 | tf_op jit(solution)/shard_map/all_to_all | solution.py:101
  263.3 2.1 fusion.48
  265.4 2.1 fusion.50
  267.6 0.9 copy.203
  268.5 4.1 all-to-all-start.5
  272.8 7.1 all-to-all-done.5
  281.9 0.7 copy-done.6
  283.2 8.9 all_to_all.179
  292.2 2.1 fusion.49
  294.3 2.1 fusion.47
  296.8 1.2 pad_maximum_fusion.3
  298.1 6.9 all-to-all-start.7
  305.0 1.1 copy.220
  306.1 20.2 %all-to-all-done.7 = bf16[2,256,192]{2,0,1:T(2,128)(2,1)S(1)} async-done(((bf16[2,256,192]{2,0,1:T(2,128)(2,1)}), bf16[2,256,192]{2,0,1:T(2,128)(2,1)S(1)}, u32[]{:S(2)}, u32[]{:S(2)}) %all-to-all-start.7) | async-done | bytes 196640 | tf_op jit(solution)/shard_map/all_to_all | solution.py:101
  326.2 3.5 all-to-all-start.9
  331.6 1.0 dynamic_update_slice.14
  332.6 0.9 copy.216
  333.5 5.1 all-to-all-done.9
  338.6 7.3 all-to-all-start.8
  346.7 20.3 %all-to-all-done.8 = bf16[2,256,192]{2,0,1:T(2,128)(2,1)S(1)} async-done(((bf16[2,256,192]{2,0,1:T(2,128)(2,1)}), bf16[2,256,192]{2,0,1:T(2,128)(2,1)S(1)}, u32[]{:S(2)}, u32[]{:S(2)}) %all-to-all-start.8) | async-done | bytes 196640 | tf_op jit(solution)/shard_map/all_to_all | solution.py:101
  367.8 14.5 %all_gather.7 = bf16[256,2,2,384]{0,2,1,3:T(2,128)(2,1)S(1)} all-gather(bf16[256,2,2,96]{0,2,1,3:T(2,128)(2,1)S(1)} %copy.218), channel_id=1, replica_groups=mesh['lat'=128,'lon'=4] {'lon'}, dimensions={3}, use_global_device_ids=true | all-gather | bytes 983040 | tf_op jit(solution)/shard_map/all_gather | solution.py:244
  382.3 2.0 fusion.198
  384.2 2.2 copy.243
  388.4 1.2 pad_maximum_fusion.4
  389.7 7.6 all-to-all-start.10
  397.4 1.4 fusion.238
  398.7 1.1 reshape.252
  399.8 1.3 fusion.239
  401.2 1.1 reshape.253
  403.4 14.8 %all-to-all-done.10 = bf16[2,256,192]{2,0,1:T(2,128)(2,1)} async-done(((bf16[2,256,192]{2,0,1:T(2,128)(2,1)}), bf16[2,256,192]{2,0,1:T(2,128)(2,1)}, u32[]{:S(2)}, u32[]{:S(2)}) %all-to-all-start.10) | async-done | bytes 196640 | tf_op jit(solution)/shard_map/all_to_all | solution.py:101
  418.2 1.2 copy.225
  420.6 0.9 copy.228
  421.5 8.1 all-to-all-start.11
  429.6 2.1 fusion.1
  431.7 454.6 %all-reduce.153.cloned.1.call-done = (f32[294912]{0:T(1024)}, f32[294912]{0:T(1024)}) async-done(((f32[294912]{0:T(1024)}, f32[294912]{0:T(1024)}), (f32[294912]{0:T(1024)}, f32[294912]{0:T(1024)})) %all-reduce.153.cloned.1.call-update) | async-done | bytes 2359312
  886.3 1.4 dynamic-slice
  887.7 1.4 dynamic-slice.1
  890.2 2.3 fusion.43
  892.6 2.3 fusion.45
  895.0 0.9 copy.232
  895.8 4.0 all-to-all-start.12
  900.0 0.9 pad_maximum_fusion
  900.9 5.6 all-to-all-done.12
  906.9 0.8 copy.237
  (889 shorter events, 104.4 us)
Async XLA Ops:
  7.2 273.3 %copy-start = (bf16[384,768]{1,0:T(8,128)(2,1)S(1)}, bf16[384,768]{1,0:T(8,128)(2,1)}, u32[]{:S(2)}) copy-start(bf16[384,768]{1,0:T(8,128)(2,1)} %param.8) | copy-start | bytes 1769476
  9.0 95.1 %all-to-all-start = ((bf16[2,128,384]{1,0,2:T(2,128)(2,1)}), bf16[2,128,384]{1,0,2:T(2,128)(2,1)S(1)}, u32[]{:S(2)}, u32[]{:S(2)}) async-start(bf16[2,128,384]{1,0,2:T(2,128)(2,1)} %copy.181), calls=%async_computation | async-start | bytes 393216 | tf_op jit(solution)/shard_map/all_to_all | solution.py:105
  16.8 30.8 %copy-start.37 = (f32[4,256]{1,0:T(4,128)}, f32[4,256]{1,0:T(4,128)S(1)}, u32[]{:S(2)}) copy-start(f32[4,256]{1,0:T(4,128)S(1)} %get-tuple-element.144) | copy-start | bytes 12292
  16.8 30.9 %copy-start.33 = (f32[4,256]{1,0:T(4,128)}, f32[4,256]{1,0:T(4,128)S(1)}, u32[]{:S(2)}) copy-start(f32[4,256]{1,0:T(4,128)S(1)} %get-tuple-element.281) | copy-start | bytes 12292
  16.8 30.9 %copy-start.34 = (f32[4,256]{1,0:T(4,128)}, f32[4,256]{1,0:T(4,128)S(1)}, u32[]{:S(2)}) copy-start(f32[4,256]{1,0:T(4,128)S(1)} %get-tuple-element.280) | copy-start | bytes 12292
  16.8 30.9 %copy-start.36 = (f32[4,256]{1,0:T(4,128)}, f32[4,256]{1,0:T(4,128)S(1)}, u32[]{:S(2)}) copy-start(f32[4,256]{1,0:T(4,128)S(1)} %get-tuple-element.283) | copy-start | bytes 12292
  16.8 30.9 %copy-start.41 = (f32[4,256]{1,0:T(4,128)}, f32[4,256]{1,0:T(4,128)S(1)}, u32[]{:S(2)}) copy-start(f32[4,256]{1,0:T(4,128)S(1)} %get-tuple-element.282) | copy-start | bytes 12292
  18.9 28.8 %copy-start.47 = (f32[1,256]{1,0:T(1,128)}, f32[1,256]{1,0:T(1,128)S(1)}, u32[]{:S(2)}) copy-start(f32[1,256]{1,0:T(1,128)S(1)} %get-tuple-element.134) | copy-start | bytes 3076
  18.9 28.8 %copy-start.49 = (f32[1,256]{1,0:T(1,128)}, f32[1,256]{1,0:T(1,128)S(1)}, u32[]{:S(2)}) copy-start(f32[1,256]{1,0:T(1,128)S(1)} %get-tuple-element.295) | copy-start | bytes 3076
  18.9 28.8 %copy-start.51 = (f32[1,256]{1,0:T(1,128)}, f32[1,256]{1,0:T(1,128)S(1)}, u32[]{:S(2)}) copy-start(f32[1,256]{1,0:T(1,128)S(1)} %get-tuple-element.296) | copy-start | bytes 3076
  19.5 28.2 %copy-start.53 = (f32[1,256]{1,0:T(1,128)}, f32[1,256]{1,0:T(1,128)S(1)}, u32[]{:S(2)}) copy-start(f32[1,256]{1,0:T(1,128)S(1)} %get-tuple-element.315) | copy-start | bytes 3076
  44.7 4.2 copy-start.103
  50.6 31.0 %copy-start.35 = (f32[4,256]{1,0:T(4,128)S(1)}, f32[4,256]{1,0:T(4,128)}, u32[]{:S(2)}) copy-start(f32[4,256]{1,0:T(4,128)} %copy-done.34) | copy-start | bytes 12292
  50.6 30.9 %copy-start.42 = (f32[4,256]{1,0:T(4,128)S(1)}, f32[4,256]{1,0:T(4,128)}, u32[]{:S(2)}) copy-start(f32[4,256]{1,0:T(4,128)} %copy-done.41) | copy-start | bytes 12292
  50.6 30.9 %copy-start.48 = (f32[1,256]{1,0:T(1,128)S(1)}, f32[1,256]{1,0:T(1,128)}, u32[]{:S(2)}) copy-start(f32[1,256]{1,0:T(1,128)} %copy-done.47) | copy-start | bytes 3076
  50.6 30.9 %copy-start.50 = (f32[1,256]{1,0:T(1,128)S(1)}, f32[1,256]{1,0:T(1,128)}, u32[]{:S(2)}) copy-start(f32[1,256]{1,0:T(1,128)} %copy-done.49) | copy-start | bytes 3076
  50.6 30.9 %copy-start.52 = (f32[1,256]{1,0:T(1,128)S(1)}, f32[1,256]{1,0:T(1,128)}, u32[]{:S(2)}) copy-start(f32[1,256]{1,0:T(1,128)} %copy-done.51) | copy-start | bytes 3076
  50.7 35.0 %copy-start.38 = (f32[4,256]{1,0:T(4,128)S(1)}, f32[4,256]{1,0:T(4,128)}, u32[]{:S(2)}) copy-start(f32[4,256]{1,0:T(4,128)} %copy-done.37) | copy-start | bytes 12292
  50.9 41.4 %copy-start.23 = (f32[7,256]{1,0:T(8,128)S(1)}, f32[7,256]{1,0:T(8,128)}, u32[]{:S(2)}) copy-start(f32[7,256]{1,0:T(8,128)} %slice.1402) | copy-start | bytes 21508
  50.9 41.4 %copy-start.24 = (f32[7,256]{1,0:T(8,128)S(1)}, f32[7,256]{1,0:T(8,128)}, u32[]{:S(2)}) copy-start(f32[7,256]{1,0:T(8,128)} %slice.1347) | copy-start | bytes 21508
  50.9 41.4 %copy-start.25 = (f32[7,256]{1,0:T(8,128)S(1)}, f32[7,256]{1,0:T(8,128)}, u32[]{:S(2)}) copy-start(f32[7,256]{1,0:T(8,128)} %slice.1410) | copy-start | bytes 21508
  50.9 41.4 %copy-start.26 = (f32[7,256]{1,0:T(8,128)S(1)}, f32[7,256]{1,0:T(8,128)}, u32[]{:S(2)}) copy-start(f32[7,256]{1,0:T(8,128)} %slice.1409) | copy-start | bytes 21508
  51.6 40.7 %copy-start.31 = (f32[7,256]{1,0:T(8,128)S(1)}, f32[7,256]{1,0:T(8,128)}, u32[]{:S(2)}) copy-start(f32[7,256]{1,0:T(8,128)} %slice.1464) | copy-start | bytes 21508
  70.1 25.7 %copy-start.14 = (f32[15,256]{1,0:T(8,128)S(1)}, f32[15,256]{1,0:T(8,128)}, u32[]{:S(2)}) copy-start(f32[15,256]{1,0:T(8,128)} %slice.1337) | copy-start | bytes 46084
  70.1 25.7 %copy-start.15 = (f32[15,256]{1,0:T(8,128)S(1)}, f32[15,256]{1,0:T(8,128)}, u32[]{:S(2)}) copy-start(f32[15,256]{1,0:T(8,128)} %slice.1420) | copy-start | bytes 46084
  70.2 25.7 %copy-start.16 = (f32[15,256]{1,0:T(8,128)S(1)}, f32[15,256]{1,0:T(8,128)}, u32[]{:S(2)}) copy-start(f32[15,256]{1,0:T(8,128)} %slice.1419) | copy-start | bytes 46084
  73.2 22.7 %copy-start.21 = (f32[15,256]{1,0:T(8,128)S(1)}, f32[15,256]{1,0:T(8,128)}, u32[]{:S(2)}) copy-start(f32[15,256]{1,0:T(8,128)} %slice.1466) | copy-start | bytes 46084
  73.2 22.7 %copy-start.77 = (f32[1,256]{1,0:T(1,128)S(1)}, f32[1,256]{1,0:T(1,128)}, u32[]{:S(2)}) copy-start(f32[1,256]{1,0:T(1,128)} %slice.1676) | copy-start | bytes 3076
  73.3 22.7 %copy-start.76 = (f32[1,256]{1,0:T(1,128)S(1)}, f32[1,256]{1,0:T(1,128)}, u32[]{:S(2)}) copy-start(f32[1,256]{1,0:T(1,128)} %slice.1673) | copy-start | bytes 3076
  73.4 22.7 %copy-start.75 = (f32[1,256]{1,0:T(1,128)S(1)}, f32[1,256]{1,0:T(1,128)}, u32[]{:S(2)}) copy-start(f32[1,256]{1,0:T(1,128)} %slice.1670) | copy-start | bytes 3076
  84.3 11.8 %copy-start.74 = (f32[1,256]{1,0:T(1,128)S(1)}, f32[1,256]{1,0:T(1,128)}, u32[]{:S(2)}) copy-start(f32[1,256]{1,0:T(1,128)} %slice.1611) | copy-start | bytes 3076
  87.2 9.0 copy-start.73
  97.2 1.8 copy-start.88
  97.2 1.9 copy-start.87
  97.2 1.9 copy-start.32
  97.2 1.9 copy-start.86
  97.2 2.0 copy-start.85
  97.3 2.0 copy-start.84
  97.3 2.0 copy-start.83
  97.4 2.0 copy-start.17
  97.4 2.0 copy-start.18
  97.4 2.0 copy-start.19
  97.4 2.0 copy-start.20
  97.4 2.1 copy-start.22
  97.5 2.1 copy-start.82
  102.0 2.1 copy-start.108
  110.6 40.8 %all-to-all-start.1 = ((bf16[2,256,192]{2,0,1:T(2,128)(2,1)}), bf16[2,256,192]{2,0,1:T(2,128)(2,1)S(1)}, u32[]{:S(2)}, u32[]{:S(2)}) async-start(bf16[2,256,192]{2,0,1:T(2,128)(2,1)} %bitcast.11), calls=%async_computation.1 | async-start | bytes 524288 | tf_op jit(solution)/shard_map/all_to_all | solution.py:101
  133.8 1.8 copy-start.95
  133.9 1.8 copy-start.96
  133.9 1.8 copy-start.97
  133.9 1.8 copy-start.98
  135.7 194.8 %copy-start.4 = (bf16[128,256]{1,0:T(8,128)(2,1)}, bf16[128,256]{1,0:T(8,128)(2,1)S(1)}, u32[]{:S(2)}) copy-start(bf16[128,256]{1,0:T(8,128)(2,1)S(1)} %select_convert_fusion.1) | copy-start | bytes 196612
  233.9 28.8 %all-to-all-start.4 = ((bf16[2,256,192]{2,0,1:T(2,128)(2,1)}), bf16[2,256,192]{2,0,1:T(2,128)(2,1)S(1)}, u32[]{:S(2)}, u32[]{:S(2)}) async-start(bf16[2,256,192]{2,0,1:T(2,128)(2,1)} %copy.199), calls=%async_computation.4 | async-start | bytes 524288 | tf_op jit(solution)/shard_map/all_to_all | solution.py:101
  267.6 5.1 copy-start.7
  268.5 11.4 %all-to-all-start.5 = ((bf16[2,512,96]{2,0,1:T(2,128)(2,1)}), bf16[2,512,96]{2,0,1:T(2,128)(2,1)S(1)}, u32[]{:S(2)}, u32[]{:S(2)}) async-start(bf16[2,512,96]{2,0,1:T(2,128)(2,1)} %copy.203), calls=%async_computation.5 | async-start | bytes 524288 | tf_op jit(solution)/shard_map/all_to_all | solution.py:109
  283.0 11.3 %copy-start.2 = (bf16[256,384]{1,0:T(8,128)(2,1)}, bf16[256,384]{1,0:T(8,128)(2,1)S(1)}, u32[]{:S(2)}) copy-start(bf16[256,384]{1,0:T(8,128)(2,1)S(1)} %fusion.2) | copy-start | bytes 589828
  298.1 28.2 %all-to-all-start.7 = ((bf16[2,256,192]{2,0,1:T(2,128)(2,1)}), bf16[2,256,192]{2,0,1:T(2,128)(2,1)S(1)}, u32[]{:S(2)}, u32[]{:S(2)}) async-start(bf16[2,256,192]{2,0,1:T(2,128)(2,1)} %bitcast.54), calls=%async_computation.7 | async-start | bytes 524288 | tf_op jit(solution)/shard_map/all_to_all | solution.py:101
  326.2 12.4 %all-to-all-start.9 = ((bf16[2,2,384,96]{3,1,0,2:T(2,128)(2,1)}), bf16[2,2,384,96]{3,1,0,2:T(2,128)(2,1)S(1)}, u32[]{:S(2)}, u32[]{:S(2)}) async-start(bf16[2,2,384,96]{3,1,0,2:T(2,128)(2,1)} %copy.220), calls=%async_computation.9 | async-start | bytes 786432 | tf_op jit(solution)/shard_map/all_to_all | solution.py:207
  338.6 28.4 %all-to-all-start.8 = ((bf16[2,256,192]{2,0,1:T(2,128)(2,1)}), bf16[2,256,192]{2,0,1:T(2,128)(2,1)S(1)}, u32[]{:S(2)}, u32[]{:S(2)}) async-start(bf16[2,256,192]{2,0,1:T(2,128)(2,1)} %copy.216), calls=%async_computation.8 | async-start | bytes 524288 | tf_op jit(solution)/shard_map/all_to_all | solution.py:101
  389.7 28.5 %all-to-all-start.10 = ((bf16[2,256,192]{2,0,1:T(2,128)(2,1)}), bf16[2,256,192]{2,0,1:T(2,128)(2,1)}, u32[]{:S(2)}, u32[]{:S(2)}) async-start(bf16[2,256,192]{2,0,1:T(2,128)(2,1)} %bitcast.67), calls=%async_computation.10 | async-start | bytes 524288 | tf_op jit(solution)/shard_map/all_to_all | solution.py:101
  397.3 489.0 %all-reduce.153.cloned.1.call-start = ((), (), s32[]{:S(2)}) async-start(), calls=%async_computation.13 | async-start | bytes 4718592
  403.4 16.7 %copy-start.5 = (bf16[128,256]{1,0:T(8,128)(2,1)S(1)}, bf16[128,256]{1,0:T(8,128)(2,1)}, u32[]{:S(2)}) copy-start(bf16[128,256]{1,0:T(8,128)(2,1)} %copy-done.4) | copy-start | bytes 196612
  421.5 468.2 %all-to-all-start.11 = ((bf16[2,256,192]{2,0,1:T(2,128)(2,1)}), bf16[2,256,192]{2,0,1:T(2,128)(2,1)S(1)}, u32[]{:S(2)}, u32[]{:S(2)}) async-start(bf16[2,256,192]{2,0,1:T(2,128)(2,1)} %copy.228), calls=%async_computation.11 | async-start | bytes 524288 | tf_op jit(solution)/shard_map/all_to_all | solution.py:101
  895.8 10.6 %all-to-all-start.12 = ((bf16[2,512,96]{2,0,1:T(2,128)(2,1)}), bf16[2,512,96]{2,0,1:T(2,128)(2,1)S(1)}, u32[]{:S(2)}, u32[]{:S(2)}) async-start(bf16[2,512,96]{2,0,1:T(2,128)(2,1)} %copy.232), calls=%async_computation.12 | async-start | bytes 524288 | tf_op jit(solution)/shard_map/all_to_all | solution.py:109
  (56 other events, 61.2 us)
Sparse Core Ops, SparseCore 0:
  403.4 482.8 all-reduce.152
where the time goes:
time: 920 us; the launch traced here: 915 us
  waiting for transfers between devices  564 us (61%)
  local copies, waits for them, and re-layouts  100 us (11%)
  blocking collectives  95.3 us (10%)
  starting transfers between devices  72.9 us (8%)
  other arithmetic  33 us (4%)
  matrix products  27.7 us (3%)
  between operations  21.3 us (2%)
    unnamed x2, waiting for transfers between devices  455 us
    all_to_all x6, waiting for transfers between devices, regroup(): lax.all_to_all(values, 'lat', split_axis=1, concat_axis=0, tiled=True)  92 us
    all_to_all x2, blocking collectives, regroup(): lax.all_to_all(values, 'lat', split_axis=1, concat_axis=0, tiled=True)  57.2 us
    all_to_all x6, starting transfers between devices, regroup(): lax.all_to_all(values, 'lat', split_axis=1, concat_axis=0, tiled=True)  57 us
    slice x234, local copies, waits for them, and re-layouts, legendre_rows(): lax.associative_scan(combine_steps, (step11, step12, step21, step22, zero...  54.5 us
  transfers between devices with their start and end apart: 11, of which 9 were waited for; matrix products, arithmetic and copies ran while one was open for 12% of the time, Pallas kernels for 0%

commit v1 on v0

v1 whole, which is shorter than its diff:
```python
import math

import jax
import jax.numpy as jnp
import ml_dtypes
import numpy as np
from jax import lax
from jax.sharding import PartitionSpec as P


def legendre_table(size):
    theta = math.pi * (np.arange(size) + 0.5) / size
    cosv, sinv = np.cos(theta), np.sin(theta)
    order = np.arange(size, dtype=np.float64)[:, None]
    start = np.empty((size, size))
    start[0] = math.sqrt(1.0 / (4.0 * math.pi))
    for m in range(1, size):
        start[m] = start[m - 1] * math.sqrt((2 * m + 1) / (2.0 * m)) * sinv
    table = np.zeros((size, size, size), dtype=ml_dtypes.bfloat16)
    before = np.zeros((size, size))
    now = np.zeros((size, size))
    for level in range(size):
        safe = np.where(order < level, order, 0.0)
        alpha = np.sqrt((4.0 * level * level - 1.0) / (level * level - safe * safe)) if level else 0.0
        beta = (
            np.sqrt(((level - 1.0) ** 2 - safe * safe).clip(0) / (4.0 * (level - 1.0) ** 2 - 1.0))
            if level > 1
            else 0.0
        )
        value = np.where(order < level, alpha * (cosv * now - beta * before), 0.0)
        value[level] = start[level]
        table[:, level, :] = value.astype(np.float32).astype(ml_dtypes.bfloat16)
        before, now = now, value
    return table


def quadrature(nlat, nlon):
    theta = math.pi * (np.arange(nlat) + 0.5) / nlat
    return (math.pi / nlat * np.sin(theta) * (2.0 * math.pi / nlon)).astype(np.float32)


def fourier_tables(nlon, modes, lat_count):
    phase = np.arange(nlon)[:, None] * np.arange(modes)[None, :] % nlon
    angle = 2.0 * math.pi / nlon * phase
    cosine = np.cos(angle).astype(np.float32).astype(ml_dtypes.bfloat16)
    sine = np.sin(angle).astype(np.float32).astype(ml_dtypes.bfloat16)
    pair = np.stack([cosine, -sine]).reshape(2, nlon, modes // lat_count, lat_count)
    plain = pair.transpose(1, 2, 0, 3).reshape(nlon, 2 * modes)
    factor = np.where(np.arange(modes) == 0, 1.0, 2.0).astype(np.float32)
    doubled = np.stack([cosine, -sine]).astype(np.float32) * factor
    doubled = doubled.astype(ml_dtypes.bfloat16).reshape(2, nlon, modes // lat_count, lat_count)
    doubled = doubled.transpose(1, 2, 0, 3).reshape(nlon, 2 * modes)
    return plain, doubled


def gelu_parts(values):
    half = 0.5 * (1.0 + lax.erf(values * (1.0 / math.sqrt(2.0))))
    slope = half + values * jnp.exp(-0.5 * values * values) * (1.0 / math.sqrt(2.0 * math.pi))
    return values * half, slope


def swap_blocks(values, axis):
    return lax.all_to_all(values, axis, split_axis=0, concat_axis=0, tiled=True)


def body(table_all, plain, doubled, quad, grid, cotangent, spectral_weight, w_in, w_out):
    lat_count = lax.axis_size("lat")
    lon_count = lax.axis_size("lon")
    lat_index = lax.axis_index("lat")
    lon_index = lax.axis_index("lon")
    rows, lon_rows, width = grid.shape
    quarter = width // lon_count
    total_lat = rows * lat_count
    total_lon = lon_rows * lon_count
    parts = 2 * rows
    packed = parts * quarter
    tables = lax.dynamic_index_in_dim(table_all, lat_index, 0, keepdims=False)
    local_quad = lax.dynamic_slice_in_dim(quad, lat_index * rows, rows)
    quad_lanes = jnp.repeat(local_quad, quarter)[None, :]
    first_half = (jnp.arange(packed) < packed // 2)[None, :]

    def lon_split(values):
        values = values.reshape(rows, lon_rows, lon_count, quarter).transpose(2, 1, 0, 3)
        got = swap_blocks(values.reshape(lon_count, lon_rows, rows * quarter), "lon")
        return got.reshape(total_lon, rows * quarter)

    def lon_merge(values):
        got = swap_blocks(values.reshape(lon_count, lon_rows, rows * quarter), "lon")
        got = got.reshape(lon_count, lon_rows, rows, quarter).transpose(2, 1, 0, 3)
        return got.reshape(rows * lon_rows, width)

    def to_fourier(values, matrix, scale):
        out = lax.dot_general(
            matrix, values, (((0,), (0,)), ((), ())), preferred_element_type=jnp.float32
        )
        if scale is not None:
            out = out * scale
        out = out.astype(jnp.bfloat16).reshape(parts, lat_count, rows, quarter)
        return out.transpose(1, 2, 0, 3).reshape(lat_count, rows, packed)

    def from_fourier(values, matrix, scale):
        values = values.reshape(lat_count, rows, parts, quarter).transpose(2, 0, 1, 3)
        values = values.reshape(parts * lat_count, rows * quarter)
        out = jnp.dot(matrix, values, preferred_element_type=jnp.float32)
        if scale is not None:
            out = out * scale
        return out.astype(jnp.bfloat16)

    def analyze(values):
        values = values.reshape(total_lat, packed)
        low = jnp.dot(tables[0], values, preferred_element_type=jnp.float32)
        high = jnp.dot(tables[1], values, preferred_element_type=jnp.float32)
        out = jnp.where(first_half, low, high).astype(jnp.bfloat16)
        return out.reshape(lat_count, rows, packed)

    def synthesize(values):
        values = values.reshape(total_lat, packed)
        dims = (((0,), (0,)), ((), ()))
        low = lax.dot_general(tables[0], values, dims, preferred_element_type=jnp.float32)
        high = lax.dot_general(tables[1], values, dims, preferred_element_type=jnp.float32)
        out = jnp.where(first_half, low, high).astype(jnp.bfloat16)
        return out.reshape(lat_count, rows, packed)

    def block_weights(weights):
        w_re, w_im = weights[:, 0], weights[:, 1]
        top = jnp.concatenate([w_re, w_im], axis=3)
        low = jnp.concatenate([-w_im, w_re], axis=3)
        one = jnp.concatenate([top, low], axis=2)
        zero = jnp.zeros_like(one)
        return jnp.concatenate(
            [jnp.concatenate([one, zero], axis=3), jnp.concatenate([zero, one], axis=3)], axis=2
        )

    with jax.named_scope("weights"):
        by_input = spectral_weight.reshape(2, rows, lon_count, quarter, quarter)
        by_input = by_input.transpose(2, 0, 1, 3, 4)
        mix_weights = block_weights(by_input)
        unmix_weights = block_weights(swap_blocks(by_input, "lon"))
    with jax.named_scope("forward_analysis"):
        spread = lon_split(grid)
        four = to_fourier(spread, plain, quad_lanes)
        spectrum = swap_blocks(analyze(swap_blocks(four, "lat")), "lat")
    with jax.named_scope("mix"):
        piece = lax.all_gather(spectrum, "lon", axis=0)
        mixed = jnp.einsum(
            "xplk,xlkn->pln", piece, mix_weights, preferred_element_type=jnp.float32
        ).astype(jnp.bfloat16)
    with jax.named_scope("forward_synthesis"):
        fields = swap_blocks(synthesize(swap_blocks(mixed, "lat")), "lat")
        wave_rows = lon_merge(from_fourier(fields, doubled, None))
    with jax.named_scope("pointwise"):
        flat_grid = grid.reshape(-1, width)
        hidden = (flat_grid.astype(jnp.float32) + wave_rows.astype(jnp.float32)).astype(
            jnp.bfloat16
        )
        back = cotangent.reshape(-1, width)
        act_grad = lax.dot_general(
            back, w_out, (((1,), (1,)), ((), ())), preferred_element_type=jnp.float32
        )
        pre = jnp.dot(hidden, w_in, preferred_element_type=jnp.float32)
        value, slope = gelu_parts(pre)
        act = value.astype(jnp.bfloat16)
        pre_grad = (act_grad * slope).astype(jnp.bfloat16)
        hidden_grad = (
            back.astype(jnp.float32)
            + lax.dot_general(
                pre_grad, w_in, (((1,), (1,)), ((), ())), preferred_element_type=jnp.float32
            )
        ).astype(jnp.bfloat16)
        block_output = (
            hidden.astype(jnp.float32) + jnp.dot(act, w_out, preferred_element_type=jnp.float32)
        ).astype(jnp.bfloat16)
    with jax.named_scope("pointwise_weights"):
        over_rows = (((0,), (0,)), ((), ()))
        out_part = lax.dot_general(act, back, over_rows, preferred_element_type=jnp.float32)
        in_part = lax.dot_general(hidden, pre_grad, over_rows, preferred_element_type=jnp.float32)
        in_part = in_part.reshape(out_part.shape)
        even = lat_index % 2 == 0
        keep = jnp.where(even, in_part, out_part)
        give = jnp.where(even, out_part, in_part)
        partner = [(i, i ^ 1) for i in range(lat_count)]
        keep = keep + lax.ppermute(give, "lat", partner)
        keep = lax.psum(keep, "lon").reshape(lat_count, -1)
        chunk = keep.shape[1] // lon_count
        keep = lax.dynamic_slice_in_dim(keep, lon_index * chunk, chunk, axis=1)
        keep = keep.astype(jnp.bfloat16)
        room = -(-chunk // (rows * 128)) * rows * 128
        extra = jnp.pad(keep, ((0, 0), (0, room - chunk))).reshape(lat_count, rows, -1)
    with jax.named_scope("backward_analysis"):
        grad_spread = lon_split(hidden_grad.reshape(grid.shape))
        field_grad = to_fourier(grad_spread, doubled, None)
        mixed_grad = swap_blocks(analyze(swap_blocks(field_grad, "lat")), "lat")
    with jax.named_scope("unmix"):
        piece = lax.all_gather(mixed_grad, "lon", axis=0)
        spectrum_grad = jnp.einsum(
            "xplk,xlnk->pln", piece, unmix_weights, preferred_element_type=jnp.float32
        ).astype(jnp.bfloat16)
        outer = jnp.einsum("pln,xplk->xlnk", spectrum, piece, preferred_element_type=jnp.float32)
        half = packed // 2
        outer = outer[:, :, :half, :half] + outer[:, :, half:, half:]
        grad_re = outer[:, :, :quarter, :quarter] + outer[:, :, quarter:, quarter:]
        grad_im = outer[:, :, :quarter, quarter:] - outer[:, :, quarter:, :quarter]
        grad_spectral = jnp.stack([grad_re, grad_im]).transpose(0, 2, 3, 1, 4)
        grad_spectral = grad_spectral.reshape(2, rows, quarter, width)
    with jax.named_scope("backward_synthesis"):
        four_grad = synthesize(swap_blocks(spectrum_grad, "lat"))
        got = swap_blocks(jnp.concatenate([four_grad, extra], axis=2), "lat")
        sums = got[:, :, packed:].reshape(lat_count // 2, 2, room)[:, :, :chunk]
        sums = jnp.sum(sums.astype(jnp.float32), axis=0)
        wave_grad = lon_merge(from_fourier(got[:, :, :packed], plain, quad_lanes))
        grad_input = (hidden_grad.astype(jnp.float32) + wave_grad.astype(jnp.float32)).astype(
            jnp.bfloat16
        )
    return (
        block_output.reshape(grid.shape),
        grad_input.reshape(grid.shape),
        grad_spectral,
        sums[0],
        sums[1],
    )


def solution(mesh):
    in_specs = (P("lat", "lon", None), P("lat", "lon", None), P(None, "lat", None, "lon"), P(), P())
    out_specs = (
        P("lat", "lon", None),
        P("lat", "lon", None),
        P(None, "lat", "lon", None),
        P(("lat", "lon")),
        P(("lat", "lon")),
    )
    lat_count = mesh.shape["lat"]

    def call(grid, cotangent, spectral_weight, w_in, w_out):
        nlat, nlon, _ = grid.shape
        table = legendre_table(nlat).reshape(nlat // lat_count, lat_count, nlat, nlat)
        table = np.ascontiguousarray(table.swapaxes(0, 1))
        plain, doubled = fourier_tables(nlon, nlat, lat_count)
        quad = quadrature(nlat, nlon)
        mapped = jax.shard_map(
            body,
            mesh=mesh,
            in_specs=(P(), P(), P(), P()) + in_specs,
            out_specs=out_specs,
            check_vma=False,
        )
        return mapped(table, plain, doubled, quad, grid, cotangent, spectral_weight, w_in, w_out)

    return call
```

time: 920 us -> 356 us (0.39)
  the two profiles are of different devices: /device:TPU:8 before, /device:TPU:32 now
where the time goes in v1:
time: 356 us; the launch traced here: 355 us
  blocking collectives  130 us (37%)
  waiting for transfers between devices  108 us (30%)
  starting transfers between devices  74 us (21%)
  matrix products  19.7 us (6%)
  local copies, waits for them, and re-layouts  15.6 us (4%)
  other arithmetic  6.04 us (2%)
    all_to_all x9, waiting for transfers between devices, swap_blocks(): return lax.all_to_all(values, axis, split_axis=0, concat_axis=0, tiled=True)  108 us
    all_to_all x9, starting transfers between devices, swap_blocks(): return lax.all_to_all(values, axis, split_axis=0, concat_axis=0, tiled=True)  72 us
    all_to_all x4, blocking collectives, swap_blocks(): return lax.all_to_all(values, axis, split_axis=0, concat_axis=0, tiled=True)  69 us
    psum x1, blocking collectives, body(): keep = lax.psum(keep, 'lon').reshape(lat_count, -1)  31.8 us
    all_gather x1, blocking collectives, body(): piece = lax.all_gather(mixed_grad, 'lon', axis=0)  14.5 us
    all_gather x1, blocking collectives, body(): piece = lax.all_gather(spectrum, 'lon', axis=0)  14.3 us
  transfers between devices with their start and end apart: 10, of which 8 were waited for; matrix products, arithmetic and copies ran while one was open for 5% of the time, Pallas kernels for 0%

profile of v1, /device:TPU:32, one launch (start us, length us, event | category | flops | bytes accessed | tf_op | source)
XLA Modules:
  0.0 354.9 jit_solution(12413179400665526800)
XLA Ops:
  0.6 1.1 copy.105
  1.8 0.7 copy.106
  2.5 4.3 %all-to-all-start = ((bf16[4,128,192]{1,2,0:T(8,128)(2,1)}), bf16[4,128,192]{1,2,0:T(8,128)(2,1)S(1)}, u32[]{:S(2)}, u32[]{:S(2)}) async-start(bf16[4,128,192]{1,2,0:T(8,128)(2,1)} %bitcast.7), calls=%async_computation | async-start | bytes 393216 | tf_op jit(solution)/shard_map/forward_analysis/all_to_all | solution.py:63
  6.8 0.8 dynamic_slice.11
  7.7 5.4 %all-to-all-done = bf16[4,128,192]{1,2,0:T(8,128)(2,1)S(1)} async-done(((bf16[4,128,192]{1,2,0:T(8,128)(2,1)}), bf16[4,128,192]{1,2,0:T(8,128)(2,1)S(1)}, u32[]{:S(2)}, u32[]{:S(2)}) %all-to-all-start) | async-done | bytes 196640 | tf_op jit(solution)/shard_map/forward_analysis/all_to_all | solution.py:63
  13.1 1.3 fusion.40
  14.5 0.8 copy.109
  15.4 19.2 %all-to-all-start.1 = ((bf16[128,2,384]{2,1,0:T(2,128)(2,1)}), bf16[128,2,384]{2,1,0:T(2,128)(2,1)S(1)}, u32[]{:S(2)}, u32[]{:S(2)}) async-start(bf16[128,2,384]{2,1,0:T(2,128)(2,1)} %copy.109), calls=%async_computation.1 | async-start | bytes 393216 | tf_op jit(solution)/shard_map/forward_analysis/all_to_all | solution.py:63
  34.6 19.8 %all-to-all-done.1 = bf16[128,2,384]{2,1,0:T(2,128)(2,1)S(1)} async-done(((bf16[128,2,384]{2,1,0:T(2,128)(2,1)}), bf16[128,2,384]{2,1,0:T(2,128)(2,1)S(1)}, u32[]{:S(2)}, u32[]{:S(2)}) %all-to-all-start.1) | async-done | bytes 196640 | tf_op jit(solution)/shard_map/forward_analysis/all_to_all | solution.py:63
  54.5 1.1 fusion.69
  55.6 1.1 fusion.29
  56.7 0.8 reshape.140
  57.5 6.2 %all-to-all-start.2 = ((bf16[128,2,384]{2,1,0:T(2,128)(2,1)}), bf16[128,2,384]{2,1,0:T(2,128)(2,1)S(1)}, u32[]{:S(2)}, u32[]{:S(2)}) async-start(bf16[128,2,384]{2,1,0:T(2,128)(2,1)} %reshape.140), calls=%async_computation.2 | async-start | bytes 393216 | tf_op jit(solution)/shard_map/forward_analysis/all_to_all | solution.py:63
  64.1 0.4 maximum_maximum_fusion
  64.5 19.0 %all-to-all-done.2 = bf16[128,2,384]{2,1,0:T(2,128)(2,1)S(1)} async-done(((bf16[128,2,384]{2,1,0:T(2,128)(2,1)}), bf16[128,2,384]{2,1,0:T(2,128)(2,1)S(1)}, u32[]{:S(2)}, u32[]{:S(2)}) %all-to-all-start.2) | async-done | bytes 196640 | tf_op jit(solution)/shard_map/forward_analysis/all_to_all | solution.py:63
  83.6 14.3 %all-gather = bf16[512,2,384]{2,1,0:T(2,128)(2,1)S(1)} all-gather(bf16[128,2,384]{2,1,0:T(2,128)(2,1)S(1)} %all-to-all-done.2), channel_id=2, replica_groups=mesh['lat'=128,'lon'=4] {'lon'}, dimensions={0}, use_global_device_ids=true | all-gather | bytes 983040 | tf_op jit(solution)/shard_map/mix/all_gather | solution.py:144
  98.0 0.8 fusion.44
  99.0 25.6 %all_to_all.65 = bf16[128,2,384]{2,1,0:T(2,128)(2,1)S(1)} all-to-all(bf16[128,2,384]{2,1,0:T(2,128)(2,1)S(1)} %copy.111), channel_id=1, replica_groups=mesh['lat'=128,'lon'=4] {'lat'}, dimensions={0} | all-to-all | bytes 393216 | tf_op jit(solution)/shard_map/forward_synthesis/all_to_all | solution.py:63
  124.7 1.2 fusion.68
  125.8 1.2 fusion.30
  127.1 25.8 %all_to_all.66 = bf16[128,2,384]{2,1,0:T(2,128)(2,1)S(1)} all-to-all(bf16[128,2,384]{2,1,0:T(2,128)(2,1)S(1)} %reshape.142), channel_id=1, replica_groups=mesh['lat'=128,'lon'=4] {'lat'}, dimensions={0} | all-to-all | bytes 393216 | tf_op jit(solution)/shard_map/forward_synthesis/all_to_all | solution.py:63
  153.2 0.3 fusion.42
  153.6 8.9 %all_to_all.67 = bf16[4,128,192]{1,2,0:T(8,128)(2,1)S(1)} all-to-all(bf16[4,128,192]{1,2,0:T(8,128)(2,1)S(1)} %bitcast.182), channel_id=1, replica_groups=mesh['lat'=128,'lon'=4] {'lon'}, dimensions={0} | all-to-all | bytes 393216 | tf_op jit(solution)/shard_map/forward_synthesis/all_to_all | solution.py:63
  163.2 1.1 multiply_convert_fusion
  164.3 0.4 fusion.18
  164.8 0.4 fusion.28
  165.4 8.7 %all_to_all.68 = bf16[4,128,192]{1,2,0:T(8,128)(2,1)S(1)} all-to-all(bf16[4,128,192]{1,2,0:T(8,128)(2,1)S(1)} %bitcast.184), channel_id=1, replica_groups=mesh['lat'=128,'lon'=4] {'lon'}, dimensions={0} | all-to-all | bytes 393216 | tf_op jit(solution)/shard_map/backward_analysis/all_to_all | solution.py:63
  174.5 0.8 copy.124
  175.3 6.5 %all-to-all-start.8 = ((bf16[128,2,384]{2,1,0:T(2,128)(2,1)}), bf16[128,2,384]{2,1,0:T(2,128)(2,1)}, u32[]{:S(2)}, u32[]{:S(2)}) async-start(bf16[128,2,384]{2,1,0:T(2,128)(2,1)} %copy.124), calls=%async_computation.8 | async-start | bytes 393216 | tf_op jit(solution)/shard_map/backward_analysis/all_to_all | solution.py:63
  181.9 0.4 fusion.87
  182.5 2.5 broadcast_select_fusion
  185.0 2.0 collective-permute-start
  187.0 0.8 copy.177
  187.8 13.6 %all-to-all-done.8 = bf16[128,2,384]{2,1,0:T(2,128)(2,1)} async-done(((bf16[128,2,384]{2,1,0:T(2,128)(2,1)}), bf16[128,2,384]{2,1,0:T(2,128)(2,1)}, u32[]{:S(2)}, u32[]{:S(2)}) %all-to-all-start.8) | async-done | bytes 196640 | tf_op jit(solution)/shard_map/backward_analysis/all_to_all | solution.py:63
  201.4 3.5 all-to-all-start.6
  204.9 1.0 reshape.153
  205.9 1.1 fusion.67
  207.0 1.1 fusion.31
  208.2 0.8 reshape.154
  208.9 4.6 %all-to-all-done.6 = bf16[4,2,2,96,96]{3,4,2,1,0:T(8,128)(2,1)S(1)} async-done(((bf16[4,2,2,96,96]{3,4,2,1,0:T(8,128)(2,1)}), bf16[4,2,2,96,96]{3,4,2,1,0:T(8,128)(2,1)S(1)}, u32[]{:S(2)}, u32[]{:S(2)}) %all-to-all-start.6) | async-done | bytes 294944 | tf_op jit(solution)/shard_map/weights/all_to_all | solution.py:63
  213.5 6.3 %all-to-all-start.9 = ((bf16[128,2,384]{2,1,0:T(2,128)(2,1)}), bf16[128,2,384]{2,1,0:T(2,128)(2,1)}, u32[]{:S(2)}, u32[]{:S(2)}) async-start(bf16[128,2,384]{2,1,0:T(2,128)(2,1)} %reshape.154), calls=%async_computation.9 | async-start | bytes 393216 | tf_op jit(solution)/shard_map/backward_analysis/all_to_all | solution.py:63
  220.2 1.2 maximum_maximum_fusion.1
  221.5 1.4 select_add_fusion
  223.2 16.2 %all-to-all-done.9 = bf16[128,2,384]{2,1,0:T(2,128)(2,1)} async-done(((bf16[128,2,384]{2,1,0:T(2,128)(2,1)}), bf16[128,2,384]{2,1,0:T(2,128)(2,1)}, u32[]{:S(2)}, u32[]{:S(2)}) %all-to-all-start.9) | async-done | bytes 196640 | tf_op jit(solution)/shard_map/backward_analysis/all_to_all | solution.py:63
  239.4 14.5 %all-gather.1 = bf16[512,2,384]{2,1,0:T(2,128)(2,1)S(1)} all-gather(bf16[128,2,384]{2,1,0:T(2,128)(2,1)} %all-to-all-done.9), channel_id=3, replica_groups=mesh['lat'=128,'lon'=4] {'lon'}, dimensions={0}, use_global_device_ids=true | all-gather | bytes 983040 | tf_op jit(solution)/shard_map/unmix/all_gather | solution.py:194
  254.1 0.8 fusion.47
  254.8 0.8 copy.126
  255.7 5.9 %all-to-all-start.10 = ((bf16[128,2,384]{2,1,0:T(2,128)(2,1)}), bf16[128,2,384]{2,1,0:T(2,128)(2,1)S(1)}, u32[]{:S(2)}, u32[]{:S(2)}) async-start(bf16[128,2,384]{2,1,0:T(2,128)(2,1)} %copy.126), calls=%async_computation.10 | async-start | bytes 393216 | tf_op jit(solution)/shard_map/backward_synthesis/all_to_all | solution.py:63
  261.6 31.8 %all-reduce.6 = bf16[128,2304]{1,0:T(8,128)(2,1)S(1)} all-reduce(f32[128,2304]{1,0:T(8,128)S(1)} %reshape.158), channel_id=1, replica_groups=mesh['lat'=128,'lon'=4] {'lon'}, use_global_device_ids=true, to_apply=%region_0.1 | all-reduce | flops 294912 | bytes 1769472 | tf_op jit(solution)/shard_map/pointwise_weights/psum | solution.py:183
  293.8 1.2 fusion.66
  295.0 1.2 fusion.32
  296.2 1.1 pad_maximum_fusion.1
  297.3 16.1 %all-to-all-start.11 = ((bf16[128,2,768]{2,1,0:T(2,128)(2,1)}), bf16[128,2,768]{2,1,0:T(2,128)(2,1)S(1)}, u32[]{:S(2)}, u32[]{:S(2)}) async-start(bf16[128,2,768]{2,1,0:T(2,128)(2,1)} %pad_maximum_fusion.1), calls=%async_computation.11 | async-start | bytes 786432 | tf_op jit(solution)/shard_map/backward_synthesis/all_to_all | solution.py:63
  313.5 1.0 fusion.27
  314.5 0.8 convolution_bitcast_fusion
  315.4 0.5 slice_add_fusion
  316.2 1.1 copy.134
  317.3 24.0 %all-to-all-done.11 = bf16[128,2,768]{2,1,0:T(2,128)(2,1)S(1)} async-done(((bf16[128,2,768]{2,1,0:T(2,128)(2,1)}), bf16[128,2,768]{2,1,0:T(2,128)(2,1)S(1)}, u32[]{:S(2)}, u32[]{:S(2)}) %all-to-all-start.11) | async-done | bytes 393248 | tf_op jit(solution)/shard_map/backward_synthesis/all_to_all | solution.py:63
  342.0 0.3 fusion.41
  342.4 0.7 copy.179
  343.1 3.9 %all-to-all-start.12 = ((bf16[4,128,192]{1,2,0:T(8,128)(2,1)}), bf16[4,128,192]{1,2,0:T(8,128)(2,1)S(1)}, u32[]{:S(2)}, u32[]{:S(2)}) async-start(bf16[4,128,192]{1,2,0:T(8,128)(2,1)} %bitcast.166), calls=%async_computation.12 | async-start | bytes 393216 | tf_op jit(solution)/shard_map/backward_synthesis/all_to_all | solution.py:63
  347.2 0.6 slice_reduce_fusion
  347.8 5.9 %all-to-all-done.12 = bf16[4,128,192]{1,2,0:T(8,128)(2,1)S(1)} async-done(((bf16[4,128,192]{1,2,0:T(8,128)(2,1)}), bf16[4,128,192]{1,2,0:T(8,128)(2,1)S(1)}, u32[]{:S(2)}, u32[]{:S(2)}) %all-to-all-start.12) | async-done | bytes 196640 | tf_op jit(solution)/shard_map/backward_synthesis/all_to_all | solution.py:63
  354.2 0.7 add_convert_fusion
  (89 shorter events, 5.7 us)
Async XLA Ops:
  0.6 162.5 %copy-start = (bf16[384,768]{1,0:T(8,128)(2,1)S(1)}, bf16[384,768]{1,0:T(8,128)(2,1)}, u32[]{:S(2)}) copy-start(bf16[384,768]{1,0:T(8,128)(2,1)} %param.12) | copy-start | bytes 1769476
  2.5 10.6 %all-to-all-start = ((bf16[4,128,192]{1,2,0:T(8,128)(2,1)}), bf16[4,128,192]{1,2,0:T(8,128)(2,1)S(1)}, u32[]{:S(2)}, u32[]{:S(2)}) async-start(bf16[4,128,192]{1,2,0:T(8,128)(2,1)} %bitcast.7), calls=%async_computation | async-start | bytes 393216 | tf_op jit(solution)/shard_map/forward_analysis/all_to_all | solution.py:63
  7.7 56.0 %copy-start.18 = (bf16[2,2,384,96]{2,3,1,0:T(8,128)(2,1)S(1)}, bf16[2,2,384,96]{2,3,1,0:T(8,128)(2,1)}, u32[]{:S(2)}) copy-start(bf16[2,2,384,96]{2,3,1,0:T(8,128)(2,1)} %param.11) | copy-start | bytes 884740
  15.4 39.0 %all-to-all-start.1 = ((bf16[128,2,384]{2,1,0:T(2,128)(2,1)}), bf16[128,2,384]{2,1,0:T(2,128)(2,1)S(1)}, u32[]{:S(2)}, u32[]{:S(2)}) async-start(bf16[128,2,384]{2,1,0:T(2,128)(2,1)} %copy.109), calls=%async_computation.1 | async-start | bytes 393216 | tf_op jit(solution)/shard_map/forward_analysis/all_to_all | solution.py:63
  57.5 26.1 %all-to-all-start.2 = ((bf16[128,2,384]{2,1,0:T(2,128)(2,1)}), bf16[128,2,384]{2,1,0:T(2,128)(2,1)S(1)}, u32[]{:S(2)}, u32[]{:S(2)}) async-start(bf16[128,2,384]{2,1,0:T(2,128)(2,1)} %reshape.140), calls=%async_computation.2 | async-start | bytes 393216 | tf_op jit(solution)/shard_map/forward_analysis/all_to_all | solution.py:63
  64.0 34.0 %copy-start.2 = (bf16[2,2,4,96,96]{3,2,4,1,0:T(4,128)(2,1)}, bf16[2,2,4,96,96]{3,2,4,1,0:T(4,128)(2,1)S(1)}, u32[]{:S(2)}) copy-start(bf16[2,2,4,96,96]{3,2,4,1,0:T(4,128)(2,1)S(1)} %reshape.133) | copy-start | bytes 884740
  83.6 14.5 %copy-start.9 = (bf16[128,2,384]{2,1,0:T(2,128)(2,1)}, bf16[128,2,384]{2,1,0:T(2,128)(2,1)S(1)}, u32[]{:S(2)}) copy-start(bf16[128,2,384]{2,1,0:T(2,128)(2,1)S(1)} %all-to-all-done.2) | copy-start | bytes 589828
  98.8 54.4 %copy-start.7 = (bf16[512,512]{1,0:T(8,128)(2,1)S(1)}, bf16[512,512]{1,0:T(8,128)(2,1)}, u32[]{:S(2)}) copy-start(bf16[512,512]{1,0:T(8,128)(2,1)} %constant.61.clone) | copy-start | bytes 1572868
  153.1 10.0 %copy-start.14 = (bf16[2,128,384]{2,1,0:T(8,128)(2,1)S(1)}, bf16[2,128,384]{2,1,0:T(8,128)(2,1)}, u32[]{:S(2)}) copy-start(bf16[2,128,384]{2,1,0:T(8,128)(2,1)} %param.9) | copy-start | bytes 589828
  162.5 1.8 copy-start.13
  162.6 1.8 copy-start.16
  163.2 18.7 %copy-start.5 = (bf16[256,384]{1,0:T(8,128)(2,1)}, bf16[256,384]{1,0:T(8,128)(2,1)S(1)}, u32[]{:S(2)}) copy-start(bf16[256,384]{1,0:T(8,128)(2,1)S(1)} %fusion.56) | copy-start | bytes 589828
  165.2 16.7 %copy-start.11 = (bf16[256,384]{1,0:T(8,128)(2,1)}, bf16[256,384]{1,0:T(8,128)(2,1)S(1)}, u32[]{:S(2)}) copy-start(bf16[256,384]{1,0:T(8,128)(2,1)S(1)} %fusion.28) | copy-start | bytes 589828
  175.3 26.1 %all-to-all-start.8 = ((bf16[128,2,384]{2,1,0:T(2,128)(2,1)}), bf16[128,2,384]{2,1,0:T(2,128)(2,1)}, u32[]{:S(2)}, u32[]{:S(2)}) async-start(bf16[128,2,384]{2,1,0:T(2,128)(2,1)} %copy.124), calls=%async_computation.8 | async-start | bytes 393216 | tf_op jit(solution)/shard_map/backward_analysis/all_to_all | solution.py:63
  182.4 4.6 %copy-start.3 = (bf16[2,2,4,96,96]{3,2,4,1,0:T(4,128)(2,1)S(1)}, bf16[2,2,4,96,96]{3,2,4,1,0:T(4,128)(2,1)}, u32[]{:S(2)}) copy-start(bf16[2,2,4,96,96]{3,2,4,1,0:T(4,128)(2,1)} %copy-done.2) | copy-start | bytes 884740
  185.0 36.5 %collective-permute-start = (f32[768,384]{1,0:T(8,128)}, f32[768,384]{1,0:T(8,128)}, u32[]{:S(2)}, u32[]{:S(2)}) collective-permute-start(f32[768,384]{1,0:T(8,128)} %get-tuple-element.42), channel_id=1, source_target_pairs={{0,4},{4,0},{8,12},{12,8},{16,20},{20,16},{24,28},{28,24},{32,36},... | collective-permute-start | bytes 3538952 | tf_op jit(solution)/shard_map/pointwise_weights/ppermute | solution.py:182
  201.4 12.1 %all-to-all-start.6 = ((bf16[4,2,2,96,96]{3,4,2,1,0:T(8,128)(2,1)}), bf16[4,2,2,96,96]{3,4,2,1,0:T(8,128)(2,1)S(1)}, u32[]{:S(2)}, u32[]{:S(2)}) async-start(bf16[4,2,2,96,96]{3,4,2,1,0:T(8,128)(2,1)} %bitcast.164), calls=%async_computation.6 | async-start | bytes 786432 | tf_op jit(solution)/shard_map/weights/all_to_all | solution.py:63
  213.5 25.9 %all-to-all-start.9 = ((bf16[128,2,384]{2,1,0:T(2,128)(2,1)}), bf16[128,2,384]{2,1,0:T(2,128)(2,1)}, u32[]{:S(2)}, u32[]{:S(2)}) async-start(bf16[128,2,384]{2,1,0:T(2,128)(2,1)} %reshape.154), calls=%async_computation.9 | async-start | bytes 393216 | tf_op jit(solution)/shard_map/backward_analysis/all_to_all | solution.py:63
  222.9 31.1 %copy-start.15 = (bf16[4,2,192,192]{3,2,0,1:T(8,128)(2,1)S(1)}, bf16[4,2,192,192]{3,2,0,1:T(8,128)(2,1)}, u32[]{:S(2)}) copy-start(bf16[4,2,192,192]{3,2,0,1:T(8,128)(2,1)} %maximum_maximum_fusion.1) | copy-start | bytes 1769476
  255.7 38.0 %all-to-all-start.10 = ((bf16[128,2,384]{2,1,0:T(2,128)(2,1)}), bf16[128,2,384]{2,1,0:T(2,128)(2,1)S(1)}, u32[]{:S(2)}, u32[]{:S(2)}) async-start(bf16[128,2,384]{2,1,0:T(2,128)(2,1)} %copy.126), calls=%async_computation.10 | async-start | bytes 393216 | tf_op jit(solution)/shard_map/backward_synthesis/all_to_all | solution.py:63
  293.4 20.1 %copy-start.4 = (bf16[256,768]{1,0:T(8,128)(2,1)S(1)}, bf16[256,768]{1,0:T(8,128)(2,1)}, u32[]{:S(2)}) copy-start(bf16[256,768]{1,0:T(8,128)(2,1)} %get-tuple-element.40) | copy-start | bytes 1179652
  293.4 20.1 %copy-start.6 = (bf16[256,384]{1,0:T(8,128)(2,1)S(1)}, bf16[256,384]{1,0:T(8,128)(2,1)}, u32[]{:S(2)}) copy-start(bf16[256,384]{1,0:T(8,128)(2,1)} %copy-done.5) | copy-start | bytes 589828
  293.4 20.0 %copy-start.17 = (bf16[768,384]{1,0:T(8,128)(2,1)S(1)}, bf16[768,384]{1,0:T(8,128)(2,1)}, u32[]{:S(2)}) copy-start(bf16[768,384]{1,0:T(8,128)(2,1)} %param.13) | copy-start | bytes 1769476
  293.8 20.8 %copy-start.10 = (bf16[128,2,384]{2,1,0:T(2,128)(2,1)S(1)}, bf16[128,2,384]{2,1,0:T(2,128)(2,1)}, u32[]{:S(2)}) copy-start(bf16[128,2,384]{2,1,0:T(2,128)(2,1)} %copy-done.9) | copy-start | bytes 589828
  297.3 43.9 %all-to-all-start.11 = ((bf16[128,2,768]{2,1,0:T(2,128)(2,1)}), bf16[128,2,768]{2,1,0:T(2,128)(2,1)S(1)}, u32[]{:S(2)}, u32[]{:S(2)}) async-start(bf16[128,2,768]{2,1,0:T(2,128)(2,1)} %pad_maximum_fusion.1), calls=%async_computation.11 | async-start | bytes 786432 | tf_op jit(solution)/shard_map/backward_synthesis/all_to_all | solution.py:63
  316.1 25.9 %copy-start.8 = (bf16[512,512]{1,0:T(8,128)(2,1)S(1)}, bf16[512,512]{1,0:T(8,128)(2,1)}, u32[]{:S(2)}) copy-start(bf16[512,512]{1,0:T(8,128)(2,1)} %constant.60.clone) | copy-start | bytes 1572868
  341.9 12.3 %copy-start.12 = (bf16[256,384]{1,0:T(8,128)(2,1)S(1)}, bf16[256,384]{1,0:T(8,128)(2,1)}, u32[]{:S(2)}) copy-start(bf16[256,384]{1,0:T(8,128)(2,1)} %copy-done.11) | copy-start | bytes 589828
  342.0 12.9 %copy-start.1 = (bf16[384,768]{1,0:T(8,128)(2,1)S(1)}, bf16[384,768]{1,0:T(8,128)(2,1)}, u32[]{:S(2)}) copy-start(bf16[384,768]{1,0:T(8,128)(2,1)} %param.12) | copy-start | bytes 1769476
  343.1 10.6 %all-to-all-start.12 = ((bf16[4,128,192]{1,2,0:T(8,128)(2,1)}), bf16[4,128,192]{1,2,0:T(8,128)(2,1)S(1)}, u32[]{:S(2)}, u32[]{:S(2)}) async-start(bf16[4,128,192]{1,2,0:T(8,128)(2,1)} %bitcast.166), calls=%async_computation.12 | async-start | bytes 393216 | tf_op jit(solution)/shard_map/backward_synthesis/all_to_all | solution.py:63

commit v2 on v1

--- a/solution.py
+++ b/solution.py
@@ -63,6 +63,32 @@
     return lax.all_to_all(values, axis, split_axis=0, concat_axis=0, tiled=True)
 
 
+def lon_exchange(blocks, lon_index, lon_count):
+    doubled = jnp.concatenate([blocks, blocks])
+    moved = [lax.dynamic_index_in_dim(blocks, lon_index, 0, keepdims=False)]
+    for shift in range(1, lon_count):
+        block = lax.dynamic_index_in_dim(doubled, lon_index + shift, 0, keepdims=False)
+        pairs = [(i, (i + shift) % lon_count) for i in range(lon_count)]
+        moved.append(lax.ppermute(block, "lon", pairs))
+    backwards = jnp.stack(moved[::-1] * 2)
+    first = lon_count - 1 - lon_index
+    return lax.dynamic_slice_in_dim(backwards, first, lon_count, 0)
+
+
+def halve(values, axis, index, mask, bit):
+    size = lax.axis_size(axis)
+    width = values.shape[-1] // 2
+    high = (index >> bit) & 1 == 1
+    keep = jnp.where(high, values[:, width:], values[:, :width])
+    give = jnp.where(high, values[:, :width], values[:, width:]).astype(jnp.bfloat16)
+    return keep, lax.ppermute(give, axis, [(i, i ^ mask) for i in range(size)])
+
+
+def add_swapped(pair):
+    keep, got = pair
+    return keep + got.astype(jnp.float32)
+
+
 def body(table_all, plain, doubled, quad, grid, cotangent, spectral_weight, w_in, w_out):
     lat_count = lax.axis_size("lat")
     lon_count = lax.axis_size("lon")
@@ -135,7 +161,7 @@
         by_input = spectral_weight.reshape(2, rows, lon_count, quarter, quarter)
         by_input = by_input.transpose(2, 0, 1, 3, 4)
         mix_weights = block_weights(by_input)
-        unmix_weights = block_weights(swap_blocks(by_input, "lon"))
+        unmix_weights = block_weights(lon_exchange(by_input, lon_index, lon_count))
     with jax.named_scope("forward_analysis"):
         spread = lon_split(grid)
         four = to_fourier(spread, plain, quad_lanes)
@@ -170,6 +196,13 @@
         block_output = (
             hidden.astype(jnp.float32) + jnp.dot(act, w_out, preferred_element_type=jnp.float32)
         ).astype(jnp.bfloat16)
+    with jax.named_scope("backward_analysis"):
+        grad_spread = lon_split(hidden_grad.reshape(grid.shape))
+        field_grad = to_fourier(grad_spread, doubled, None)
+        field_grad, hidden, pre_grad, act = lax.optimization_barrier(
+            (field_grad, hidden, pre_grad, act)
+        )
+        field_grad = swap_blocks(field_grad, "lat")
     with jax.named_scope("pointwise_weights"):
         over_rows = (((0,), (0,)), ((), ()))
         out_part = lax.dot_general(act, back, over_rows, preferred_element_type=jnp.float32)
@@ -177,19 +210,21 @@
         in_part = in_part.reshape(out_part.shape)
         even = lat_index % 2 == 0
         keep = jnp.where(even, in_part, out_part)
-        give = jnp.where(even, out_part, in_part)
-        partner = [(i, i ^ 1) for i in range(lat_count)]
-        keep = keep + lax.ppermute(give, "lat", partner)
-        keep = lax.psum(keep, "lon").reshape(lat_count, -1)
-        chunk = keep.shape[1] // lon_count
-        keep = lax.dynamic_slice_in_dim(keep, lon_index * chunk, chunk, axis=1)
-        keep = keep.astype(jnp.bfloat16)
-        room = -(-chunk // (rows * 128)) * rows * 128
-        extra = jnp.pad(keep, ((0, 0), (0, room - chunk))).reshape(lat_count, rows, -1)
+        give = jnp.where(even, out_part, in_part).astype(jnp.bfloat16)
+        got = lax.ppermute(give, "lat", [(i, i ^ 1) for i in range(lat_count)])
+        sums = add_swapped((keep, got)).reshape(lat_count, -1)
+        sums = halve(sums, "lon", lon_index, 3, 1)
     with jax.named_scope("backward_analysis"):
-        grad_spread = lon_split(hidden_grad.reshape(grid.shape))
-        field_grad = to_fourier(grad_spread, doubled, None)
-        mixed_grad = swap_blocks(analyze(swap_blocks(field_grad, "lat")), "lat")
+        field_grad, keep = lax.optimization_barrier((field_grad, sums[0]))
+        mixed_grad = analyze(field_grad)
+        mixed_grad, keep, got = lax.optimization_barrier((mixed_grad, keep, sums[1]))
+        mixed_grad = swap_blocks(mixed_grad, "lat")
+    with jax.named_scope("pointwise_weights"):
+        sums = halve(add_swapped((keep, got)), "lon", lon_index, 1, 0)
+        sums = halve(add_swapped(sums), "lat", lat_index, 6, 2)
+    with jax.named_scope("backward_analysis"):
+        mixed_grad, keep = lax.optimization_barrier((mixed_grad, sums[0]))
+        wait = sums[1]
     with jax.named_scope("unmix"):
         piece = lax.all_gather(mixed_grad, "lon", axis=0)
         spectrum_grad = jnp.einsum(
@@ -203,10 +238,18 @@
         grad_spectral = jnp.stack([grad_re, grad_im]).transpose(0, 2, 3, 1, 4)
         grad_spectral = grad_spectral.reshape(2, rows, quarter, width)
     with jax.named_scope("backward_synthesis"):
-        four_grad = synthesize(swap_blocks(spectrum_grad, "lat"))
+        spectrum_grad, keep, got = lax.optimization_barrier((spectrum_grad, keep, wait))
+        spectrum_grad = swap_blocks(spectrum_grad, "lat")
+        sums = halve(add_swapped((keep, got)), "lat", lat_index, 2, 1)
+        chunk = sums[0].shape[1]
+        room = -(-chunk // (rows * 128)) * rows * 128
+        extra = jnp.pad(add_swapped(sums).astype(jnp.bfloat16), ((0, 0), (0, room - chunk)))
+        spectrum_grad, extra = lax.optimization_barrier((spectrum_grad, extra))
+        four_grad = synthesize(spectrum_grad)
+        extra = extra.reshape(lat_count, rows, room // rows)
         got = swap_blocks(jnp.concatenate([four_grad, extra], axis=2), "lat")
-        sums = got[:, :, packed:].reshape(lat_count // 2, 2, room)[:, :, :chunk]
-        sums = jnp.sum(sums.astype(jnp.float32), axis=0)
+        sums = got[:, :, packed:].reshape(lat_count // 8, 4, 2, room)[..., :chunk]
+        sums = jnp.sum(sums.astype(jnp.float32), axis=0).swapaxes(0, 1).reshape(2, -1)
         wave_grad = lon_merge(from_fourier(got[:, :, :packed], plain, quad_lanes))
         grad_input = (hidden_grad.astype(jnp.float32) + wave_grad.astype(jnp.float32)).astype(
             jnp.bfloat16

time: 356 us -> 338 us (0.949)
  blocking collectives: 130 us -> 28.4 us
  waiting for transfers between devices: 108 us -> 153 us
  starting transfers between devices: 74 us -> 103 us
  local copies, waits for them, and re-layouts: 15.6 us -> 25.4 us
    all_to_all x4 -> x0, blocking collectives: 69 us -> none  [swap_blocks(): return lax.all_to_all(values, axis, split_axis=0, concat_axis=0, tiled=True)]
    all_to_all x9 -> x12, waiting for transfers between devices: 108 us -> 151 us  [swap_blocks(): return lax.all_to_all(values, axis, split_axis=0, concat_axis=0, tiled=True)]
    psum x1 -> x0, blocking collectives: 31.8 us -> none  [body(): keep = lax.psum(keep, 'lon').reshape(lat_count, -1)]
    ppermute x1 -> x8, starting transfers between devices: 2.05 us -> 24.3 us  [the longest x4 13.6 us: halve(): lax.ppermute(give, axis, [(i, i ^ mask) for i in range(size)])]
    all_to_all x9 -> x12, starting transfers between devices: 72 us -> 78.3 us  [swap_blocks(): return lax.all_to_all(values, axis, split_axis=0, concat_axis=0, tiled=True)]
    unnamed x43 -> x64, local copies, waits for them, and re-layouts: 2.85 us -> 7.34 us
  transfers between devices with their start and end apart: 10 -> 20, of which waited for: 8 -> 13; matrix products, arithmetic and copies ran while one was open for 5% -> 8% of each run, Pallas kernels for 0% -> 0%
where the time goes in v2:
time: 338 us; the launch traced here: 337 us
  waiting for transfers between devices  153 us (45%)
  starting transfers between devices  103 us (30%)
  blocking collectives  28.4 us (8%)
  local copies, waits for them, and re-layouts  25.4 us (8%)
  matrix products  18.6 us (6%)
  other arithmetic  7.45 us (2%)
    all_to_all x12, waiting for transfers between devices, swap_blocks(): return lax.all_to_all(values, axis, split_axis=0, concat_axis=0, tiled=True)  151 us
    all_to_all x12, starting transfers between devices, swap_blocks(): return lax.all_to_all(values, axis, split_axis=0, concat_axis=0, tiled=True)  78.3 us
    all_gather x1, blocking collectives, body(): piece = lax.all_gather(spectrum, 'lon', axis=0)  14.3 us
    all_gather x1, blocking collectives, body(): piece = lax.all_gather(mixed_grad, 'lon', axis=0)  14 us
    ppermute x4, starting transfers between devices, halve(): lax.ppermute(give, axis, [(i, i ^ mask) for i in range(size)])  13.6 us
    ppermute x3, starting transfers between devices, lon_exchange(): moved.append(lax.ppermute(block, 'lon', pairs))  8.74 us
    unnamed x64, local copies, waits for them, and re-layouts  7.34 us
  transfers between devices with their start and end apart: 20, of which 13 were waited for; matrix products, arithmetic and copies ran while one was open for 8% of the time, Pallas kernels for 0%

profile of v2, /device:TPU:32, one launch (start us, length us, event | category | flops | bytes accessed | tf_op | source)
XLA Modules:
  0.0 336.6 jit_solution(18179304413803397702)
XLA Ops:
  0.6 1.1 copy.117
  2.5 4.3 %all-to-all-start = ((bf16[4,128,192]{1,2,0:T(8,128)(2,1)}), bf16[4,128,192]{1,2,0:T(8,128)(2,1)S(1)}, u32[]{:S(2)}, u32[]{:S(2)}) async-start(bf16[4,128,192]{1,2,0:T(8,128)(2,1)} %bitcast.7), calls=%async_computation | async-start | bytes 393216 | tf_op jit(solution)/shard_map/forward_analysis/all_to_all | solution.py:63
  7.7 5.4 %all-to-all-done = bf16[4,128,192]{1,2,0:T(8,128)(2,1)S(1)} async-done(((bf16[4,128,192]{1,2,0:T(8,128)(2,1)}), bf16[4,128,192]{1,2,0:T(8,128)(2,1)S(1)}, u32[]{:S(2)}, u32[]{:S(2)}) %all-to-all-start) | async-done | bytes 196640 | tf_op jit(solution)/shard_map/forward_analysis/all_to_all | solution.py:63
  13.1 1.3 fusion.40
  14.5 0.8 copy.121
  15.4 19.2 %all-to-all-start.1 = ((bf16[128,2,384]{2,1,0:T(2,128)(2,1)}), bf16[128,2,384]{2,1,0:T(2,128)(2,1)S(1)}, u32[]{:S(2)}, u32[]{:S(2)}) async-start(bf16[128,2,384]{2,1,0:T(2,128)(2,1)} %copy.121), calls=%async_computation.1 | async-start | bytes 393216 | tf_op jit(solution)/shard_map/forward_analysis/all_to_all | solution.py:63
  34.6 19.8 %all-to-all-done.1 = bf16[128,2,384]{2,1,0:T(2,128)(2,1)S(1)} async-done(((bf16[128,2,384]{2,1,0:T(2,128)(2,1)}), bf16[128,2,384]{2,1,0:T(2,128)(2,1)S(1)}, u32[]{:S(2)}, u32[]{:S(2)}) %all-to-all-start.1) | async-done | bytes 196640 | tf_op jit(solution)/shard_map/forward_analysis/all_to_all | solution.py:63
  54.5 1.1 fusion.69
  55.6 1.1 fusion.29
  56.7 0.8 reshape.146
  57.5 6.2 %all-to-all-start.2 = ((bf16[128,2,384]{2,1,0:T(2,128)(2,1)}), bf16[128,2,384]{2,1,0:T(2,128)(2,1)S(1)}, u32[]{:S(2)}, u32[]{:S(2)}) async-start(bf16[128,2,384]{2,1,0:T(2,128)(2,1)} %reshape.146), calls=%async_computation.2 | async-start | bytes 393216 | tf_op jit(solution)/shard_map/forward_analysis/all_to_all | solution.py:63
  64.5 19.0 %all-to-all-done.2 = bf16[128,2,384]{2,1,0:T(2,128)(2,1)S(1)} async-done(((bf16[128,2,384]{2,1,0:T(2,128)(2,1)}), bf16[128,2,384]{2,1,0:T(2,128)(2,1)S(1)}, u32[]{:S(2)}, u32[]{:S(2)}) %all-to-all-start.2) | async-done | bytes 196640 | tf_op jit(solution)/shard_map/forward_analysis/all_to_all | solution.py:63
  83.6 14.3 %all-gather = bf16[512,2,384]{2,1,0:T(2,128)(2,1)S(1)} all-gather(bf16[128,2,384]{2,1,0:T(2,128)(2,1)S(1)} %all-to-all-done.2), channel_id=2, replica_groups=mesh['lat'=128,'lon'=4] {'lon'}, dimensions={0}, use_global_device_ids=true | all-gather | bytes 983040 | tf_op jit(solution)/shard_map/mix/all_gather | solution.py:170
  98.0 0.8 fusion.44
  98.8 0.8 copy.123
  99.7 5.9 %all-to-all-start.3 = ((bf16[128,2,384]{2,1,0:T(2,128)(2,1)}), bf16[128,2,384]{2,1,0:T(2,128)(2,1)S(1)}, u32[]{:S(2)}, u32[]{:S(2)}) async-start(bf16[128,2,384]{2,1,0:T(2,128)(2,1)} %copy.123), calls=%async_computation.3 | async-start | bytes 393216 | tf_op jit(solution)/shard_map/forward_synthesis/all_to_all | solution.py:63
  105.9 2.8 collective-permute-start
  108.8 2.8 collective-permute-start.1
  111.7 3.2 collective-permute-start.2
  114.9 10.5 %all-to-all-done.3 = bf16[128,2,384]{2,1,0:T(2,128)(2,1)S(1)} async-done(((bf16[128,2,384]{2,1,0:T(2,128)(2,1)}), bf16[128,2,384]{2,1,0:T(2,128)(2,1)S(1)}, u32[]{:S(2)}, u32[]{:S(2)}) %all-to-all-start.3) | async-done | bytes 196640 | tf_op jit(solution)/shard_map/forward_synthesis/all_to_all | solution.py:63
  125.5 1.2 fusion.68
  126.7 1.2 fusion.30
  127.8 0.8 reshape.148
  128.6 6.2 %all-to-all-start.4 = ((bf16[128,2,384]{2,1,0:T(2,128)(2,1)}), bf16[128,2,384]{2,1,0:T(2,128)(2,1)S(1)}, u32[]{:S(2)}, u32[]{:S(2)}) async-start(bf16[128,2,384]{2,1,0:T(2,128)(2,1)} %reshape.148), calls=%async_computation.4 | async-start | bytes 393216 | tf_op jit(solution)/shard_map/forward_synthesis/all_to_all | solution.py:63
  137.3 17.3 %all-to-all-done.4 = bf16[128,2,384]{2,1,0:T(2,128)(2,1)S(1)} async-done(((bf16[128,2,384]{2,1,0:T(2,128)(2,1)}), bf16[128,2,384]{2,1,0:T(2,128)(2,1)S(1)}, u32[]{:S(2)}, u32[]{:S(2)}) %all-to-all-start.4) | async-done | bytes 196640 | tf_op jit(solution)/shard_map/forward_synthesis/all_to_all | solution.py:63
  156.1 3.9 %all-to-all-start.5 = ((bf16[4,128,192]{1,2,0:T(8,128)(2,1)}), bf16[4,128,192]{1,2,0:T(8,128)(2,1)S(1)}, u32[]{:S(2)}, u32[]{:S(2)}) async-start(bf16[4,128,192]{1,2,0:T(8,128)(2,1)} %bitcast.185), calls=%async_computation.5 | async-start | bytes 393216 | tf_op jit(solution)/shard_map/forward_synthesis/all_to_all | solution.py:63
  160.6 5.7 %all-to-all-done.5 = bf16[4,128,192]{1,2,0:T(8,128)(2,1)S(1)} async-done(((bf16[4,128,192]{1,2,0:T(8,128)(2,1)}), bf16[4,128,192]{1,2,0:T(8,128)(2,1)S(1)}, u32[]{:S(2)}, u32[]{:S(2)}) %all-to-all-start.5) | async-done | bytes 196640 | tf_op jit(solution)/shard_map/forward_synthesis/all_to_all | solution.py:63
  167.0 1.1 multiply_convert_fusion
  169.9 3.4 %all-to-all-start.6 = ((bf16[4,128,192]{1,2,0:T(8,128)(2,1)}), bf16[4,128,192]{1,2,0:T(8,128)(2,1)S(1)}, u32[]{:S(2)}, u32[]{:S(2)}) async-start(bf16[4,128,192]{1,2,0:T(8,128)(2,1)} %bitcast.34), calls=%async_computation.6 | async-start | bytes 393216 | tf_op jit(solution)/shard_map/backward_analysis/all_to_all | solution.py:63
  174.0 5.6 %all-to-all-done.6 = bf16[4,128,192]{1,2,0:T(8,128)(2,1)S(1)} async-done(((bf16[4,128,192]{1,2,0:T(8,128)(2,1)}), bf16[4,128,192]{1,2,0:T(8,128)(2,1)S(1)}, u32[]{:S(2)}, u32[]{:S(2)}) %all-to-all-start.6) | async-done | bytes 196640 | tf_op jit(solution)/shard_map/backward_analysis/all_to_all | solution.py:63
  181.2 1.5 select_convert_fusion
  182.7 1.9 collective-permute-start.3
  186.7 1.7 fusion.88
  188.4 0.8 copy.139
  189.3 6.7 %all-to-all-start.7 = ((bf16[128,2,384]{2,1,0:T(2,128)(2,1)}), bf16[128,2,384]{2,1,0:T(2,128)(2,1)}, u32[]{:S(2)}, u32[]{:S(2)}) async-start(bf16[128,2,384]{2,1,0:T(2,128)(2,1)} %copy.139), calls=%async_computation.7 | async-start | bytes 393216 | tf_op jit(solution)/shard_map/backward_analysis/all_to_all | solution.py:63
  196.0 1.2 convert_add_fusion
  197.5 3.1 collective-permute-start.4
  200.7 14.9 %all-to-all-done.7 = bf16[128,2,384]{2,1,0:T(2,128)(2,1)} async-done(((bf16[128,2,384]{2,1,0:T(2,128)(2,1)}), bf16[128,2,384]{2,1,0:T(2,128)(2,1)}, u32[]{:S(2)}, u32[]{:S(2)}) %all-to-all-start.7) | async-done | bytes 196640 | tf_op jit(solution)/shard_map/backward_analysis/all_to_all | solution.py:63
  215.6 1.0 reshape.161
  216.6 1.1 fusion.67
  217.7 1.1 fusion.31
  218.9 0.8 reshape.162
  219.8 2.5 collective-permute-start.5
  222.3 1.0 dynamic-slice_bitcast_fusion.1
  223.2 6.2 %all-to-all-start.8 = ((bf16[128,2,384]{2,1,0:T(2,128)(2,1)}), bf16[128,2,384]{2,1,0:T(2,128)(2,1)S(1)}, u32[]{:S(2)}, u32[]{:S(2)}) async-start(bf16[128,2,384]{2,1,0:T(2,128)(2,1)} %reshape.162), calls=%async_computation.8 | async-start | bytes 393216 | tf_op jit(solution)/shard_map/backward_analysis/all_to_all | solution.py:63
  230.1 4.6 %collective-permute-start.6 = (bf16[128,288]{1,0:T(8,128)(2,1)S(1)}, bf16[128,288]{1,0:T(8,128)(2,1)S(1)}, u32[]{:S(2)}, u32[]{:S(2)}) collective-permute-start(bf16[128,288]{1,0:T(8,128)(2,1)S(1)} %select_convert_fusion.3), channel_id=1, source_target_pairs={{0,24},{4,28},{8,16},{12,20},{16,8},{20,12},{24,0},{28,4},{32,56},... | collective-permute-start | bytes 221192 | tf_op jit(solution)/shard_map/pointwise_weights/ppermute | solution.py:84
  234.8 14.4 %all-to-all-done.8 = bf16[128,2,384]{2,1,0:T(2,128)(2,1)S(1)} async-done(((bf16[128,2,384]{2,1,0:T(2,128)(2,1)}), bf16[128,2,384]{2,1,0:T(2,128)(2,1)S(1)}, u32[]{:S(2)}, u32[]{:S(2)}) %all-to-all-start.8) | async-done | bytes 196640 | tf_op jit(solution)/shard_map/backward_analysis/all_to_all | solution.py:63
  249.2 14.0 %all-gather.1 = bf16[512,2,384]{2,1,0:T(2,128)(2,1)S(1)} all-gather(bf16[128,2,384]{2,1,0:T(2,128)(2,1)S(1)} %all-to-all-done.8), channel_id=3, replica_groups=mesh['lat'=128,'lon'=4] {'lon'}, dimensions={0}, use_global_device_ids=true | all-gather | bytes 983040 | tf_op jit(solution)/shard_map/unmix/all_gather | solution.py:229
  263.4 0.8 fusion.47
  264.2 0.9 copy.141
  265.0 6.6 %all-to-all-start.9 = ((bf16[128,2,384]{2,1,0:T(2,128)(2,1)}), bf16[128,2,384]{2,1,0:T(2,128)(2,1)S(1)}, u32[]{:S(2)}, u32[]{:S(2)}) async-start(bf16[128,2,384]{2,1,0:T(2,128)(2,1)} %copy.141), calls=%async_computation.9 | async-start | bytes 393216 | tf_op jit(solution)/shard_map/backward_synthesis/all_to_all | solution.py:63
  271.7 3.5 %collective-permute-start.7 = (bf16[128,144]{1,0:T(8,128)(2,1)S(1)}, bf16[128,144]{1,0:T(8,128)(2,1)S(1)}, u32[]{:S(2)}, u32[]{:S(2)}) collective-permute-start(bf16[128,144]{1,0:T(8,128)(2,1)S(1)} %select_convert_fusion.4), channel_id=1, source_target_pairs={{0,8},{4,12},{8,0},{12,4},{16,24},{20,28},{24,16},{28,20},{32,40},... | collective-permute-start | bytes 110600 | tf_op jit(solution)/shard_map/backward_synthesis/ppermute | solution.py:84
  275.3 1.0 fusion.27
  276.3 1.9 collective-permute-done.7
  278.4 13.1 %all-to-all-done.9 = bf16[128,2,384]{2,1,0:T(2,128)(2,1)S(1)} async-done(((bf16[128,2,384]{2,1,0:T(2,128)(2,1)}), bf16[128,2,384]{2,1,0:T(2,128)(2,1)S(1)}, u32[]{:S(2)}, u32[]{:S(2)}) %all-to-all-start.9) | async-done | bytes 196640 | tf_op jit(solution)/shard_map/backward_synthesis/all_to_all | solution.py:63
  291.5 1.2 fusion.66
  292.7 1.2 fusion.32
  293.9 0.9 pad_maximum_fusion.1
  294.9 6.3 %all-to-all-start.10 = ((bf16[128,2,512]{2,1,0:T(2,128)(2,1)}), bf16[128,2,512]{2,1,0:T(2,128)(2,1)S(1)}, u32[]{:S(2)}, u32[]{:S(2)}) async-start(bf16[128,2,512]{2,1,0:T(2,128)(2,1)} %pad_maximum_fusion.1), calls=%async_computation.10 | async-start | bytes 524288 | tf_op jit(solution)/shard_map/backward_synthesis/all_to_all | solution.py:63
  301.2 0.8 convolution_bitcast_fusion
  302.8 1.1 copy.149
  303.9 19.8 %all-to-all-done.10 = bf16[128,2,512]{2,1,0:T(2,128)(2,1)S(1)} async-done(((bf16[128,2,512]{2,1,0:T(2,128)(2,1)}), bf16[128,2,512]{2,1,0:T(2,128)(2,1)S(1)}, u32[]{:S(2)}, u32[]{:S(2)}) %all-to-all-start.10) | async-done | bytes 262176 | tf_op jit(solution)/shard_map/backward_synthesis/all_to_all | solution.py:63
  325.3 3.4 %all-to-all-start.11 = ((bf16[4,128,192]{1,2,0:T(8,128)(2,1)}), bf16[4,128,192]{1,2,0:T(8,128)(2,1)S(1)}, u32[]{:S(2)}, u32[]{:S(2)}) async-start(bf16[4,128,192]{1,2,0:T(8,128)(2,1)} %bitcast.184), calls=%async_computation.11 | async-start | bytes 393216 | tf_op jit(solution)/shard_map/backward_synthesis/all_to_all | solution.py:63
  330.1 5.1 %all-to-all-done.11 = bf16[4,128,192]{1,2,0:T(8,128)(2,1)S(1)} async-done(((bf16[4,128,192]{1,2,0:T(8,128)(2,1)}), bf16[4,128,192]{1,2,0:T(8,128)(2,1)S(1)}, u32[]{:S(2)}, u32[]{:S(2)}) %all-to-all-start.11) | async-done | bytes 196640 | tf_op jit(solution)/shard_map/backward_synthesis/all_to_all | solution.py:63
  (143 shorter events, 21.2 us)
Async XLA Ops:
  0.6 166.3 %copy-start = (bf16[384,768]{1,0:T(8,128)(2,1)S(1)}, bf16[384,768]{1,0:T(8,128)(2,1)}, u32[]{:S(2)}) copy-start(bf16[384,768]{1,0:T(8,128)(2,1)} %param.12) | copy-start | bytes 1769476
  2.5 10.6 %all-to-all-start = ((bf16[4,128,192]{1,2,0:T(8,128)(2,1)}), bf16[4,128,192]{1,2,0:T(8,128)(2,1)S(1)}, u32[]{:S(2)}, u32[]{:S(2)}) async-start(bf16[4,128,192]{1,2,0:T(8,128)(2,1)} %bitcast.7), calls=%async_computation | async-start | bytes 393216 | tf_op jit(solution)/shard_map/forward_analysis/all_to_all | solution.py:63
  7.7 56.0 %copy-start.26 = (bf16[2,2,384,96]{2,3,1,0:T(8,128)(2,1)S(1)}, bf16[2,2,384,96]{2,3,1,0:T(8,128)(2,1)}, u32[]{:S(2)}) copy-start(bf16[2,2,384,96]{2,3,1,0:T(8,128)(2,1)} %param.11) | copy-start | bytes 884740
  15.4 39.0 %all-to-all-start.1 = ((bf16[128,2,384]{2,1,0:T(2,128)(2,1)}), bf16[128,2,384]{2,1,0:T(2,128)(2,1)S(1)}, u32[]{:S(2)}, u32[]{:S(2)}) async-start(bf16[128,2,384]{2,1,0:T(2,128)(2,1)} %copy.121), calls=%async_computation.1 | async-start | bytes 393216 | tf_op jit(solution)/shard_map/forward_analysis/all_to_all | solution.py:63
  57.5 26.1 %all-to-all-start.2 = ((bf16[128,2,384]{2,1,0:T(2,128)(2,1)}), bf16[128,2,384]{2,1,0:T(2,128)(2,1)S(1)}, u32[]{:S(2)}, u32[]{:S(2)}) async-start(bf16[128,2,384]{2,1,0:T(2,128)(2,1)} %reshape.146), calls=%async_computation.2 | async-start | bytes 393216 | tf_op jit(solution)/shard_map/forward_analysis/all_to_all | solution.py:63
  83.6 15.2 %copy-start.7 = (bf16[128,2,384]{2,1,0:T(2,128)(2,1)}, bf16[128,2,384]{2,1,0:T(2,128)(2,1)S(1)}, u32[]{:S(2)}) copy-start(bf16[128,2,384]{2,1,0:T(2,128)(2,1)S(1)} %all-to-all-done.2) | copy-start | bytes 589828
  99.7 25.8 %all-to-all-start.3 = ((bf16[128,2,384]{2,1,0:T(2,128)(2,1)}), bf16[128,2,384]{2,1,0:T(2,128)(2,1)S(1)}, u32[]{:S(2)}, u32[]{:S(2)}) async-start(bf16[128,2,384]{2,1,0:T(2,128)(2,1)} %copy.123), calls=%async_computation.3 | async-start | bytes 393216 | tf_op jit(solution)/shard_map/forward_synthesis/all_to_all | solution.py:63
  105.9 29.3 %collective-permute-start = (bf16[2,2,96,96]{3,2,1,0:T(8,128)(2,1)S(1)}, bf16[2,2,96,96]{3,2,1,0:T(8,128)(2,1)S(1)}, u32[]{:S(2)}, u32[]{:S(2)}) collective-permute-start(bf16[2,2,96,96]{3,2,1,0:T(8,128)(2,1)S(1)} %bitcast.209), channel_id=1, source_target_pairs={{0,3},{1,0},{2,1},{3,2},{4,7},{5,4},{6,5},{7,6},{8,11},{9,8},{10,9... | collective-permute-start | bytes 221192 | tf_op jit(solution)/shard_map/weights/ppermute | solution.py:72
  108.8 27.2 %collective-permute-start.1 = (bf16[2,2,96,96]{3,2,1,0:T(8,128)(2,1)S(1)}, bf16[2,2,96,96]{3,2,1,0:T(8,128)(2,1)S(1)}, u32[]{:S(2)}, u32[]{:S(2)}) collective-permute-start(bf16[2,2,96,96]{3,2,1,0:T(8,128)(2,1)S(1)} %bitcast.210), channel_id=1, source_target_pairs={{0,2},{1,3},{2,0},{3,1},{4,6},{5,7},{6,4},{7,5},{8,10},{9,11},{10,... | collective-permute-start | bytes 221192 | tf_op jit(solution)/shard_map/weights/ppermute | solution.py:72
  111.6 43.4 %copy-start.5 = (bf16[512,512]{1,0:T(8,128)(2,1)S(1)}, bf16[512,512]{1,0:T(8,128)(2,1)}, u32[]{:S(2)}) copy-start(bf16[512,512]{1,0:T(8,128)(2,1)} %constant.81.clone) | copy-start | bytes 1572868
  111.7 25.0 %collective-permute-start.2 = (bf16[2,2,96,96]{3,2,1,0:T(8,128)(2,1)S(1)}, bf16[2,2,96,96]{3,2,1,0:T(8,128)(2,1)S(1)}, u32[]{:S(2)}, u32[]{:S(2)}) collective-permute-start(bf16[2,2,96,96]{3,2,1,0:T(8,128)(2,1)S(1)} %bitcast.211), channel_id=1, source_target_pairs={{0,1},{1,2},{2,3},{3,0},{4,5},{5,6},{6,7},{7,4},{8,9},{9,10},{10,1... | collective-permute-start | bytes 221192 | tf_op jit(solution)/shard_map/weights/ppermute | solution.py:72
  128.6 26.1 %all-to-all-start.4 = ((bf16[128,2,384]{2,1,0:T(2,128)(2,1)}), bf16[128,2,384]{2,1,0:T(2,128)(2,1)S(1)}, u32[]{:S(2)}, u32[]{:S(2)}) async-start(bf16[128,2,384]{2,1,0:T(2,128)(2,1)} %reshape.148), calls=%async_computation.4 | async-start | bytes 393216 | tf_op jit(solution)/shard_map/forward_synthesis/all_to_all | solution.py:63
  135.2 31.1 %copy-start.11 = (bf16[2,2,1,96,96]{4,3,1,0,2:T(8,128)(2,1)}, bf16[2,2,1,96,96]{4,3,1,0,2:T(8,128)(2,1)S(1)}, u32[]{:S(2)}) copy-start(bf16[2,2,1,96,96]{4,3,1,0,2:T(8,128)(2,1)S(1)} %copy.132) | copy-start | bytes 221188
  135.2 31.4 %copy-start.24 = (bf16[2,2,96,96]{3,2,1,0:T(8,128)(2,1)}, bf16[2,2,96,96]{3,2,1,0:T(8,128)(2,1)S(1)}, u32[]{:S(2)}) copy-start(bf16[2,2,96,96]{3,2,1,0:T(8,128)(2,1)S(1)} %collective-permute-done) | copy-start | bytes 221188
  135.9 30.4 %copy-start.20 = (bf16[2,2,96,96]{3,2,1,0:T(8,128)(2,1)}, bf16[2,2,96,96]{3,2,1,0:T(8,128)(2,1)S(1)}, u32[]{:S(2)}) copy-start(bf16[2,2,96,96]{3,2,1,0:T(8,128)(2,1)S(1)} %collective-permute-done.1) | copy-start | bytes 221188
  136.7 29.7 %copy-start.22 = (bf16[2,2,96,96]{3,2,1,0:T(8,128)(2,1)}, bf16[2,2,96,96]{3,2,1,0:T(8,128)(2,1)S(1)}, u32[]{:S(2)}) copy-start(bf16[2,2,96,96]{3,2,1,0:T(8,128)(2,1)S(1)} %collective-permute-done.2) | copy-start | bytes 221188
  154.9 12.0 %copy-start.14 = (bf16[2,128,384]{2,1,0:T(8,128)(2,1)S(1)}, bf16[2,128,384]{2,1,0:T(8,128)(2,1)}, u32[]{:S(2)}) copy-start(bf16[2,128,384]{2,1,0:T(8,128)(2,1)} %param.9) | copy-start | bytes 589828
  156.1 10.3 %all-to-all-start.5 = ((bf16[4,128,192]{1,2,0:T(8,128)(2,1)}), bf16[4,128,192]{1,2,0:T(8,128)(2,1)S(1)}, u32[]{:S(2)}, u32[]{:S(2)}) async-start(bf16[4,128,192]{1,2,0:T(8,128)(2,1)} %bitcast.185), calls=%async_computation.5 | async-start | bytes 393216 | tf_op jit(solution)/shard_map/forward_synthesis/all_to_all | solution.py:63
  166.4 1.8 copy-start.17
  166.4 1.8 copy-start.18
  167.0 13.6 %copy-start.3 = (bf16[256,384]{1,0:T(8,128)(2,1)}, bf16[256,384]{1,0:T(8,128)(2,1)S(1)}, u32[]{:S(2)}) copy-start(bf16[256,384]{1,0:T(8,128)(2,1)S(1)} %fusion.56) | copy-start | bytes 589828
  168.2 5.2 %copy-start.25 = (bf16[2,2,96,96]{3,2,1,0:T(8,128)(2,1)S(1)}, bf16[2,2,96,96]{3,2,1,0:T(8,128)(2,1)}, u32[]{:S(2)}) copy-start(bf16[2,2,96,96]{3,2,1,0:T(8,128)(2,1)} %copy-done.24) | copy-start | bytes 221188
  169.0 11.6 %copy-start.9 = (bf16[256,384]{1,0:T(8,128)(2,1)}, bf16[256,384]{1,0:T(8,128)(2,1)S(1)}, u32[]{:S(2)}) copy-start(bf16[256,384]{1,0:T(8,128)(2,1)S(1)} %fusion.28) | copy-start | bytes 589828
  169.9 9.7 %all-to-all-start.6 = ((bf16[4,128,192]{1,2,0:T(8,128)(2,1)}), bf16[4,128,192]{1,2,0:T(8,128)(2,1)S(1)}, u32[]{:S(2)}, u32[]{:S(2)}) async-start(bf16[4,128,192]{1,2,0:T(8,128)(2,1)} %bitcast.34), calls=%async_computation.6 | async-start | bytes 393216 | tf_op jit(solution)/shard_map/backward_analysis/all_to_all | solution.py:63
  181.2 3.5 %copy-start.21 = (bf16[2,2,96,96]{3,2,1,0:T(8,128)(2,1)S(1)}, bf16[2,2,96,96]{3,2,1,0:T(8,128)(2,1)}, u32[]{:S(2)}) copy-start(bf16[2,2,96,96]{3,2,1,0:T(8,128)(2,1)} %copy-done.20) | copy-start | bytes 221188
  181.2 4.1 %copy-start.23 = (bf16[2,2,96,96]{3,2,1,0:T(8,128)(2,1)S(1)}, bf16[2,2,96,96]{3,2,1,0:T(8,128)(2,1)}, u32[]{:S(2)}) copy-start(bf16[2,2,96,96]{3,2,1,0:T(8,128)(2,1)} %copy-done.22) | copy-start | bytes 221188
  181.2 4.8 %copy-start.12 = (bf16[2,2,1,96,96]{4,3,1,0,2:T(8,128)(2,1)S(1)}, bf16[2,2,1,96,96]{4,3,1,0,2:T(8,128)(2,1)}, u32[]{:S(2)}) copy-start(bf16[2,2,1,96,96]{4,3,1,0,2:T(8,128)(2,1)} %copy-done.11) | copy-start | bytes 221188
  181.2 7.2 %copy-start.13 = (bf16[4,128,2,96]{1,3,0,2:T(8,128)(2,1)S(1)}, bf16[4,128,2,96]{1,3,0,2:T(8,128)(2,1)}, u32[]{:S(2)}) copy-start(bf16[4,128,2,96]{1,3,0,2:T(8,128)(2,1)} %copy.138) | copy-start | bytes 589828
  182.7 13.3 %collective-permute-start.3 = (bf16[768,384]{1,0:T(8,128)(2,1)S(1)}, bf16[768,384]{1,0:T(8,128)(2,1)}, u32[]{:S(2)}, u32[]{:S(2)}) collective-permute-start(bf16[768,384]{1,0:T(8,128)(2,1)S(1)} %get-tuple-element.75), channel_id=1, source_target_pairs={{0,4},{4,0},{8,12},{12,8},{16,20},{20,16},{24,28},{28,24},{32,36},... | collective-permute-start | bytes 1769480 | tf_op jit(solution)/shard_map/pointwise_weights/ppermute | solution.py:214
  189.3 26.3 %all-to-all-start.7 = ((bf16[128,2,384]{2,1,0:T(2,128)(2,1)}), bf16[128,2,384]{2,1,0:T(2,128)(2,1)}, u32[]{:S(2)}, u32[]{:S(2)}) async-start(bf16[128,2,384]{2,1,0:T(2,128)(2,1)} %copy.139), calls=%async_computation.7 | async-start | bytes 393216 | tf_op jit(solution)/shard_map/backward_analysis/all_to_all | solution.py:63
  197.5 22.1 %collective-permute-start.4 = (bf16[128,1152]{1,0:T(8,128)(2,1)S(1)}, bf16[128,1152]{1,0:T(8,128)(2,1)S(1)}, u32[]{:S(2)}, u32[]{:S(2)}) collective-permute-start(bf16[128,1152]{1,0:T(8,128)(2,1)S(1)} %select_convert_fusion.1), channel_id=1, source_target_pairs={{0,3},{1,2},{2,1},{3,0},{4,7},{5,6},{6,5},{7,4},{8,11},{9,10},{10,... | collective-permute-start | bytes 884744 | tf_op jit(solution)/shard_map/pointwise_weights/ppermute | solution.py:84
  200.7 28.7 %copy-start.15 = (bf16[4,2,96,96]{3,2,0,1:T(8,128)(2,1)S(1)}, bf16[4,2,96,96]{3,2,0,1:T(8,128)(2,1)}, u32[]{:S(2)}) copy-start(bf16[4,2,96,96]{3,2,0,1:T(8,128)(2,1)} %get-tuple-element.64) | copy-start | bytes 442372
  200.7 28.7 %copy-start.16 = (bf16[4,2,96,96]{3,2,0,1:T(8,128)(2,1)S(1)}, bf16[4,2,96,96]{3,2,0,1:T(8,128)(2,1)}, u32[]{:S(2)}) copy-start(bf16[4,2,96,96]{3,2,0,1:T(8,128)(2,1)} %get-tuple-element.65) | copy-start | bytes 442372
  219.8 10.0 %collective-permute-start.5 = (bf16[128,576]{1,0:T(8,128)(2,1)S(1)}, bf16[128,576]{1,0:T(8,128)(2,1)S(1)}, u32[]{:S(2)}, u32[]{:S(2)}) collective-permute-start(bf16[128,576]{1,0:T(8,128)(2,1)S(1)} %select_convert_fusion.2), channel_id=1, source_target_pairs={{0,1},{1,0},{2,3},{3,2},{4,5},{5,4},{6,7},{7,6},{8,9},{9,8},{10,11... | collective-permute-start | bytes 442376 | tf_op jit(solution)/shard_map/pointwise_weights/ppermute | solution.py:84
  223.2 26.0 %all-to-all-start.8 = ((bf16[128,2,384]{2,1,0:T(2,128)(2,1)}), bf16[128,2,384]{2,1,0:T(2,128)(2,1)S(1)}, u32[]{:S(2)}, u32[]{:S(2)}) async-start(bf16[128,2,384]{2,1,0:T(2,128)(2,1)} %reshape.162), calls=%async_computation.8 | async-start | bytes 393216 | tf_op jit(solution)/shard_map/backward_analysis/all_to_all | solution.py:63
  230.1 34.1 %collective-permute-start.6 = (bf16[128,288]{1,0:T(8,128)(2,1)S(1)}, bf16[128,288]{1,0:T(8,128)(2,1)S(1)}, u32[]{:S(2)}, u32[]{:S(2)}) collective-permute-start(bf16[128,288]{1,0:T(8,128)(2,1)S(1)} %select_convert_fusion.3), channel_id=1, source_target_pairs={{0,24},{4,28},{8,16},{12,20},{16,8},{20,12},{24,0},{28,4},{32,56},... | collective-permute-start | bytes 221192 | tf_op jit(solution)/shard_map/pointwise_weights/ppermute | solution.py:84
  263.4 11.9 %copy-start.2 = (bf16[256,768]{1,0:T(8,128)(2,1)S(1)}, bf16[256,768]{1,0:T(8,128)(2,1)}, u32[]{:S(2)}) copy-start(bf16[256,768]{1,0:T(8,128)(2,1)} %get-tuple-element.24) | copy-start | bytes 1179652
  263.4 11.9 %copy-start.4 = (bf16[256,384]{1,0:T(8,128)(2,1)S(1)}, bf16[256,384]{1,0:T(8,128)(2,1)}, u32[]{:S(2)}) copy-start(bf16[256,384]{1,0:T(8,128)(2,1)} %copy-done.3) | copy-start | bytes 589828
  263.4 11.9 %copy-start.19 = (bf16[768,384]{1,0:T(8,128)(2,1)S(1)}, bf16[768,384]{1,0:T(8,128)(2,1)}, u32[]{:S(2)}) copy-start(bf16[768,384]{1,0:T(8,128)(2,1)} %param.13) | copy-start | bytes 1769476
  265.0 26.4 %all-to-all-start.9 = ((bf16[128,2,384]{2,1,0:T(2,128)(2,1)}), bf16[128,2,384]{2,1,0:T(2,128)(2,1)S(1)}, u32[]{:S(2)}, u32[]{:S(2)}) async-start(bf16[128,2,384]{2,1,0:T(2,128)(2,1)} %copy.141), calls=%async_computation.9 | async-start | bytes 393216 | tf_op jit(solution)/shard_map/backward_synthesis/all_to_all | solution.py:63
  271.7 29.4 %copy-start.8 = (bf16[128,2,384]{2,1,0:T(2,128)(2,1)S(1)}, bf16[128,2,384]{2,1,0:T(2,128)(2,1)}, u32[]{:S(2)}) copy-start(bf16[128,2,384]{2,1,0:T(2,128)(2,1)} %copy-done.7) | copy-start | bytes 589828
  271.7 6.5 %collective-permute-start.7 = (bf16[128,144]{1,0:T(8,128)(2,1)S(1)}, bf16[128,144]{1,0:T(8,128)(2,1)S(1)}, u32[]{:S(2)}, u32[]{:S(2)}) collective-permute-start(bf16[128,144]{1,0:T(8,128)(2,1)S(1)} %select_convert_fusion.4), channel_id=1, source_target_pairs={{0,8},{4,12},{8,0},{12,4},{16,24},{20,28},{24,16},{28,20},{32,40},... | collective-permute-start | bytes 110600 | tf_op jit(solution)/shard_map/backward_synthesis/ppermute | solution.py:84
  294.9 28.8 %all-to-all-start.10 = ((bf16[128,2,512]{2,1,0:T(2,128)(2,1)}), bf16[128,2,512]{2,1,0:T(2,128)(2,1)S(1)}, u32[]{:S(2)}, u32[]{:S(2)}) async-start(bf16[128,2,512]{2,1,0:T(2,128)(2,1)} %pad_maximum_fusion.1), calls=%async_computation.10 | async-start | bytes 524288 | tf_op jit(solution)/shard_map/backward_synthesis/all_to_all | solution.py:63
  302.7 21.4 %copy-start.6 = (bf16[512,512]{1,0:T(8,128)(2,1)S(1)}, bf16[512,512]{1,0:T(8,128)(2,1)}, u32[]{:S(2)}) copy-start(bf16[512,512]{1,0:T(8,128)(2,1)} %constant.80.clone) | copy-start | bytes 1572868
  324.0 11.8 %copy-start.10 = (bf16[256,384]{1,0:T(8,128)(2,1)S(1)}, bf16[256,384]{1,0:T(8,128)(2,1)}, u32[]{:S(2)}) copy-start(bf16[256,384]{1,0:T(8,128)(2,1)} %copy-done.9) | copy-start | bytes 589828
  324.1 12.4 %copy-start.1 = (bf16[384,768]{1,0:T(8,128)(2,1)S(1)}, bf16[384,768]{1,0:T(8,128)(2,1)}, u32[]{:S(2)}) copy-start(bf16[384,768]{1,0:T(8,128)(2,1)} %param.12) | copy-start | bytes 1769476
  325.3 10.0 %all-to-all-start.11 = ((bf16[4,128,192]{1,2,0:T(8,128)(2,1)}), bf16[4,128,192]{1,2,0:T(8,128)(2,1)S(1)}, u32[]{:S(2)}, u32[]{:S(2)}) async-start(bf16[4,128,192]{1,2,0:T(8,128)(2,1)} %bitcast.184), calls=%async_computation.11 | async-start | bytes 393216 | tf_op jit(solution)/shard_map/backward_synthesis/all_to_all | solution.py:63

commit v3 on v2

v3 whole, which is shorter than its diff:
```python
import math

import jax
import jax.numpy as jnp
import ml_dtypes
import numpy as np
from jax import lax
from jax.sharding import PartitionSpec as P


def legendre_table(size):
    theta = math.pi * (np.arange(size) + 0.5) / size
    cosv, sinv = np.cos(theta), np.sin(theta)
    order = np.arange(size, dtype=np.float64)[:, None]
    start = np.empty((size, size))
    start[0] = math.sqrt(1.0 / (4.0 * math.pi))
    for m in range(1, size):
        start[m] = start[m - 1] * math.sqrt((2 * m + 1) / (2.0 * m)) * sinv
    table = np.zeros((size, size, size), dtype=ml_dtypes.bfloat16)
    before = np.zeros((size, size))
    now = np.zeros((size, size))
    for level in range(size):
        safe = np.where(order < level, order, 0.0)
        alpha = np.sqrt((4.0 * level * level - 1.0) / (level * level - safe * safe)) if level else 0.0
        beta = (
            np.sqrt(((level - 1.0) ** 2 - safe * safe).clip(0) / (4.0 * (level - 1.0) ** 2 - 1.0))
            if level > 1
            else 0.0
        )
        value = np.where(order < level, alpha * (cosv * now - beta * before), 0.0)
        value[level] = start[level]
        table[:, level, :] = value.astype(np.float32).astype(ml_dtypes.bfloat16)
        before, now = now, value
    return table


def quadrature(nlat, nlon):
    theta = math.pi * (np.arange(nlat) + 0.5) / nlat
    return (math.pi / nlat * np.sin(theta) * (2.0 * math.pi / nlon)).astype(np.float32)


def fourier_tables(nlon, modes, lon_count):
    phase = np.arange(nlon)[:, None] * np.arange(modes)[None, :] % nlon
    angle = 2.0 * math.pi / nlon * phase
    pair = np.stack([np.cos(angle), -np.sin(angle)]).astype(np.float32).astype(ml_dtypes.bfloat16)
    factor = np.where(np.arange(modes) == 0, 1.0, 2.0).astype(np.float32)
    doubled = (pair.astype(np.float32) * factor).astype(ml_dtypes.bfloat16)

    def arrange(values):
        values = values.reshape(2, nlon, lon_count, modes // lon_count).transpose(2, 1, 0, 3)
        return np.ascontiguousarray(values.reshape(lon_count, nlon, -1))

    return arrange(pair), arrange(doubled)


def gelu_parts(values):
    half = 0.5 * (1.0 + lax.erf(values * (1.0 / math.sqrt(2.0))))
    slope = half + values * jnp.exp(-0.5 * values * values) * (1.0 / math.sqrt(2.0 * math.pi))
    return values * half, slope


def swap_blocks(values, axis):
    return lax.all_to_all(values, axis, split_axis=0, concat_axis=0, tiled=True)


def lon_gather_async(block, lon_index, lon_count):
    moved = [block]
    for shift in range(1, lon_count):
        pairs = [(i, (i + shift) % lon_count) for i in range(lon_count)]
        moved.append(lax.ppermute(block, "lon", pairs))
    backwards = jnp.stack(moved[::-1] + moved[:0:-1])
    return lax.dynamic_slice_in_dim(backwards, lon_count - 1 - lon_index, lon_count, 0)


def halve(values, axis, index, mask, bit):
    size = lax.axis_size(axis)
    width = values.shape[-1] // 2
    high = (index >> bit) & 1 == 1
    keep = jnp.where(high, values[:, width:], values[:, :width])
    give = jnp.where(high, values[:, :width], values[:, width:]).astype(jnp.bfloat16)
    return keep, lax.ppermute(give, axis, [(i, i ^ mask) for i in range(size)])


def add_swapped(pair):
    keep, got = pair
    return keep + got.astype(jnp.float32)


def body(table_all, plain_all, doubled_all, quad, grid, cotangent, spectral_weight, w_in, w_out):
    lat_count = lax.axis_size("lat")
    lon_count = lax.axis_size("lon")
    lat_index = lax.axis_index("lat")
    lon_index = lax.axis_index("lon")
    rows, lon_rows, width = grid.shape
    quarter = width // lon_count
    total_lat = rows * lat_count
    total_lon = lon_rows * lon_count
    half = lat_count // 2
    order = lon_index * half + lat_index % half
    table = lax.dynamic_index_in_dim(table_all, order, 0, keepdims=False)
    plain = lax.dynamic_index_in_dim(plain_all, lon_index, 0, keepdims=False)
    doubled = lax.dynamic_index_in_dim(doubled_all, lon_index, 0, keepdims=False)
    local_quad = lax.dynamic_slice_in_dim(quad, lat_index * rows, rows)
    quad_lanes = jnp.repeat(local_quad, width)[None, :]

    def lon_gather(values):
        values = values.transpose(1, 0, 2).reshape(lon_rows, rows * width)
        return lax.all_gather(values, "lon", axis=0, tiled=True)

    def to_fourier(values, matrix, scale):
        out = lax.dot_general(
            matrix, values, (((0,), (0,)), ((), ())), preferred_element_type=jnp.float32
        )
        if scale is not None:
            out = out * scale
        return out.astype(jnp.bfloat16).reshape(lat_count, rows, width)

    def from_fourier(values, matrix, scale):
        values = values.reshape(lat_count, rows * width)
        out = jnp.dot(matrix, values, preferred_element_type=jnp.float32)
        if scale is not None:
            out = out * scale
        out = out.astype(jnp.bfloat16).reshape(lon_count, lon_rows, rows * width)
        out = jnp.sum(swap_blocks(out, "lon").astype(jnp.float32), axis=0)
        return out.reshape(lon_rows, rows, width).transpose(1, 0, 2).reshape(-1, width)

    def analyze(values):
        out = jnp.dot(table, values.reshape(total_lat, width), preferred_element_type=jnp.float32)
        return out.astype(jnp.bfloat16).reshape(lat_count, rows, width)

    def synthesize(values):
        out = lax.dot_general(
            table,
            values.reshape(total_lat, width),
            (((0,), (0,)), ((), ())),
            preferred_element_type=jnp.float32,
        )
        return out.astype(jnp.bfloat16).reshape(lat_count, rows, width)

    def complex_product(values, weights, sign):
        out = jnp.einsum("plc,lcn->pln", values, weights, preferred_element_type=jnp.float32)
        by_re, by_im = out[:, :, :width], out[:, :, width:]
        out_re = by_re[:half] + sign * by_im[half:]
        out_im = by_re[half:] - sign * by_im[:half]
        return jnp.concatenate([out_re, out_im]).astype(jnp.bfloat16)

    with jax.named_scope("forward_analysis"):
        four = to_fourier(lon_gather(grid), plain, quad_lanes)
        four, own_weight = lax.optimization_barrier((four, spectral_weight))
        four = swap_blocks(four, "lat")
    with jax.named_scope("weights"):
        weights = lon_gather_async(own_weight, lon_index, lon_count)
        mix_weights = weights.transpose(2, 3, 1, 0, 4).reshape(rows, width, 2 * width)
        unmix_weights = weights.transpose(2, 0, 4, 1, 3).reshape(rows, width, 2 * width)
    with jax.named_scope("forward_analysis"):
        spectrum = swap_blocks(analyze(four), "lat")
    with jax.named_scope("mix"):
        mixed = complex_product(spectrum, mix_weights, -1.0)
    with jax.named_scope("forward_synthesis"):
        fields = swap_blocks(synthesize(swap_blocks(mixed, "lat")), "lat")
        wave_rows = from_fourier(fields, doubled, None)
    with jax.named_scope("pointwise"):
        hidden = (grid.reshape(-1, width).astype(jnp.float32) + wave_rows).astype(jnp.bfloat16)
        back = cotangent.reshape(-1, width)
        act_grad = lax.dot_general(
            back, w_out, (((1,), (1,)), ((), ())), preferred_element_type=jnp.float32
        )
        pre = jnp.dot(hidden, w_in, preferred_element_type=jnp.float32)
        value, slope = gelu_parts(pre)
        act = value.astype(jnp.bfloat16)
        pre_grad = (act_grad * slope).astype(jnp.bfloat16)
        hidden_grad = (
            back.astype(jnp.float32)
            + lax.dot_general(
                pre_grad, w_in, (((1,), (1,)), ((), ())), preferred_element_type=jnp.float32
            )
        ).astype(jnp.bfloat16)
        block_output = (
            hidden.astype(jnp.float32) + jnp.dot(act, w_out, preferred_element_type=jnp.float32)
        ).astype(jnp.bfloat16)
    with jax.named_scope("backward_analysis"):
        gathered = lon_gather(hidden_grad.reshape(grid.shape))
        gathered, hidden, pre_grad, act = lax.optimization_barrier(
            (gathered, hidden, pre_grad, act)
        )
        field_grad = swap_blocks(to_fourier(gathered, doubled, None), "lat")
    with jax.named_scope("pointwise_weights"):
        over_rows = (((0,), (0,)), ((), ()))
        out_part = lax.dot_general(act, back, over_rows, preferred_element_type=jnp.float32)
        in_part = lax.dot_general(hidden, pre_grad, over_rows, preferred_element_type=jnp.float32)
        in_part = in_part.reshape(out_part.shape)
        even = lat_index % 2 == 0
        keep = jnp.where(even, in_part, out_part)
        give = jnp.where(even, out_part, in_part).astype(jnp.bfloat16)
        got = lax.ppermute(give, "lat", [(i, i ^ 1) for i in range(lat_count)])
    with jax.named_scope("backward_analysis"):
        mixed_grad = analyze(field_grad)
        mixed_grad, keep, got = lax.optimization_barrier((mixed_grad, keep, got))
        mixed_grad = swap_blocks(mixed_grad, "lat")
    with jax.named_scope("pointwise_weights"):
        sums = add_swapped((keep, got)).reshape(lat_count, -1)
        keep, got = halve(sums, "lon", lon_index, 3, 1)
    with jax.named_scope("unmix"):
        spectrum_grad = complex_product(mixed_grad, unmix_weights, 1.0)
        spectrum_grad, keep, got, left, right = lax.optimization_barrier(
            (spectrum_grad, keep, got, spectrum, mixed_grad)
        )
    with jax.named_scope("backward_synthesis"):
        spectrum_grad = swap_blocks(spectrum_grad, "lat")
    with jax.named_scope("pointwise_weights"):
        keep, got = halve(add_swapped((keep, got)), "lon", lon_index, 1, 0)
    with jax.named_scope("unmix"):
        turned = jnp.concatenate([right[half:], -right[:half]])
        right = jnp.stack([right, turned])
        high = lon_index >> 1 == 1
        low_rows, high_rows = left[..., : width // 2], left[..., width // 2 :]
        outer = "pli,rpld->rlid"
        spec_keep = jnp.einsum(
            outer,
            jnp.where(high, high_rows, low_rows),
            right,
            preferred_element_type=jnp.float32,
        )
        spec_give = jnp.einsum(
            outer,
            jnp.where(high, low_rows, high_rows),
            right,
            preferred_element_type=jnp.float32,
        ).astype(jnp.bfloat16)
        spec_got = lax.ppermute(
            spec_give, "lon", [(i, lon_count - 1 - i) for i in range(lon_count)]
        )
    with jax.named_scope("backward_synthesis"):
        four_grad = synthesize(spectrum_grad)
        chunk = keep.shape[1]
        room = -(-chunk // (rows * 128)) * rows * 128
        extra = jnp.pad(add_swapped((keep, got)).astype(jnp.bfloat16), ((0, 0), (0, room - chunk)))
        extra = extra.reshape(lat_count, rows, room // rows)
        four_grad = jnp.concatenate([four_grad, extra], axis=2)
        four_grad, spec_keep, spec_got = lax.optimization_barrier((four_grad, spec_keep, spec_got))
        four_grad = swap_blocks(four_grad, "lat")
        wave_grad = from_fourier(four_grad[:, :, :width], plain, quad_lanes)
        grad_input = (hidden_grad.astype(jnp.float32) + wave_grad).astype(jnp.bfloat16)
    with jax.named_scope("unmix"):
        total = spec_keep + spec_got.astype(jnp.float32)
        high = lon_index & 1 == 1
        low_rows, high_rows = total[:, :, :quarter], total[:, :, quarter:]
        spec_give = jnp.where(high, low_rows, high_rows).astype(jnp.bfloat16)
        spec_got = lax.ppermute(spec_give, "lon", [(i, i ^ 1) for i in range(lon_count)])
        grad_spectral = jnp.where(high, high_rows, low_rows) + spec_got.astype(jnp.float32)
    with jax.named_scope("pointwise_weights"):
        sums = four_grad[:, :, width:].reshape(half, 2, room)[:, :, :chunk]
        sums = jnp.sum(sums.astype(jnp.float32), axis=0)
    return (
        block_output.reshape(grid.shape),
        grad_input.reshape(grid.shape),
        grad_spectral,
        sums[0],
        sums[1],
    )


def solution(mesh):
    in_specs = (P("lat", "lon", None), P("lat", "lon", None), P(None, "lat", None, "lon"), P(), P())
    out_specs = (
        P("lat", "lon", None),
        P("lat", "lon", None),
        P(None, "lat", "lon", None),
        P(("lat", "lon")),
        P(("lat", "lon")),
    )

    def call(grid, cotangent, spectral_weight, w_in, w_out):
        nlat, nlon, _ = grid.shape
        table = legendre_table(nlat)
        plain, doubled = fourier_tables(nlon, nlat, mesh.shape["lon"])
        quad = quadrature(nlat, nlon)
        mapped = jax.shard_map(
            body,
            mesh=mesh,
            in_specs=(P(), P(), P(), P()) + in_specs,
            out_specs=out_specs,
            check_vma=False,
        )
        return mapped(table, plain, doubled, quad, grid, cotangent, spectral_weight, w_in, w_out)

    return call
```

time: 338 us -> 346 us (1.024)
  blocking collectives: 28.4 us -> 85.2 us
  waiting for transfers between devices: 153 us -> 120 us
  starting transfers between devices: 103 us -> 90.2 us
  local copies, waits for them, and re-layouts: 25.4 us -> 21.5 us
    all_to_all x0 -> x2, blocking collectives: none -> 51.7 us  [swap_blocks(): return lax.all_to_all(values, axis, split_axis=0, concat_axis=0, tiled=True)]
    all_to_all x12 -> x8, waiting for transfers between devices: 151 us -> 120 us  [swap_blocks(): return lax.all_to_all(values, axis, split_axis=0, concat_axis=0, tiled=True)]
    all_to_all x12 -> x8, starting transfers between devices: 78.3 us -> 67.2 us  [swap_blocks(): return lax.all_to_all(values, axis, split_axis=0, concat_axis=0, tiled=True)]
    ppermute x4 -> x2, starting transfers between devices: 13.6 us -> 6.9 us  [halve(): lax.ppermute(give, axis, [(i, i ^ mask) for i in range(size)])]
    ppermute x3 -> x5, starting transfers between devices: 8.74 us -> 14 us  [the longest x3 9.22 us: lon_gather_async(): moved.append(lax.ppermute(block, 'lon', pairs))]
    all_gather x2, blocking collectives: 28.4 us -> 33.5 us  [lon_gather(): return lax.all_gather(values, 'lon', axis=0, tiled=True)]
    dot_general x11 -> x8, matrix products: 11.5 us -> 7.03 us  [the longest x2 2.31 us: synthesize(): lax.dot_general(table, values.reshape(total_lat, width), (((0,), (0,)), (...]
    dot_general x2, matrix products: 0.65 us -> 4.39 us  [from_fourier(): out = jnp.dot(matrix, values, preferred_element_type=jnp.float32)]
  transfers between devices with their start and end apart: 20 -> 16, of which waited for: 13 -> 8; matrix products, arithmetic and copies ran while one was open for 8% -> 9% of each run, Pallas kernels for 0% -> 0%
where the time goes in v3:
time: 346 us; the launch traced here: 345 us
  waiting for transfers between devices  120 us (35%)
  starting transfers between devices  90.2 us (26%)
  blocking collectives  85.2 us (25%)
  local copies, waits for them, and re-layouts  21.5 us (6%)
  matrix products  18.1 us (5%)
  other arithmetic  8.8 us (3%)
    all_to_all x8, waiting for transfers between devices, swap_blocks(): return lax.all_to_all(values, axis, split_axis=0, concat_axis=0, tiled=True)  120 us
    all_to_all x8, starting transfers between devices, swap_blocks(): return lax.all_to_all(values, axis, split_axis=0, concat_axis=0, tiled=True)  67.2 us
    all_to_all x2, blocking collectives, swap_blocks(): return lax.all_to_all(values, axis, split_axis=0, concat_axis=0, tiled=True)  51.7 us
    all_gather x2, blocking collectives, lon_gather(): return lax.all_gather(values, 'lon', axis=0, tiled=True)  33.5 us
    ppermute x3, starting transfers between devices, lon_gather_async(): moved.append(lax.ppermute(block, 'lon', pairs))  9.22 us
    unnamed x40, local copies, waits for them, and re-layouts  7.29 us
  transfers between devices with their start and end apart: 16, of which 8 were waited for; matrix products, arithmetic and copies ran while one was open for 9% of the time, Pallas kernels for 0%

profile of v3, /device:TPU:32, one launch (start us, length us, event | category | flops | bytes accessed | tf_op | source)
XLA Modules:
  0.0 345.0 jit_solution(10720651901556182420)
XLA Ops:
  0.7 1.2 copy.43
  1.8 17.5 %all_gather.6 = bf16[512,768]{0,1:T(8,128)(2,1)S(1)} all-gather(bf16[128,768]{0,1:T(8,128)(2,1)S(1)} %bitcast.108), channel_id=1, replica_groups=mesh['lat'=128,'lon'=4] {'lon'}, dimensions={0}, use_global_device_ids=true | all-gather | bytes 983040 | tf_op jit(solution)/shard_map/forward_analysis/all_gather | solution.py:108
  19.3 0.8 dynamic_slice.20
  20.1 1.3 fusion.2
  22.2 3.0 collective-permute-start
  25.2 3.9 %collective-permute-start.1 = (bf16[2,2,384,96]{2,3,0,1:T(8,128)(2,1)S(1)}, bf16[2,2,384,96]{2,3,0,1:T(8,128)(2,1)S(1)}, u32[]{:S(2)}, u32[]{:S(2)}) collective-permute-start(bf16[2,2,384,96]{2,3,0,1:T(8,128)(2,1)S(1)} %copy.45), channel_id=1, source_target_pairs={{0,2},{1,3},{2,0},{3,1},{4,6},{5,7},{6,4},{7,5},{8,10},{9,11},{10,... | collective-permute-start | bytes 884744 | tf_op jit(solution)/shard_map/weights/ppermute | solution.py:70
  29.1 2.3 collective-permute-start.2
  31.4 19.2 %all-to-all-start = ((bf16[128,2,384]{2,1,0:T(2,128)(2,1)}), bf16[128,2,384]{2,1,0:T(2,128)(2,1)S(1)}, u32[]{:S(2)}, u32[]{:S(2)}) async-start(bf16[128,2,384]{2,1,0:T(2,128)(2,1)} %reshape.106), calls=%async_computation | async-start | bytes 393216 | tf_op jit(solution)/shard_map/forward_analysis/all_to_all | solution.py:63
  50.7 0.8 bitcast_dynamic-update-slice_fusion.5
  51.4 0.7 bitcast_dynamic-update-slice_fusion.3
  52.2 0.7 bitcast_dynamic-update-slice_fusion.1
  52.9 0.7 bitcast_dynamic-update-slice_fusion
  53.7 16.8 %all-to-all-done = bf16[128,2,384]{2,1,0:T(2,128)(2,1)S(1)} async-done(((bf16[128,2,384]{2,1,0:T(2,128)(2,1)}), bf16[128,2,384]{2,1,0:T(2,128)(2,1)S(1)}, u32[]{:S(2)}, u32[]{:S(2)}) %all-to-all-start) | async-done | bytes 196640 | tf_op jit(solution)/shard_map/forward_analysis/all_to_all | solution.py:63
  70.5 1.1 convolution_convert_fusion.5
  71.7 0.8 reshape.109
  72.4 6.2 %all-to-all-start.1 = ((bf16[128,2,384]{2,1,0:T(2,128)(2,1)}), bf16[128,2,384]{2,1,0:T(2,128)(2,1)S(1)}, u32[]{:S(2)}, u32[]{:S(2)}) async-start(bf16[128,2,384]{2,1,0:T(2,128)(2,1)} %reshape.109), calls=%async_computation.1 | async-start | bytes 393216 | tf_op jit(solution)/shard_map/forward_analysis/all_to_all | solution.py:63
  78.7 0.8 bitcast_dynamic-update-slice_fusion.6
  79.4 0.7 bitcast_dynamic-update-slice_fusion.4
  80.2 0.8 bitcast_dynamic-update-slice_fusion.2
  81.0 1.4 constant_dynamic-slice_fusion
  82.4 16.1 %all-to-all-done.1 = bf16[128,2,384]{2,1,0:T(2,128)(2,1)S(1)} async-done(((bf16[128,2,384]{2,1,0:T(2,128)(2,1)}), bf16[128,2,384]{2,1,0:T(2,128)(2,1)S(1)}, u32[]{:S(2)}, u32[]{:S(2)}) %all-to-all-start.1) | async-done | bytes 196640 | tf_op jit(solution)/shard_map/forward_analysis/all_to_all | solution.py:63
  99.4 25.9 %all_to_all.50 = bf16[128,2,384]{2,1,0:T(2,128)(2,1)S(1)} all-to-all(bf16[128,2,384]{2,1,0:T(2,128)(2,1)S(1)} %copy.51), channel_id=1, replica_groups=mesh['lat'=128,'lon'=4] {'lat'}, dimensions={0} | all-to-all | bytes 393216 | tf_op jit(solution)/shard_map/forward_synthesis/all_to_all | solution.py:63
  125.4 1.2 convolution_convert_fusion.4
  126.6 25.8 %all_to_all.51 = bf16[128,2,384]{2,1,0:T(2,128)(2,1)S(1)} all-to-all(bf16[128,2,384]{2,1,0:T(2,128)(2,1)S(1)} %reshape.111), channel_id=1, replica_groups=mesh['lat'=128,'lon'=4] {'lat'}, dimensions={0} | all-to-all | bytes 393216 | tf_op jit(solution)/shard_map/forward_synthesis/all_to_all | solution.py:63
  152.5 2.1 convolution_convert_fusion
  154.6 4.1 %all-to-all-start.4 = ((bf16[4,128,768]{2,1,0:T(8,128)(2,1)}), bf16[4,128,768]{2,1,0:T(8,128)(2,1)S(1)}, u32[]{:S(2)}, u32[]{:S(2)}) async-start(bf16[4,128,768]{2,1,0:T(8,128)(2,1)} %bitcast.12), calls=%async_computation.4 | async-start | bytes 1572864 | tf_op jit(solution)/shard_map/forward_synthesis/all_to_all | solution.py:63
  158.7 12.6 %all-to-all-done.4 = bf16[4,128,768]{2,1,0:T(8,128)(2,1)S(1)} async-done(((bf16[4,128,768]{2,1,0:T(8,128)(2,1)}), bf16[4,128,768]{2,1,0:T(8,128)(2,1)S(1)}, u32[]{:S(2)}, u32[]{:S(2)}) %all-to-all-start.4) | async-done | bytes 786464 | tf_op jit(solution)/shard_map/forward_synthesis/all_to_all | solution.py:63
  173.8 16.1 %all_gather.7 = bf16[512,768]{0,1:T(8,128)(2,1)S(1)} all-gather(bf16[128,768]{0,1:T(8,128)(2,1)S(1)} %bitcast.115), channel_id=1, replica_groups=mesh['lat'=128,'lon'=4] {'lon'}, dimensions={0}, use_global_device_ids=true | all-gather | bytes 983040 | tf_op jit(solution)/shard_map/backward_analysis/all_gather | solution.py:108
  189.8 1.3 convolution_convert_fusion.6
  191.9 5.9 %all-to-all-start.5 = ((bf16[128,2,384]{2,1,0:T(2,128)(2,1)}), bf16[128,2,384]{2,1,0:T(2,128)(2,1)S(1)}, u32[]{:S(2)}, u32[]{:S(2)}) async-start(bf16[128,2,384]{2,1,0:T(2,128)(2,1)} %reshape.120), calls=%async_computation.5 | async-start | bytes 393216 | tf_op jit(solution)/shard_map/backward_analysis/all_to_all | solution.py:63
  198.4 1.4 broadcast_select_fusion
  199.8 0.9 select_convert_fusion
  200.8 2.1 collective-permute-start.3
  202.8 1.4 fusion.73
  204.2 1.2 copy.54
  205.5 0.8 reshape.117
  206.3 11.4 %all-to-all-done.5 = bf16[128,2,384]{2,1,0:T(2,128)(2,1)S(1)} async-done(((bf16[128,2,384]{2,1,0:T(2,128)(2,1)}), bf16[128,2,384]{2,1,0:T(2,128)(2,1)S(1)}, u32[]{:S(2)}, u32[]{:S(2)}) %all-to-all-start.5) | async-done | bytes 196640 | tf_op jit(solution)/shard_map/backward_analysis/all_to_all | solution.py:63
  217.7 1.1 convolution_convert_fusion.3
  218.9 0.8 reshape.122
  219.6 6.6 %all-to-all-start.6 = ((bf16[128,2,384]{2,1,0:T(2,128)(2,1)}), bf16[128,2,384]{2,1,0:T(2,128)(2,1)}, u32[]{:S(2)}, u32[]{:S(2)}) async-start(bf16[128,2,384]{2,1,0:T(2,128)(2,1)} %reshape.122), calls=%async_computation.6 | async-start | bytes 393216 | tf_op jit(solution)/shard_map/backward_analysis/all_to_all | solution.py:63
  226.3 1.2 convert_add_fusion.1
  227.8 3.0 collective-permute-start.4
  230.9 15.0 %all-to-all-done.6 = bf16[128,2,384]{2,1,0:T(2,128)(2,1)} async-done(((bf16[128,2,384]{2,1,0:T(2,128)(2,1)}), bf16[128,2,384]{2,1,0:T(2,128)(2,1)}, u32[]{:S(2)}, u32[]{:S(2)}) %all-to-all-start.6) | async-done | bytes 196640 | tf_op jit(solution)/shard_map/backward_analysis/all_to_all | solution.py:63
  245.8 1.3 convolution_bitcast_fusion.1
  247.3 0.8 select_convert_fusion.3
  248.1 3.9 %collective-permute-start.5 = (bf16[128,576]{1,0:T(8,128)(2,1)}, bf16[128,576]{1,0:T(8,128)(2,1)}, u32[]{:S(2)}, u32[]{:S(2)}) collective-permute-start(bf16[128,576]{1,0:T(8,128)(2,1)} %select_convert_fusion.3), channel_id=1, source_target_pairs={{0,1},{1,0},{2,3},{3,2},{4,5},{5,4},{6,7},{7,6},{8,9},{9,8},{10,11... | collective-permute-start | bytes 442376 | tf_op jit(solution)/shard_map/pointwise_weights/ppermute | solution.py:81
  251.9 0.9 copy.57
  252.8 7.6 %all-to-all-start.7 = ((bf16[128,2,384]{2,1,0:T(2,128)(2,1)}), bf16[128,2,384]{2,1,0:T(2,128)(2,1)S(1)}, u32[]{:S(2)}, u32[]{:S(2)}) async-start(bf16[128,2,384]{2,1,0:T(2,128)(2,1)} %copy.57), calls=%async_computation.7 | async-start | bytes 393216 | tf_op jit(solution)/shard_map/backward_synthesis/all_to_all | solution.py:63
  260.4 1.0 copy.86
  262.1 2.8 collective-permute-start.6
  265.3 1.1 add_convert_fusion.1
  266.4 13.8 %all-to-all-done.7 = bf16[128,2,384]{2,1,0:T(2,128)(2,1)S(1)} async-done(((bf16[128,2,384]{2,1,0:T(2,128)(2,1)}), bf16[128,2,384]{2,1,0:T(2,128)(2,1)S(1)}, u32[]{:S(2)}, u32[]{:S(2)}) %all-to-all-start.7) | async-done | bytes 196640 | tf_op jit(solution)/shard_map/backward_synthesis/all_to_all | solution.py:63
  280.3 1.2 convolution_convert_fusion.2
  281.6 1.1 pad_maximum_fusion
  282.7 14.0 %all-to-all-start.8 = ((bf16[128,2,768]{2,1,0:T(2,128)(2,1)}), bf16[128,2,768]{2,1,0:T(2,128)(2,1)S(1)}, u32[]{:S(2)}, u32[]{:S(2)}) async-start(bf16[128,2,768]{2,1,0:T(2,128)(2,1)} %pad_maximum_fusion), calls=%async_computation.8 | async-start | bytes 786432 | tf_op jit(solution)/shard_map/backward_synthesis/all_to_all | solution.py:63
  296.8 0.8 select_convert_fusion.1
  297.6 2.0 collective-permute-start.7
  299.6 24.9 %all-to-all-done.8 = bf16[128,2,768]{2,1,0:T(2,128)(2,1)S(1)} async-done(((bf16[128,2,768]{2,1,0:T(2,128)(2,1)}), bf16[128,2,768]{2,1,0:T(2,128)(2,1)S(1)}, u32[]{:S(2)}, u32[]{:S(2)}) %all-to-all-start.8) | async-done | bytes 393248 | tf_op jit(solution)/shard_map/backward_synthesis/all_to_all | solution.py:63
  324.9 2.2 multiply_convert_fusion
  327.1 3.5 %all-to-all-start.9 = ((bf16[4,128,768]{2,1,0:T(8,128)(2,1)}), bf16[4,128,768]{2,1,0:T(8,128)(2,1)S(1)}, u32[]{:S(2)}, u32[]{:S(2)}) async-start(bf16[4,128,768]{2,1,0:T(8,128)(2,1)} %bitcast.29), calls=%async_computation.9 | async-start | bytes 1572864 | tf_op jit(solution)/shard_map/backward_synthesis/all_to_all | solution.py:63
  330.6 1.0 fusion.3
  331.7 1.0 convert_add_fusion.2
  332.7 0.9 copy.65
  334.5 9.3 %all-to-all-done.9 = bf16[4,128,768]{2,1,0:T(8,128)(2,1)S(1)} async-done(((bf16[4,128,768]{2,1,0:T(8,128)(2,1)}), bf16[4,128,768]{2,1,0:T(8,128)(2,1)S(1)}, u32[]{:S(2)}, u32[]{:S(2)}) %all-to-all-start.9) | async-done | bytes 786464 | tf_op jit(solution)/shard_map/backward_synthesis/all_to_all | solution.py:63
  (87 shorter events, 10.0 us)
Async XLA Ops:
  0.6 171.2 %copy-start = (bf16[384,768]{1,0:T(8,128)(2,1)S(1)}, bf16[384,768]{1,0:T(8,128)(2,1)}, u32[]{:S(2)}) copy-start(bf16[384,768]{1,0:T(8,128)(2,1)} %param.12) | copy-start | bytes 1769476
  0.6 21.5 %copy-start.11 = (bf16[2,2,384,96]{2,3,1,0:T(8,128)(2,1)S(1)}, bf16[2,2,384,96]{2,3,1,0:T(8,128)(2,1)}, u32[]{:S(2)}) copy-start(bf16[2,2,384,96]{2,3,1,0:T(8,128)(2,1)} %param.11) | copy-start | bytes 884740
  22.2 28.5 %collective-permute-start = (bf16[2,2,384,96]{2,3,0,1:T(8,128)(2,1)S(1)}, bf16[2,2,384,96]{2,3,0,1:T(8,128)(2,1)S(1)}, u32[]{:S(2)}, u32[]{:S(2)}) collective-permute-start(bf16[2,2,384,96]{2,3,0,1:T(8,128)(2,1)S(1)} %copy.45), channel_id=1, source_target_pairs={{0,3},{1,0},{2,1},{3,2},{4,7},{5,4},{6,5},{7,6},{8,11},{9,8},{10,9... | collective-permute-start | bytes 884744 | tf_op jit(solution)/shard_map/weights/ppermute | solution.py:70
  25.2 26.2 %collective-permute-start.1 = (bf16[2,2,384,96]{2,3,0,1:T(8,128)(2,1)S(1)}, bf16[2,2,384,96]{2,3,0,1:T(8,128)(2,1)S(1)}, u32[]{:S(2)}, u32[]{:S(2)}) collective-permute-start(bf16[2,2,384,96]{2,3,0,1:T(8,128)(2,1)S(1)} %copy.45), channel_id=1, source_target_pairs={{0,2},{1,3},{2,0},{3,1},{4,6},{5,7},{6,4},{7,5},{8,10},{9,11},{10,... | collective-permute-start | bytes 884744 | tf_op jit(solution)/shard_map/weights/ppermute | solution.py:70
  29.1 23.1 %collective-permute-start.2 = (bf16[2,2,384,96]{2,3,0,1:T(8,128)(2,1)S(1)}, bf16[2,2,384,96]{2,3,0,1:T(8,128)(2,1)S(1)}, u32[]{:S(2)}, u32[]{:S(2)}) collective-permute-start(bf16[2,2,384,96]{2,3,0,1:T(8,128)(2,1)S(1)} %copy.45), channel_id=1, source_target_pairs={{0,1},{1,2},{2,3},{3,0},{4,5},{5,6},{6,7},{7,4},{8,9},{9,10},{10,1... | collective-permute-start | bytes 884744 | tf_op jit(solution)/shard_map/weights/ppermute | solution.py:70
  31.4 39.0 %all-to-all-start = ((bf16[128,2,384]{2,1,0:T(2,128)(2,1)}), bf16[128,2,384]{2,1,0:T(2,128)(2,1)S(1)}, u32[]{:S(2)}, u32[]{:S(2)}) async-start(bf16[128,2,384]{2,1,0:T(2,128)(2,1)} %reshape.106), calls=%async_computation | async-start | bytes 393216 | tf_op jit(solution)/shard_map/forward_analysis/all_to_all | solution.py:63
  72.4 26.1 %all-to-all-start.1 = ((bf16[128,2,384]{2,1,0:T(2,128)(2,1)}), bf16[128,2,384]{2,1,0:T(2,128)(2,1)S(1)}, u32[]{:S(2)}, u32[]{:S(2)}) async-start(bf16[128,2,384]{2,1,0:T(2,128)(2,1)} %reshape.109), calls=%async_computation.1 | async-start | bytes 393216 | tf_op jit(solution)/shard_map/forward_analysis/all_to_all | solution.py:63
  98.5 0.7 copy-start.7
  154.6 16.7 %all-to-all-start.4 = ((bf16[4,128,768]{2,1,0:T(8,128)(2,1)}), bf16[4,128,768]{2,1,0:T(8,128)(2,1)S(1)}, u32[]{:S(2)}, u32[]{:S(2)}) async-start(bf16[4,128,768]{2,1,0:T(8,128)(2,1)} %bitcast.12), calls=%async_computation.4 | async-start | bytes 1572864 | tf_op jit(solution)/shard_map/forward_synthesis/all_to_all | solution.py:63
  171.5 0.9 copy-start.12
  171.6 1.1 copy-start.13
  171.8 26.0 %copy-start.5 = (bf16[2,128,384]{2,1,0:T(8,128)(2,1)}, bf16[2,128,384]{2,1,0:T(8,128)(2,1)S(1)}, u32[]{:S(2)}) copy-start(bf16[2,128,384]{2,1,0:T(8,128)(2,1)S(1)} %copy.53) | copy-start | bytes 589828
  172.2 26.2 %copy-start.3 = (bf16[256,768]{1,0:T(8,128)(2,1)}, bf16[256,768]{1,0:T(8,128)(2,1)S(1)}, u32[]{:S(2)}) copy-start(bf16[256,768]{1,0:T(8,128)(2,1)S(1)} %get-tuple-element.27) | copy-start | bytes 1179652
  173.6 18.3 %copy-start.9 = (bf16[256,384]{1,0:T(8,128)(2,1)}, bf16[256,384]{1,0:T(8,128)(2,1)S(1)}, u32[]{:S(2)}) copy-start(bf16[256,384]{1,0:T(8,128)(2,1)S(1)} %fusion.4) | copy-start | bytes 589828
  191.9 25.8 %all-to-all-start.5 = ((bf16[128,2,384]{2,1,0:T(2,128)(2,1)}), bf16[128,2,384]{2,1,0:T(2,128)(2,1)S(1)}, u32[]{:S(2)}, u32[]{:S(2)}) async-start(bf16[128,2,384]{2,1,0:T(2,128)(2,1)} %reshape.120), calls=%async_computation.5 | async-start | bytes 393216 | tf_op jit(solution)/shard_map/backward_analysis/all_to_all | solution.py:63
  200.8 18.9 %collective-permute-start.3 = (bf16[768,384]{1,0:T(8,128)(2,1)}, bf16[768,384]{1,0:T(8,128)(2,1)}, u32[]{:S(2)}, u32[]{:S(2)}) collective-permute-start(bf16[768,384]{1,0:T(8,128)(2,1)} %select_convert_fusion), channel_id=1, source_target_pairs={{0,4},{4,0},{8,12},{12,8},{16,20},{20,16},{24,28},{28,24},{32,36},... | collective-permute-start | bytes 1769480 | tf_op jit(solution)/shard_map/pointwise_weights/ppermute | solution.py:195
  206.3 20.0 %copy-start.2 = (f32[768,384]{1,0:T(8,128)S(1)}, f32[768,384]{1,0:T(8,128)}, u32[]{:S(2)}) copy-start(f32[768,384]{1,0:T(8,128)} %get-tuple-element.29) | copy-start | bytes 3538948
  219.6 26.2 %all-to-all-start.6 = ((bf16[128,2,384]{2,1,0:T(2,128)(2,1)}), bf16[128,2,384]{2,1,0:T(2,128)(2,1)}, u32[]{:S(2)}, u32[]{:S(2)}) async-start(bf16[128,2,384]{2,1,0:T(2,128)(2,1)} %reshape.122), calls=%async_computation.6 | async-start | bytes 393216 | tf_op jit(solution)/shard_map/backward_analysis/all_to_all | solution.py:63
  227.8 19.5 %collective-permute-start.4 = (bf16[128,1152]{1,0:T(8,128)(2,1)S(1)}, bf16[128,1152]{1,0:T(8,128)(2,1)S(1)}, u32[]{:S(2)}, u32[]{:S(2)}) collective-permute-start(bf16[128,1152]{1,0:T(8,128)(2,1)S(1)} %select_convert_fusion.2), channel_id=1, source_target_pairs={{0,3},{1,2},{2,1},{3,0},{4,7},{5,6},{6,5},{7,4},{8,11},{9,10},{10,... | collective-permute-start | bytes 884744 | tf_op jit(solution)/shard_map/pointwise_weights/ppermute | solution.py:81
  247.2 14.2 %copy-start.8 = (bf16[128,2,384]{2,1,0:T(2,128)(2,1)S(1)}, bf16[128,2,384]{2,1,0:T(2,128)(2,1)}, u32[]{:S(2)}) copy-start(bf16[128,2,384]{2,1,0:T(2,128)(2,1)} %copy-done.7) | copy-start | bytes 589828
  248.1 17.2 %collective-permute-start.5 = (bf16[128,576]{1,0:T(8,128)(2,1)}, bf16[128,576]{1,0:T(8,128)(2,1)}, u32[]{:S(2)}, u32[]{:S(2)}) collective-permute-start(bf16[128,576]{1,0:T(8,128)(2,1)} %select_convert_fusion.3), channel_id=1, source_target_pairs={{0,1},{1,0},{2,3},{3,2},{4,5},{5,4},{6,7},{7,6},{8,9},{9,8},{10,11... | collective-permute-start | bytes 442376 | tf_op jit(solution)/shard_map/pointwise_weights/ppermute | solution.py:81
  252.8 27.4 %all-to-all-start.7 = ((bf16[128,2,384]{2,1,0:T(2,128)(2,1)}), bf16[128,2,384]{2,1,0:T(2,128)(2,1)S(1)}, u32[]{:S(2)}, u32[]{:S(2)}) async-start(bf16[128,2,384]{2,1,0:T(2,128)(2,1)} %copy.57), calls=%async_computation.7 | async-start | bytes 393216 | tf_op jit(solution)/shard_map/backward_synthesis/all_to_all | solution.py:63
  262.1 20.5 %collective-permute-start.6 = (bf16[2,2,192,384]{3,2,0,1:T(8,128)(2,1)S(1)}, bf16[2,2,192,384]{3,2,0,1:T(8,128)(2,1)S(1)}, u32[]{:S(2)}, u32[]{:S(2)}) collective-permute-start(bf16[2,2,192,384]{3,2,0,1:T(8,128)(2,1)S(1)} %fusion.1), channel_id=1, source_target_pairs={{0,3},{1,2},{2,1},{3,0},{4,7},{5,6},{6,5},{7,4},{8,11},{9,10},{10,... | collective-permute-start | bytes 1769480 | tf_op jit(solution)/shard_map/unmix/ppermute | solution.py:230
  282.7 41.9 %all-to-all-start.8 = ((bf16[128,2,768]{2,1,0:T(2,128)(2,1)}), bf16[128,2,768]{2,1,0:T(2,128)(2,1)S(1)}, u32[]{:S(2)}, u32[]{:S(2)}) async-start(bf16[128,2,768]{2,1,0:T(2,128)(2,1)} %pad_maximum_fusion), calls=%async_computation.8 | async-start | bytes 786432 | tf_op jit(solution)/shard_map/backward_synthesis/all_to_all | solution.py:63
  297.6 34.1 %collective-permute-start.7 = (bf16[2,2,96,384]{3,2,0,1:T(8,128)(2,1)}, bf16[2,2,96,384]{3,2,0,1:T(8,128)(2,1)}, u32[]{:S(2)}, u32[]{:S(2)}) collective-permute-start(bf16[2,2,96,384]{3,2,0,1:T(8,128)(2,1)} %select_convert_fusion.1), channel_id=1, source_target_pairs={{0,1},{1,0},{2,3},{3,2},{4,5},{5,4},{6,7},{7,6},{8,9},{9,8},{10,11... | collective-permute-start | bytes 884744 | tf_op jit(solution)/shard_map/unmix/ppermute | solution.py:249
  324.8 5.8 %copy-start.4 = (bf16[256,768]{1,0:T(8,128)(2,1)S(1)}, bf16[256,768]{1,0:T(8,128)(2,1)}, u32[]{:S(2)}) copy-start(bf16[256,768]{1,0:T(8,128)(2,1)} %copy-done.3) | copy-start | bytes 1179652
  324.8 5.8 %copy-start.6 = (bf16[2,128,384]{2,1,0:T(8,128)(2,1)S(1)}, bf16[2,128,384]{2,1,0:T(8,128)(2,1)}, u32[]{:S(2)}) copy-start(bf16[2,128,384]{2,1,0:T(8,128)(2,1)} %copy-done.5) | copy-start | bytes 589828
  324.8 5.8 %copy-start.14 = (bf16[768,384]{1,0:T(8,128)(2,1)S(1)}, bf16[768,384]{1,0:T(8,128)(2,1)}, u32[]{:S(2)}) copy-start(bf16[768,384]{1,0:T(8,128)(2,1)} %param.13) | copy-start | bytes 1769476
  327.1 16.7 %all-to-all-start.9 = ((bf16[4,128,768]{2,1,0:T(8,128)(2,1)}), bf16[4,128,768]{2,1,0:T(8,128)(2,1)S(1)}, u32[]{:S(2)}, u32[]{:S(2)}) async-start(bf16[4,128,768]{2,1,0:T(8,128)(2,1)} %bitcast.29), calls=%async_computation.9 | async-start | bytes 1572864 | tf_op jit(solution)/shard_map/backward_synthesis/all_to_all | solution.py:63
  333.6 10.7 %copy-start.10 = (bf16[256,384]{1,0:T(8,128)(2,1)S(1)}, bf16[256,384]{1,0:T(8,128)(2,1)}, u32[]{:S(2)}) copy-start(bf16[256,384]{1,0:T(8,128)(2,1)} %copy-done.9) | copy-start | bytes 589828
  333.9 11.1 %copy-start.1 = (bf16[384,768]{1,0:T(8,128)(2,1)S(1)}, bf16[384,768]{1,0:T(8,128)(2,1)}, u32[]{:S(2)}) copy-start(bf16[384,768]{1,0:T(8,128)(2,1)} %param.12) | copy-start | bytes 1769476

commit v4 on v3

--- a/solution.py
+++ b/solution.py
@@ -63,27 +63,35 @@
     return lax.all_to_all(values, axis, split_axis=0, concat_axis=0, tiled=True)
 
 
-def lon_gather_async(block, lon_index, lon_count):
+def lon_sends(block, lon_count):
     moved = [block]
     for shift in range(1, lon_count):
         pairs = [(i, (i + shift) % lon_count) for i in range(lon_count)]
         moved.append(lax.ppermute(block, "lon", pairs))
+    return moved
+
+
+def in_order(moved, lon_index):
     backwards = jnp.stack(moved[::-1] + moved[:0:-1])
-    return lax.dynamic_slice_in_dim(backwards, lon_count - 1 - lon_index, lon_count, 0)
-
-
-def halve(values, axis, index, mask, bit):
-    size = lax.axis_size(axis)
-    width = values.shape[-1] // 2
-    high = (index >> bit) & 1 == 1
-    keep = jnp.where(high, values[:, width:], values[:, :width])
-    give = jnp.where(high, values[:, :width], values[:, width:]).astype(jnp.bfloat16)
-    return keep, lax.ppermute(give, axis, [(i, i ^ mask) for i in range(size)])
-
-
-def add_swapped(pair):
-    keep, got = pair
-    return keep + got.astype(jnp.float32)
+    return lax.dynamic_slice_in_dim(backwards, len(moved) - 1 - lon_index, len(moved), 0)
+
+
+def scatter_sum(values, axis, index, count, shifted):
+    chunk = values.shape[-1] // count
+    narrow = values.astype(jnp.bfloat16)
+    parts = [lax.dynamic_slice_in_dim(values, index * chunk, chunk, axis=1)]
+    for shift in range(1, count):
+        to = (index + shift) % count
+        block = lax.dynamic_slice_in_dim(narrow, to * chunk, chunk, axis=1)
+        parts.append(lax.ppermute(block, axis, shifted(shift)))
+    return parts
+
+
+def add_parts(parts):
+    total = parts[0]
+    for part in parts[1:]:
+        total = total + part.astype(jnp.float32)
+    return total
 
 
 def body(table_all, plain_all, doubled_all, quad, grid, cotangent, spectral_weight, w_in, w_out):
@@ -146,14 +154,14 @@
 
     with jax.named_scope("forward_analysis"):
         four = to_fourier(lon_gather(grid), plain, quad_lanes)
-        four, own_weight = lax.optimization_barrier((four, spectral_weight))
-        four = swap_blocks(four, "lat")
+        four = analyze(swap_blocks(four, "lat"))
+        four, *moved = lax.optimization_barrier((four, *lon_sends(spectral_weight, lon_count)))
     with jax.named_scope("weights"):
-        weights = lon_gather_async(own_weight, lon_index, lon_count)
+        weights = in_order(moved, lon_index)
         mix_weights = weights.transpose(2, 3, 1, 0, 4).reshape(rows, width, 2 * width)
         unmix_weights = weights.transpose(2, 0, 4, 1, 3).reshape(rows, width, 2 * width)
     with jax.named_scope("forward_analysis"):
-        spectrum = swap_blocks(analyze(four), "lat")
+        spectrum = swap_blocks(four, "lat")
     with jax.named_scope("mix"):
         mixed = complex_product(spectrum, mix_weights, -1.0)
     with jax.named_scope("forward_synthesis"):
@@ -198,17 +206,29 @@
         mixed_grad, keep, got = lax.optimization_barrier((mixed_grad, keep, got))
         mixed_grad = swap_blocks(mixed_grad, "lat")
     with jax.named_scope("pointwise_weights"):
-        sums = add_swapped((keep, got)).reshape(lat_count, -1)
-        keep, got = halve(sums, "lon", lon_index, 3, 1)
+        sums = add_parts([keep, got]).reshape(lat_count, -1)
+        parts = scatter_sum(
+            sums,
+            "lon",
+            lon_index,
+            lon_count,
+            lambda s: [(i, (i + s) % lon_count) for i in range(lon_count)],
+        )
     with jax.named_scope("unmix"):
         spectrum_grad = complex_product(mixed_grad, unmix_weights, 1.0)
-        spectrum_grad, keep, got, left, right = lax.optimization_barrier(
-            (spectrum_grad, keep, got, spectrum, mixed_grad)
+        spectrum_grad, left, right, *parts = lax.optimization_barrier(
+            (spectrum_grad, spectrum, mixed_grad, *parts)
         )
     with jax.named_scope("backward_synthesis"):
         spectrum_grad = swap_blocks(spectrum_grad, "lat")
     with jax.named_scope("pointwise_weights"):
-        keep, got = halve(add_swapped((keep, got)), "lon", lon_index, 1, 0)
+        parts = scatter_sum(
+            add_parts(parts),
+            "lat",
+            (lat_index >> 1) & 3,
+            4,
+            lambda s: [(i, (i & ~6) | ((i + 2 * s) & 6)) for i in range(lat_count)],
+        )
     with jax.named_scope("unmix"):
         turned = jnp.concatenate([right[half:], -right[:half]])
         right = jnp.stack([right, turned])
@@ -232,9 +252,10 @@
         )
     with jax.named_scope("backward_synthesis"):
         four_grad = synthesize(spectrum_grad)
-        chunk = keep.shape[1]
+        extra = add_parts(parts).astype(jnp.bfloat16)
+        chunk = extra.shape[1]
         room = -(-chunk // (rows * 128)) * rows * 128
-        extra = jnp.pad(add_swapped((keep, got)).astype(jnp.bfloat16), ((0, 0), (0, room - chunk)))
+        extra = jnp.pad(extra, ((0, 0), (0, room - chunk)))
         extra = extra.reshape(lat_count, rows, room // rows)
         four_grad = jnp.concatenate([four_grad, extra], axis=2)
         four_grad, spec_keep, spec_got = lax.optimization_barrier((four_grad, spec_keep, spec_got))
@@ -249,8 +270,8 @@
         spec_got = lax.ppermute(spec_give, "lon", [(i, i ^ 1) for i in range(lon_count)])
         grad_spectral = jnp.where(high, high_rows, low_rows) + spec_got.astype(jnp.float32)
     with jax.named_scope("pointwise_weights"):
-        sums = four_grad[:, :, width:].reshape(half, 2, room)[:, :, :chunk]
-        sums = jnp.sum(sums.astype(jnp.float32), axis=0)
+        sums = four_grad[:, :, width:].reshape(lat_count // 8, 4, 2, room)[..., :chunk]
+        sums = jnp.sum(sums.astype(jnp.float32), axis=0).swapaxes(0, 1).reshape(2, -1)
     return (
         block_output.reshape(grid.shape),
         grad_input.reshape(grid.shape),

time: 346 us -> 356 us (1.029)
  starting transfers between devices: 90.2 us -> 125 us
  waiting for transfers between devices: 120 us -> 93.9 us
    all_to_all x8, waiting for transfers between devices: 120 us -> 93.3 us  [swap_blocks(): return lax.all_to_all(values, axis, split_axis=0, concat_axis=0, tiled=True)]
    all_to_all x8, starting transfers between devices: 67.2 us -> 85 us  [swap_blocks(): return lax.all_to_all(values, axis, split_axis=0, concat_axis=0, tiled=True)]
    ppermute x5 -> x9, starting transfers between devices: 16.1 us -> 31 us  [the longest x6 20.5 us: scatter_sum(): parts.append(lax.ppermute(block, axis, shifted(shift)))]
    unnamed x40 -> x41, local copies, waits for them, and re-layouts: 7.29 us -> 7.37 us
  transfers between devices with their start and end apart: 16 -> 20, of which waited for: 8 -> 9; matrix products, arithmetic and copies ran while one was open for 9% -> 9% of each run, Pallas kernels for 0% -> 0%
where the time goes in v4:
time: 356 us; the launch traced here: 355 us
  starting transfers between devices  125 us (35%)
  waiting for transfers between devices  93.9 us (26%)
  blocking collectives  85.2 us (24%)
  local copies, waits for them, and re-layouts  23.9 us (7%)
  matrix products  18.1 us (5%)
  other arithmetic  7.18 us (2%)
    all_to_all x8, waiting for transfers between devices, swap_blocks(): return lax.all_to_all(values, axis, split_axis=0, concat_axis=0, tiled=True)  93.3 us
    all_to_all x8, starting transfers between devices, swap_blocks(): return lax.all_to_all(values, axis, split_axis=0, concat_axis=0, tiled=True)  85 us
    all_to_all x2, blocking collectives, swap_blocks(): return lax.all_to_all(values, axis, split_axis=0, concat_axis=0, tiled=True)  51.7 us
    all_gather x2, blocking collectives, lon_gather(): return lax.all_gather(values, 'lon', axis=0, tiled=True)  33.5 us
    ppermute x6, starting transfers between devices, scatter_sum(): parts.append(lax.ppermute(block, axis, shifted(shift)))  20.5 us
    ppermute x3, starting transfers between devices, lon_sends(): moved.append(lax.ppermute(block, 'lon', pairs))  10.4 us
    unnamed x41, local copies, waits for them, and re-layouts  7.37 us
  transfers between devices with their start and end apart: 20, of which 9 were waited for; matrix products, arithmetic and copies ran while one was open for 9% of the time, Pallas kernels for 0%

profile of v4, /device:TPU:32, one launch (start us, length us, event | category | flops | bytes accessed | tf_op | source)
XLA Modules:
  0.0 355.0 jit_solution(10783322653403852702)
XLA Ops:
  0.7 1.2 copy.43
  1.8 17.5 %all_gather.6 = bf16[512,768]{0,1:T(8,128)(2,1)S(1)} all-gather(bf16[128,768]{0,1:T(8,128)(2,1)S(1)} %bitcast.109), channel_id=1, replica_groups=mesh['lat'=128,'lon'=4] {'lon'}, dimensions={0}, use_global_device_ids=true | all-gather | bytes 983040 | tf_op jit(solution)/shard_map/forward_analysis/all_gather | solution.py:116
  20.1 1.3 fusion.2
  22.2 19.2 %all-to-all-start = ((bf16[128,2,384]{2,1,0:T(2,128)(2,1)}), bf16[128,2,384]{2,1,0:T(2,128)(2,1)S(1)}, u32[]{:S(2)}, u32[]{:S(2)}) async-start(bf16[128,2,384]{2,1,0:T(2,128)(2,1)} %reshape.111), calls=%async_computation | async-start | bytes 393216 | tf_op jit(solution)/shard_map/forward_analysis/all_to_all | solution.py:63
  41.4 2.9 collective-permute-start
  44.3 3.4 collective-permute-start.1
  47.8 4.1 %collective-permute-start.2 = (bf16[2,2,384,96]{2,3,0,1:T(8,128)(2,1)S(1)}, bf16[2,2,384,96]{2,3,0,1:T(8,128)(2,1)S(1)}, u32[]{:S(2)}, u32[]{:S(2)}) collective-permute-start(bf16[2,2,384,96]{2,3,0,1:T(8,128)(2,1)S(1)} %copy.45), channel_id=1, source_target_pairs={{0,3},{1,0},{2,1},{3,2},{4,7},{5,4},{6,5},{7,6},{8,11},{9,8},{10,9... | collective-permute-start | bytes 884744 | tf_op jit(solution)/shard_map/forward_analysis/ppermute | solution.py:70
  51.9 9.3 %all-to-all-done = bf16[128,2,384]{2,1,0:T(2,128)(2,1)S(1)} async-done(((bf16[128,2,384]{2,1,0:T(2,128)(2,1)}), bf16[128,2,384]{2,1,0:T(2,128)(2,1)S(1)}, u32[]{:S(2)}, u32[]{:S(2)}) %all-to-all-start) | async-done | bytes 196640 | tf_op jit(solution)/shard_map/forward_analysis/all_to_all | solution.py:63
  61.2 1.1 convolution_convert_fusion.5
  62.4 0.8 reshape.113
  63.9 15.4 %all-to-all-start.1 = ((bf16[128,2,384]{2,1,0:T(2,128)(2,1)}), bf16[128,2,384]{2,1,0:T(2,128)(2,1)S(1)}, u32[]{:S(2)}, u32[]{:S(2)}) async-start(bf16[128,2,384]{2,1,0:T(2,128)(2,1)} %reshape.113), calls=%async_computation.1 | async-start | bytes 393216 | tf_op jit(solution)/shard_map/forward_analysis/all_to_all | solution.py:63
  79.3 0.8 bitcast_dynamic-update-slice_fusion.3
  80.0 0.8 bitcast_dynamic-update-slice_fusion.1
  81.5 0.8 bitcast_dynamic-update-slice_fusion.6
  82.3 0.8 bitcast_dynamic-update-slice_fusion.4
  83.8 1.4 constant_dynamic-slice_fusion.7
  85.2 13.9 %all-to-all-done.1 = bf16[128,2,384]{2,1,0:T(2,128)(2,1)S(1)} async-done(((bf16[128,2,384]{2,1,0:T(2,128)(2,1)}), bf16[128,2,384]{2,1,0:T(2,128)(2,1)S(1)}, u32[]{:S(2)}, u32[]{:S(2)}) %all-to-all-start.1) | async-done | bytes 196640 | tf_op jit(solution)/shard_map/forward_analysis/all_to_all | solution.py:63
  100.0 25.9 %all_to_all.50 = bf16[128,2,384]{2,1,0:T(2,128)(2,1)S(1)} all-to-all(bf16[128,2,384]{2,1,0:T(2,128)(2,1)S(1)} %copy.51), channel_id=1, replica_groups=mesh['lat'=128,'lon'=4] {'lat'}, dimensions={0} | all-to-all | bytes 393216 | tf_op jit(solution)/shard_map/forward_synthesis/all_to_all | solution.py:63
  126.0 1.2 convolution_convert_fusion.4
  127.2 25.8 %all_to_all.51 = bf16[128,2,384]{2,1,0:T(2,128)(2,1)S(1)} all-to-all(bf16[128,2,384]{2,1,0:T(2,128)(2,1)S(1)} %reshape.116), channel_id=1, replica_groups=mesh['lat'=128,'lon'=4] {'lat'}, dimensions={0} | all-to-all | bytes 393216 | tf_op jit(solution)/shard_map/forward_synthesis/all_to_all | solution.py:63
  153.0 2.1 convolution_convert_fusion
  155.2 3.9 %all-to-all-start.4 = ((bf16[4,128,768]{2,1,0:T(8,128)(2,1)}), bf16[4,128,768]{2,1,0:T(8,128)(2,1)S(1)}, u32[]{:S(2)}, u32[]{:S(2)}) async-start(bf16[4,128,768]{2,1,0:T(8,128)(2,1)} %bitcast.12), calls=%async_computation.4 | async-start | bytes 1572864 | tf_op jit(solution)/shard_map/forward_synthesis/all_to_all | solution.py:63
  159.1 12.6 %all-to-all-done.4 = bf16[4,128,768]{2,1,0:T(8,128)(2,1)S(1)} async-done(((bf16[4,128,768]{2,1,0:T(8,128)(2,1)}), bf16[4,128,768]{2,1,0:T(8,128)(2,1)S(1)}, u32[]{:S(2)}, u32[]{:S(2)}) %all-to-all-start.4) | async-done | bytes 786464 | tf_op jit(solution)/shard_map/forward_synthesis/all_to_all | solution.py:63
  174.2 16.1 %all_gather.7 = bf16[512,768]{0,1:T(8,128)(2,1)S(1)} all-gather(bf16[128,768]{0,1:T(8,128)(2,1)S(1)} %bitcast.116), channel_id=1, replica_groups=mesh['lat'=128,'lon'=4] {'lon'}, dimensions={0}, use_global_device_ids=true | all-gather | bytes 983040 | tf_op jit(solution)/shard_map/backward_analysis/all_gather | solution.py:116
  190.2 1.3 convolution_convert_fusion.6
  192.3 5.9 %all-to-all-start.5 = ((bf16[128,2,384]{2,1,0:T(2,128)(2,1)}), bf16[128,2,384]{2,1,0:T(2,128)(2,1)S(1)}, u32[]{:S(2)}, u32[]{:S(2)}) async-start(bf16[128,2,384]{2,1,0:T(2,128)(2,1)} %reshape.125), calls=%async_computation.5 | async-start | bytes 393216 | tf_op jit(solution)/shard_map/backward_analysis/all_to_all | solution.py:63
  198.8 1.4 broadcast_select_fusion
  200.4 2.1 collective-permute-start.3
  202.4 15.6 %all-to-all-done.5 = bf16[128,2,384]{2,1,0:T(2,128)(2,1)S(1)} async-done(((bf16[128,2,384]{2,1,0:T(2,128)(2,1)}), bf16[128,2,384]{2,1,0:T(2,128)(2,1)S(1)}, u32[]{:S(2)}, u32[]{:S(2)}) %all-to-all-start.5) | async-done | bytes 196640 | tf_op jit(solution)/shard_map/backward_analysis/all_to_all | solution.py:63
  218.1 1.1 convolution_convert_fusion.3
  219.3 0.8 reshape.127
  220.0 6.6 %all-to-all-start.6 = ((bf16[128,2,384]{2,1,0:T(2,128)(2,1)}), bf16[128,2,384]{2,1,0:T(2,128)(2,1)}, u32[]{:S(2)}, u32[]{:S(2)}) async-start(bf16[128,2,384]{2,1,0:T(2,128)(2,1)} %reshape.127), calls=%async_computation.6 | async-start | bytes 393216 | tf_op jit(solution)/shard_map/backward_analysis/all_to_all | solution.py:63
  226.8 1.4 fusion.73
  228.2 1.2 copy.54
  229.4 0.8 reshape.122
  230.2 1.5 convert_add_fusion.1
  232.0 0.9 constant_dynamic-slice_fusion.3
  232.9 3.9 %collective-permute-start.4 = (bf16[128,576]{1,0:T(8,128)(2,1)}, bf16[128,576]{1,0:T(8,128)(2,1)S(1)}, u32[]{:S(2)}, u32[]{:S(2)}) collective-permute-start(bf16[128,576]{1,0:T(8,128)(2,1)} %get-tuple-element.74), channel_id=1, source_target_pairs={{0,1},{1,2},{2,3},{3,0},{4,5},{5,6},{6,7},{7,4},{8,9},{9,10},{10,1... | collective-permute-start | bytes 442376 | tf_op jit(solution)/shard_map/pointwise_weights/ppermute | solution.py:86
  236.8 2.6 collective-permute-start.5
  239.4 4.0 %collective-permute-start.6 = (bf16[128,576]{1,0:T(8,128)(2,1)S(1)}, bf16[128,576]{1,0:T(8,128)(2,1)S(1)}, u32[]{:S(2)}, u32[]{:S(2)}) collective-permute-start(bf16[128,576]{1,0:T(8,128)(2,1)S(1)} %get-tuple-element.72), channel_id=1, source_target_pairs={{0,3},{1,0},{2,1},{3,2},{4,7},{5,4},{6,5},{7,6},{8,11},{9,8},{10,9... | collective-permute-start | bytes 442376 | tf_op jit(solution)/shard_map/pointwise_weights/ppermute | solution.py:86
  243.5 2.7 all-to-all-done.6
  246.2 1.3 convolution_bitcast_fusion.1
  248.4 0.8 constant_dynamic-slice_fusion.2
  249.1 4.6 %collective-permute-start.9 = (bf16[128,144]{1,0:T(8,128)(2,1)}, bf16[128,144]{1,0:T(8,128)(2,1)S(1)}, u32[]{:S(2)}, u32[]{:S(2)}) collective-permute-start(bf16[128,144]{1,0:T(8,128)(2,1)} %get-tuple-element.82), channel_id=1, source_target_pairs={{0,24},{4,28},{8,0},{12,4},{16,8},{20,12},{24,16},{28,20},{32,56},... | collective-permute-start | bytes 110600 | tf_op jit(solution)/shard_map/pointwise_weights/ppermute | solution.py:86
  253.7 2.8 collective-permute-start.8
  256.5 2.8 collective-permute-start.7
  259.3 0.9 copy.57
  260.1 15.5 %all-to-all-start.7 = ((bf16[128,2,384]{2,1,0:T(2,128)(2,1)}), bf16[128,2,384]{2,1,0:T(2,128)(2,1)S(1)}, u32[]{:S(2)}, u32[]{:S(2)}) async-start(bf16[128,2,384]{2,1,0:T(2,128)(2,1)} %copy.57), calls=%async_computation.7 | async-start | bytes 393216 | tf_op jit(solution)/shard_map/backward_synthesis/all_to_all | solution.py:63
  275.6 1.0 copy.86
  277.4 4.9 %collective-permute-start.10 = (bf16[2,2,192,384]{3,2,0,1:T(8,128)(2,1)S(1)}, bf16[2,2,192,384]{3,2,0,1:T(8,128)(2,1)S(1)}, u32[]{:S(2)}, u32[]{:S(2)}) collective-permute-start(bf16[2,2,192,384]{3,2,0,1:T(8,128)(2,1)S(1)} %fusion.1), channel_id=1, source_target_pairs={{0,3},{1,2},{2,1},{3,0},{4,7},{5,6},{6,5},{7,4},{8,11},{9,10},{10,... | collective-permute-start | bytes 1769480 | tf_op jit(solution)/shard_map/unmix/ppermute | solution.py:250
  282.6 1.0 add_convert_fusion.1
  283.7 11.8 %all-to-all-done.7 = bf16[128,2,384]{2,1,0:T(2,128)(2,1)S(1)} async-done(((bf16[128,2,384]{2,1,0:T(2,128)(2,1)}), bf16[128,2,384]{2,1,0:T(2,128)(2,1)S(1)}, u32[]{:S(2)}, u32[]{:S(2)}) %all-to-all-start.7) | async-done | bytes 196640 | tf_op jit(solution)/shard_map/backward_synthesis/all_to_all | solution.py:63
  295.6 1.2 convolution_convert_fusion.2
  296.8 1.0 pad_maximum_fusion.1
  297.8 14.2 %all-to-all-start.8 = ((bf16[128,2,512]{2,1,0:T(2,128)(2,1)}), bf16[128,2,512]{2,1,0:T(2,128)(2,1)S(1)}, u32[]{:S(2)}, u32[]{:S(2)}) async-start(bf16[128,2,512]{2,1,0:T(2,128)(2,1)} %pad_maximum_fusion.1), calls=%async_computation.8 | async-start | bytes 524288 | tf_op jit(solution)/shard_map/backward_synthesis/all_to_all | solution.py:63
  312.1 0.8 select_convert_fusion.1
  312.9 2.3 collective-permute-start.11
  315.2 19.3 %all-to-all-done.8 = bf16[128,2,512]{2,1,0:T(2,128)(2,1)S(1)} async-done(((bf16[128,2,512]{2,1,0:T(2,128)(2,1)}), bf16[128,2,512]{2,1,0:T(2,128)(2,1)S(1)}, u32[]{:S(2)}, u32[]{:S(2)}) %all-to-all-start.8) | async-done | bytes 262176 | tf_op jit(solution)/shard_map/backward_synthesis/all_to_all | solution.py:63
  334.7 2.2 multiply_convert_fusion
  337.0 4.2 %all-to-all-start.9 = ((bf16[4,128,768]{2,1,0:T(8,128)(2,1)}), bf16[4,128,768]{2,1,0:T(8,128)(2,1)S(1)}, u32[]{:S(2)}, u32[]{:S(2)}) async-start(bf16[4,128,768]{2,1,0:T(8,128)(2,1)} %bitcast.29), calls=%async_computation.9 | async-start | bytes 1572864 | tf_op jit(solution)/shard_map/backward_synthesis/all_to_all | solution.py:63
  341.2 1.0 fusion.3
  342.2 1.0 convert_add_fusion.2
  343.3 0.9 copy.65
  345.7 8.1 %all-to-all-done.9 = bf16[4,128,768]{2,1,0:T(8,128)(2,1)S(1)} async-done(((bf16[4,128,768]{2,1,0:T(8,128)(2,1)}), bf16[4,128,768]{2,1,0:T(8,128)(2,1)S(1)}, u32[]{:S(2)}, u32[]{:S(2)}) %all-to-all-start.9) | async-done | bytes 786464 | tf_op jit(solution)/shard_map/backward_synthesis/all_to_all | solution.py:63
  (99 shorter events, 14.3 us)
Async XLA Ops:
  0.6 171.6 %copy-start = (bf16[384,768]{1,0:T(8,128)(2,1)S(1)}, bf16[384,768]{1,0:T(8,128)(2,1)}, u32[]{:S(2)}) copy-start(bf16[384,768]{1,0:T(8,128)(2,1)} %param.12) | copy-start | bytes 1769476
  0.7 40.7 %copy-start.10 = (bf16[2,2,384,96]{2,3,1,0:T(8,128)(2,1)S(1)}, bf16[2,2,384,96]{2,3,1,0:T(8,128)(2,1)}, u32[]{:S(2)}) copy-start(bf16[2,2,384,96]{2,3,1,0:T(8,128)(2,1)} %param.11) | copy-start | bytes 884740
  22.2 39.0 %all-to-all-start = ((bf16[128,2,384]{2,1,0:T(2,128)(2,1)}), bf16[128,2,384]{2,1,0:T(2,128)(2,1)S(1)}, u32[]{:S(2)}, u32[]{:S(2)}) async-start(bf16[128,2,384]{2,1,0:T(2,128)(2,1)} %reshape.111), calls=%async_computation | async-start | bytes 393216 | tf_op jit(solution)/shard_map/forward_analysis/all_to_all | solution.py:63
  41.4 21.7 %collective-permute-start = (bf16[2,2,384,96]{2,3,0,1:T(8,128)(2,1)S(1)}, bf16[2,2,384,96]{2,3,0,1:T(8,128)(2,1)S(1)}, u32[]{:S(2)}, u32[]{:S(2)}) collective-permute-start(bf16[2,2,384,96]{2,3,0,1:T(8,128)(2,1)S(1)} %copy.45), channel_id=1, source_target_pairs={{0,1},{1,2},{2,3},{3,0},{4,5},{5,6},{6,7},{7,4},{8,9},{9,10},{10,1... | collective-permute-start | bytes 884744 | tf_op jit(solution)/shard_map/forward_analysis/ppermute | solution.py:70
  44.3 18.8 %collective-permute-start.1 = (bf16[2,2,384,96]{2,3,0,1:T(8,128)(2,1)S(1)}, bf16[2,2,384,96]{2,3,0,1:T(8,128)(2,1)S(1)}, u32[]{:S(2)}, u32[]{:S(2)}) collective-permute-start(bf16[2,2,384,96]{2,3,0,1:T(8,128)(2,1)S(1)} %copy.45), channel_id=1, source_target_pairs={{0,2},{1,3},{2,0},{3,1},{4,6},{5,7},{6,4},{7,5},{8,10},{9,11},{10,... | collective-permute-start | bytes 884744 | tf_op jit(solution)/shard_map/forward_analysis/ppermute | solution.py:70
  47.8 15.4 %collective-permute-start.2 = (bf16[2,2,384,96]{2,3,0,1:T(8,128)(2,1)S(1)}, bf16[2,2,384,96]{2,3,0,1:T(8,128)(2,1)S(1)}, u32[]{:S(2)}, u32[]{:S(2)}) collective-permute-start(bf16[2,2,384,96]{2,3,0,1:T(8,128)(2,1)S(1)} %copy.45), channel_id=1, source_target_pairs={{0,3},{1,0},{2,1},{3,2},{4,7},{5,4},{6,5},{7,6},{8,11},{9,8},{10,9... | collective-permute-start | bytes 884744 | tf_op jit(solution)/shard_map/forward_analysis/ppermute | solution.py:70
  63.9 35.2 %all-to-all-start.1 = ((bf16[128,2,384]{2,1,0:T(2,128)(2,1)}), bf16[128,2,384]{2,1,0:T(2,128)(2,1)S(1)}, u32[]{:S(2)}, u32[]{:S(2)}) async-start(bf16[128,2,384]{2,1,0:T(2,128)(2,1)} %reshape.113), calls=%async_computation.1 | async-start | bytes 393216 | tf_op jit(solution)/shard_map/forward_analysis/all_to_all | solution.py:63
  99.1 0.7 copy-start.6
  155.2 16.5 %all-to-all-start.4 = ((bf16[4,128,768]{2,1,0:T(8,128)(2,1)}), bf16[4,128,768]{2,1,0:T(8,128)(2,1)S(1)}, u32[]{:S(2)}, u32[]{:S(2)}) async-start(bf16[4,128,768]{2,1,0:T(8,128)(2,1)} %bitcast.12), calls=%async_computation.4 | async-start | bytes 1572864 | tf_op jit(solution)/shard_map/forward_synthesis/all_to_all | solution.py:63
  171.9 0.9 copy-start.11
  172.0 1.1 copy-start.12
  172.2 26.0 %copy-start.4 = (bf16[2,128,384]{2,1,0:T(8,128)(2,1)}, bf16[2,128,384]{2,1,0:T(8,128)(2,1)S(1)}, u32[]{:S(2)}) copy-start(bf16[2,128,384]{2,1,0:T(8,128)(2,1)S(1)} %copy.53) | copy-start | bytes 589828
  172.6 26.2 %copy-start.2 = (bf16[256,768]{1,0:T(8,128)(2,1)}, bf16[256,768]{1,0:T(8,128)(2,1)S(1)}, u32[]{:S(2)}) copy-start(bf16[256,768]{1,0:T(8,128)(2,1)S(1)} %get-tuple-element.35) | copy-start | bytes 1179652
  174.0 18.3 %copy-start.8 = (bf16[256,384]{1,0:T(8,128)(2,1)}, bf16[256,384]{1,0:T(8,128)(2,1)S(1)}, u32[]{:S(2)}) copy-start(bf16[256,384]{1,0:T(8,128)(2,1)S(1)} %fusion.4) | copy-start | bytes 589828
  192.3 25.8 %all-to-all-start.5 = ((bf16[128,2,384]{2,1,0:T(2,128)(2,1)}), bf16[128,2,384]{2,1,0:T(2,128)(2,1)S(1)}, u32[]{:S(2)}, u32[]{:S(2)}) async-start(bf16[128,2,384]{2,1,0:T(2,128)(2,1)} %reshape.125), calls=%async_computation.5 | async-start | bytes 393216 | tf_op jit(solution)/shard_map/backward_analysis/all_to_all | solution.py:63
  200.4 19.7 %collective-permute-start.3 = (bf16[768,384]{1,0:T(8,128)(2,1)S(1)}, bf16[768,384]{1,0:T(8,128)(2,1)S(1)}, u32[]{:S(2)}, u32[]{:S(2)}) collective-permute-start(bf16[768,384]{1,0:T(8,128)(2,1)S(1)} %select_convert_fusion), channel_id=1, source_target_pairs={{0,4},{4,0},{8,12},{12,8},{16,20},{20,16},{24,28},{28,24},{32,36},... | collective-permute-start | bytes 1769480 | tf_op jit(solution)/shard_map/pointwise_weights/ppermute | solution.py:203
  220.0 9.4 %copy-start.14 = (bf16[768,384]{1,0:T(8,128)(2,1)}, bf16[768,384]{1,0:T(8,128)(2,1)S(1)}, u32[]{:S(2)}) copy-start(bf16[768,384]{1,0:T(8,128)(2,1)S(1)} %collective-permute-done.3) | copy-start | bytes 1769476
  220.0 26.2 %all-to-all-start.6 = ((bf16[128,2,384]{2,1,0:T(2,128)(2,1)}), bf16[128,2,384]{2,1,0:T(2,128)(2,1)}, u32[]{:S(2)}, u32[]{:S(2)}) async-start(bf16[128,2,384]{2,1,0:T(2,128)(2,1)} %reshape.127), calls=%async_computation.6 | async-start | bytes 393216 | tf_op jit(solution)/shard_map/backward_analysis/all_to_all | solution.py:63
  232.9 14.7 %collective-permute-start.4 = (bf16[128,576]{1,0:T(8,128)(2,1)}, bf16[128,576]{1,0:T(8,128)(2,1)S(1)}, u32[]{:S(2)}, u32[]{:S(2)}) collective-permute-start(bf16[128,576]{1,0:T(8,128)(2,1)} %get-tuple-element.74), channel_id=1, source_target_pairs={{0,1},{1,2},{2,3},{3,0},{4,5},{5,6},{6,7},{7,4},{8,9},{9,10},{10,1... | collective-permute-start | bytes 442376 | tf_op jit(solution)/shard_map/pointwise_weights/ppermute | solution.py:86
  236.8 10.9 %collective-permute-start.5 = (bf16[128,576]{1,0:T(8,128)(2,1)S(1)}, bf16[128,576]{1,0:T(8,128)(2,1)S(1)}, u32[]{:S(2)}, u32[]{:S(2)}) collective-permute-start(bf16[128,576]{1,0:T(8,128)(2,1)S(1)} %get-tuple-element.73), channel_id=1, source_target_pairs={{0,2},{1,3},{2,0},{3,1},{4,6},{5,7},{6,4},{7,5},{8,10},{9,11},{10,... | collective-permute-start | bytes 442376 | tf_op jit(solution)/shard_map/pointwise_weights/ppermute | solution.py:86
  239.4 8.9 %collective-permute-start.6 = (bf16[128,576]{1,0:T(8,128)(2,1)S(1)}, bf16[128,576]{1,0:T(8,128)(2,1)S(1)}, u32[]{:S(2)}, u32[]{:S(2)}) collective-permute-start(bf16[128,576]{1,0:T(8,128)(2,1)S(1)} %get-tuple-element.72), channel_id=1, source_target_pairs={{0,3},{1,0},{2,1},{3,2},{4,7},{5,4},{6,5},{7,6},{8,11},{9,8},{10,9... | collective-permute-start | bytes 442376 | tf_op jit(solution)/shard_map/pointwise_weights/ppermute | solution.py:86
  247.6 29.0 %copy-start.7 = (bf16[128,2,384]{2,1,0:T(2,128)(2,1)S(1)}, bf16[128,2,384]{2,1,0:T(2,128)(2,1)}, u32[]{:S(2)}) copy-start(bf16[128,2,384]{2,1,0:T(2,128)(2,1)} %copy-done.6) | copy-start | bytes 589828
  249.1 33.5 %collective-permute-start.9 = (bf16[128,144]{1,0:T(8,128)(2,1)}, bf16[128,144]{1,0:T(8,128)(2,1)S(1)}, u32[]{:S(2)}, u32[]{:S(2)}) collective-permute-start(bf16[128,144]{1,0:T(8,128)(2,1)} %get-tuple-element.82), channel_id=1, source_target_pairs={{0,24},{4,28},{8,0},{12,4},{16,8},{20,12},{24,16},{28,20},{32,56},... | collective-permute-start | bytes 110600 | tf_op jit(solution)/shard_map/pointwise_weights/ppermute | solution.py:86
  253.7 28.9 %collective-permute-start.8 = (bf16[128,144]{1,0:T(8,128)(2,1)}, bf16[128,144]{1,0:T(8,128)(2,1)}, u32[]{:S(2)}, u32[]{:S(2)}) collective-permute-start(bf16[128,144]{1,0:T(8,128)(2,1)} %get-tuple-element.83), channel_id=1, source_target_pairs={{0,16},{4,20},{8,24},{12,28},{16,0},{20,4},{24,8},{28,12},{32,48},... | collective-permute-start | bytes 110600 | tf_op jit(solution)/shard_map/pointwise_weights/ppermute | solution.py:86
  256.5 26.1 %collective-permute-start.7 = (bf16[128,144]{1,0:T(8,128)(2,1)S(1)}, bf16[128,144]{1,0:T(8,128)(2,1)}, u32[]{:S(2)}, u32[]{:S(2)}) collective-permute-start(bf16[128,144]{1,0:T(8,128)(2,1)S(1)} %get-tuple-element.81), channel_id=1, source_target_pairs={{0,8},{4,12},{8,16},{12,20},{16,24},{20,28},{24,0},{28,4},{32,40},... | collective-permute-start | bytes 110600 | tf_op jit(solution)/shard_map/pointwise_weights/ppermute | solution.py:86
  260.1 35.3 %all-to-all-start.7 = ((bf16[128,2,384]{2,1,0:T(2,128)(2,1)}), bf16[128,2,384]{2,1,0:T(2,128)(2,1)S(1)}, u32[]{:S(2)}, u32[]{:S(2)}) async-start(bf16[128,2,384]{2,1,0:T(2,128)(2,1)} %copy.57), calls=%async_computation.7 | async-start | bytes 393216 | tf_op jit(solution)/shard_map/backward_synthesis/all_to_all | solution.py:63
  277.4 20.4 %collective-permute-start.10 = (bf16[2,2,192,384]{3,2,0,1:T(8,128)(2,1)S(1)}, bf16[2,2,192,384]{3,2,0,1:T(8,128)(2,1)S(1)}, u32[]{:S(2)}, u32[]{:S(2)}) collective-permute-start(bf16[2,2,192,384]{3,2,0,1:T(8,128)(2,1)S(1)} %fusion.1), channel_id=1, source_target_pairs={{0,3},{1,2},{2,1},{3,0},{4,7},{5,6},{6,5},{7,4},{8,11},{9,10},{10,... | collective-permute-start | bytes 1769480 | tf_op jit(solution)/shard_map/unmix/ppermute | solution.py:250
  297.8 36.7 %all-to-all-start.8 = ((bf16[128,2,512]{2,1,0:T(2,128)(2,1)}), bf16[128,2,512]{2,1,0:T(2,128)(2,1)S(1)}, u32[]{:S(2)}, u32[]{:S(2)}) async-start(bf16[128,2,512]{2,1,0:T(2,128)(2,1)} %pad_maximum_fusion.1), calls=%async_computation.8 | async-start | bytes 524288 | tf_op jit(solution)/shard_map/backward_synthesis/all_to_all | solution.py:63
  312.9 29.3 %collective-permute-start.11 = (bf16[2,2,96,384]{3,2,0,1:T(8,128)(2,1)}, bf16[2,2,96,384]{3,2,0,1:T(8,128)(2,1)}, u32[]{:S(2)}, u32[]{:S(2)}) collective-permute-start(bf16[2,2,96,384]{3,2,0,1:T(8,128)(2,1)} %select_convert_fusion.1), channel_id=1, source_target_pairs={{0,1},{1,0},{2,3},{3,2},{4,5},{5,4},{6,7},{7,6},{8,9},{9,8},{10,11... | collective-permute-start | bytes 884744 | tf_op jit(solution)/shard_map/unmix/ppermute | solution.py:270
  334.6 6.5 %copy-start.3 = (bf16[256,768]{1,0:T(8,128)(2,1)S(1)}, bf16[256,768]{1,0:T(8,128)(2,1)}, u32[]{:S(2)}) copy-start(bf16[256,768]{1,0:T(8,128)(2,1)} %copy-done.2) | copy-start | bytes 1179652
  334.7 6.5 %copy-start.5 = (bf16[2,128,384]{2,1,0:T(8,128)(2,1)S(1)}, bf16[2,128,384]{2,1,0:T(8,128)(2,1)}, u32[]{:S(2)}) copy-start(bf16[2,128,384]{2,1,0:T(8,128)(2,1)} %copy-done.4) | copy-start | bytes 589828
  334.7 6.5 %copy-start.13 = (bf16[768,384]{1,0:T(8,128)(2,1)S(1)}, bf16[768,384]{1,0:T(8,128)(2,1)}, u32[]{:S(2)}) copy-start(bf16[768,384]{1,0:T(8,128)(2,1)} %param.13) | copy-start | bytes 1769476
  337.0 16.9 %all-to-all-start.9 = ((bf16[4,128,768]{2,1,0:T(8,128)(2,1)}), bf16[4,128,768]{2,1,0:T(8,128)(2,1)S(1)}, u32[]{:S(2)}, u32[]{:S(2)}) async-start(bf16[4,128,768]{2,1,0:T(8,128)(2,1)} %bitcast.29), calls=%async_computation.9 | async-start | bytes 1572864 | tf_op jit(solution)/shard_map/backward_synthesis/all_to_all | solution.py:63
  344.1 10.1 %copy-start.9 = (bf16[256,384]{1,0:T(8,128)(2,1)S(1)}, bf16[256,384]{1,0:T(8,128)(2,1)}, u32[]{:S(2)}) copy-start(bf16[256,384]{1,0:T(8,128)(2,1)} %copy-done.8) | copy-start | bytes 589828
  345.0 10.0 %copy-start.1 = (bf16[384,768]{1,0:T(8,128)(2,1)S(1)}, bf16[384,768]{1,0:T(8,128)(2,1)}, u32[]{:S(2)}) copy-start(bf16[384,768]{1,0:T(8,128)(2,1)} %param.12) | copy-start | bytes 1769476

commit v5 on v4

--- a/solution.py
+++ b/solution.py
@@ -1,3 +1,4 @@
+import functools
 import math
 
 import jax
@@ -5,6 +6,8 @@
 import ml_dtypes
 import numpy as np
 from jax import lax
+from jax.experimental import pallas as pl
+from jax.experimental.pallas import tpu as pltpu
 from jax.sharding import PartitionSpec as P
 
 
@@ -63,17 +66,42 @@
     return lax.all_to_all(values, axis, split_axis=0, concat_axis=0, tiled=True)
 
 
-def lon_sends(block, lon_count):
-    moved = [block]
-    for shift in range(1, lon_count):
-        pairs = [(i, (i + shift) % lon_count) for i in range(lon_count)]
-        moved.append(lax.ppermute(block, "lon", pairs))
-    return moved
-
-
-def in_order(moved, lon_index):
-    backwards = jnp.stack(moved[::-1] + moved[:0:-1])
-    return lax.dynamic_slice_in_dim(backwards, len(moved) - 1 - lon_index, len(moved), 0)
+def fourier_kernel(rows, lon_rows, place_ref, matrix_ref, scale_ref, values_ref, out_ref):
+    width = values_ref.shape[2]
+    for row in range(rows):
+        longitudes = values_ref[:, row * lon_rows : (row + 1) * lon_rows, :]
+        out = jnp.dot(
+            matrix_ref[0],
+            longitudes.reshape(-1, width),
+            preferred_element_type=jnp.float32,
+        )
+        lanes = slice(row * width, (row + 1) * width)
+        out_ref[:, lanes] = (out * scale_ref[:, lanes]).astype(jnp.bfloat16)
+
+
+def to_fourier(values, matrices, scale, lon_index, rows, lon_rows):
+    lon_count, _, width = values.shape
+    _, orders, longitudes = matrices.shape
+    return pl.pallas_call(
+        functools.partial(fourier_kernel, rows, lon_rows),
+        grid_spec=pltpu.PrefetchScalarGridSpec(
+            num_scalar_prefetch=1,
+            grid=(1,),
+            in_specs=[
+                pl.BlockSpec((1, orders, longitudes), lambda i, place: (place[0], 0, 0)),
+                pl.BlockSpec((1, rows * width), lambda i, place: (0, 0)),
+                pl.BlockSpec((lon_count, rows * lon_rows, width), lambda i, place: (0, 0, 0)),
+            ],
+            out_specs=pl.BlockSpec((orders, rows * width), lambda i, place: (0, 0)),
+        ),
+        out_shape=jax.ShapeDtypeStruct((orders, rows * width), jnp.bfloat16),
+        compiler_params=pltpu.CompilerParams(vmem_limit_bytes=16 * 1024 * 1024),
+        cost_estimate=pl.CostEstimate(
+            flops=2 * orders * longitudes * rows * width,
+            bytes_accessed=2 * (longitudes + orders) * rows * width + 2 * orders * longitudes,
+            transcendentals=0,
+        ),
+    )(lon_index.reshape(1).astype(jnp.int32), matrices, scale, values)
 
 
 def scatter_sum(values, axis, index, count, shifted):
@@ -94,7 +122,7 @@
     return total
 
 
-def body(table_all, plain_all, doubled_all, quad, grid, cotangent, spectral_weight, w_in, w_out):
+def body(table_all, plain_all, doubled_all, plain_t, doubled_t, quad, grid, cotangent, spectral_weight, w_in, w_out):
     lat_count = lax.axis_size("lat")
     lon_count = lax.axis_size("lon")
     lat_index = lax.axis_index("lat")
@@ -111,17 +139,9 @@
     local_quad = lax.dynamic_slice_in_dim(quad, lat_index * rows, rows)
     quad_lanes = jnp.repeat(local_quad, width)[None, :]
 
-    def lon_gather(values):
-        values = values.transpose(1, 0, 2).reshape(lon_rows, rows * width)
-        return lax.all_gather(values, "lon", axis=0, tiled=True)
-
-    def to_fourier(values, matrix, scale):
-        out = lax.dot_general(
-            matrix, values, (((0,), (0,)), ((), ())), preferred_element_type=jnp.float32
-        )
-        if scale is not None:
-            out = out * scale
-        return out.astype(jnp.bfloat16).reshape(lat_count, rows, width)
+    def to_orders(values, matrices, scale):
+        out = to_fourier(values, matrices, scale, lon_index, rows, lon_rows)
+        return out.reshape(lat_count, rows, width)
 
     def from_fourier(values, matrix, scale):
         values = values.reshape(lat_count, rows * width)
@@ -145,25 +165,25 @@
         )
         return out.astype(jnp.bfloat16).reshape(lat_count, rows, width)
 
-    def complex_product(values, weights, sign):
-        out = jnp.einsum("plc,lcn->pln", values, weights, preferred_element_type=jnp.float32)
-        by_re, by_im = out[:, :, :width], out[:, :, width:]
+    def complex_product(values, dims, sign):
+        by_re = jnp.einsum(dims, values, weights[0], preferred_element_type=jnp.float32)
+        by_im = jnp.einsum(dims, values, weights[1], preferred_element_type=jnp.float32)
         out_re = by_re[:half] + sign * by_im[half:]
         out_im = by_re[half:] - sign * by_im[:half]
         return jnp.concatenate([out_re, out_im]).astype(jnp.bfloat16)
 
     with jax.named_scope("forward_analysis"):
-        four = to_fourier(lon_gather(grid), plain, quad_lanes)
-        four = analyze(swap_blocks(four, "lat"))
-        four, *moved = lax.optimization_barrier((four, *lon_sends(spectral_weight, lon_count)))
+        own_weight = spectral_weight.transpose(0, 1, 3, 2).reshape(-1, width)
+        sent = jnp.concatenate([grid.reshape(-1, width), own_weight])
+        gathered = lax.all_gather(sent, "lon", axis=0)
+        four = swap_blocks(to_orders(gathered, plain_t, quad_lanes), "lat")
     with jax.named_scope("weights"):
-        weights = in_order(moved, lon_index)
-        mix_weights = weights.transpose(2, 3, 1, 0, 4).reshape(rows, width, 2 * width)
-        unmix_weights = weights.transpose(2, 0, 4, 1, 3).reshape(rows, width, 2 * width)
+        weights = gathered[:, rows * lon_rows :].reshape(lon_count, 2, rows, quarter, width)
+        weights = weights.transpose(1, 2, 0, 3, 4).reshape(2, rows, width, width)
     with jax.named_scope("forward_analysis"):
-        spectrum = swap_blocks(four, "lat")
+        spectrum = swap_blocks(analyze(four), "lat")
     with jax.named_scope("mix"):
-        mixed = complex_product(spectrum, mix_weights, -1.0)
+        mixed = complex_product(spectrum, "plc,ldc->pld", -1.0)
     with jax.named_scope("forward_synthesis"):
         fields = swap_blocks(synthesize(swap_blocks(mixed, "lat")), "lat")
         wave_rows = from_fourier(fields, doubled, None)
@@ -187,11 +207,11 @@
             hidden.astype(jnp.float32) + jnp.dot(act, w_out, preferred_element_type=jnp.float32)
         ).astype(jnp.bfloat16)
     with jax.named_scope("backward_analysis"):
-        gathered = lon_gather(hidden_grad.reshape(grid.shape))
+        gathered = lax.all_gather(hidden_grad, "lon", axis=0)
         gathered, hidden, pre_grad, act = lax.optimization_barrier(
             (gathered, hidden, pre_grad, act)
         )
-        field_grad = swap_blocks(to_fourier(gathered, doubled, None), "lat")
+        field_grad = swap_blocks(to_orders(gathered, doubled_t, jnp.ones_like(quad_lanes)), "lat")
     with jax.named_scope("pointwise_weights"):
         over_rows = (((0,), (0,)), ((), ()))
         out_part = lax.dot_general(act, back, over_rows, preferred_element_type=jnp.float32)
@@ -215,10 +235,7 @@
             lambda s: [(i, (i + s) % lon_count) for i in range(lon_count)],
         )
     with jax.named_scope("unmix"):
-        spectrum_grad = complex_product(mixed_grad, unmix_weights, 1.0)
-        spectrum_grad, left, right, *parts = lax.optimization_barrier(
-            (spectrum_grad, spectrum, mixed_grad, *parts)
-        )
+        spectrum_grad = complex_product(mixed_grad, "pld,ldc->plc", 1.0)
     with jax.named_scope("backward_synthesis"):
         spectrum_grad = swap_blocks(spectrum_grad, "lat")
     with jax.named_scope("pointwise_weights"):
@@ -229,27 +246,6 @@
             4,
             lambda s: [(i, (i & ~6) | ((i + 2 * s) & 6)) for i in range(lat_count)],
         )
-    with jax.named_scope("unmix"):
-        turned = jnp.concatenate([right[half:], -right[:half]])
-        right = jnp.stack([right, turned])
-        high = lon_index >> 1 == 1
-        low_rows, high_rows = left[..., : width // 2], left[..., width // 2 :]
-        outer = "pli,rpld->rlid"
-        spec_keep = jnp.einsum(
-            outer,
-            jnp.where(high, high_rows, low_rows),
-            right,
-            preferred_element_type=jnp.float32,
-        )
-        spec_give = jnp.einsum(
-            outer,
-            jnp.where(high, low_rows, high_rows),
-            right,
-            preferred_element_type=jnp.float32,
-        ).astype(jnp.bfloat16)
-        spec_got = lax.ppermute(
-            spec_give, "lon", [(i, lon_count - 1 - i) for i in range(lon_count)]
-        )
     with jax.named_scope("backward_synthesis"):
         four_grad = synthesize(spectrum_grad)
         extra = add_parts(parts).astype(jnp.bfloat16)
@@ -258,17 +254,23 @@
         extra = jnp.pad(extra, ((0, 0), (0, room - chunk)))
         extra = extra.reshape(lat_count, rows, room // rows)
         four_grad = jnp.concatenate([four_grad, extra], axis=2)
-        four_grad, spec_keep, spec_got = lax.optimization_barrier((four_grad, spec_keep, spec_got))
+        four_grad, left, right = lax.optimization_barrier((four_grad, spectrum, mixed_grad))
         four_grad = swap_blocks(four_grad, "lat")
         wave_grad = from_fourier(four_grad[:, :, :width], plain, quad_lanes)
         grad_input = (hidden_grad.astype(jnp.float32) + wave_grad).astype(jnp.bfloat16)
     with jax.named_scope("unmix"):
-        total = spec_keep + spec_got.astype(jnp.float32)
-        high = lon_index & 1 == 1
-        low_rows, high_rows = total[:, :, :quarter], total[:, :, quarter:]
-        spec_give = jnp.where(high, low_rows, high_rows).astype(jnp.bfloat16)
-        spec_got = lax.ppermute(spec_give, "lon", [(i, i ^ 1) for i in range(lon_count)])
-        grad_spectral = jnp.where(high, high_rows, low_rows) + spec_got.astype(jnp.float32)
+        right = jnp.stack([right, jnp.concatenate([right[half:], -right[:half]])])
+        outer = jnp.einsum("pli,rpld->rlid", left, right, preferred_element_type=jnp.float32)
+        outer = outer.reshape(2, rows, lon_count, quarter, width)
+        own = lax.dynamic_index_in_dim(outer, lon_index, 2, keepdims=False)
+        narrow = outer.astype(jnp.bfloat16)
+        grad_spectral = [own]
+        for shift in range(1, lon_count):
+            to = (lon_index + shift) % lon_count
+            block = lax.dynamic_index_in_dim(narrow, to, 2, keepdims=False)
+            pairs = [(i, (i + shift) % lon_count) for i in range(lon_count)]
+            grad_spectral.append(lax.ppermute(block, "lon", pairs))
+        grad_spectral = add_parts(grad_spectral)
     with jax.named_scope("pointwise_weights"):
         sums = four_grad[:, :, width:].reshape(lat_count // 8, 4, 2, room)[..., :chunk]
         sums = jnp.sum(sums.astype(jnp.float32), axis=0).swapaxes(0, 1).reshape(2, -1)
@@ -295,14 +297,17 @@
         nlat, nlon, _ = grid.shape
         table = legendre_table(nlat)
         plain, doubled = fourier_tables(nlon, nlat, mesh.shape["lon"])
+        plain_t = np.ascontiguousarray(plain.swapaxes(1, 2))
+        doubled_t = np.ascontiguousarray(doubled.swapaxes(1, 2))
         quad = quadrature(nlat, nlon)
         mapped = jax.shard_map(
             body,
             mesh=mesh,
-            in_specs=(P(), P(), P(), P()) + in_specs,
+            in_specs=(P(),) * 6 + in_specs,
             out_specs=out_specs,
             check_vma=False,
         )
-        return mapped(table, plain, doubled, quad, grid, cotangent, spectral_weight, w_in, w_out)
+        tables = (table, plain, doubled, plain_t, doubled_t, quad)
+        return mapped(*tables, grid, cotangent, spectral_weight, w_in, w_out)
 
     return call

time: 356 us -> 360 us (1.011)
  waiting for transfers between devices: 93.9 us -> 161 us
  blocking collectives: 85.2 us -> 40.2 us
  starting transfers between devices: 125 us -> 98.5 us
  between operations: 1.46 us -> 14.9 us
  local copies, waits for them, and re-layouts: 23.9 us -> 16.2 us
    all_gather x0 -> x1, waiting for transfers between devices: none -> 42.2 us  [body(): gathered = lax.all_gather(sent, 'lon', axis=0)]
    all_to_all x2 -> x1, blocking collectives: 51.7 us -> 25.9 us  [swap_blocks(): return lax.all_to_all(values, axis, split_axis=0, concat_axis=0, tiled=True)]
    all_to_all x8 -> x9, waiting for transfers between devices: 93.3 us -> 114 us  [swap_blocks(): return lax.all_to_all(values, axis, split_axis=0, concat_axis=0, tiled=True)]
    all_gather x2 -> x1, blocking collectives: 33.5 us -> 14.4 us  [body(): gathered = lax.all_gather(hidden_grad, 'lon', axis=0)]
    all_to_all x8 -> x9, starting transfers between devices: 85 us -> 67.2 us  [swap_blocks(): return lax.all_to_all(values, axis, split_axis=0, concat_axis=0, tiled=True)]
    ppermute x5 -> x3, starting transfers between devices: 17.6 us -> 10.4 us  [body(): grad_spectral.append(lax.ppermute(block, 'lon', pairs))]
    unnamed x41 -> x42, local copies, waits for them, and re-layouts: 7.37 us -> 2.48 us
    ppermute x6, waiting for transfers between devices: 0.64 us -> 4.62 us  [scatter_sum(): parts.append(lax.ppermute(block, axis, shifted(shift)))]
  transfers between devices with their start and end apart: 20 -> 20, of which waited for: 9 -> 12; matrix products, arithmetic and copies ran while one was open for 9% -> 7% of each run, Pallas kernels for 0% -> 0%
where the time goes in v5:
time: 360 us; the launch traced here: 359 us
  waiting for transfers between devices  161 us (45%)
  starting transfers between devices  98.5 us (27%)
  blocking collectives  40.2 us (11%)
  matrix products  19.5 us (5%)
  local copies, waits for them, and re-layouts  16.2 us (4%)
  between operations  14.9 us (4%)
  other arithmetic  7.99 us (2%)
    all_to_all x9, waiting for transfers between devices, swap_blocks(): return lax.all_to_all(values, axis, split_axis=0, concat_axis=0, tiled=True)  114 us
    all_to_all x9, starting transfers between devices, swap_blocks(): return lax.all_to_all(values, axis, split_axis=0, concat_axis=0, tiled=True)  67.2 us
    all_gather x1, waiting for transfers between devices, body(): gathered = lax.all_gather(sent, 'lon', axis=0)  42.2 us
    all_to_all x1, blocking collectives, swap_blocks(): return lax.all_to_all(values, axis, split_axis=0, concat_axis=0, tiled=True)  25.9 us
    ppermute x6, starting transfers between devices, scatter_sum(): parts.append(lax.ppermute(block, axis, shifted(shift)))  18.7 us
    all_gather x1, blocking collectives, body(): gathered = lax.all_gather(hidden_grad, 'lon', axis=0)  14.4 us
    ppermute x3, starting transfers between devices, body(): grad_spectral.append(lax.ppermute(block, 'lon', pairs))  10.4 us
  transfers between devices with their start and end apart: 20, of which 12 were waited for; matrix products, arithmetic and copies ran while one was open for 7% of the time, Pallas kernels for 0%

profile of v5, /device:TPU:32, one launch (start us, length us, event | category | flops | bytes accessed | tf_op | source)
XLA Modules:
  0.0 359.0 jit_solution(11459010313298504550)
XLA Ops:
  7.2 1.9 pad_maximum_fusion
  9.2 0.8 dynamic_slice.54
  10.0 42.2 %all-gather.4.cloned.1.call-done = bf16[2560,384]{1,0:T(8,128)(2,1)} async-done(((bf16[640,384]{1,0:T(8,128)(2,1)}), bf16[2560,384]{1,0:T(8,128)(2,1)}) %all-gather.4.cloned.1.call-update) | async-done | bytes 1966096 | tf_op jit(solution)/shard_map/forward_analysis/all_gather | solution.py:178
  52.3 1.5 copy-done.2
  54.1 0.7 reshape.117
  54.9 16.4 %all-to-all-start = ((bf16[128,2,384]{2,1,0:T(2,128)(2,1)}), bf16[128,2,384]{2,1,0:T(2,128)(2,1)S(1)}, u32[]{:S(2)}, u32[]{:S(2)}) async-start(bf16[128,2,384]{2,1,0:T(2,128)(2,1)} %reshape.117), calls=%async_computation | async-start | bytes 393216 | tf_op jit(solution)/shard_map/forward_analysis/all_to_all | solution.py:66
  71.3 19.8 %all-to-all-done = bf16[128,2,384]{2,1,0:T(2,128)(2,1)S(1)} async-done(((bf16[128,2,384]{2,1,0:T(2,128)(2,1)}), bf16[128,2,384]{2,1,0:T(2,128)(2,1)S(1)}, u32[]{:S(2)}, u32[]{:S(2)}) %all-to-all-start) | async-done | bytes 196640 | tf_op jit(solution)/shard_map/forward_analysis/all_to_all | solution.py:66
  91.2 1.1 convolution_convert_fusion.4
  92.4 0.8 reshape.119
  93.1 6.2 %all-to-all-start.1 = ((bf16[128,2,384]{2,1,0:T(2,128)(2,1)}), bf16[128,2,384]{2,1,0:T(2,128)(2,1)S(1)}, u32[]{:S(2)}, u32[]{:S(2)}) async-start(bf16[128,2,384]{2,1,0:T(2,128)(2,1)} %reshape.119), calls=%async_computation.1 | async-start | bytes 393216 | tf_op jit(solution)/shard_map/forward_analysis/all_to_all | solution.py:66
  99.8 19.4 %all-to-all-done.1 = bf16[128,2,384]{2,1,0:T(2,128)(2,1)S(1)} async-done(((bf16[128,2,384]{2,1,0:T(2,128)(2,1)}), bf16[128,2,384]{2,1,0:T(2,128)(2,1)S(1)}, u32[]{:S(2)}, u32[]{:S(2)}) %all-to-all-start.1) | async-done | bytes 196640 | tf_op jit(solution)/shard_map/forward_analysis/all_to_all | solution.py:66
  120.1 25.9 %all_to_all.50 = bf16[128,2,384]{2,1,0:T(2,128)(2,1)S(1)} all-to-all(bf16[128,2,384]{2,1,0:T(2,128)(2,1)S(1)} %copy.44), channel_id=1, replica_groups=mesh['lat'=128,'lon'=4] {'lat'}, dimensions={0} | all-to-all | bytes 393216 | tf_op jit(solution)/shard_map/forward_synthesis/all_to_all | solution.py:66
  146.1 1.2 convolution_convert_fusion.3
  147.3 0.8 reshape.121
  148.0 6.2 %all-to-all-start.3 = ((bf16[128,2,384]{2,1,0:T(2,128)(2,1)}), bf16[128,2,384]{2,1,0:T(2,128)(2,1)S(1)}, u32[]{:S(2)}, u32[]{:S(2)}) async-start(bf16[128,2,384]{2,1,0:T(2,128)(2,1)} %reshape.121), calls=%async_computation.3 | async-start | bytes 393216 | tf_op jit(solution)/shard_map/forward_synthesis/all_to_all | solution.py:66
  154.2 19.8 %all-to-all-done.3 = bf16[128,2,384]{2,1,0:T(2,128)(2,1)S(1)} async-done(((bf16[128,2,384]{2,1,0:T(2,128)(2,1)}), bf16[128,2,384]{2,1,0:T(2,128)(2,1)S(1)}, u32[]{:S(2)}, u32[]{:S(2)}) %all-to-all-start.3) | async-done | bytes 196640 | tf_op jit(solution)/shard_map/forward_synthesis/all_to_all | solution.py:66
  174.0 2.2 convolution_convert_fusion
  176.2 3.7 %all-to-all-start.4 = ((bf16[4,128,768]{2,1,0:T(8,128)(2,1)}), bf16[4,128,768]{2,1,0:T(8,128)(2,1)S(1)}, u32[]{:S(2)}, u32[]{:S(2)}) async-start(bf16[4,128,768]{2,1,0:T(8,128)(2,1)} %bitcast.123), calls=%async_computation.4 | async-start | bytes 1572864 | tf_op jit(solution)/shard_map/forward_synthesis/all_to_all | solution.py:66
  179.9 12.6 %all-to-all-done.4 = bf16[4,128,768]{2,1,0:T(8,128)(2,1)S(1)} async-done(((bf16[4,128,768]{2,1,0:T(8,128)(2,1)}), bf16[4,128,768]{2,1,0:T(8,128)(2,1)S(1)}, u32[]{:S(2)}, u32[]{:S(2)}) %all-to-all-start.4) | async-done | bytes 786464 | tf_op jit(solution)/shard_map/forward_synthesis/all_to_all | solution.py:66
  193.1 1.1 multiply_convert_fusion.1
  195.1 14.4 %all-gather.1 = bf16[1024,384]{1,0:T(8,128)(2,1)S(1)} all-gather(bf16[256,384]{1,0:T(8,128)(2,1)S(1)} %fusion.2), channel_id=3, replica_groups=mesh['lat'=128,'lon'=4] {'lon'}, dimensions={0}, use_global_device_ids=true | all-gather | bytes 983040 | tf_op jit(solution)/shard_map/backward_analysis/all_gather | solution.py:210
  209.8 0.7 reshape.128
  210.5 6.4 %all-to-all-start.5 = ((bf16[128,2,384]{2,1,0:T(2,128)(2,1)}), bf16[128,2,384]{2,1,0:T(2,128)(2,1)}, u32[]{:S(2)}, u32[]{:S(2)}) async-start(bf16[128,2,384]{2,1,0:T(2,128)(2,1)} %reshape.128), calls=%async_computation.5 | async-start | bytes 393216 | tf_op jit(solution)/shard_map/backward_analysis/all_to_all | solution.py:66
  217.4 2.5 broadcast_select_fusion
  220.1 2.1 collective-permute-start
  222.1 14.2 %all-to-all-done.5 = bf16[128,2,384]{2,1,0:T(2,128)(2,1)} async-done(((bf16[128,2,384]{2,1,0:T(2,128)(2,1)}), bf16[128,2,384]{2,1,0:T(2,128)(2,1)}, u32[]{:S(2)}, u32[]{:S(2)}) %all-to-all-start.5) | async-done | bytes 196640 | tf_op jit(solution)/shard_map/backward_analysis/all_to_all | solution.py:66
  236.3 1.0 reshape.129
  237.3 1.1 convolution_convert_fusion.2
  238.5 0.8 reshape.130
  239.2 6.6 %all-to-all-start.6 = ((bf16[128,2,384]{2,1,0:T(2,128)(2,1)}), bf16[128,2,384]{2,1,0:T(2,128)(2,1)}, u32[]{:S(2)}, u32[]{:S(2)}) async-start(bf16[128,2,384]{2,1,0:T(2,128)(2,1)} %reshape.130), calls=%async_computation.6 | async-start | bytes 393216 | tf_op jit(solution)/shard_map/backward_analysis/all_to_all | solution.py:66
  245.8 1.2 convert_add_fusion
  247.6 2.9 collective-permute-start.3
  250.5 2.8 collective-permute-start.2
  253.2 2.9 collective-permute-start.1
  256.2 9.2 %all-to-all-done.6 = bf16[128,2,384]{2,1,0:T(2,128)(2,1)} async-done(((bf16[128,2,384]{2,1,0:T(2,128)(2,1)}), bf16[128,2,384]{2,1,0:T(2,128)(2,1)}, u32[]{:S(2)}, u32[]{:S(2)}) %all-to-all-start.6) | async-done | bytes 196640 | tf_op jit(solution)/shard_map/backward_analysis/all_to_all | solution.py:66
  265.3 1.2 convolution_bitcast_fusion
  266.6 1.2 convolution_bitcast_fusion.1
  267.9 0.9 copy.49
  268.7 7.0 %all-to-all-start.7 = ((bf16[128,2,384]{2,1,0:T(2,128)(2,1)}), bf16[128,2,384]{2,1,0:T(2,128)(2,1)S(1)}, u32[]{:S(2)}, u32[]{:S(2)}) async-start(bf16[128,2,384]{2,1,0:T(2,128)(2,1)} %copy.49), calls=%async_computation.7 | async-start | bytes 393216 | tf_op jit(solution)/shard_map/backward_synthesis/all_to_all | solution.py:66
  276.1 4.6 %collective-permute-start.6 = (bf16[128,144]{1,0:T(8,128)(2,1)S(1)}, bf16[128,144]{1,0:T(8,128)(2,1)S(1)}, u32[]{:S(2)}, u32[]{:S(2)}) collective-permute-start(bf16[128,144]{1,0:T(8,128)(2,1)S(1)} %get-tuple-element.46), channel_id=1, source_target_pairs={{0,24},{4,28},{8,0},{12,4},{16,8},{20,12},{24,16},{28,20},{32,56},... | collective-permute-start | bytes 110600 | tf_op jit(solution)/shard_map/pointwise_weights/ppermute | solution.py:114
  280.7 2.8 collective-permute-start.5
  283.5 2.8 collective-permute-start.4
  286.3 2.3 collective-permute-done.5
  288.5 2.4 collective-permute-done.4
  291.0 4.5 %all-to-all-done.7 = bf16[128,2,384]{2,1,0:T(2,128)(2,1)S(1)} async-done(((bf16[128,2,384]{2,1,0:T(2,128)(2,1)}), bf16[128,2,384]{2,1,0:T(2,128)(2,1)S(1)}, u32[]{:S(2)}, u32[]{:S(2)}) %all-to-all-start.7) | async-done | bytes 196640 | tf_op jit(solution)/shard_map/backward_synthesis/all_to_all | solution.py:66
  295.6 1.2 convolution_convert_fusion.1
  296.9 1.0 pad_maximum_fusion.1
  297.9 10.3 %all-to-all-start.8 = ((bf16[128,2,512]{2,1,0:T(2,128)(2,1)}), bf16[128,2,512]{2,1,0:T(2,128)(2,1)S(1)}, u32[]{:S(2)}, u32[]{:S(2)}) async-start(bf16[128,2,512]{2,1,0:T(2,128)(2,1)} %pad_maximum_fusion.1), calls=%async_computation.8 | async-start | bytes 524288 | tf_op jit(solution)/shard_map/backward_synthesis/all_to_all | solution.py:66
  308.3 1.0 copy.85
  310.1 0.7 copy.82
  310.8 4.1 %collective-permute-start.9 = (bf16[2,2,96,384]{3,2,1,0:T(8,128)(2,1)}, bf16[2,2,96,384]{3,2,1,0:T(8,128)(2,1)}, u32[]{:S(2)}, u32[]{:S(2)}) collective-permute-start(bf16[2,2,96,384]{3,2,1,0:T(8,128)(2,1)} %bitcast.106), channel_id=1, source_target_pairs={{0,3},{1,0},{2,1},{3,2},{4,7},{5,4},{6,5},{7,6},{8,11},{9,8},{10,9... | collective-permute-start | bytes 884744 | tf_op jit(solution)/shard_map/unmix/ppermute | solution.py:272
  314.9 0.8 copy.83
  315.7 3.4 collective-permute-start.8
  319.0 0.8 copy.84
  319.8 2.9 collective-permute-start.7
  322.7 7.9 %all-to-all-done.8 = bf16[128,2,512]{2,1,0:T(2,128)(2,1)S(1)} async-done(((bf16[128,2,512]{2,1,0:T(2,128)(2,1)}), bf16[128,2,512]{2,1,0:T(2,128)(2,1)S(1)}, u32[]{:S(2)}, u32[]{:S(2)}) %all-to-all-start.8) | async-done | bytes 262176 | tf_op jit(solution)/shard_map/backward_synthesis/all_to_all | solution.py:66
  330.7 0.7 copy-done.15
  331.6 2.2 multiply_convert_fusion
  333.8 4.5 %all-to-all-start.9 = ((bf16[4,128,768]{2,1,0:T(8,128)(2,1)}), bf16[4,128,768]{2,1,0:T(8,128)(2,1)S(1)}, u32[]{:S(2)}, u32[]{:S(2)}) async-start(bf16[4,128,768]{2,1,0:T(8,128)(2,1)} %bitcast.122), calls=%async_computation.9 | async-start | bytes 1572864 | tf_op jit(solution)/shard_map/backward_synthesis/all_to_all | solution.py:66
  338.3 2.1 fusion.1
  340.5 2.1 fusion.8
  342.8 0.7 squeeze.48
  344.1 6.9 %all-to-all-done.9 = bf16[4,128,768]{2,1,0:T(8,128)(2,1)S(1)} async-done(((bf16[4,128,768]{2,1,0:T(8,128)(2,1)}), bf16[4,128,768]{2,1,0:T(8,128)(2,1)S(1)}, u32[]{:S(2)}, u32[]{:S(2)}) %all-to-all-start.9) | async-done | bytes 786464 | tf_op jit(solution)/shard_map/backward_synthesis/all_to_all | solution.py:66
  351.5 0.7 fusion.13
  (102 shorter events, 7.8 us)
Async XLA Ops:
  7.2 185.9 %copy-start = (bf16[384,768]{1,0:T(8,128)(2,1)S(1)}, bf16[384,768]{1,0:T(8,128)(2,1)}, u32[]{:S(2)}) copy-start(bf16[384,768]{1,0:T(8,128)(2,1)} %param.14) | copy-start | bytes 1769476
  7.2 45.1 %copy-start.5 = (bf16[4,128,512]{2,1,0:T(8,128)(2,1)S(1)}, bf16[4,128,512]{2,1,0:T(8,128)(2,1)}, u32[]{:S(2)}) copy-start(bf16[4,128,512]{2,1,0:T(8,128)(2,1)} %constant.133.clone.matrix_ref) | copy-start | bytes 1572868
  7.2 45.1 %all-gather.4.cloned.1.call-start = ((), (), s32[]{:S(2)}) async-start(), calls=%async_computation.10 | async-start | bytes 2457600 | tf_op jit(solution)/shard_map/forward_analysis/all_gather | solution.py:178
  52.3 1.5 copy-start.2
  54.1 45.2 %copy-start.3 = (bf16[2560,384]{1,0:T(8,128)(2,1)S(1)}, bf16[2560,384]{1,0:T(8,128)(2,1)}, u32[]{:S(2)}) copy-start(bf16[2560,384]{1,0:T(8,128)(2,1)} %all-gather.4.cloned.1.call-done) | copy-start | bytes 5898244
  54.9 36.3 %all-to-all-start = ((bf16[128,2,384]{2,1,0:T(2,128)(2,1)}), bf16[128,2,384]{2,1,0:T(2,128)(2,1)S(1)}, u32[]{:S(2)}, u32[]{:S(2)}) async-start(bf16[128,2,384]{2,1,0:T(2,128)(2,1)} %reshape.117), calls=%async_computation | async-start | bytes 393216 | tf_op jit(solution)/shard_map/forward_analysis/all_to_all | solution.py:66
  93.1 26.1 %all-to-all-start.1 = ((bf16[128,2,384]{2,1,0:T(2,128)(2,1)}), bf16[128,2,384]{2,1,0:T(2,128)(2,1)S(1)}, u32[]{:S(2)}, u32[]{:S(2)}) async-start(bf16[128,2,384]{2,1,0:T(2,128)(2,1)} %reshape.119), calls=%async_computation.1 | async-start | bytes 393216 | tf_op jit(solution)/shard_map/forward_analysis/all_to_all | solution.py:66
  119.2 0.7 copy-start.8
  148.0 26.0 %all-to-all-start.3 = ((bf16[128,2,384]{2,1,0:T(2,128)(2,1)}), bf16[128,2,384]{2,1,0:T(2,128)(2,1)S(1)}, u32[]{:S(2)}, u32[]{:S(2)}) async-start(bf16[128,2,384]{2,1,0:T(2,128)(2,1)} %reshape.121), calls=%async_computation.3 | async-start | bytes 393216 | tf_op jit(solution)/shard_map/forward_synthesis/all_to_all | solution.py:66
  176.2 16.3 %all-to-all-start.4 = ((bf16[4,128,768]{2,1,0:T(8,128)(2,1)}), bf16[4,128,768]{2,1,0:T(8,128)(2,1)S(1)}, u32[]{:S(2)}, u32[]{:S(2)}) async-start(bf16[4,128,768]{2,1,0:T(8,128)(2,1)} %bitcast.123), calls=%async_computation.4 | async-start | bytes 1572864 | tf_op jit(solution)/shard_map/forward_synthesis/all_to_all | solution.py:66
  179.9 13.1 %copy-start.16 = (bf16[2,128,384]{2,1,0:T(8,128)(2,1)S(1)}, bf16[2,128,384]{2,1,0:T(8,128)(2,1)}, u32[]{:S(2)}) copy-start(bf16[2,128,384]{2,1,0:T(8,128)(2,1)} %param.11) | copy-start | bytes 589828
  193.0 1.3 copy-start.17
  193.0 1.2 copy-start.18
  193.1 23.8 %copy-start.10 = (bf16[256,384]{1,0:T(8,128)(2,1)}, bf16[256,384]{1,0:T(8,128)(2,1)S(1)}, u32[]{:S(2)}) copy-start(bf16[256,384]{1,0:T(8,128)(2,1)S(1)} %fusion.14) | copy-start | bytes 589828
  194.7 14.8 %copy-start.13 = (bf16[256,768]{1,0:T(8,128)(2,1)}, bf16[256,768]{1,0:T(8,128)(2,1)S(1)}, u32[]{:S(2)}) copy-start(bf16[256,768]{1,0:T(8,128)(2,1)S(1)} %fusion) | copy-start | bytes 1179652
  194.7 14.8 %copy-start.4 = (bf16[4,128,512]{2,1,0:T(8,128)(2,1)S(1)}, bf16[4,128,512]{2,1,0:T(8,128)(2,1)}, u32[]{:S(2)}) copy-start(bf16[4,128,512]{2,1,0:T(8,128)(2,1)} %constant.134.clone.matrix_ref) | copy-start | bytes 1572868
  195.1 15.4 %copy-start.11 = (bf16[256,384]{1,0:T(8,128)(2,1)}, bf16[256,384]{1,0:T(8,128)(2,1)S(1)}, u32[]{:S(2)}) copy-start(bf16[256,384]{1,0:T(8,128)(2,1)S(1)} %fusion.2) | copy-start | bytes 589828
  209.5 7.4 %copy-start.14 = (bf16[256,768]{1,0:T(8,128)(2,1)S(1)}, bf16[256,768]{1,0:T(8,128)(2,1)}, u32[]{:S(2)}) copy-start(bf16[256,768]{1,0:T(8,128)(2,1)} %copy-done.13) | copy-start | bytes 1179652
  210.5 25.8 %all-to-all-start.5 = ((bf16[128,2,384]{2,1,0:T(2,128)(2,1)}), bf16[128,2,384]{2,1,0:T(2,128)(2,1)}, u32[]{:S(2)}, u32[]{:S(2)}) async-start(bf16[128,2,384]{2,1,0:T(2,128)(2,1)} %reshape.128), calls=%async_computation.5 | async-start | bytes 393216 | tf_op jit(solution)/shard_map/backward_analysis/all_to_all | solution.py:66
  220.0 25.8 %copy-start.6 = (f32[768,384]{1,0:T(8,128)S(1)}, f32[768,384]{1,0:T(8,128)}, u32[]{:S(2)}) copy-start(f32[768,384]{1,0:T(8,128)} %get-tuple-element.20) | copy-start | bytes 3538948
  220.1 19.2 %collective-permute-start = (bf16[768,384]{1,0:T(8,128)(2,1)S(1)}, bf16[768,384]{1,0:T(8,128)(2,1)}, u32[]{:S(2)}, u32[]{:S(2)}) collective-permute-start(bf16[768,384]{1,0:T(8,128)(2,1)S(1)} %select_convert_fusion), channel_id=1, source_target_pairs={{0,4},{4,0},{8,12},{12,8},{16,20},{20,16},{24,28},{28,24},{32,36},... | collective-permute-start | bytes 1769480 | tf_op jit(solution)/shard_map/pointwise_weights/ppermute | solution.py:223
  239.2 26.1 %all-to-all-start.6 = ((bf16[128,2,384]{2,1,0:T(2,128)(2,1)}), bf16[128,2,384]{2,1,0:T(2,128)(2,1)}, u32[]{:S(2)}, u32[]{:S(2)}) async-start(bf16[128,2,384]{2,1,0:T(2,128)(2,1)} %reshape.130), calls=%async_computation.6 | async-start | bytes 393216 | tf_op jit(solution)/shard_map/backward_analysis/all_to_all | solution.py:66
  247.6 28.2 %collective-permute-start.3 = (bf16[128,576]{1,0:T(8,128)(2,1)S(1)}, bf16[128,576]{1,0:T(8,128)(2,1)S(1)}, u32[]{:S(2)}, u32[]{:S(2)}) collective-permute-start(bf16[128,576]{1,0:T(8,128)(2,1)S(1)} %get-tuple-element.39), channel_id=1, source_target_pairs={{0,3},{1,0},{2,1},{3,2},{4,7},{5,4},{6,5},{7,6},{8,11},{9,8},{10,9... | collective-permute-start | bytes 442376 | tf_op jit(solution)/shard_map/pointwise_weights/ppermute | solution.py:114
  250.5 25.3 %collective-permute-start.2 = (bf16[128,576]{1,0:T(8,128)(2,1)S(1)}, bf16[128,576]{1,0:T(8,128)(2,1)S(1)}, u32[]{:S(2)}, u32[]{:S(2)}) collective-permute-start(bf16[128,576]{1,0:T(8,128)(2,1)S(1)} %get-tuple-element.40), channel_id=1, source_target_pairs={{0,2},{1,3},{2,0},{3,1},{4,6},{5,7},{6,4},{7,5},{8,10},{9,11},{10,... | collective-permute-start | bytes 442376 | tf_op jit(solution)/shard_map/pointwise_weights/ppermute | solution.py:114
  253.2 22.5 %collective-permute-start.1 = (bf16[128,576]{1,0:T(8,128)(2,1)S(1)}, bf16[128,576]{1,0:T(8,128)(2,1)S(1)}, u32[]{:S(2)}, u32[]{:S(2)}) collective-permute-start(bf16[128,576]{1,0:T(8,128)(2,1)S(1)} %get-tuple-element.38), channel_id=1, source_target_pairs={{0,1},{1,2},{2,3},{3,0},{4,5},{5,6},{6,7},{7,4},{8,9},{9,10},{10,1... | collective-permute-start | bytes 442376 | tf_op jit(solution)/shard_map/pointwise_weights/ppermute | solution.py:114
  268.7 26.8 %all-to-all-start.7 = ((bf16[128,2,384]{2,1,0:T(2,128)(2,1)}), bf16[128,2,384]{2,1,0:T(2,128)(2,1)S(1)}, u32[]{:S(2)}, u32[]{:S(2)}) async-start(bf16[128,2,384]{2,1,0:T(2,128)(2,1)} %copy.49), calls=%async_computation.7 | async-start | bytes 393216 | tf_op jit(solution)/shard_map/backward_synthesis/all_to_all | solution.py:66
  276.1 10.1 %collective-permute-start.6 = (bf16[128,144]{1,0:T(8,128)(2,1)S(1)}, bf16[128,144]{1,0:T(8,128)(2,1)S(1)}, u32[]{:S(2)}, u32[]{:S(2)}) collective-permute-start(bf16[128,144]{1,0:T(8,128)(2,1)S(1)} %get-tuple-element.46), channel_id=1, source_target_pairs={{0,24},{4,28},{8,0},{12,4},{16,8},{20,12},{24,16},{28,20},{32,56},... | collective-permute-start | bytes 110600 | tf_op jit(solution)/shard_map/pointwise_weights/ppermute | solution.py:114
  280.7 7.8 %collective-permute-start.5 = (bf16[128,144]{1,0:T(8,128)(2,1)S(1)}, bf16[128,144]{1,0:T(8,128)(2,1)S(1)}, u32[]{:S(2)}, u32[]{:S(2)}) collective-permute-start(bf16[128,144]{1,0:T(8,128)(2,1)S(1)} %get-tuple-element.47), channel_id=1, source_target_pairs={{0,16},{4,20},{8,24},{12,28},{16,0},{20,4},{24,8},{28,12},{32,48},... | collective-permute-start | bytes 110600 | tf_op jit(solution)/shard_map/pointwise_weights/ppermute | solution.py:114
  283.5 7.4 %collective-permute-start.4 = (bf16[128,144]{1,0:T(8,128)(2,1)S(1)}, bf16[128,144]{1,0:T(8,128)(2,1)S(1)}, u32[]{:S(2)}, u32[]{:S(2)}) collective-permute-start(bf16[128,144]{1,0:T(8,128)(2,1)S(1)} %get-tuple-element.45), channel_id=1, source_target_pairs={{0,8},{4,12},{8,16},{12,20},{16,24},{20,28},{24,0},{28,4},{32,40},... | collective-permute-start | bytes 110600 | tf_op jit(solution)/shard_map/pointwise_weights/ppermute | solution.py:114
  295.6 13.7 %copy-start.9 = (bf16[128,2,384]{2,1,0:T(2,128)(2,1)S(1)}, bf16[128,2,384]{2,1,0:T(2,128)(2,1)}, u32[]{:S(2)}) copy-start(bf16[128,2,384]{2,1,0:T(2,128)(2,1)} %copy-done.8) | copy-start | bytes 589828
  297.9 32.8 %all-to-all-start.8 = ((bf16[128,2,512]{2,1,0:T(2,128)(2,1)}), bf16[128,2,512]{2,1,0:T(2,128)(2,1)S(1)}, u32[]{:S(2)}, u32[]{:S(2)}) async-start(bf16[128,2,512]{2,1,0:T(2,128)(2,1)} %pad_maximum_fusion.1), calls=%async_computation.8 | async-start | bytes 524288 | tf_op jit(solution)/shard_map/backward_synthesis/all_to_all | solution.py:66
  310.8 29.7 %collective-permute-start.9 = (bf16[2,2,96,384]{3,2,1,0:T(8,128)(2,1)}, bf16[2,2,96,384]{3,2,1,0:T(8,128)(2,1)}, u32[]{:S(2)}, u32[]{:S(2)}) collective-permute-start(bf16[2,2,96,384]{3,2,1,0:T(8,128)(2,1)} %bitcast.106), channel_id=1, source_target_pairs={{0,3},{1,0},{2,1},{3,2},{4,7},{5,4},{6,5},{7,6},{8,11},{9,8},{10,9... | collective-permute-start | bytes 884744 | tf_op jit(solution)/shard_map/unmix/ppermute | solution.py:272
  315.7 24.8 %collective-permute-start.8 = (bf16[2,2,96,384]{3,2,1,0:T(8,128)(2,1)}, bf16[2,2,96,384]{3,2,1,0:T(8,128)(2,1)}, u32[]{:S(2)}, u32[]{:S(2)}) collective-permute-start(bf16[2,2,96,384]{3,2,1,0:T(8,128)(2,1)} %bitcast.107), channel_id=1, source_target_pairs={{0,2},{1,3},{2,0},{3,1},{4,6},{5,7},{6,4},{7,5},{8,10},{9,11},{10,... | collective-permute-start | bytes 884744 | tf_op jit(solution)/shard_map/unmix/ppermute | solution.py:272
  319.8 20.7 %collective-permute-start.7 = (bf16[2,2,96,384]{3,2,1,0:T(8,128)(2,1)}, bf16[2,2,96,384]{3,2,1,0:T(8,128)(2,1)}, u32[]{:S(2)}, u32[]{:S(2)}) collective-permute-start(bf16[2,2,96,384]{3,2,1,0:T(8,128)(2,1)} %bitcast.108), channel_id=1, source_target_pairs={{0,1},{1,2},{2,3},{3,0},{4,5},{5,6},{6,7},{7,4},{8,9},{9,10},{10,1... | collective-permute-start | bytes 884744 | tf_op jit(solution)/shard_map/unmix/ppermute | solution.py:272
  330.7 0.7 copy-start.15
  331.5 6.8 %copy-start.7 = (bf16[256,768]{1,0:T(8,128)(2,1)S(1)}, bf16[256,768]{1,0:T(8,128)(2,1)}, u32[]{:S(2)}) copy-start(bf16[256,768]{1,0:T(8,128)(2,1)} %get-tuple-element.18) | copy-start | bytes 1179652
  333.8 17.2 %all-to-all-start.9 = ((bf16[4,128,768]{2,1,0:T(8,128)(2,1)}), bf16[4,128,768]{2,1,0:T(8,128)(2,1)S(1)}, u32[]{:S(2)}, u32[]{:S(2)}) async-start(bf16[4,128,768]{2,1,0:T(8,128)(2,1)} %bitcast.122), calls=%async_computation.9 | async-start | bytes 1572864 | tf_op jit(solution)/shard_map/backward_synthesis/all_to_all | solution.py:66
  340.5 2.1 slice-start
  342.6 8.8 %copy-start.12 = (bf16[256,384]{1,0:T(8,128)(2,1)S(1)}, bf16[256,384]{1,0:T(8,128)(2,1)}, u32[]{:S(2)}) copy-start(bf16[256,384]{1,0:T(8,128)(2,1)} %copy-done.11) | copy-start | bytes 589828
  343.5 8.7 %copy-start.1 = (bf16[384,768]{1,0:T(8,128)(2,1)S(1)}, bf16[384,768]{1,0:T(8,128)(2,1)}, u32[]{:S(2)}) copy-start(bf16[384,768]{1,0:T(8,128)(2,1)} %param.14) | copy-start | bytes 1769476
Sparse Core Ops, SparseCore 0:
  10.7 41.5 all-gather.3

commit v6 on v5

--- a/solution.py
+++ b/solution.py
@@ -173,12 +173,13 @@
         return jnp.concatenate([out_re, out_im]).astype(jnp.bfloat16)
 
     with jax.named_scope("forward_analysis"):
-        own_weight = spectral_weight.transpose(0, 1, 3, 2).reshape(-1, width)
-        sent = jnp.concatenate([grid.reshape(-1, width), own_weight])
-        gathered = lax.all_gather(sent, "lon", axis=0)
+        gathered = lax.all_gather(grid.reshape(-1, width), "lon", axis=0)
+        gathered, own_weight = lax.optimization_barrier((gathered, spectral_weight))
         four = swap_blocks(to_orders(gathered, plain_t, quad_lanes), "lat")
     with jax.named_scope("weights"):
-        weights = gathered[:, rows * lon_rows :].reshape(lon_count, 2, rows, quarter, width)
+        own_weight = own_weight.transpose(0, 1, 3, 2).reshape(-1, width)
+        weights = lax.all_gather(own_weight, "lon", axis=0)
+        weights = weights.reshape(lon_count, 2, rows, quarter, width)
         weights = weights.transpose(1, 2, 0, 3, 4).reshape(2, rows, width, width)
     with jax.named_scope("forward_analysis"):
         spectrum = swap_blocks(analyze(four), "lat")

time: 360 us -> 332 us (0.922)
  waiting for transfers between devices: 161 us -> 118 us
  blocking collectives: 40.2 us -> 54.2 us
    all_gather x1, waiting for transfers between devices: 42.2 us -> 0.02 us  [body(): weights = lax.all_gather(own_weight, 'lon', axis=0)]
    all_gather x0 -> x1, blocking collectives: none -> 14 us  [body(): gathered = lax.all_gather(grid.reshape(-1, width), 'lon', axis=0)]
  transfers between devices with their start and end apart: 20 -> 20, of which waited for: 12 -> 11; matrix products, arithmetic and copies ran while one was open for 7% -> 9% of each run, Pallas kernels for 0% -> 0%
where the time goes in v6:
time: 332 us; the launch traced here: 331 us
  waiting for transfers between devices  118 us (36%)
  starting transfers between devices  102 us (31%)
  blocking collectives  54.2 us (16%)
  matrix products  19.5 us (6%)
  local copies, waits for them, and re-layouts  15.9 us (5%)
  between operations  14.9 us (4%)
  other arithmetic  6.05 us (2%)
    all_to_all x9, waiting for transfers between devices, swap_blocks(): return lax.all_to_all(values, axis, split_axis=0, concat_axis=0, tiled=True)  113 us
    all_to_all x9, starting transfers between devices, swap_blocks(): return lax.all_to_all(values, axis, split_axis=0, concat_axis=0, tiled=True)  70.7 us
    all_to_all x1, blocking collectives, swap_blocks(): return lax.all_to_all(values, axis, split_axis=0, concat_axis=0, tiled=True)  25.9 us
    ppermute x6, starting transfers between devices, scatter_sum(): parts.append(lax.ppermute(block, axis, shifted(shift)))  18.7 us
    all_gather x1, blocking collectives, body(): gathered = lax.all_gather(hidden_grad, 'lon', axis=0)  14.3 us
    all_gather x1, blocking collectives, body(): gathered = lax.all_gather(grid.reshape(-1, width), 'lon', axis=0)  14 us
    ppermute x3, starting transfers between devices, body(): grad_spectral.append(lax.ppermute(block, 'lon', pairs))  10.4 us
  transfers between devices with their start and end apart: 20, of which 11 were waited for; matrix products, arithmetic and copies ran while one was open for 9% of the time, Pallas kernels for 0%

profile of v6, /device:TPU:32, one launch (start us, length us, event | category | flops | bytes accessed | tf_op | source)
XLA Modules:
  0.0 330.7 jit_solution(14278298088166365555)
XLA Ops:
  7.2 14.0 %all_gather.12.values_ref = bf16[4,256,384]{2,1,0:T(8,128)(2,1)S(1)} all-gather(bf16[1,256,384]{2,1,0:T(8,128)(2,1)} %bitcast.125), channel_id=1, replica_groups=mesh['lat'=128,'lon'=4] {'lon'}, dimensions={0}, use_global_device_ids=true | all-gather | bytes 983040 | tf_op jit(solution)/shard_map/forward_analysis/all_gather | solution.py:176
  21.3 0.8 dynamic_slice.54
  22.4 0.7 reshape.120
  23.1 19.2 %all-to-all-start = ((bf16[128,2,384]{2,1,0:T(2,128)(2,1)}), bf16[128,2,384]{2,1,0:T(2,128)(2,1)S(1)}, u32[]{:S(2)}, u32[]{:S(2)}) async-start(bf16[128,2,384]{2,1,0:T(2,128)(2,1)} %reshape.120), calls=%async_computation | async-start | bytes 393216 | tf_op jit(solution)/shard_map/forward_analysis/all_to_all | solution.py:66
  42.3 19.8 %all-to-all-done = bf16[128,2,384]{2,1,0:T(2,128)(2,1)S(1)} async-done(((bf16[128,2,384]{2,1,0:T(2,128)(2,1)}), bf16[128,2,384]{2,1,0:T(2,128)(2,1)S(1)}, u32[]{:S(2)}, u32[]{:S(2)}) %all-to-all-start) | async-done | bytes 196640 | tf_op jit(solution)/shard_map/forward_analysis/all_to_all | solution.py:66
  62.2 1.1 convolution_convert_fusion.4
  63.4 0.8 reshape.122
  64.1 6.2 %all-to-all-start.1 = ((bf16[128,2,384]{2,1,0:T(2,128)(2,1)}), bf16[128,2,384]{2,1,0:T(2,128)(2,1)S(1)}, u32[]{:S(2)}, u32[]{:S(2)}) async-start(bf16[128,2,384]{2,1,0:T(2,128)(2,1)} %reshape.122), calls=%async_computation.1 | async-start | bytes 393216 | tf_op jit(solution)/shard_map/forward_analysis/all_to_all | solution.py:66
  70.4 1.4 fusion.45
  71.9 18.3 %all-to-all-done.1 = bf16[128,2,384]{2,1,0:T(2,128)(2,1)S(1)} async-done(((bf16[128,2,384]{2,1,0:T(2,128)(2,1)}), bf16[128,2,384]{2,1,0:T(2,128)(2,1)S(1)}, u32[]{:S(2)}, u32[]{:S(2)}) %all-to-all-start.1) | async-done | bytes 196640 | tf_op jit(solution)/shard_map/forward_analysis/all_to_all | solution.py:66
  91.2 25.9 %all_to_all.50 = bf16[128,2,384]{2,1,0:T(2,128)(2,1)S(1)} all-to-all(bf16[128,2,384]{2,1,0:T(2,128)(2,1)S(1)} %copy.44), channel_id=1, replica_groups=mesh['lat'=128,'lon'=4] {'lat'}, dimensions={0} | all-to-all | bytes 393216 | tf_op jit(solution)/shard_map/forward_synthesis/all_to_all | solution.py:66
  117.1 1.2 convolution_convert_fusion.3
  118.3 0.8 reshape.124
  119.0 6.1 %all-to-all-start.3 = ((bf16[128,2,384]{2,1,0:T(2,128)(2,1)}), bf16[128,2,384]{2,1,0:T(2,128)(2,1)S(1)}, u32[]{:S(2)}, u32[]{:S(2)}) async-start(bf16[128,2,384]{2,1,0:T(2,128)(2,1)} %reshape.124), calls=%async_computation.3 | async-start | bytes 393216 | tf_op jit(solution)/shard_map/forward_synthesis/all_to_all | solution.py:66
  125.2 19.8 %all-to-all-done.3 = bf16[128,2,384]{2,1,0:T(2,128)(2,1)S(1)} async-done(((bf16[128,2,384]{2,1,0:T(2,128)(2,1)}), bf16[128,2,384]{2,1,0:T(2,128)(2,1)S(1)}, u32[]{:S(2)}, u32[]{:S(2)}) %all-to-all-start.3) | async-done | bytes 196640 | tf_op jit(solution)/shard_map/forward_synthesis/all_to_all | solution.py:66
  145.0 2.2 convolution_convert_fusion
  147.2 4.5 %all-to-all-start.4 = ((bf16[4,128,768]{2,1,0:T(8,128)(2,1)}), bf16[4,128,768]{2,1,0:T(8,128)(2,1)S(1)}, u32[]{:S(2)}, u32[]{:S(2)}) async-start(bf16[4,128,768]{2,1,0:T(8,128)(2,1)} %bitcast.115), calls=%async_computation.4 | async-start | bytes 1572864 | tf_op jit(solution)/shard_map/forward_synthesis/all_to_all | solution.py:66
  151.9 12.4 %all-to-all-done.4 = bf16[4,128,768]{2,1,0:T(8,128)(2,1)S(1)} async-done(((bf16[4,128,768]{2,1,0:T(8,128)(2,1)}), bf16[4,128,768]{2,1,0:T(8,128)(2,1)S(1)}, u32[]{:S(2)}, u32[]{:S(2)}) %all-to-all-start.4) | async-done | bytes 786464 | tf_op jit(solution)/shard_map/forward_synthesis/all_to_all | solution.py:66
  164.8 1.1 multiply_convert_fusion.1
  166.8 14.3 %all-gather = bf16[1024,384]{1,0:T(8,128)(2,1)S(1)} all-gather(bf16[256,384]{1,0:T(8,128)(2,1)S(1)} %fusion.2), channel_id=2, replica_groups=mesh['lat'=128,'lon'=4] {'lon'}, dimensions={0}, use_global_device_ids=true | all-gather | bytes 983040 | tf_op jit(solution)/shard_map/backward_analysis/all_gather | solution.py:211
  181.4 0.7 reshape.130
  182.1 6.3 %all-to-all-start.5 = ((bf16[128,2,384]{2,1,0:T(2,128)(2,1)}), bf16[128,2,384]{2,1,0:T(2,128)(2,1)}, u32[]{:S(2)}, u32[]{:S(2)}) async-start(bf16[128,2,384]{2,1,0:T(2,128)(2,1)} %reshape.130), calls=%async_computation.5 | async-start | bytes 393216 | tf_op jit(solution)/shard_map/backward_analysis/all_to_all | solution.py:66
  189.1 2.5 broadcast_select_fusion
  191.7 2.2 collective-permute-start
  193.9 14.2 %all-to-all-done.5 = bf16[128,2,384]{2,1,0:T(2,128)(2,1)} async-done(((bf16[128,2,384]{2,1,0:T(2,128)(2,1)}), bf16[128,2,384]{2,1,0:T(2,128)(2,1)}, u32[]{:S(2)}, u32[]{:S(2)}) %all-to-all-start.5) | async-done | bytes 196640 | tf_op jit(solution)/shard_map/backward_analysis/all_to_all | solution.py:66
  208.1 1.0 reshape.131
  209.1 1.1 convolution_convert_fusion.2
  210.2 0.8 reshape.132
  211.0 6.6 %all-to-all-start.6 = ((bf16[128,2,384]{2,1,0:T(2,128)(2,1)}), bf16[128,2,384]{2,1,0:T(2,128)(2,1)}, u32[]{:S(2)}, u32[]{:S(2)}) async-start(bf16[128,2,384]{2,1,0:T(2,128)(2,1)} %reshape.132), calls=%async_computation.6 | async-start | bytes 393216 | tf_op jit(solution)/shard_map/backward_analysis/all_to_all | solution.py:66
  217.6 1.2 convert_add_fusion
  219.3 2.9 collective-permute-start.3
  222.2 2.8 collective-permute-start.2
  225.0 2.9 collective-permute-start.1
  227.9 9.2 %all-to-all-done.6 = bf16[128,2,384]{2,1,0:T(2,128)(2,1)} async-done(((bf16[128,2,384]{2,1,0:T(2,128)(2,1)}), bf16[128,2,384]{2,1,0:T(2,128)(2,1)}, u32[]{:S(2)}, u32[]{:S(2)}) %all-to-all-start.6) | async-done | bytes 196640 | tf_op jit(solution)/shard_map/backward_analysis/all_to_all | solution.py:66
  237.1 1.2 convolution_bitcast_fusion
  238.3 1.2 convolution_bitcast_fusion.1
  239.6 0.9 copy.49
  240.5 7.0 %all-to-all-start.7 = ((bf16[128,2,384]{2,1,0:T(2,128)(2,1)}), bf16[128,2,384]{2,1,0:T(2,128)(2,1)S(1)}, u32[]{:S(2)}, u32[]{:S(2)}) async-start(bf16[128,2,384]{2,1,0:T(2,128)(2,1)} %copy.49), calls=%async_computation.7 | async-start | bytes 393216 | tf_op jit(solution)/shard_map/backward_synthesis/all_to_all | solution.py:66
  247.8 4.6 %collective-permute-start.6 = (bf16[128,144]{1,0:T(8,128)(2,1)S(1)}, bf16[128,144]{1,0:T(8,128)(2,1)S(1)}, u32[]{:S(2)}, u32[]{:S(2)}) collective-permute-start(bf16[128,144]{1,0:T(8,128)(2,1)S(1)} %get-tuple-element.50), channel_id=1, source_target_pairs={{0,24},{4,28},{8,0},{12,4},{16,8},{20,12},{24,16},{28,20},{32,56},... | collective-permute-start | bytes 110600 | tf_op jit(solution)/shard_map/pointwise_weights/ppermute | solution.py:114
  252.4 2.8 collective-permute-start.5
  255.2 2.8 collective-permute-start.4
  258.0 2.3 collective-permute-done.5
  260.2 2.4 collective-permute-done.4
  262.8 4.5 %all-to-all-done.7 = bf16[128,2,384]{2,1,0:T(2,128)(2,1)S(1)} async-done(((bf16[128,2,384]{2,1,0:T(2,128)(2,1)}), bf16[128,2,384]{2,1,0:T(2,128)(2,1)S(1)}, u32[]{:S(2)}, u32[]{:S(2)}) %all-to-all-start.7) | async-done | bytes 196640 | tf_op jit(solution)/shard_map/backward_synthesis/all_to_all | solution.py:66
  267.4 1.2 convolution_convert_fusion.1
  268.6 1.0 pad_maximum_fusion
  269.6 10.3 %all-to-all-start.8 = ((bf16[128,2,512]{2,1,0:T(2,128)(2,1)}), bf16[128,2,512]{2,1,0:T(2,128)(2,1)S(1)}, u32[]{:S(2)}, u32[]{:S(2)}) async-start(bf16[128,2,512]{2,1,0:T(2,128)(2,1)} %pad_maximum_fusion), calls=%async_computation.8 | async-start | bytes 524288 | tf_op jit(solution)/shard_map/backward_synthesis/all_to_all | solution.py:66
  280.0 1.0 copy.85
  281.8 0.8 copy.82
  282.6 4.1 %collective-permute-start.9 = (bf16[2,2,96,384]{3,2,1,0:T(8,128)(2,1)}, bf16[2,2,96,384]{3,2,1,0:T(8,128)(2,1)}, u32[]{:S(2)}, u32[]{:S(2)}) collective-permute-start(bf16[2,2,96,384]{3,2,1,0:T(8,128)(2,1)} %bitcast.101), channel_id=1, source_target_pairs={{0,3},{1,0},{2,1},{3,2},{4,7},{5,4},{6,5},{7,6},{8,11},{9,8},{10,9... | collective-permute-start | bytes 884744 | tf_op jit(solution)/shard_map/unmix/ppermute | solution.py:273
  286.7 0.7 copy.83
  287.4 3.4 %collective-permute-start.8 = (bf16[2,2,96,384]{3,2,1,0:T(8,128)(2,1)}, bf16[2,2,96,384]{3,2,1,0:T(8,128)(2,1)}, u32[]{:S(2)}, u32[]{:S(2)}) collective-permute-start(bf16[2,2,96,384]{3,2,1,0:T(8,128)(2,1)} %bitcast.102), channel_id=1, source_target_pairs={{0,2},{1,3},{2,0},{3,1},{4,6},{5,7},{6,4},{7,5},{8,10},{9,11},{10,... | collective-permute-start | bytes 884744 | tf_op jit(solution)/shard_map/unmix/ppermute | solution.py:273
  290.8 0.7 copy.84
  291.6 2.9 collective-permute-start.7
  294.5 7.9 %all-to-all-done.8 = bf16[128,2,512]{2,1,0:T(2,128)(2,1)S(1)} async-done(((bf16[128,2,512]{2,1,0:T(2,128)(2,1)}), bf16[128,2,512]{2,1,0:T(2,128)(2,1)S(1)}, u32[]{:S(2)}, u32[]{:S(2)}) %all-to-all-start.8) | async-done | bytes 262176 | tf_op jit(solution)/shard_map/backward_synthesis/all_to_all | solution.py:66
  302.4 0.7 copy-done.13
  303.3 2.2 multiply_convert_fusion
  305.5 4.6 %all-to-all-start.9 = ((bf16[4,128,768]{2,1,0:T(8,128)(2,1)}), bf16[4,128,768]{2,1,0:T(8,128)(2,1)S(1)}, u32[]{:S(2)}, u32[]{:S(2)}) async-start(bf16[4,128,768]{2,1,0:T(8,128)(2,1)} %bitcast.114), calls=%async_computation.9 | async-start | bytes 1572864 | tf_op jit(solution)/shard_map/backward_synthesis/all_to_all | solution.py:66
  310.1 2.2 fusion.1
  312.2 2.1 fusion.8
  314.5 0.7 squeeze.48
  315.2 0.7 squeeze.49
  315.9 6.9 %all-to-all-done.9 = bf16[4,128,768]{2,1,0:T(8,128)(2,1)S(1)} async-done(((bf16[4,128,768]{2,1,0:T(8,128)(2,1)}), bf16[4,128,768]{2,1,0:T(8,128)(2,1)S(1)}, u32[]{:S(2)}, u32[]{:S(2)}) %all-to-all-start.9) | async-done | bytes 786464 | tf_op jit(solution)/shard_map/backward_synthesis/all_to_all | solution.py:66
  323.2 0.7 fusion.13
  (98 shorter events, 7.0 us)
Async XLA Ops:
  7.2 157.6 %copy-start = (bf16[384,768]{1,0:T(8,128)(2,1)S(1)}, bf16[384,768]{1,0:T(8,128)(2,1)}, u32[]{:S(2)}) copy-start(bf16[384,768]{1,0:T(8,128)(2,1)} %param.14) | copy-start | bytes 1769476
  7.2 14.9 %copy-start.3 = (bf16[4,128,512]{2,1,0:T(8,128)(2,1)S(1)}, bf16[4,128,512]{2,1,0:T(8,128)(2,1)}, u32[]{:S(2)}) copy-start(bf16[4,128,512]{2,1,0:T(8,128)(2,1)} %constant.133.clone.matrix_ref) | copy-start | bytes 1572868
  7.2 63.2 %all-gather.3.cloned.1.call-start = ((), (), s32[]{:S(2)}) async-start(), calls=%async_computation.10 | async-start | bytes 1474560 | tf_op jit(solution)/shard_map/weights/all_gather | solution.py:181
  23.1 39.0 %all-to-all-start = ((bf16[128,2,384]{2,1,0:T(2,128)(2,1)}), bf16[128,2,384]{2,1,0:T(2,128)(2,1)S(1)}, u32[]{:S(2)}, u32[]{:S(2)}) async-start(bf16[128,2,384]{2,1,0:T(2,128)(2,1)} %reshape.120), calls=%async_computation | async-start | bytes 393216 | tf_op jit(solution)/shard_map/forward_analysis/all_to_all | solution.py:66
  64.1 26.1 %all-to-all-start.1 = ((bf16[128,2,384]{2,1,0:T(2,128)(2,1)}), bf16[128,2,384]{2,1,0:T(2,128)(2,1)S(1)}, u32[]{:S(2)}, u32[]{:S(2)}) async-start(bf16[128,2,384]{2,1,0:T(2,128)(2,1)} %reshape.122), calls=%async_computation.1 | async-start | bytes 393216 | tf_op jit(solution)/shard_map/forward_analysis/all_to_all | solution.py:66
  90.2 0.7 copy-start.6
  119.0 26.0 %all-to-all-start.3 = ((bf16[128,2,384]{2,1,0:T(2,128)(2,1)}), bf16[128,2,384]{2,1,0:T(2,128)(2,1)S(1)}, u32[]{:S(2)}, u32[]{:S(2)}) async-start(bf16[128,2,384]{2,1,0:T(2,128)(2,1)} %reshape.124), calls=%async_computation.3 | async-start | bytes 393216 | tf_op jit(solution)/shard_map/forward_synthesis/all_to_all | solution.py:66
  125.2 26.5 %copy-start.14 = (bf16[2,128,384]{2,1,0:T(8,128)(2,1)S(1)}, bf16[2,128,384]{2,1,0:T(8,128)(2,1)}, u32[]{:S(2)}) copy-start(bf16[2,128,384]{2,1,0:T(8,128)(2,1)} %param.11) | copy-start | bytes 589828
  147.2 17.0 %all-to-all-start.4 = ((bf16[4,128,768]{2,1,0:T(8,128)(2,1)}), bf16[4,128,768]{2,1,0:T(8,128)(2,1)S(1)}, u32[]{:S(2)}, u32[]{:S(2)}) async-start(bf16[4,128,768]{2,1,0:T(8,128)(2,1)} %bitcast.115), calls=%async_computation.4 | async-start | bytes 1572864 | tf_op jit(solution)/shard_map/forward_synthesis/all_to_all | solution.py:66
  164.5 1.4 copy-start.15
  164.5 1.4 copy-start.16
  164.8 23.7 %copy-start.8 = (bf16[2,128,384]{2,1,0:T(8,128)(2,1)}, bf16[2,128,384]{2,1,0:T(8,128)(2,1)S(1)}, u32[]{:S(2)}) copy-start(bf16[2,128,384]{2,1,0:T(8,128)(2,1)S(1)} %copy.46) | copy-start | bytes 589828
  166.4 14.7 %copy-start.11 = (bf16[256,768]{1,0:T(8,128)(2,1)}, bf16[256,768]{1,0:T(8,128)(2,1)S(1)}, u32[]{:S(2)}) copy-start(bf16[256,768]{1,0:T(8,128)(2,1)S(1)} %fusion) | copy-start | bytes 1179652
  166.4 14.7 %copy-start.2 = (bf16[4,128,512]{2,1,0:T(8,128)(2,1)S(1)}, bf16[4,128,512]{2,1,0:T(8,128)(2,1)}, u32[]{:S(2)}) copy-start(bf16[4,128,512]{2,1,0:T(8,128)(2,1)} %constant.134.clone.matrix_ref) | copy-start | bytes 1572868
  166.8 15.3 %copy-start.9 = (bf16[256,384]{1,0:T(8,128)(2,1)}, bf16[256,384]{1,0:T(8,128)(2,1)S(1)}, u32[]{:S(2)}) copy-start(bf16[256,384]{1,0:T(8,128)(2,1)S(1)} %fusion.2) | copy-start | bytes 589828
  181.1 7.4 %copy-start.12 = (bf16[256,768]{1,0:T(8,128)(2,1)S(1)}, bf16[256,768]{1,0:T(8,128)(2,1)}, u32[]{:S(2)}) copy-start(bf16[256,768]{1,0:T(8,128)(2,1)} %copy-done.11) | copy-start | bytes 1179652
  182.1 25.9 %all-to-all-start.5 = ((bf16[128,2,384]{2,1,0:T(2,128)(2,1)}), bf16[128,2,384]{2,1,0:T(2,128)(2,1)}, u32[]{:S(2)}, u32[]{:S(2)}) async-start(bf16[128,2,384]{2,1,0:T(2,128)(2,1)} %reshape.130), calls=%async_computation.5 | async-start | bytes 393216 | tf_op jit(solution)/shard_map/backward_analysis/all_to_all | solution.py:66
  191.6 25.9 %copy-start.4 = (f32[768,384]{1,0:T(8,128)S(1)}, f32[768,384]{1,0:T(8,128)}, u32[]{:S(2)}) copy-start(f32[768,384]{1,0:T(8,128)} %get-tuple-element.24) | copy-start | bytes 3538948
  191.7 19.3 %collective-permute-start = (bf16[768,384]{1,0:T(8,128)(2,1)S(1)}, bf16[768,384]{1,0:T(8,128)(2,1)}, u32[]{:S(2)}, u32[]{:S(2)}) collective-permute-start(bf16[768,384]{1,0:T(8,128)(2,1)S(1)} %select_convert_fusion), channel_id=1, source_target_pairs={{0,4},{4,0},{8,12},{12,8},{16,20},{20,16},{24,28},{28,24},{32,36},... | collective-permute-start | bytes 1769480 | tf_op jit(solution)/shard_map/pointwise_weights/ppermute | solution.py:224
  211.0 26.1 %all-to-all-start.6 = ((bf16[128,2,384]{2,1,0:T(2,128)(2,1)}), bf16[128,2,384]{2,1,0:T(2,128)(2,1)}, u32[]{:S(2)}, u32[]{:S(2)}) async-start(bf16[128,2,384]{2,1,0:T(2,128)(2,1)} %reshape.132), calls=%async_computation.6 | async-start | bytes 393216 | tf_op jit(solution)/shard_map/backward_analysis/all_to_all | solution.py:66
  219.3 28.2 %collective-permute-start.3 = (bf16[128,576]{1,0:T(8,128)(2,1)S(1)}, bf16[128,576]{1,0:T(8,128)(2,1)S(1)}, u32[]{:S(2)}, u32[]{:S(2)}) collective-permute-start(bf16[128,576]{1,0:T(8,128)(2,1)S(1)} %get-tuple-element.43), channel_id=1, source_target_pairs={{0,3},{1,0},{2,1},{3,2},{4,7},{5,4},{6,5},{7,6},{8,11},{9,8},{10,9... | collective-permute-start | bytes 442376 | tf_op jit(solution)/shard_map/pointwise_weights/ppermute | solution.py:114
  222.2 25.3 %collective-permute-start.2 = (bf16[128,576]{1,0:T(8,128)(2,1)S(1)}, bf16[128,576]{1,0:T(8,128)(2,1)S(1)}, u32[]{:S(2)}, u32[]{:S(2)}) collective-permute-start(bf16[128,576]{1,0:T(8,128)(2,1)S(1)} %get-tuple-element.44), channel_id=1, source_target_pairs={{0,2},{1,3},{2,0},{3,1},{4,6},{5,7},{6,4},{7,5},{8,10},{9,11},{10,... | collective-permute-start | bytes 442376 | tf_op jit(solution)/shard_map/pointwise_weights/ppermute | solution.py:114
  225.0 22.5 %collective-permute-start.1 = (bf16[128,576]{1,0:T(8,128)(2,1)S(1)}, bf16[128,576]{1,0:T(8,128)(2,1)S(1)}, u32[]{:S(2)}, u32[]{:S(2)}) collective-permute-start(bf16[128,576]{1,0:T(8,128)(2,1)S(1)} %get-tuple-element.42), channel_id=1, source_target_pairs={{0,1},{1,2},{2,3},{3,0},{4,5},{5,6},{6,7},{7,4},{8,9},{9,10},{10,1... | collective-permute-start | bytes 442376 | tf_op jit(solution)/shard_map/pointwise_weights/ppermute | solution.py:114
  240.5 26.8 %all-to-all-start.7 = ((bf16[128,2,384]{2,1,0:T(2,128)(2,1)}), bf16[128,2,384]{2,1,0:T(2,128)(2,1)S(1)}, u32[]{:S(2)}, u32[]{:S(2)}) async-start(bf16[128,2,384]{2,1,0:T(2,128)(2,1)} %copy.49), calls=%async_computation.7 | async-start | bytes 393216 | tf_op jit(solution)/shard_map/backward_synthesis/all_to_all | solution.py:66
  247.8 10.1 %collective-permute-start.6 = (bf16[128,144]{1,0:T(8,128)(2,1)S(1)}, bf16[128,144]{1,0:T(8,128)(2,1)S(1)}, u32[]{:S(2)}, u32[]{:S(2)}) collective-permute-start(bf16[128,144]{1,0:T(8,128)(2,1)S(1)} %get-tuple-element.50), channel_id=1, source_target_pairs={{0,24},{4,28},{8,0},{12,4},{16,8},{20,12},{24,16},{28,20},{32,56},... | collective-permute-start | bytes 110600 | tf_op jit(solution)/shard_map/pointwise_weights/ppermute | solution.py:114
  252.4 7.8 %collective-permute-start.5 = (bf16[128,144]{1,0:T(8,128)(2,1)S(1)}, bf16[128,144]{1,0:T(8,128)(2,1)S(1)}, u32[]{:S(2)}, u32[]{:S(2)}) collective-permute-start(bf16[128,144]{1,0:T(8,128)(2,1)S(1)} %get-tuple-element.51), channel_id=1, source_target_pairs={{0,16},{4,20},{8,24},{12,28},{16,0},{20,4},{24,8},{28,12},{32,48},... | collective-permute-start | bytes 110600 | tf_op jit(solution)/shard_map/pointwise_weights/ppermute | solution.py:114
  255.2 7.4 %collective-permute-start.4 = (bf16[128,144]{1,0:T(8,128)(2,1)S(1)}, bf16[128,144]{1,0:T(8,128)(2,1)S(1)}, u32[]{:S(2)}, u32[]{:S(2)}) collective-permute-start(bf16[128,144]{1,0:T(8,128)(2,1)S(1)} %get-tuple-element.49), channel_id=1, source_target_pairs={{0,8},{4,12},{8,16},{12,20},{16,24},{20,28},{24,0},{28,4},{32,40},... | collective-permute-start | bytes 110600 | tf_op jit(solution)/shard_map/pointwise_weights/ppermute | solution.py:114
  267.3 13.7 %copy-start.7 = (bf16[128,2,384]{2,1,0:T(2,128)(2,1)S(1)}, bf16[128,2,384]{2,1,0:T(2,128)(2,1)}, u32[]{:S(2)}) copy-start(bf16[128,2,384]{2,1,0:T(2,128)(2,1)} %copy-done.6) | copy-start | bytes 589828
  269.6 32.8 %all-to-all-start.8 = ((bf16[128,2,512]{2,1,0:T(2,128)(2,1)}), bf16[128,2,512]{2,1,0:T(2,128)(2,1)S(1)}, u32[]{:S(2)}, u32[]{:S(2)}) async-start(bf16[128,2,512]{2,1,0:T(2,128)(2,1)} %pad_maximum_fusion), calls=%async_computation.8 | async-start | bytes 524288 | tf_op jit(solution)/shard_map/backward_synthesis/all_to_all | solution.py:66
  282.6 29.6 %collective-permute-start.9 = (bf16[2,2,96,384]{3,2,1,0:T(8,128)(2,1)}, bf16[2,2,96,384]{3,2,1,0:T(8,128)(2,1)}, u32[]{:S(2)}, u32[]{:S(2)}) collective-permute-start(bf16[2,2,96,384]{3,2,1,0:T(8,128)(2,1)} %bitcast.101), channel_id=1, source_target_pairs={{0,3},{1,0},{2,1},{3,2},{4,7},{5,4},{6,5},{7,6},{8,11},{9,8},{10,9... | collective-permute-start | bytes 884744 | tf_op jit(solution)/shard_map/unmix/ppermute | solution.py:273
  287.4 24.8 %collective-permute-start.8 = (bf16[2,2,96,384]{3,2,1,0:T(8,128)(2,1)}, bf16[2,2,96,384]{3,2,1,0:T(8,128)(2,1)}, u32[]{:S(2)}, u32[]{:S(2)}) collective-permute-start(bf16[2,2,96,384]{3,2,1,0:T(8,128)(2,1)} %bitcast.102), channel_id=1, source_target_pairs={{0,2},{1,3},{2,0},{3,1},{4,6},{5,7},{6,4},{7,5},{8,10},{9,11},{10,... | collective-permute-start | bytes 884744 | tf_op jit(solution)/shard_map/unmix/ppermute | solution.py:273
  291.6 20.7 %collective-permute-start.7 = (bf16[2,2,96,384]{3,2,1,0:T(8,128)(2,1)}, bf16[2,2,96,384]{3,2,1,0:T(8,128)(2,1)}, u32[]{:S(2)}, u32[]{:S(2)}) collective-permute-start(bf16[2,2,96,384]{3,2,1,0:T(8,128)(2,1)} %bitcast.103), channel_id=1, source_target_pairs={{0,1},{1,2},{2,3},{3,0},{4,5},{5,6},{6,7},{7,4},{8,9},{9,10},{10,1... | collective-permute-start | bytes 884744 | tf_op jit(solution)/shard_map/unmix/ppermute | solution.py:273
  302.4 0.7 copy-start.13
  303.3 6.8 %copy-start.5 = (bf16[256,768]{1,0:T(8,128)(2,1)S(1)}, bf16[256,768]{1,0:T(8,128)(2,1)}, u32[]{:S(2)}) copy-start(bf16[256,768]{1,0:T(8,128)(2,1)} %get-tuple-element.22) | copy-start | bytes 1179652
  305.5 17.2 %all-to-all-start.9 = ((bf16[4,128,768]{2,1,0:T(8,128)(2,1)}), bf16[4,128,768]{2,1,0:T(8,128)(2,1)S(1)}, u32[]{:S(2)}, u32[]{:S(2)}) async-start(bf16[4,128,768]{2,1,0:T(8,128)(2,1)} %bitcast.114), calls=%async_computation.9 | async-start | bytes 1572864 | tf_op jit(solution)/shard_map/backward_synthesis/all_to_all | solution.py:66
  312.2 2.1 slice-start
  314.3 8.8 %copy-start.10 = (bf16[256,384]{1,0:T(8,128)(2,1)S(1)}, bf16[256,384]{1,0:T(8,128)(2,1)}, u32[]{:S(2)}) copy-start(bf16[256,384]{1,0:T(8,128)(2,1)} %copy-done.9) | copy-start | bytes 589828
  315.2 8.7 %copy-start.1 = (bf16[384,768]{1,0:T(8,128)(2,1)S(1)}, bf16[384,768]{1,0:T(8,128)(2,1)}, u32[]{:S(2)}) copy-start(bf16[384,768]{1,0:T(8,128)(2,1)} %param.14) | copy-start | bytes 1769476
Sparse Core Ops, SparseCore 0:
  21.4 36.3 all-gather.2

commit v7 on v6

v7 whole, which is shorter than its diff:
```python
import functools
import math

import jax
import jax.numpy as jnp
import ml_dtypes
import numpy as np
from jax import lax
from jax.experimental import pallas as pl
from jax.experimental.pallas import tpu as pltpu
from jax.sharding import PartitionSpec as P


def legendre_table(size):
    theta = math.pi * (np.arange(size) + 0.5) / size
    cosv, sinv = np.cos(theta), np.sin(theta)
    order = np.arange(size, dtype=np.float64)[:, None]
    start = np.empty((size, size))
    start[0] = math.sqrt(1.0 / (4.0 * math.pi))
    for m in range(1, size):
        start[m] = start[m - 1] * math.sqrt((2 * m + 1) / (2.0 * m)) * sinv
    table = np.zeros((size, size, size), dtype=ml_dtypes.bfloat16)
    before = np.zeros((size, size))
    now = np.zeros((size, size))
    for level in range(size):
        safe = np.where(order < level, order, 0.0)
        alpha = np.sqrt((4.0 * level * level - 1.0) / (level * level - safe * safe)) if level else 0.0
        beta = (
            np.sqrt(((level - 1.0) ** 2 - safe * safe).clip(0) / (4.0 * (level - 1.0) ** 2 - 1.0))
            if level > 1
            else 0.0
        )
        value = np.where(order < level, alpha * (cosv * now - beta * before), 0.0)
        value[level] = start[level]
        table[:, level, :] = value.astype(np.float32).astype(ml_dtypes.bfloat16)
        before, now = now, value
    return table


def quadrature(nlat, nlon):
    theta = math.pi * (np.arange(nlat) + 0.5) / nlat
    return (math.pi / nlat * np.sin(theta) * (2.0 * math.pi / nlon)).astype(np.float32)


def fourier_tables(nlon, modes, lon_count, rows):
    phase = np.arange(nlon)[:, None] * np.arange(modes)[None, :] % nlon
    angle = 2.0 * math.pi / nlon * phase
    pair = np.stack([np.cos(angle), -np.sin(angle)]).astype(np.float32).astype(ml_dtypes.bfloat16)
    factor = np.where(np.arange(modes) == 0, 1.0, 2.0).astype(np.float32)
    doubled = (pair.astype(np.float32) * factor).astype(ml_dtypes.bfloat16)

    def arrange(values):
        values = values.reshape(2, lon_count, nlon // lon_count, lon_count, modes // lon_count)
        values = values.transpose(3, 0, 4, 1, 2)
        out = np.zeros(values.shape[:3] + (rows, lon_count, rows, values.shape[4]), values.dtype)
        for row in range(rows):
            out[:, :, :, row, :, row] = values
        return out.reshape(lon_count, 2 * modes // lon_count * rows, nlon * rows)

    return arrange(pair), arrange(doubled)


def gelu_parts(values):
    half = 0.5 * (1.0 + lax.erf(values * (1.0 / math.sqrt(2.0))))
    slope = half + values * jnp.exp(-0.5 * values * values) * (1.0 / math.sqrt(2.0 * math.pi))
    return values * half, slope


def swap_blocks(values, axis):
    return lax.all_to_all(values, axis, split_axis=0, concat_axis=0, tiled=True)


def product_kernel(dims, matrix_ref, *refs):
    *scale_ref, values_ref, out_ref = refs
    width = out_ref.shape[-1]
    values = values_ref[...].reshape(-1, width)
    out = lax.dot_general(matrix_ref[0], values, dims, preferred_element_type=jnp.float32)
    if scale_ref:
        out = out * scale_ref[0][...]
    out_ref[...] = out.astype(jnp.bfloat16).reshape(out_ref.shape)


def beside_kernel(dims, matrix_ref, values_ref, extra_ref, out_ref):
    width = values_ref.shape[-1]
    values = values_ref[...].reshape(-1, width)
    out = lax.dot_general(matrix_ref[0], values, dims, preferred_element_type=jnp.float32)
    out_ref[:, :, :width] = out.astype(jnp.bfloat16).reshape(values_ref.shape)
    out_ref[:, :, width:] = extra_ref[...]


def mix_kernel(conjugate, weights_ref, values_ref, out_ref):
    rows, width = weights_ref.shape[1], weights_ref.shape[3]
    values = values_ref[...].reshape(-1, width)
    level = lax.broadcasted_iota(jnp.int32, values.shape, 0) & (rows - 1)
    dims = (((1,), (0 if conjugate else 1,)), ((), ()))

    def product(part):
        total = None
        for row in range(rows):
            out = lax.dot_general(
                values, weights_ref[part, row], dims, preferred_element_type=jnp.float32
            )
            total = out if row == 0 else jnp.where(level == row, out, total)
        return total

    by_re, by_im = product(0), product(1)
    if conjugate:
        by_im = -by_im
    half = values.shape[0] // 2
    out = jnp.concatenate([by_re[:half] - by_im[half:], by_re[half:] + by_im[:half]])
    out_ref[...] = out.astype(jnp.bfloat16).reshape(out_ref.shape)


def placed(kernel, place_ref, *refs):
    kernel(*refs)


def whole(shape):
    return pl.BlockSpec(shape, lambda *_: (0,) * len(shape))


def call_kernel(kernel, place, matrices, operands, blocks, out_shape, flops):
    specs = [whole(block) for block in blocks]
    prefetch = ()
    if place is not None:
        specs.insert(0, pl.BlockSpec((1,) + matrices.shape[1:], lambda i, at: (at[0], 0, 0)))
        operands = [matrices] + operands
        prefetch = (place.reshape(1).astype(jnp.int32),)
        kernel = functools.partial(placed, kernel)
    moved = 2 * (math.prod(out_shape) + sum(math.prod(block) for block in blocks))
    return pl.pallas_call(
        kernel,
        grid_spec=pltpu.PrefetchScalarGridSpec(
            num_scalar_prefetch=len(prefetch),
            grid=(1,),
            in_specs=specs,
            out_specs=whole(out_shape),
        ),
        out_shape=jax.ShapeDtypeStruct(out_shape, jnp.bfloat16),
        compiler_params=pltpu.CompilerParams(vmem_limit_bytes=20 * 1024 * 1024),
        cost_estimate=pl.CostEstimate(flops=flops, bytes_accessed=moved, transcendentals=0),
    )(*prefetch, *operands)


PLAIN = (((1,), (0,)), ((), ()))
TURNED = (((0,), (0,)), ((), ()))


def place_product(dims, place, matrices, scale, values, block, out_shape):
    operands, blocks = [values], [block]
    if scale is not None:
        operands, blocks = [scale, values], [scale.shape, block]
    flops = 2 * math.prod(matrices.shape[1:]) * out_shape[-1]
    kernel = functools.partial(product_kernel, dims)
    return call_kernel(kernel, place, matrices, operands, blocks, out_shape, flops)


def scatter_sum(values, axis, index, count, shifted):
    chunk = values.shape[-1] // count
    narrow = values.astype(jnp.bfloat16)
    parts = [lax.dynamic_slice_in_dim(values, index * chunk, chunk, axis=1)]
    for shift in range(1, count):
        to = (index + shift) % count
        block = lax.dynamic_slice_in_dim(narrow, to * chunk, chunk, axis=1)
        parts.append(lax.ppermute(block, axis, shifted(shift)))
    return parts


def add_parts(parts):
    total = parts[0]
    for part in parts[1:]:
        total = total + part.astype(jnp.float32)
    return total


def body(tables, plain, doubled, plain_t, doubled_t, quad, grid, cotangent, *weights_in):
    spectral_weight, w_in, w_out = weights_in
    lat_count = lax.axis_size("lat")
    lon_count = lax.axis_size("lon")
    lat_index = lax.axis_index("lat")
    lon_index = lax.axis_index("lon")
    rows, lon_rows, width = grid.shape
    quarter = width // lon_count
    half = lat_count // 2
    order = lon_index * half + lat_index % half
    local_quad = lax.dynamic_slice_in_dim(quad, lat_index * rows, rows)
    order_quad = jnp.tile(local_quad, lat_count)[:, None]
    row_quad = jnp.tile(jnp.repeat(local_quad, lon_rows), lon_count)[:, None]
    total_lat = rows * lat_count
    spread = (lat_count, rows, width)
    gathered_shape = (lon_count, rows * lon_rows, width)

    def to_orders(values, matrices, scale):
        return place_product(PLAIN, lon_index, matrices, scale, values, gathered_shape, spread)

    def from_orders(values, matrices, scale):
        out = place_product(PLAIN, lon_index, matrices, scale, values, spread, gathered_shape)
        return jnp.sum(swap_blocks(out, "lon").astype(jnp.float32), axis=0)

    def legendre(dims, values):
        kernel = functools.partial(product_kernel, dims)
        flops = 2 * total_lat * total_lat * width
        blocks = [table.shape, spread]
        return call_kernel(kernel, None, None, [table, values], blocks, spread, flops)

    def complex_product(values, conjugate):
        return call_kernel(
            functools.partial(mix_kernel, conjugate),
            None,
            None,
            [weights, values],
            [weights.shape, spread],
            spread,
            8 * rows * values.size * width,
        )

    with jax.named_scope("forward_analysis"):
        gathered = lax.all_gather(grid.reshape(-1, width), "lon", axis=0)
        gathered, order = lax.optimization_barrier((gathered, order))
        table = lax.dynamic_slice_in_dim(tables, order, 1)
        own_weight = spectral_weight
        own_weight = own_weight.transpose(0, 1, 3, 2)[:, :, None]
        four = swap_blocks(to_orders(gathered, plain_t, order_quad), "lat")
    with jax.named_scope("weights"):
        weights = jnp.zeros((2, rows, lon_count, quarter, width), jnp.bfloat16)
        weights = lax.dynamic_update_slice_in_dim(weights, own_weight, lon_index, 2)
        for shift in range(1, lon_count):
            pairs = [(i, (i + shift) % lon_count) for i in range(lon_count)]
            moved = lax.ppermute(own_weight, "lon", pairs)
            source = (lon_index + lon_count - shift) % lon_count
            weights = lax.dynamic_update_slice_in_dim(weights, moved, source, 2)
        weights = weights.reshape(2, rows, width, width)
    with jax.named_scope("forward_analysis"):
        spectrum = swap_blocks(legendre(PLAIN, four), "lat")
    with jax.named_scope("mix"):
        mixed = complex_product(spectrum, False)
    with jax.named_scope("forward_synthesis"):
        fields = swap_blocks(legendre(TURNED, swap_blocks(mixed, "lat")), "lat")
        wave_rows = from_orders(fields, doubled, None)
    with jax.named_scope("pointwise"):
        hidden = (grid.reshape(-1, width).astype(jnp.float32) + wave_rows).astype(jnp.bfloat16)
        back = cotangent.reshape(-1, width)
        act_grad = lax.dot_general(
            back, w_out, (((1,), (1,)), ((), ())), preferred_element_type=jnp.float32
        )
        pre = jnp.dot(hidden, w_in, preferred_element_type=jnp.float32)
        value, slope = gelu_parts(pre)
        act = value.astype(jnp.bfloat16)
        pre_grad = (act_grad * slope).astype(jnp.bfloat16)
        hidden_grad = (
            back.astype(jnp.float32)
            + lax.dot_general(
                pre_grad, w_in, (((1,), (1,)), ((), ())), preferred_element_type=jnp.float32
            )
        ).astype(jnp.bfloat16)
        block_output = (
            hidden.astype(jnp.float32) + jnp.dot(act, w_out, preferred_element_type=jnp.float32)
        ).astype(jnp.bfloat16)
    with jax.named_scope("backward_analysis"):
        gathered = lax.all_gather(hidden_grad, "lon", axis=0)
        gathered, hidden, pre_grad, act = lax.optimization_barrier(
            (gathered, hidden, pre_grad, act)
        )
        field_grad = swap_blocks(to_orders(gathered, doubled_t, None), "lat")
    with jax.named_scope("pointwise_weights"):
        over_rows = (((0,), (0,)), ((), ()))
        out_part = lax.dot_general(act, back, over_rows, preferred_element_type=jnp.float32)
        in_part = lax.dot_general(hidden, pre_grad, over_rows, preferred_element_type=jnp.float32)
        in_part = in_part.reshape(out_part.shape)
        even = lat_index % 2 == 0
        keep = jnp.where(even, in_part, out_part)
        give = jnp.where(even, out_part, in_part).astype(jnp.bfloat16)
        got = lax.ppermute(give, "lat", [(i, i ^ 1) for i in range(lat_count)])
    with jax.named_scope("backward_analysis"):
        mixed_grad = legendre(PLAIN, field_grad)
        mixed_grad, keep, got = lax.optimization_barrier((mixed_grad, keep, got))
        mixed_grad = swap_blocks(mixed_grad, "lat")
    with jax.named_scope("pointwise_weights"):
        sums = add_parts([keep, got]).reshape(lat_count, -1)
        parts = scatter_sum(
            sums,
            "lon",
            lon_index,
            lon_count,
            lambda s: [(i, (i + s) % lon_count) for i in range(lon_count)],
        )
    with jax.named_scope("unmix"):
        spectrum_grad = complex_product(mixed_grad, True)
    with jax.named_scope("backward_synthesis"):
        spectrum_grad = swap_blocks(spectrum_grad, "lat")
    with jax.named_scope("pointwise_weights"):
        parts = scatter_sum(
            add_parts(parts),
            "lat",
            (lat_index >> 1) & 3,
            4,
            lambda s: [(i, (i & ~6) | ((i + 2 * s) & 6)) for i in range(lat_count)],
        )
    with jax.named_scope("backward_synthesis"):
        extra = add_parts(parts).astype(jnp.bfloat16)
        chunk = extra.shape[1]
        room = -(-chunk // (rows * 128)) * rows * 128
        extra = jnp.pad(extra, ((0, 0), (0, room - chunk)))
        extra = extra.reshape(lat_count, rows, room // rows)
        four_grad = call_kernel(
            functools.partial(beside_kernel, TURNED),
            None,
            None,
            [table, spectrum_grad, extra],
            [table.shape, spread, extra.shape],
            (lat_count, rows, width + extra.shape[2]),
            2 * total_lat * total_lat * width,
        )
        four_grad, left, right = lax.optimization_barrier((four_grad, spectrum, mixed_grad))
        four_grad = swap_blocks(four_grad, "lat")
        wave_grad = from_orders(four_grad, plain, row_quad)
        grad_input = (hidden_grad.astype(jnp.float32) + wave_grad).astype(jnp.bfloat16)
    with jax.named_scope("unmix"):
        right = jnp.stack([right, jnp.concatenate([right[half:], -right[:half]])])
        outer = jnp.einsum("pli,rpld->rlid", left, right, preferred_element_type=jnp.float32)
        outer = outer.reshape(2, rows, lon_count, quarter, width)
        own = lax.dynamic_index_in_dim(outer, lon_index, 2, keepdims=False)
        narrow = outer.astype(jnp.bfloat16)
        grad_spectral = [own]
        for shift in range(1, lon_count):
            to = (lon_index + shift) % lon_count
            block = lax.dynamic_index_in_dim(narrow, to, 2, keepdims=False)
            pairs = [(i, (i + shift) % lon_count) for i in range(lon_count)]
            grad_spectral.append(lax.ppermute(block, "lon", pairs))
        grad_spectral = add_parts(grad_spectral)
    with jax.named_scope("pointwise_weights"):
        sums = four_grad[:, :, width:].reshape(lat_count // 8, 4, 2, room)[..., :chunk]
        sums = jnp.sum(sums.astype(jnp.float32), axis=0).swapaxes(0, 1).reshape(2, -1)
    return (
        block_output.reshape(grid.shape),
        grad_input.reshape(grid.shape),
        grad_spectral,
        sums[0],
        sums[1],
    )


def solution(mesh):
    in_specs = (P("lat", "lon", None), P("lat", "lon", None), P(None, "lat", None, "lon"), P(), P())
    out_specs = (
        P("lat", "lon", None),
        P("lat", "lon", None),
        P(None, "lat", "lon", None),
        P(("lat", "lon")),
        P(("lat", "lon")),
    )

    def call(grid, cotangent, spectral_weight, w_in, w_out):
        nlat, nlon, _ = grid.shape
        table = legendre_table(nlat)
        rows = nlat // mesh.shape["lat"]
        plain_t, doubled_t = fourier_tables(nlon, nlat, mesh.shape["lon"], rows)
        plain = np.ascontiguousarray(plain_t.swapaxes(1, 2))
        doubled = np.ascontiguousarray(doubled_t.swapaxes(1, 2))
        quad = quadrature(nlat, nlon)
        mapped = jax.shard_map(
            body,
            mesh=mesh,
            in_specs=(P(),) * 6 + in_specs,
            out_specs=out_specs,
            check_vma=False,
        )
        tables = (table, plain, doubled, plain_t, doubled_t, quad)
        return mapped(*tables, grid, cotangent, spectral_weight, w_in, w_out)

    return call
```

time: 332 us -> 315 us (0.949)
  waiting for transfers between devices: 118 us -> 81.2 us
  blocking collectives: 54.2 us -> 80.1 us
  between operations: 14.9 us -> 1.34 us
  matrix products: 19.5 us -> 7.33 us
  Pallas kernels: 0.59 us -> 10.1 us
  starting transfers between devices: 102 us -> 111 us
  other arithmetic: 6.05 us -> 10 us
    all_to_all x9 -> x8, waiting for transfers between devices: 113 us -> 76.5 us  [swap_blocks(): return lax.all_to_all(values, axis, split_axis=0, concat_axis=0, tiled=True)]
    all_to_all x1 -> x2, blocking collectives: 25.9 us -> 51.7 us  [swap_blocks(): return lax.all_to_all(values, axis, split_axis=0, concat_axis=0, tiled=True)]
    dot_general x10 -> x0, matrix products: 12 us -> none  [the longest x2 4.35 us: from_fourier(): out = jnp.dot(matrix, values, preferred_element_type=jnp.float32)]
    ppermute x0 -> x3, starting transfers between devices: none -> 10.4 us  [body(): moved = lax.ppermute(own_weight, 'lon', pairs)]
    pallas_call x2 -> x10, Pallas kernels: 0.59 us -> 10.1 us  [call_kernel(): pl.pallas_call(kernel, grid_spec=pltpu.PrefetchScalarGridSpec(num_scalar_...]
    reshape x10 -> x0, local copies, waits for them, and re-layouts: 5.02 us -> none  [the longest x2 1.51 us: analyze(): return out.astype(jnp.bfloat16).reshape(lat_count, rows, width)]
    all_to_all x9 -> x8, starting transfers between devices: 70.7 us -> 68.9 us  [swap_blocks(): return lax.all_to_all(values, axis, split_axis=0, concat_axis=0, tiled=True)]
  transfers between devices with their start and end apart: 20 -> 21, of which waited for: 11 -> 10; matrix products, arithmetic and copies ran while one was open for 9% -> 7% of each run, Pallas kernels for 0% -> 1%
where the time goes in v7:
time: 315 us; the launch traced here: 313 us
  starting transfers between devices  111 us (35%)
  waiting for transfers between devices  81.2 us (26%)
  blocking collectives  80.1 us (25%)
  local copies, waits for them, and re-layouts  12.8 us (4%)
  Pallas kernels  10.1 us (3%)
  other arithmetic  10 us (3%)
  matrix products  7.33 us (2%)
    all_to_all x8, waiting for transfers between devices, swap_blocks(): return lax.all_to_all(values, axis, split_axis=0, concat_axis=0, tiled=True)  76.5 us
    all_to_all x8, starting transfers between devices, swap_blocks(): return lax.all_to_all(values, axis, split_axis=0, concat_axis=0, tiled=True)  68.9 us
    all_to_all x2, blocking collectives, swap_blocks(): return lax.all_to_all(values, axis, split_axis=0, concat_axis=0, tiled=True)  51.7 us
    ppermute x6, starting transfers between devices, scatter_sum(): parts.append(lax.ppermute(block, axis, shifted(shift)))  18.7 us
    all_gather x1, blocking collectives, body(): gathered = lax.all_gather(hidden_grad, 'lon', axis=0)  14.4 us
    all_gather x1, blocking collectives, body(): gathered = lax.all_gather(grid.reshape(-1, width), 'lon', axis=0)  14 us
    ppermute x3, starting transfers between devices, body(): grad_spectral.append(lax.ppermute(block, 'lon', pairs))  10.5 us
    ppermute x3, starting transfers between devices, body(): moved = lax.ppermute(own_weight, 'lon', pairs)  10.4 us
  transfers between devices with their start and end apart: 21, of which 10 were waited for; matrix products, arithmetic and copies ran while one was open for 7% of the time, Pallas kernels for 1%

profile of v7, /device:TPU:32, one launch (start us, length us, event | category | flops | bytes accessed | tf_op | source)
XLA Modules:
  0.0 313.4 jit_solution(9023670941162787984)
XLA Ops:
  0.7 14.0 %all_gather.9.refs_2_ = bf16[4,256,384]{2,1,0:T(8,128)(2,1)S(1)} all-gather(bf16[1,256,384]{2,1,0:T(8,128)(2,1)} %bitcast.72), channel_id=1, replica_groups=mesh['lat'=128,'lon'=4] {'lon'}, dimensions={0}, use_global_device_ids=true | all-gather | bytes 983040 | tf_op jit(solution)/shard_map/forward_analysis/all_gather | solution.py:218
  14.7 0.8 dynamic_slice.45
  15.5 1.6 copy-done.5
  17.1 1.1 forward_analysis.2
  18.2 19.2 %all-to-all-start = ((bf16[128,2,384]{2,1,0:T(2,128)(2,1)}), bf16[128,2,384]{2,1,0:T(2,128)(2,1)S(1)}, u32[]{:S(2)}, u32[]{:S(2)}) async-start(bf16[128,2,384]{2,1,0:T(2,128)(2,1)} %forward_analysis.2), calls=%async_computation | async-start | bytes 393216 | tf_op jit(solution)/shard_map/forward_analysis/all_to_all | solution.py:70
  37.4 3.9 %collective-permute-start = (bf16[2,2,1,96,384]{4,3,1,0,2:T(8,128)(2,1)S(1)}, bf16[2,2,1,96,384]{4,3,1,0,2:T(8,128)(2,1)S(1)}, u32[]{:S(2)}, u32[]{:S(2)}) collective-permute-start(bf16[2,2,1,96,384]{4,3,1,0,2:T(8,128)(2,1)S(1)} %bitcast.76), channel_id=1, source_target_pairs={{0,1},{1,2},{2,3},{3,0},{4,5},{5,6},{6,7},{7,4},{8,9},{9,10},{10,1... | collective-permute-start | bytes 884744 | tf_op jit(solution)/shard_map/weights/ppermute | solution.py:229
  41.3 4.6 %collective-permute-start.1 = (bf16[2,2,1,96,384]{4,3,1,0,2:T(8,128)(2,1)S(1)}, bf16[2,2,1,96,384]{4,3,1,0,2:T(8,128)(2,1)S(1)}, u32[]{:S(2)}, u32[]{:S(2)}) collective-permute-start(bf16[2,2,1,96,384]{4,3,1,0,2:T(8,128)(2,1)S(1)} %bitcast.77), channel_id=1, source_target_pairs={{0,2},{1,3},{2,0},{3,1},{4,6},{5,7},{6,4},{7,5},{8,10},{9,11},{10,... | collective-permute-start | bytes 884744 | tf_op jit(solution)/shard_map/weights/ppermute | solution.py:229
  45.9 1.9 collective-permute-start.2
  47.9 0.9 constant_dynamic-slice_fusion.10.matrix_ref
  48.8 8.4 %all-to-all-done.refs_0_ = bf16[128,2,384]{2,1,0:T(2,128)(2,1)S(1)} async-done(((bf16[128,2,384]{2,1,0:T(2,128)(2,1)}), bf16[128,2,384]{2,1,0:T(2,128)(2,1)S(1)}, u32[]{:S(2)}, u32[]{:S(2)}) %all-to-all-start) | async-done | bytes 196640 | tf_op jit(solution)/shard_map/forward_analysis/all_to_all | solution.py:70
  57.2 0.9 forward_analysis.3
  58.2 7.7 %all-to-all-start.1 = ((bf16[128,2,384]{2,1,0:T(2,128)(2,1)}), bf16[128,2,384]{2,1,0:T(2,128)(2,1)S(1)}, u32[]{:S(2)}, u32[]{:S(2)}) async-start(bf16[128,2,384]{2,1,0:T(2,128)(2,1)} %forward_analysis.3), calls=%async_computation.1 | async-start | bytes 393216 | tf_op jit(solution)/shard_map/forward_analysis/all_to_all | solution.py:70
  66.3 19.4 %all-to-all-done.1.values_ref = bf16[128,2,384]{2,1,0:T(2,128)(2,1)S(1)} async-done(((bf16[128,2,384]{2,1,0:T(2,128)(2,1)}), bf16[128,2,384]{2,1,0:T(2,128)(2,1)S(1)}, u32[]{:S(2)}, u32[]{:S(2)}) %all-to-all-start.1) | async-done | bytes 196640 | tf_op jit(solution)/shard_map/forward_analysis/all_to_all | solution.py:70
  85.7 0.7 mix.1
  86.4 25.9 %all_to_all.50.refs_0_ = bf16[128,2,384]{2,1,0:T(2,128)(2,1)S(1)} all-to-all(bf16[128,2,384]{2,1,0:T(2,128)(2,1)S(1)} %mix.1), channel_id=1, replica_groups=mesh['lat'=128,'lon'=4] {'lat'}, dimensions={0} | all-to-all | bytes 393216 | tf_op jit(solution)/shard_map/forward_synthesis/all_to_all | solution.py:70
  112.5 25.8 %all_to_all.51.refs_1_ = bf16[128,2,384]{2,1,0:T(2,128)(2,1)S(1)} all-to-all(bf16[128,2,384]{2,1,0:T(2,128)(2,1)S(1)} %forward_synthesis.2), channel_id=1, replica_groups=mesh['lat'=128,'lon'=4] {'lat'}, dimensions={0} | all-to-all | bytes 393216 | tf_op jit(solution)/shard_map/forward_synthesis/all_to_all | solution.py:70
  138.3 1.3 forward_synthesis.3
  139.7 3.5 %all-to-all-start.4 = ((bf16[4,256,384]{2,1,0:T(8,128)(2,1)}), bf16[4,256,384]{2,1,0:T(8,128)(2,1)S(1)}, u32[]{:S(2)}, u32[]{:S(2)}) async-start(bf16[4,256,384]{2,1,0:T(8,128)(2,1)} %forward_synthesis.3), calls=%async_computation.4 | async-start | bytes 1572864 | tf_op jit(solution)/shard_map/forward_synthesis/all_to_all | solution.py:70
  143.2 12.8 %all-to-all-done.4 = bf16[4,256,384]{2,1,0:T(8,128)(2,1)S(1)} async-done(((bf16[4,256,384]{2,1,0:T(8,128)(2,1)}), bf16[4,256,384]{2,1,0:T(8,128)(2,1)S(1)}, u32[]{:S(2)}, u32[]{:S(2)}) %all-to-all-start.4) | async-done | bytes 786464 | tf_op jit(solution)/shard_map/forward_synthesis/all_to_all | solution.py:70
  156.1 1.0 fusion.9
  157.1 1.2 multiply_convert_fusion
  159.2 14.4 %all-gather = bf16[1024,384]{1,0:T(8,128)(2,1)S(1)} all-gather(bf16[256,384]{1,0:T(8,128)(2,1)S(1)} %fusion.2), channel_id=2, replica_groups=mesh['lat'=128,'lon'=4] {'lon'}, dimensions={0}, use_global_device_ids=true | all-gather | bytes 983040 | tf_op jit(solution)/shard_map/backward_analysis/all_gather | solution.py:260
  173.6 1.1 backward_analysis.2
  174.7 5.9 %all-to-all-start.5 = ((bf16[128,2,384]{2,1,0:T(2,128)(2,1)}), bf16[128,2,384]{2,1,0:T(2,128)(2,1)S(1)}, u32[]{:S(2)}, u32[]{:S(2)}) async-start(bf16[128,2,384]{2,1,0:T(2,128)(2,1)} %backward_analysis.2), calls=%async_computation.5 | async-start | bytes 393216 | tf_op jit(solution)/shard_map/backward_analysis/all_to_all | solution.py:70
  180.6 1.4 fusion.15
  182.0 1.5 reshape.61
  183.6 2.4 broadcast_select_fusion
  185.9 0.9 select_convert_fusion
  186.9 2.0 collective-permute-start.3
  188.9 11.5 %all-to-all-done.5.refs_0_ = bf16[128,2,384]{2,1,0:T(2,128)(2,1)S(1)} async-done(((bf16[128,2,384]{2,1,0:T(2,128)(2,1)}), bf16[128,2,384]{2,1,0:T(2,128)(2,1)S(1)}, u32[]{:S(2)}, u32[]{:S(2)}) %all-to-all-start.5) | async-done | bytes 196640 | tf_op jit(solution)/shard_map/backward_analysis/all_to_all | solution.py:70
  200.5 0.9 backward_analysis.3
  201.4 6.2 %all-to-all-start.6 = ((bf16[128,2,384]{2,1,0:T(2,128)(2,1)}), bf16[128,2,384]{2,1,0:T(2,128)(2,1)S(1)}, u32[]{:S(2)}, u32[]{:S(2)}) async-start(bf16[128,2,384]{2,1,0:T(2,128)(2,1)} %backward_analysis.3), calls=%async_computation.6 | async-start | bytes 393216 | tf_op jit(solution)/shard_map/backward_analysis/all_to_all | solution.py:70
  207.7 2.4 convert_add_fusion
  210.0 1.5 reshape.62
  211.6 1.0 constant_dynamic-slice_fusion.9
  212.6 3.4 %collective-permute-start.6 = (bf16[128,576]{1,0:T(8,128)(2,1)}, bf16[128,576]{1,0:T(8,128)(2,1)S(1)}, u32[]{:S(2)}, u32[]{:S(2)}) collective-permute-start(bf16[128,576]{1,0:T(8,128)(2,1)} %get-tuple-element.37), channel_id=1, source_target_pairs={{0,3},{1,0},{2,1},{3,2},{4,7},{5,4},{6,5},{7,6},{8,11},{9,8},{10,9... | collective-permute-start | bytes 442376 | tf_op jit(solution)/shard_map/pointwise_weights/ppermute | solution.py:165
  216.0 2.8 collective-permute-start.5
  218.8 2.4 collective-permute-start.4
  221.3 6.2 %all-to-all-done.6.values_ref = bf16[128,2,384]{2,1,0:T(2,128)(2,1)S(1)} async-done(((bf16[128,2,384]{2,1,0:T(2,128)(2,1)}), bf16[128,2,384]{2,1,0:T(2,128)(2,1)S(1)}, u32[]{:S(2)}, u32[]{:S(2)}) %all-to-all-start.6) | async-done | bytes 196640 | tf_op jit(solution)/shard_map/backward_analysis/all_to_all | solution.py:70
  227.5 1.4 unmix.1
  228.8 10.0 %all-to-all-start.7 = ((bf16[128,2,384]{2,1,0:T(2,128)(2,1)}), bf16[128,2,384]{2,1,0:T(2,128)(2,1)S(1)}, u32[]{:S(2)}, u32[]{:S(2)}) async-start(bf16[128,2,384]{2,1,0:T(2,128)(2,1)} %unmix.1), calls=%async_computation.7 | async-start | bytes 393216 | tf_op jit(solution)/shard_map/backward_synthesis/all_to_all | solution.py:70
  239.5 1.2 fusion.13
  240.9 4.6 %collective-permute-start.9 = (bf16[128,144]{1,0:T(8,128)(2,1)S(1)}, bf16[128,144]{1,0:T(8,128)(2,1)S(1)}, u32[]{:S(2)}, u32[]{:S(2)}) collective-permute-start(bf16[128,144]{1,0:T(8,128)(2,1)S(1)} %get-tuple-element.42), channel_id=1, source_target_pairs={{0,24},{4,28},{8,0},{12,4},{16,8},{20,12},{24,16},{28,20},{32,56},... | collective-permute-start | bytes 110600 | tf_op jit(solution)/shard_map/pointwise_weights/ppermute | solution.py:165
  245.4 2.8 collective-permute-start.8
  248.2 2.8 collective-permute-start.7
  251.1 2.2 collective-permute-done.8
  253.2 2.4 collective-permute-done.7
  255.8 2.8 all-to-all-done.7.values_ref
  258.6 1.0 backward_synthesis.2
  259.6 11.8 %all-to-all-start.8 = ((bf16[128,2,512]{2,1,0:T(2,128)(2,1)}), bf16[128,2,512]{2,1,0:T(2,128)(2,1)S(1)}, u32[]{:S(2)}, u32[]{:S(2)}) async-start(bf16[128,2,512]{2,1,0:T(2,128)(2,1)} %backward_synthesis.2), calls=%async_computation.8 | async-start | bytes 524288 | tf_op jit(solution)/shard_map/backward_synthesis/all_to_all | solution.py:70
  273.2 0.7 copy.63
  273.9 4.7 %collective-permute-start.12 = (bf16[2,2,96,384]{3,2,1,0:T(8,128)(2,1)}, bf16[2,2,96,384]{3,2,1,0:T(8,128)(2,1)}, u32[]{:S(2)}, u32[]{:S(2)}) collective-permute-start(bf16[2,2,96,384]{3,2,1,0:T(8,128)(2,1)} %bitcast.61), channel_id=1, source_target_pairs={{0,3},{1,0},{2,1},{3,2},{4,7},{5,4},{6,5},{7,6},{8,11},{9,8},{10,9... | collective-permute-start | bytes 884744 | tf_op jit(solution)/shard_map/unmix/ppermute | solution.py:329
  278.7 0.8 copy.64
  279.4 3.4 %collective-permute-start.11 = (bf16[2,2,96,384]{3,2,1,0:T(8,128)(2,1)}, bf16[2,2,96,384]{3,2,1,0:T(8,128)(2,1)}, u32[]{:S(2)}, u32[]{:S(2)}) collective-permute-start(bf16[2,2,96,384]{3,2,1,0:T(8,128)(2,1)} %bitcast.62), channel_id=1, source_target_pairs={{0,2},{1,3},{2,0},{3,1},{4,6},{5,7},{6,4},{7,5},{8,10},{9,11},{10,... | collective-permute-start | bytes 884744 | tf_op jit(solution)/shard_map/unmix/ppermute | solution.py:329
  282.8 0.8 copy.65
  283.5 2.4 collective-permute-start.10
  286.2 7.7 %all-to-all-done.8.refs_2_ = bf16[128,2,512]{2,1,0:T(2,128)(2,1)S(1)} async-done(((bf16[128,2,512]{2,1,0:T(2,128)(2,1)}), bf16[128,2,512]{2,1,0:T(2,128)(2,1)S(1)}, u32[]{:S(2)}, u32[]{:S(2)}) %all-to-all-start.8) | async-done | bytes 262176 | tf_op jit(solution)/shard_map/backward_synthesis/all_to_all | solution.py:70
  293.9 1.4 backward_synthesis.3
  295.3 4.7 %all-to-all-start.9 = ((bf16[4,256,384]{2,1,0:T(8,128)(2,1)}), bf16[4,256,384]{2,1,0:T(8,128)(2,1)S(1)}, u32[]{:S(2)}, u32[]{:S(2)}) async-start(bf16[4,256,384]{2,1,0:T(8,128)(2,1)} %backward_synthesis.3), calls=%async_computation.9 | async-start | bytes 1572864 | tf_op jit(solution)/shard_map/backward_synthesis/all_to_all | solution.py:70
  300.0 1.0 fusion.1
  301.0 2.2 fusion.8
  303.5 0.7 squeeze.24
  304.8 7.8 %all-to-all-done.9 = bf16[4,256,384]{2,1,0:T(8,128)(2,1)S(1)} async-done(((bf16[4,256,384]{2,1,0:T(8,128)(2,1)}), bf16[4,256,384]{2,1,0:T(8,128)(2,1)S(1)}, u32[]{:S(2)}, u32[]{:S(2)}) %all-to-all-start.9) | async-done | bytes 786464 | tf_op jit(solution)/shard_map/backward_synthesis/all_to_all | solution.py:70
  312.7 0.7 add_convert_fusion
  (74 shorter events, 5.7 us)
Async XLA Ops:
  0.6 156.4 %copy-start = (bf16[384,768]{1,0:T(8,128)(2,1)S(1)}, bf16[384,768]{1,0:T(8,128)(2,1)}, u32[]{:S(2)}) copy-start(bf16[384,768]{1,0:T(8,128)(2,1)} %param.14) | copy-start | bytes 1769476
  15.5 1.6 copy-start.5
  17.1 20.3 %copy-start.14 = (bf16[2,2,384,96]{2,3,1,0:T(8,128)(2,1)S(1)}, bf16[2,2,384,96]{2,3,1,0:T(8,128)(2,1)}, u32[]{:S(2)}) copy-start(bf16[2,2,384,96]{2,3,1,0:T(8,128)(2,1)} %param.13) | copy-start | bytes 884740
  18.2 39.0 %all-to-all-start = ((bf16[128,2,384]{2,1,0:T(2,128)(2,1)}), bf16[128,2,384]{2,1,0:T(2,128)(2,1)S(1)}, u32[]{:S(2)}, u32[]{:S(2)}) async-start(bf16[128,2,384]{2,1,0:T(2,128)(2,1)} %forward_analysis.2), calls=%async_computation | async-start | bytes 393216 | tf_op jit(solution)/shard_map/forward_analysis/all_to_all | solution.py:70
  37.4 28.6 %collective-permute-start = (bf16[2,2,1,96,384]{4,3,1,0,2:T(8,128)(2,1)S(1)}, bf16[2,2,1,96,384]{4,3,1,0,2:T(8,128)(2,1)S(1)}, u32[]{:S(2)}, u32[]{:S(2)}) collective-permute-start(bf16[2,2,1,96,384]{4,3,1,0,2:T(8,128)(2,1)S(1)} %bitcast.76), channel_id=1, source_target_pairs={{0,1},{1,2},{2,3},{3,0},{4,5},{5,6},{6,7},{7,4},{8,9},{9,10},{10,1... | collective-permute-start | bytes 884744 | tf_op jit(solution)/shard_map/weights/ppermute | solution.py:229
  41.3 24.8 %collective-permute-start.1 = (bf16[2,2,1,96,384]{4,3,1,0,2:T(8,128)(2,1)S(1)}, bf16[2,2,1,96,384]{4,3,1,0,2:T(8,128)(2,1)S(1)}, u32[]{:S(2)}, u32[]{:S(2)}) collective-permute-start(bf16[2,2,1,96,384]{4,3,1,0,2:T(8,128)(2,1)S(1)} %bitcast.77), channel_id=1, source_target_pairs={{0,2},{1,3},{2,0},{3,1},{4,6},{5,7},{6,4},{7,5},{8,10},{9,11},{10,... | collective-permute-start | bytes 884744 | tf_op jit(solution)/shard_map/weights/ppermute | solution.py:229
  45.9 20.3 %collective-permute-start.2 = (bf16[2,2,1,96,384]{4,3,1,0,2:T(8,128)(2,1)S(1)}, bf16[2,2,1,96,384]{4,3,1,0,2:T(8,128)(2,1)S(1)}, u32[]{:S(2)}, u32[]{:S(2)}) collective-permute-start(bf16[2,2,1,96,384]{4,3,1,0,2:T(8,128)(2,1)S(1)} %bitcast.78), channel_id=1, source_target_pairs={{0,3},{1,0},{2,1},{3,2},{4,7},{5,4},{6,5},{7,6},{8,11},{9,8},{10,9... | collective-permute-start | bytes 884744 | tf_op jit(solution)/shard_map/weights/ppermute | solution.py:229
  58.2 27.5 %all-to-all-start.1 = ((bf16[128,2,384]{2,1,0:T(2,128)(2,1)}), bf16[128,2,384]{2,1,0:T(2,128)(2,1)S(1)}, u32[]{:S(2)}, u32[]{:S(2)}) async-start(bf16[128,2,384]{2,1,0:T(2,128)(2,1)} %forward_analysis.3), calls=%async_computation.1 | async-start | bytes 393216 | tf_op jit(solution)/shard_map/forward_analysis/all_to_all | solution.py:70
  85.7 52.7 %copy-start.3 = (bf16[4,1024,256]{2,1,0:T(8,128)(2,1)S(1)}, bf16[4,1024,256]{2,1,0:T(8,128)(2,1)}, u32[]{:S(2)}) copy-start(bf16[4,1024,256]{2,1,0:T(8,128)(2,1)} %constant.138.clone.refs_0_) | copy-start | bytes 6291460
  139.7 16.3 %all-to-all-start.4 = ((bf16[4,256,384]{2,1,0:T(8,128)(2,1)}), bf16[4,256,384]{2,1,0:T(8,128)(2,1)S(1)}, u32[]{:S(2)}, u32[]{:S(2)}) async-start(bf16[4,256,384]{2,1,0:T(8,128)(2,1)} %forward_synthesis.3), calls=%async_computation.4 | async-start | bytes 1572864 | tf_op jit(solution)/shard_map/forward_synthesis/all_to_all | solution.py:70
  157.1 1.2 copy-start.11
  157.1 1.2 copy-start.12
  158.7 14.8 %copy-start.2 = (bf16[4,256,1024]{2,1,0:T(8,128)(2,1)S(1)}, bf16[4,256,1024]{2,1,0:T(8,128)(2,1)}, u32[]{:S(2)}) copy-start(bf16[4,256,1024]{2,1,0:T(8,128)(2,1)} %constant.140.clone.refs_0_) | copy-start | bytes 6291460
  159.1 15.6 %copy-start.9 = (bf16[256,384]{1,0:T(8,128)(2,1)}, bf16[256,384]{1,0:T(8,128)(2,1)S(1)}, u32[]{:S(2)}) copy-start(bf16[256,384]{1,0:T(8,128)(2,1)S(1)} %fusion.2) | copy-start | bytes 589828
  174.7 25.8 %all-to-all-start.5 = ((bf16[128,2,384]{2,1,0:T(2,128)(2,1)}), bf16[128,2,384]{2,1,0:T(2,128)(2,1)S(1)}, u32[]{:S(2)}, u32[]{:S(2)}) async-start(bf16[128,2,384]{2,1,0:T(2,128)(2,1)} %backward_analysis.2), calls=%async_computation.5 | async-start | bytes 393216 | tf_op jit(solution)/shard_map/backward_analysis/all_to_all | solution.py:70
  182.0 1.5 copy-start.7
  186.9 14.5 %collective-permute-start.3 = (bf16[768,384]{1,0:T(8,128)(2,1)}, bf16[768,384]{1,0:T(8,128)(2,1)S(1)}, u32[]{:S(2)}, u32[]{:S(2)}) collective-permute-start(bf16[768,384]{1,0:T(8,128)(2,1)} %select_convert_fusion), channel_id=1, source_target_pairs={{0,4},{4,0},{8,12},{12,8},{16,20},{20,16},{24,28},{28,24},{32,36},... | collective-permute-start | bytes 1769480 | tf_op jit(solution)/shard_map/pointwise_weights/ppermute | solution.py:273
  201.4 26.1 %all-to-all-start.6 = ((bf16[128,2,384]{2,1,0:T(2,128)(2,1)}), bf16[128,2,384]{2,1,0:T(2,128)(2,1)S(1)}, u32[]{:S(2)}, u32[]{:S(2)}) async-start(bf16[128,2,384]{2,1,0:T(2,128)(2,1)} %backward_analysis.3), calls=%async_computation.6 | async-start | bytes 393216 | tf_op jit(solution)/shard_map/backward_analysis/all_to_all | solution.py:70
  212.6 26.2 %collective-permute-start.6 = (bf16[128,576]{1,0:T(8,128)(2,1)}, bf16[128,576]{1,0:T(8,128)(2,1)S(1)}, u32[]{:S(2)}, u32[]{:S(2)}) collective-permute-start(bf16[128,576]{1,0:T(8,128)(2,1)} %get-tuple-element.37), channel_id=1, source_target_pairs={{0,3},{1,0},{2,1},{3,2},{4,7},{5,4},{6,5},{7,6},{8,11},{9,8},{10,9... | collective-permute-start | bytes 442376 | tf_op jit(solution)/shard_map/pointwise_weights/ppermute | solution.py:165
  216.0 22.8 %collective-permute-start.5 = (bf16[128,576]{1,0:T(8,128)(2,1)}, bf16[128,576]{1,0:T(8,128)(2,1)}, u32[]{:S(2)}, u32[]{:S(2)}) collective-permute-start(bf16[128,576]{1,0:T(8,128)(2,1)} %get-tuple-element.38), channel_id=1, source_target_pairs={{0,2},{1,3},{2,0},{3,1},{4,6},{5,7},{6,4},{7,5},{8,10},{9,11},{10,... | collective-permute-start | bytes 442376 | tf_op jit(solution)/shard_map/pointwise_weights/ppermute | solution.py:165
  218.8 20.7 %collective-permute-start.4 = (bf16[128,576]{1,0:T(8,128)(2,1)}, bf16[128,576]{1,0:T(8,128)(2,1)}, u32[]{:S(2)}, u32[]{:S(2)}) collective-permute-start(bf16[128,576]{1,0:T(8,128)(2,1)} %get-tuple-element.36), channel_id=1, source_target_pairs={{0,1},{1,2},{2,3},{3,0},{4,5},{5,6},{6,7},{7,4},{8,9},{9,10},{10,1... | collective-permute-start | bytes 442376 | tf_op jit(solution)/shard_map/pointwise_weights/ppermute | solution.py:165
  228.8 29.8 %all-to-all-start.7 = ((bf16[128,2,384]{2,1,0:T(2,128)(2,1)}), bf16[128,2,384]{2,1,0:T(2,128)(2,1)S(1)}, u32[]{:S(2)}, u32[]{:S(2)}) async-start(bf16[128,2,384]{2,1,0:T(2,128)(2,1)} %unmix.1), calls=%async_computation.7 | async-start | bytes 393216 | tf_op jit(solution)/shard_map/backward_synthesis/all_to_all | solution.py:70
  238.8 0.7 copy-start.15
  240.9 10.2 %collective-permute-start.9 = (bf16[128,144]{1,0:T(8,128)(2,1)S(1)}, bf16[128,144]{1,0:T(8,128)(2,1)S(1)}, u32[]{:S(2)}, u32[]{:S(2)}) collective-permute-start(bf16[128,144]{1,0:T(8,128)(2,1)S(1)} %get-tuple-element.42), channel_id=1, source_target_pairs={{0,24},{4,28},{8,0},{12,4},{16,8},{20,12},{24,16},{28,20},{32,56},... | collective-permute-start | bytes 110600 | tf_op jit(solution)/shard_map/pointwise_weights/ppermute | solution.py:165
  245.4 7.8 %collective-permute-start.8 = (bf16[128,144]{1,0:T(8,128)(2,1)S(1)}, bf16[128,144]{1,0:T(8,128)(2,1)S(1)}, u32[]{:S(2)}, u32[]{:S(2)}) collective-permute-start(bf16[128,144]{1,0:T(8,128)(2,1)S(1)} %get-tuple-element.43), channel_id=1, source_target_pairs={{0,16},{4,20},{8,24},{12,28},{16,0},{20,4},{24,8},{28,12},{32,48},... | collective-permute-start | bytes 110600 | tf_op jit(solution)/shard_map/pointwise_weights/ppermute | solution.py:165
  248.2 7.4 %collective-permute-start.7 = (bf16[128,144]{1,0:T(8,128)(2,1)S(1)}, bf16[128,144]{1,0:T(8,128)(2,1)S(1)}, u32[]{:S(2)}, u32[]{:S(2)}) collective-permute-start(bf16[128,144]{1,0:T(8,128)(2,1)S(1)} %get-tuple-element.41), channel_id=1, source_target_pairs={{0,8},{4,12},{8,16},{12,20},{16,24},{20,28},{24,0},{28,4},{32,40},... | collective-permute-start | bytes 110600 | tf_op jit(solution)/shard_map/pointwise_weights/ppermute | solution.py:165
  259.6 34.3 %all-to-all-start.8 = ((bf16[128,2,512]{2,1,0:T(2,128)(2,1)}), bf16[128,2,512]{2,1,0:T(2,128)(2,1)S(1)}, u32[]{:S(2)}, u32[]{:S(2)}) async-start(bf16[128,2,512]{2,1,0:T(2,128)(2,1)} %backward_synthesis.2), calls=%async_computation.8 | async-start | bytes 524288 | tf_op jit(solution)/shard_map/backward_synthesis/all_to_all | solution.py:70
  272.9 10.7 %copy-start.6 = (f32[2,2,384,384]{2,3,1,0:T(8,128)}, f32[2,2,384,384]{2,3,1,0:T(8,128)S(1)}, u32[]{:S(2)}) copy-start(f32[2,2,384,384]{2,3,1,0:T(8,128)S(1)} %fusion.10) | copy-start | bytes 7077892
  273.1 20.7 %copy-start.4 = (bf16[4,1024,256]{2,1,0:T(8,128)(2,1)S(1)}, bf16[4,1024,256]{2,1,0:T(8,128)(2,1)}, u32[]{:S(2)}) copy-start(bf16[4,1024,256]{2,1,0:T(8,128)(2,1)} %constant.137.clone.refs_0_) | copy-start | bytes 6291460
  273.9 27.1 %collective-permute-start.12 = (bf16[2,2,96,384]{3,2,1,0:T(8,128)(2,1)}, bf16[2,2,96,384]{3,2,1,0:T(8,128)(2,1)}, u32[]{:S(2)}, u32[]{:S(2)}) collective-permute-start(bf16[2,2,96,384]{3,2,1,0:T(8,128)(2,1)} %bitcast.61), channel_id=1, source_target_pairs={{0,3},{1,0},{2,1},{3,2},{4,7},{5,4},{6,5},{7,6},{8,11},{9,8},{10,9... | collective-permute-start | bytes 884744 | tf_op jit(solution)/shard_map/unmix/ppermute | solution.py:329
  279.4 21.6 %collective-permute-start.11 = (bf16[2,2,96,384]{3,2,1,0:T(8,128)(2,1)}, bf16[2,2,96,384]{3,2,1,0:T(8,128)(2,1)}, u32[]{:S(2)}, u32[]{:S(2)}) collective-permute-start(bf16[2,2,96,384]{3,2,1,0:T(8,128)(2,1)} %bitcast.62), channel_id=1, source_target_pairs={{0,2},{1,3},{2,0},{3,1},{4,6},{5,7},{6,4},{7,5},{8,10},{9,11},{10,... | collective-permute-start | bytes 884744 | tf_op jit(solution)/shard_map/unmix/ppermute | solution.py:329
  283.5 17.5 %collective-permute-start.10 = (bf16[2,2,96,384]{3,2,1,0:T(8,128)(2,1)}, bf16[2,2,96,384]{3,2,1,0:T(8,128)(2,1)S(1)}, u32[]{:S(2)}, u32[]{:S(2)}) collective-permute-start(bf16[2,2,96,384]{3,2,1,0:T(8,128)(2,1)} %bitcast.63), channel_id=1, source_target_pairs={{0,1},{1,2},{2,3},{3,0},{4,5},{5,6},{6,7},{7,4},{8,9},{9,10},{10,1... | collective-permute-start | bytes 884744 | tf_op jit(solution)/shard_map/unmix/ppermute | solution.py:329
  295.3 4.7 %copy-start.8 = (bf16[256,768]{1,0:T(8,128)(2,1)S(1)}, bf16[256,768]{1,0:T(8,128)(2,1)}, u32[]{:S(2)}) copy-start(bf16[256,768]{1,0:T(8,128)(2,1)} %get-tuple-element.22) | copy-start | bytes 1179652
  295.3 4.7 %copy-start.13 = (bf16[768,384]{1,0:T(8,128)(2,1)S(1)}, bf16[768,384]{1,0:T(8,128)(2,1)}, u32[]{:S(2)}) copy-start(bf16[768,384]{1,0:T(8,128)(2,1)} %param.15) | copy-start | bytes 1769476
  295.3 17.3 %all-to-all-start.9 = ((bf16[4,256,384]{2,1,0:T(8,128)(2,1)}), bf16[4,256,384]{2,1,0:T(8,128)(2,1)S(1)}, u32[]{:S(2)}, u32[]{:S(2)}) async-start(bf16[4,256,384]{2,1,0:T(8,128)(2,1)} %backward_synthesis.3), calls=%async_computation.9 | async-start | bytes 1572864 | tf_op jit(solution)/shard_map/backward_synthesis/all_to_all | solution.py:70
  301.0 12.4 %copy-start.1 = (bf16[384,768]{1,0:T(8,128)(2,1)S(1)}, bf16[384,768]{1,0:T(8,128)(2,1)}, u32[]{:S(2)}) copy-start(bf16[384,768]{1,0:T(8,128)(2,1)} %param.14) | copy-start | bytes 1769476
  303.3 9.4 %copy-start.10 = (bf16[256,384]{1,0:T(8,128)(2,1)S(1)}, bf16[256,384]{1,0:T(8,128)(2,1)}, u32[]{:S(2)}) copy-start(bf16[256,384]{1,0:T(8,128)(2,1)} %copy-done.9) | copy-start | bytes 589828

commit v8 on v7

--- a/solution.py
+++ b/solution.py
@@ -70,14 +70,57 @@
     return lax.all_to_all(values, axis, split_axis=0, concat_axis=0, tiled=True)
 
 
-def product_kernel(dims, matrix_ref, *refs):
-    *scale_ref, values_ref, out_ref = refs
+PLAIN = (((1,), (0,)), ((), ()))
+TURNED = (((0,), (0,)), ((), ()))
+MIB = 1024 * 1024
+
+
+def product_kernel(dims, matrix_ref, values_ref, out_ref):
     width = out_ref.shape[-1]
     values = values_ref[...].reshape(-1, width)
     out = lax.dot_general(matrix_ref[0], values, dims, preferred_element_type=jnp.float32)
-    if scale_ref:
-        out = out * scale_ref[0][...]
     out_ref[...] = out.astype(jnp.bfloat16).reshape(out_ref.shape)
+
+
+def fourier_kernel(period, place_ref, matrix_ref, quad_ref, values_ref, out_ref):
+    width = out_ref.shape[-1]
+    values = values_ref[...].reshape(-1, width)
+    out = lax.dot_general(matrix_ref[0], values, PLAIN, preferred_element_type=jnp.float32)
+    row = lax.broadcasted_iota(jnp.int32, out.shape, 0) & (2 * period - 1)
+    first = quad_ref[2 * place_ref[1]]
+    second = quad_ref[2 * place_ref[1] + 1]
+    out = out * jnp.where(row < period, first, second)
+    out_ref[...] = out.astype(jnp.bfloat16).reshape(out_ref.shape)
+
+
+def gradient_kernel(place_ref, act_ref, back_ref, hidden_ref, pre_grad_ref, *refs):
+    own_ref, *sent_refs, in_ref, out_ref, flat_ref = refs
+    count = len(sent_refs) + 1
+    _, lat_count, chunk = own_ref.shape
+    dims = (((0,), (0,)), ((), ()))
+    pairs = ((hidden_ref, pre_grad_ref, in_ref), (act_ref, back_ref, out_ref))
+    for part, (left_ref, right_ref, ref) in enumerate(pairs):
+        total = lax.dot_general(
+            left_ref[...], right_ref[...], dims, preferred_element_type=jnp.float32
+        )
+        size, width = total.shape
+        step = size // lat_count
+        for tile in range(width // 128):
+            ref[tile * size : (tile + 1) * size, :] = total[:, tile * 128 : (tile + 1) * 128]
+        for i in range(step):
+            for tile in range(width // 128):
+                lane = i * width + tile * 128
+                rows = ref[pl.ds(tile * size + i, lat_count, stride=step), :]
+                flat_ref[part, :, lane : lane + 128] = rows
+    for place in range(count):
+
+        @pl.when(place_ref[0] == place)
+        def _():
+            own_ref[...] = flat_ref[:, :, place * chunk : (place + 1) * chunk]
+            for shift, ref in enumerate(sent_refs, 1):
+                to = (place + shift) % count
+                block = flat_ref[:, :, to * chunk : (to + 1) * chunk]
+                ref[...] = block.astype(jnp.bfloat16)
 
 
 def beside_kernel(dims, matrix_ref, values_ref, extra_ref, out_ref):
@@ -119,49 +162,82 @@
     return pl.BlockSpec(shape, lambda *_: (0,) * len(shape))
 
 
-def call_kernel(kernel, place, matrices, operands, blocks, out_shape, flops):
-    specs = [whole(block) for block in blocks]
-    prefetch = ()
-    if place is not None:
-        specs.insert(0, pl.BlockSpec((1,) + matrices.shape[1:], lambda i, at: (at[0], 0, 0)))
-        operands = [matrices] + operands
-        prefetch = (place.reshape(1).astype(jnp.int32),)
-        kernel = functools.partial(placed, kernel)
+def call_kernel(kernel, operands, blocks, out_shape, flops):
     moved = 2 * (math.prod(out_shape) + sum(math.prod(block) for block in blocks))
     return pl.pallas_call(
         kernel,
+        grid=(1,),
+        in_specs=[whole(block) for block in blocks],
+        out_specs=whole(out_shape),
+        out_shape=jax.ShapeDtypeStruct(out_shape, jnp.bfloat16),
+        compiler_params=pltpu.CompilerParams(vmem_limit_bytes=20 * MIB),
+        cost_estimate=pl.CostEstimate(flops=flops, bytes_accessed=moved, transcendentals=0),
+    )(*operands)
+
+
+def fourier_product(period, place, matrices, quad, values, block, out_shape, grant):
+    kernel = functools.partial(fourier_kernel, period)
+    specs = [
+        pl.BlockSpec((1,) + matrices.shape[1:], lambda i, at: (at[0], 0, 0)),
+        pl.BlockSpec(memory_space=pltpu.SMEM),
+        whole(block),
+    ]
+    operands = (matrices, quad, values)
+    if quad is None:
+        kernel = functools.partial(placed, functools.partial(product_kernel, PLAIN))
+        specs.pop(1)
+        operands = (matrices, values)
+    moved = 2 * (math.prod(out_shape) + math.prod(block) + math.prod(matrices.shape[1:]))
+    return pl.pallas_call(
+        kernel,
         grid_spec=pltpu.PrefetchScalarGridSpec(
-            num_scalar_prefetch=len(prefetch),
-            grid=(1,),
-            in_specs=specs,
-            out_specs=whole(out_shape),
+            num_scalar_prefetch=1, grid=(1,), in_specs=specs, out_specs=whole(out_shape)
         ),
         out_shape=jax.ShapeDtypeStruct(out_shape, jnp.bfloat16),
-        compiler_params=pltpu.CompilerParams(vmem_limit_bytes=20 * 1024 * 1024),
-        cost_estimate=pl.CostEstimate(flops=flops, bytes_accessed=moved, transcendentals=0),
-    )(*prefetch, *operands)
-
-
-PLAIN = (((1,), (0,)), ((), ()))
-TURNED = (((0,), (0,)), ((), ()))
-
-
-def place_product(dims, place, matrices, scale, values, block, out_shape):
-    operands, blocks = [values], [block]
-    if scale is not None:
-        operands, blocks = [scale, values], [scale.shape, block]
-    flops = 2 * math.prod(matrices.shape[1:]) * out_shape[-1]
-    kernel = functools.partial(product_kernel, dims)
-    return call_kernel(kernel, place, matrices, operands, blocks, out_shape, flops)
+        compiler_params=pltpu.CompilerParams(vmem_limit_bytes=grant * MIB),
+        cost_estimate=pl.CostEstimate(
+            flops=2 * math.prod(matrices.shape[1:]) * out_shape[-1],
+            bytes_accessed=moved,
+            transcendentals=0,
+        ),
+    )(place, *operands)
+
+
+def gradient_blocks(lon_index, lon_count, lat_count, act, back, hidden, pre_grad):
+    in_shape = (hidden.shape[1], pre_grad.shape[1])
+    size = math.prod(in_shape)
+    blocks = (2, lat_count, size // (lat_count * lon_count))
+    dtypes = [jnp.float32] + [jnp.bfloat16] * (lon_count - 1)
+    operands = (act, back, hidden, pre_grad)
+    return pl.pallas_call(
+        gradient_kernel,
+        grid_spec=pltpu.PrefetchScalarGridSpec(
+            num_scalar_prefetch=1,
+            grid=(1,),
+            in_specs=[whole(operand.shape) for operand in operands],
+            out_specs=[whole(blocks)] * lon_count,
+            scratch_shapes=[
+                pltpu.VMEM((size // 128, 128), jnp.float32),
+                pltpu.VMEM((size // 128, 128), jnp.float32),
+                pltpu.VMEM((2, lat_count, size // lat_count), jnp.float32),
+            ],
+        ),
+        out_shape=[jax.ShapeDtypeStruct(blocks, dtype) for dtype in dtypes],
+        compiler_params=pltpu.CompilerParams(vmem_limit_bytes=24 * MIB),
+        cost_estimate=pl.CostEstimate(
+            flops=4 * size * act.shape[0], bytes_accessed=8 * size, transcendentals=0
+        ),
+    )(lon_index.reshape(1).astype(jnp.int32), *operands)
 
 
 def scatter_sum(values, axis, index, count, shifted):
-    chunk = values.shape[-1] // count
+    last = values.ndim - 1
+    chunk = values.shape[last] // count
     narrow = values.astype(jnp.bfloat16)
-    parts = [lax.dynamic_slice_in_dim(values, index * chunk, chunk, axis=1)]
+    parts = [lax.dynamic_slice_in_dim(values, index * chunk, chunk, axis=last)]
     for shift in range(1, count):
         to = (index + shift) % count
-        block = lax.dynamic_slice_in_dim(narrow, to * chunk, chunk, axis=1)
+        block = lax.dynamic_slice_in_dim(narrow, to * chunk, chunk, axis=last)
         parts.append(lax.ppermute(block, axis, shifted(shift)))
     return parts
 
@@ -183,31 +259,29 @@
     quarter = width // lon_count
     half = lat_count // 2
     order = lon_index * half + lat_index % half
-    local_quad = lax.dynamic_slice_in_dim(quad, lat_index * rows, rows)
-    order_quad = jnp.tile(local_quad, lat_count)[:, None]
-    row_quad = jnp.tile(jnp.repeat(local_quad, lon_rows), lon_count)[:, None]
+    place = jnp.stack([lon_index, lat_index]).astype(jnp.int32)
     total_lat = rows * lat_count
     spread = (lat_count, rows, width)
     gathered_shape = (lon_count, rows * lon_rows, width)
 
-    def to_orders(values, matrices, scale):
-        return place_product(PLAIN, lon_index, matrices, scale, values, gathered_shape, spread)
+    def to_orders(values, matrices, scale, grant):
+        return fourier_product(1, place, matrices, scale, values, gathered_shape, spread, grant)
 
     def from_orders(values, matrices, scale):
-        out = place_product(PLAIN, lon_index, matrices, scale, values, spread, gathered_shape)
+        out = fourier_product(
+            lon_rows, place, matrices, scale, values, spread, gathered_shape, 20
+        )
         return jnp.sum(swap_blocks(out, "lon").astype(jnp.float32), axis=0)
 
     def legendre(dims, values):
         kernel = functools.partial(product_kernel, dims)
         flops = 2 * total_lat * total_lat * width
         blocks = [table.shape, spread]
-        return call_kernel(kernel, None, None, [table, values], blocks, spread, flops)
+        return call_kernel(kernel, [table, values], blocks, spread, flops)
 
     def complex_product(values, conjugate):
         return call_kernel(
             functools.partial(mix_kernel, conjugate),
-            None,
-            None,
             [weights, values],
             [weights.shape, spread],
             spread,
@@ -220,7 +294,7 @@
         table = lax.dynamic_slice_in_dim(tables, order, 1)
         own_weight = spectral_weight
         own_weight = own_weight.transpose(0, 1, 3, 2)[:, :, None]
-        four = swap_blocks(to_orders(gathered, plain_t, order_quad), "lat")
+        four = swap_blocks(to_orders(gathered, plain_t, quad, 60), "lat")
     with jax.named_scope("weights"):
         weights = jnp.zeros((2, rows, lon_count, quarter, width), jnp.bfloat16)
         weights = lax.dynamic_update_slice_in_dim(weights, own_weight, lon_index, 2)
@@ -261,33 +335,15 @@
         gathered, hidden, pre_grad, act = lax.optimization_barrier(
             (gathered, hidden, pre_grad, act)
         )
-        field_grad = swap_blocks(to_orders(gathered, doubled_t, None), "lat")
+        field_grad = swap_blocks(to_orders(gathered, doubled_t, None, 20), "lat")
     with jax.named_scope("pointwise_weights"):
-        over_rows = (((0,), (0,)), ((), ()))
-        out_part = lax.dot_general(act, back, over_rows, preferred_element_type=jnp.float32)
-        in_part = lax.dot_general(hidden, pre_grad, over_rows, preferred_element_type=jnp.float32)
-        in_part = in_part.reshape(out_part.shape)
-        even = lat_index % 2 == 0
-        keep = jnp.where(even, in_part, out_part)
-        give = jnp.where(even, out_part, in_part).astype(jnp.bfloat16)
-        got = lax.ppermute(give, "lat", [(i, i ^ 1) for i in range(lat_count)])
+        parts = [*gradient_blocks(lon_index, lon_count, lat_count, act, back, hidden, pre_grad)]
+        for shift in range(1, lon_count):
+            pairs = [(i, (i + shift) % lon_count) for i in range(lon_count)]
+            parts[shift] = lax.ppermute(parts[shift], "lon", pairs)
     with jax.named_scope("backward_analysis"):
         mixed_grad = legendre(PLAIN, field_grad)
-        mixed_grad, keep, got = lax.optimization_barrier((mixed_grad, keep, got))
         mixed_grad = swap_blocks(mixed_grad, "lat")
-    with jax.named_scope("pointwise_weights"):
-        sums = add_parts([keep, got]).reshape(lat_count, -1)
-        parts = scatter_sum(
-            sums,
-            "lon",
-            lon_index,
-            lon_count,
-            lambda s: [(i, (i + s) % lon_count) for i in range(lon_count)],
-        )
-    with jax.named_scope("unmix"):
-        spectrum_grad = complex_product(mixed_grad, True)
-    with jax.named_scope("backward_synthesis"):
-        spectrum_grad = swap_blocks(spectrum_grad, "lat")
     with jax.named_scope("pointwise_weights"):
         parts = scatter_sum(
             add_parts(parts),
@@ -296,6 +352,17 @@
             4,
             lambda s: [(i, (i & ~6) | ((i + 2 * s) & 6)) for i in range(lat_count)],
         )
+    with jax.named_scope("unmix"):
+        spectrum_grad = complex_product(mixed_grad, True)
+        spectrum_grad, *parts = lax.optimization_barrier((spectrum_grad, *parts))
+    with jax.named_scope("backward_synthesis"):
+        spectrum_grad = swap_blocks(spectrum_grad, "lat")
+    with jax.named_scope("pointwise_weights"):
+        sums = add_parts(parts)
+        even = lat_index % 2 == 0
+        give = jnp.where(even, sums[1], sums[0]).astype(jnp.bfloat16)
+        got = lax.ppermute(give, "lat", [(i, i ^ 1) for i in range(lat_count)])
+        parts = [jnp.where(even, sums[0], sums[1]), got]
     with jax.named_scope("backward_synthesis"):
         extra = add_parts(parts).astype(jnp.bfloat16)
         chunk = extra.shape[1]
@@ -304,8 +371,6 @@
         extra = extra.reshape(lat_count, rows, room // rows)
         four_grad = call_kernel(
             functools.partial(beside_kernel, TURNED),
-            None,
-            None,
             [table, spectrum_grad, extra],
             [table.shape, spread, extra.shape],
             (lat_count, rows, width + extra.shape[2]),
@@ -313,7 +378,7 @@
         )
         four_grad, left, right = lax.optimization_barrier((four_grad, spectrum, mixed_grad))
         four_grad = swap_blocks(four_grad, "lat")
-        wave_grad = from_orders(four_grad, plain, row_quad)
+        wave_grad = from_orders(four_grad, plain, quad)
         grad_input = (hidden_grad.astype(jnp.float32) + wave_grad).astype(jnp.bfloat16)
     with jax.named_scope("unmix"):
         right = jnp.stack([right, jnp.concatenate([right[half:], -right[:half]])])

time: 315 us -> 316 us (level)
  blocking collectives: 80.1 us -> 99 us
  waiting for transfers between devices: 81.2 us -> 73.3 us
  starting transfers between devices: 111 us -> 105 us
  Pallas kernels: 10.1 us -> 15.3 us
  matrix products: 7.33 us -> 2.78 us
  other arithmetic: 10 us -> 6.6 us
    all_to_all x2 -> x3, blocking collectives: 51.7 us -> 67.1 us  [swap_blocks(): return lax.all_to_all(values, axis, split_axis=0, concat_axis=0, tiled=True)]
    ppermute x0 -> x3, starting transfers between devices: none -> 9.82 us  [body(): parts[shift] = lax.ppermute(parts[shift], 'lon', pairs)]
    ppermute x6 -> x3, starting transfers between devices: 18.7 us -> 10.1 us  [scatter_sum(): parts.append(lax.ppermute(block, axis, shifted(shift)))]
    all_to_all x8 -> x7, starting transfers between devices: 68.9 us -> 63.2 us  [swap_blocks(): return lax.all_to_all(values, axis, split_axis=0, concat_axis=0, tiled=True)]
    pallas_call x10 -> x11, Pallas kernels: 10.1 us -> 15.3 us  [the longest x4 8.28 us: fourier_product(): pl.pallas_call(kernel, grid_spec=pltpu.PrefetchScalarGridSpec(num_scalar_...]
    ppermute x6 -> x3, waiting for transfers between devices: 4.6 us -> 0.01 us  [scatter_sum(): parts.append(lax.ppermute(block, axis, shifted(shift)))]
    all_to_all x8 -> x7, waiting for transfers between devices: 76.5 us -> 72.2 us  [swap_blocks(): return lax.all_to_all(values, axis, split_axis=0, concat_axis=0, tiled=True)]
    dot_general x2 -> x0, matrix products: 3.79 us -> none  [the longest x1 2.38 us: body(): lax.dot_general(act, back, over_rows, preferred_element_type=jnp.float32)]
  transfers between devices with their start and end apart: 21 -> 20, of which waited for: 10 -> 8; matrix products, arithmetic and copies ran while one was open for 7% -> 5% of each run, Pallas kernels for 1% -> 2%
where the time goes in v8:
time: 316 us; the launch traced here: 315 us
  starting transfers between devices  105 us (33%)
  blocking collectives  99 us (31%)
  waiting for transfers between devices  73.3 us (23%)
  Pallas kernels  15.3 us (5%)
  local copies, waits for them, and re-layouts  11 us (3%)
  other arithmetic  6.6 us (2%)
    all_to_all x7, waiting for transfers between devices, swap_blocks(): return lax.all_to_all(values, axis, split_axis=0, concat_axis=0, tiled=True)  72.2 us
    all_to_all x3, blocking collectives, swap_blocks(): return lax.all_to_all(values, axis, split_axis=0, concat_axis=0, tiled=True)  67.1 us
    all_to_all x7, starting transfers between devices, swap_blocks(): return lax.all_to_all(values, axis, split_axis=0, concat_axis=0, tiled=True)  63.2 us
    all_gather x1, blocking collectives, body(): gathered = lax.all_gather(grid.reshape(-1, width), 'lon', axis=0)  17.3 us
    all_gather x1, blocking collectives, body(): gathered = lax.all_gather(hidden_grad, 'lon', axis=0)  14.7 us
    ppermute x3, starting transfers between devices, body(): moved = lax.ppermute(own_weight, 'lon', pairs)  10.4 us
    ppermute x3, starting transfers between devices, scatter_sum(): parts.append(lax.ppermute(block, axis, shifted(shift)))  10.1 us
    ppermute x3, starting transfers between devices, body(): parts[shift] = lax.ppermute(parts[shift], 'lon', pairs)  9.82 us
  transfers between devices with their start and end apart: 20, of which 8 were waited for; matrix products, arithmetic and copies ran while one was open for 5% of the time, Pallas kernels for 2%

profile of v8, /device:TPU:32, one launch (start us, length us, event | category | flops | bytes accessed | tf_op | source)
XLA Modules:
  0.0 314.7 jit_solution(850006593816648601)
XLA Ops:
  0.7 17.3 %all_gather.9.values_ref = bf16[4,256,384]{2,1,0:T(8,128)(2,1)} all-gather(bf16[1,256,384]{2,1,0:T(8,128)(2,1)} %bitcast.70), channel_id=1, replica_groups=mesh['lat'=128,'lon'=4] {'lon'}, dimensions={0}, use_global_device_ids=true | all-gather | bytes 983040 | tf_op jit(solution)/shard_map/forward_analysis/all_gather | solution.py:292
  18.0 0.6 pad_add_fusion.place_ref
  18.5 3.2 %forward_analysis.2 = bf16[128,2,384]{2,1,0:T(2,128)(2,1)} custom-call(s32[2]{0:T(128)} %pad_add_fusion.place_ref, bf16[4,256,1024]{2,1,0:T(8,128)(2,1)} %constant.131.clone.matrix_ref, f32[256]{0:T(256)} %constant.133.clone.quad_ref, bf16[4,256,384]{2,1,0:T(8,128)(2,1)} %all_gather.9.values_ref), custom_call_target="tpu_custom_call" | custom-call | flops 201326592 | bytes 1507328 | tf_op jit(solution)/shard_map/forward_analysis/pallas_call | solution.py:191
  21.8 19.2 %all-to-all-start = ((bf16[128,2,384]{2,1,0:T(2,128)(2,1)}), bf16[128,2,384]{2,1,0:T(2,128)(2,1)S(1)}, u32[]{:S(2)}, u32[]{:S(2)}) async-start(bf16[128,2,384]{2,1,0:T(2,128)(2,1)} %forward_analysis.2), calls=%async_computation | async-start | bytes 393216 | tf_op jit(solution)/shard_map/forward_analysis/all_to_all | solution.py:70
  40.9 3.4 %collective-permute-start.1 = (bf16[2,2,1,96,384]{4,3,1,0,2:T(8,128)(2,1)S(1)}, bf16[2,2,1,96,384]{4,3,1,0,2:T(8,128)(2,1)S(1)}, u32[]{:S(2)}, u32[]{:S(2)}) collective-permute-start(bf16[2,2,1,96,384]{4,3,1,0,2:T(8,128)(2,1)S(1)} %bitcast.71), channel_id=1, source_target_pairs={{0,2},{1,3},{2,0},{3,1},{4,6},{5,7},{6,4},{7,5},{8,10},{9,11},{10,... | collective-permute-start | bytes 884744 | tf_op jit(solution)/shard_map/weights/ppermute | solution.py:303
  44.3 1.9 collective-permute-start
  46.3 5.1 %collective-permute-start.2 = (bf16[2,2,1,96,384]{4,3,1,0,2:T(8,128)(2,1)S(1)}, bf16[2,2,1,96,384]{4,3,1,0,2:T(8,128)(2,1)}, u32[]{:S(2)}, u32[]{:S(2)}) collective-permute-start(bf16[2,2,1,96,384]{4,3,1,0,2:T(8,128)(2,1)S(1)} %bitcast.73), channel_id=1, source_target_pairs={{0,3},{1,0},{2,1},{3,2},{4,7},{5,4},{6,5},{7,6},{8,11},{9,8},{10,9... | collective-permute-start | bytes 884744 | tf_op jit(solution)/shard_map/weights/ppermute | solution.py:303
  51.4 0.9 constant_dynamic-slice_fusion.8.matrix_ref
  52.3 8.4 %all-to-all-done.values_ref = bf16[128,2,384]{2,1,0:T(2,128)(2,1)S(1)} async-done(((bf16[128,2,384]{2,1,0:T(2,128)(2,1)}), bf16[128,2,384]{2,1,0:T(2,128)(2,1)S(1)}, u32[]{:S(2)}, u32[]{:S(2)}) %all-to-all-start) | async-done | bytes 196640 | tf_op jit(solution)/shard_map/forward_analysis/all_to_all | solution.py:70
  60.8 0.9 forward_analysis.3
  61.7 7.7 %all-to-all-start.1 = ((bf16[128,2,384]{2,1,0:T(2,128)(2,1)}), bf16[128,2,384]{2,1,0:T(2,128)(2,1)S(1)}, u32[]{:S(2)}, u32[]{:S(2)}) async-start(bf16[128,2,384]{2,1,0:T(2,128)(2,1)} %forward_analysis.3), calls=%async_computation.1 | async-start | bytes 393216 | tf_op jit(solution)/shard_map/forward_analysis/all_to_all | solution.py:70
  69.6 1.0 bitcast_dynamic-update-slice_fusion.3
  70.7 1.0 bitcast_dynamic-update-slice_fusion.1
  71.7 17.5 %all-to-all-done.1.values_ref = bf16[128,2,384]{2,1,0:T(2,128)(2,1)S(1)} async-done(((bf16[128,2,384]{2,1,0:T(2,128)(2,1)}), bf16[128,2,384]{2,1,0:T(2,128)(2,1)S(1)}, u32[]{:S(2)}, u32[]{:S(2)}) %all-to-all-start.1) | async-done | bytes 196640 | tf_op jit(solution)/shard_map/forward_analysis/all_to_all | solution.py:70
  89.2 0.7 mix.1
  89.9 25.9 %all_to_all.50.values_ref = bf16[128,2,384]{2,1,0:T(2,128)(2,1)S(1)} all-to-all(bf16[128,2,384]{2,1,0:T(2,128)(2,1)S(1)} %mix.1), channel_id=1, replica_groups=mesh['lat'=128,'lon'=4] {'lat'}, dimensions={0} | all-to-all | bytes 393216 | tf_op jit(solution)/shard_map/forward_synthesis/all_to_all | solution.py:70
  116.1 25.8 %all_to_all.51.refs_1_ = bf16[128,2,384]{2,1,0:T(2,128)(2,1)S(1)} all-to-all(bf16[128,2,384]{2,1,0:T(2,128)(2,1)S(1)} %forward_synthesis.2), channel_id=1, replica_groups=mesh['lat'=128,'lon'=4] {'lat'}, dimensions={0} | all-to-all | bytes 393216 | tf_op jit(solution)/shard_map/forward_synthesis/all_to_all | solution.py:70
  141.9 1.0 forward_synthesis.3
  142.9 15.4 %all_to_all.52 = bf16[4,256,384]{2,1,0:T(8,128)(2,1)S(1)} all-to-all(bf16[4,256,384]{2,1,0:T(8,128)(2,1)S(1)} %forward_synthesis.3), channel_id=1, replica_groups=mesh['lat'=128,'lon'=4] {'lon'}, dimensions={0} | all-to-all | bytes 1572864 | tf_op jit(solution)/shard_map/forward_synthesis/all_to_all | solution.py:70
  158.5 0.4 multiply_convert_fusion
  158.9 0.5 copy-done.6
  159.7 0.5 fusion.pre_grad_ref
  160.5 14.7 %all-gather = bf16[1024,384]{1,0:T(8,128)(2,1)S(1)} all-gather(bf16[256,384]{1,0:T(8,128)(2,1)S(1)} %fusion.2), channel_id=2, replica_groups=mesh['lat'=128,'lon'=4] {'lon'}, dimensions={0}, use_global_device_ids=true | all-gather | bytes 983040 | tf_op jit(solution)/shard_map/backward_analysis/all_gather | solution.py:334
  175.2 1.7 backward_analysis.2
  176.9 6.0 %all-to-all-start.5 = ((bf16[128,2,384]{2,1,0:T(2,128)(2,1)}), bf16[128,2,384]{2,1,0:T(2,128)(2,1)S(1)}, u32[]{:S(2)}, u32[]{:S(2)}) async-start(bf16[128,2,384]{2,1,0:T(2,128)(2,1)} %backward_analysis.2), calls=%async_computation.5 | async-start | bytes 393216 | tf_op jit(solution)/shard_map/backward_analysis/all_to_all | solution.py:70
  182.8 1.9 pointwise_weights.1
  184.7 0.9 copy-done.7
  185.6 1.9 collective-permute-start.3
  187.5 4.3 %collective-permute-start.4 = (bf16[2,128,576]{2,1,0:T(8,128)(2,1)}, bf16[2,128,576]{2,1,0:T(8,128)(2,1)}, u32[]{:S(2)}, u32[]{:S(2)}) collective-permute-start(bf16[2,128,576]{2,1,0:T(8,128)(2,1)} %get-tuple-element.31), channel_id=1, source_target_pairs={{0,2},{1,3},{2,0},{3,1},{4,6},{5,7},{6,4},{7,5},{8,10},{9,11},{10,... | collective-permute-start | bytes 884744 | tf_op jit(solution)/shard_map/pointwise_weights/ppermute | solution.py:343
  191.8 3.7 %collective-permute-start.5 = (bf16[2,128,576]{2,1,0:T(8,128)(2,1)}, bf16[2,128,576]{2,1,0:T(8,128)(2,1)}, u32[]{:S(2)}, u32[]{:S(2)}) collective-permute-start(bf16[2,128,576]{2,1,0:T(8,128)(2,1)} %get-tuple-element.32), channel_id=1, source_target_pairs={{0,3},{1,0},{2,1},{3,2},{4,7},{5,4},{6,5},{7,6},{8,11},{9,8},{10,9... | collective-permute-start | bytes 884744 | tf_op jit(solution)/shard_map/pointwise_weights/ppermute | solution.py:343
  195.4 7.2 %all-to-all-done.5.values_ref = bf16[128,2,384]{2,1,0:T(2,128)(2,1)S(1)} async-done(((bf16[128,2,384]{2,1,0:T(2,128)(2,1)}), bf16[128,2,384]{2,1,0:T(2,128)(2,1)S(1)}, u32[]{:S(2)}, u32[]{:S(2)}) %all-to-all-start.5) | async-done | bytes 196640 | tf_op jit(solution)/shard_map/backward_analysis/all_to_all | solution.py:70
  202.7 0.9 backward_analysis.3
  203.6 8.9 %all-to-all-start.6 = ((bf16[128,2,384]{2,1,0:T(2,128)(2,1)}), bf16[128,2,384]{2,1,0:T(2,128)(2,1)S(1)}, u32[]{:S(2)}, u32[]{:S(2)}) async-start(bf16[128,2,384]{2,1,0:T(2,128)(2,1)} %backward_analysis.3), calls=%async_computation.6 | async-start | bytes 393216 | tf_op jit(solution)/shard_map/backward_analysis/all_to_all | solution.py:70
  212.5 1.4 fusion.15
  214.0 0.9 constant_dynamic-slice_fusion.4
  214.9 4.6 %collective-permute-start.8 = (bf16[2,128,144]{2,1,0:T(8,128)(2,1)}, bf16[2,128,144]{2,1,0:T(8,128)(2,1)S(1)}, u32[]{:S(2)}, u32[]{:S(2)}) collective-permute-start(bf16[2,128,144]{2,1,0:T(8,128)(2,1)} %get-tuple-element.48), channel_id=1, source_target_pairs={{0,24},{4,28},{8,0},{12,4},{16,8},{20,12},{24,16},{28,20},{32,56},... | collective-permute-start | bytes 221192 | tf_op jit(solution)/shard_map/pointwise_weights/ppermute | solution.py:241
  219.5 2.8 collective-permute-start.7
  222.2 2.8 collective-permute-start.6
  225.1 7.1 %all-to-all-done.6.values_ref = bf16[128,2,384]{2,1,0:T(2,128)(2,1)S(1)} async-done(((bf16[128,2,384]{2,1,0:T(2,128)(2,1)}), bf16[128,2,384]{2,1,0:T(2,128)(2,1)S(1)}, u32[]{:S(2)}, u32[]{:S(2)}) %all-to-all-start.6) | async-done | bytes 196640 | tf_op jit(solution)/shard_map/backward_analysis/all_to_all | solution.py:70
  232.3 1.4 unmix.1
  233.7 11.6 %all-to-all-start.7 = ((bf16[128,2,384]{2,1,0:T(2,128)(2,1)}), bf16[128,2,384]{2,1,0:T(2,128)(2,1)S(1)}, u32[]{:S(2)}, u32[]{:S(2)}) async-start(bf16[128,2,384]{2,1,0:T(2,128)(2,1)} %unmix.1), calls=%async_computation.7 | async-start | bytes 393216 | tf_op jit(solution)/shard_map/backward_synthesis/all_to_all | solution.py:70
  245.4 2.1 collective-permute-start.9
  247.4 1.1 collective-permute-done.9
  248.6 16.5 %all-to-all-done.7.values_ref = bf16[128,2,384]{2,1,0:T(2,128)(2,1)S(1)} async-done(((bf16[128,2,384]{2,1,0:T(2,128)(2,1)}), bf16[128,2,384]{2,1,0:T(2,128)(2,1)S(1)}, u32[]{:S(2)}, u32[]{:S(2)}) %all-to-all-start.7) | async-done | bytes 196640 | tf_op jit(solution)/shard_map/backward_synthesis/all_to_all | solution.py:70
  265.1 1.0 backward_synthesis.2
  266.1 6.3 %all-to-all-start.8 = ((bf16[128,2,512]{2,1,0:T(2,128)(2,1)}), bf16[128,2,512]{2,1,0:T(2,128)(2,1)S(1)}, u32[]{:S(2)}, u32[]{:S(2)}) async-start(bf16[128,2,512]{2,1,0:T(2,128)(2,1)} %backward_synthesis.2), calls=%async_computation.8 | async-start | bytes 524288 | tf_op jit(solution)/shard_map/backward_synthesis/all_to_all | solution.py:70
  272.8 0.6 pad_maximum_fusion
  273.3 0.5 fusion.10
  274.0 1.3 copy-done.10
  275.4 0.7 copy.49
  276.1 0.7 copy.47
  276.9 0.8 copy.48
  277.6 4.0 %collective-permute-start.11 = (bf16[2,2,96,384]{3,2,1,0:T(8,128)(2,1)}, bf16[2,2,96,384]{3,2,1,0:T(8,128)(2,1)}, u32[]{:S(2)}, u32[]{:S(2)}) collective-permute-start(bf16[2,2,96,384]{3,2,1,0:T(8,128)(2,1)} %bitcast.58), channel_id=1, source_target_pairs={{0,2},{1,3},{2,0},{3,1},{4,6},{5,7},{6,4},{7,5},{8,10},{9,11},{10,... | collective-permute-start | bytes 884744 | tf_op jit(solution)/shard_map/unmix/ppermute | solution.py:394
  281.6 2.8 collective-permute-start.12
  284.4 3.1 collective-permute-start.10
  287.4 7.4 %all-to-all-done.8.values_ref = bf16[128,2,512]{2,1,0:T(2,128)(2,1)S(1)} async-done(((bf16[128,2,512]{2,1,0:T(2,128)(2,1)}), bf16[128,2,512]{2,1,0:T(2,128)(2,1)S(1)}, u32[]{:S(2)}, u32[]{:S(2)}) %all-to-all-start.8) | async-done | bytes 262176 | tf_op jit(solution)/shard_map/backward_synthesis/all_to_all | solution.py:70
  294.9 2.4 backward_synthesis.3
  297.3 3.6 %all-to-all-start.9 = ((bf16[4,256,384]{2,1,0:T(8,128)(2,1)}), bf16[4,256,384]{2,1,0:T(8,128)(2,1)S(1)}, u32[]{:S(2)}, u32[]{:S(2)}) async-start(bf16[4,256,384]{2,1,0:T(8,128)(2,1)} %backward_synthesis.3), calls=%async_computation.9 | async-start | bytes 1572864 | tf_op jit(solution)/shard_map/backward_synthesis/all_to_all | solution.py:70
  300.9 1.0 fusion.1
  302.0 2.3 fusion.8
  304.5 0.7 squeeze.29
  305.2 0.7 squeeze.28
  305.9 8.0 %all-to-all-done.9 = bf16[4,256,384]{2,1,0:T(8,128)(2,1)S(1)} async-done(((bf16[4,256,384]{2,1,0:T(8,128)(2,1)}), bf16[4,256,384]{2,1,0:T(8,128)(2,1)S(1)}, u32[]{:S(2)}, u32[]{:S(2)}) %all-to-all-start.9) | async-done | bytes 786464 | tf_op jit(solution)/shard_map/backward_synthesis/all_to_all | solution.py:70
  313.9 0.7 add_convert_fusion
  (66 shorter events, 2.6 us)
Async XLA Ops:
  0.6 157.8 %copy-start = (bf16[384,768]{1,0:T(8,128)(2,1)S(1)}, bf16[384,768]{1,0:T(8,128)(2,1)}, u32[]{:S(2)}) copy-start(bf16[384,768]{1,0:T(8,128)(2,1)} %param.14) | copy-start | bytes 1769476
  18.5 22.4 %copy-start.16 = (bf16[2,2,384,96]{2,3,1,0:T(8,128)(2,1)S(1)}, bf16[2,2,384,96]{2,3,1,0:T(8,128)(2,1)}, u32[]{:S(2)}) copy-start(bf16[2,2,384,96]{2,3,1,0:T(8,128)(2,1)} %param.13) | copy-start | bytes 884740
  21.8 39.0 %all-to-all-start = ((bf16[128,2,384]{2,1,0:T(2,128)(2,1)}), bf16[128,2,384]{2,1,0:T(2,128)(2,1)S(1)}, u32[]{:S(2)}, u32[]{:S(2)}) async-start(bf16[128,2,384]{2,1,0:T(2,128)(2,1)} %forward_analysis.2), calls=%async_computation | async-start | bytes 393216 | tf_op jit(solution)/shard_map/forward_analysis/all_to_all | solution.py:70
  40.9 29.7 %collective-permute-start.1 = (bf16[2,2,1,96,384]{4,3,1,0,2:T(8,128)(2,1)S(1)}, bf16[2,2,1,96,384]{4,3,1,0,2:T(8,128)(2,1)S(1)}, u32[]{:S(2)}, u32[]{:S(2)}) collective-permute-start(bf16[2,2,1,96,384]{4,3,1,0,2:T(8,128)(2,1)S(1)} %bitcast.71), channel_id=1, source_target_pairs={{0,2},{1,3},{2,0},{3,1},{4,6},{5,7},{6,4},{7,5},{8,10},{9,11},{10,... | collective-permute-start | bytes 884744 | tf_op jit(solution)/shard_map/weights/ppermute | solution.py:303
  44.3 25.3 %collective-permute-start = (bf16[2,2,1,96,384]{4,3,1,0,2:T(8,128)(2,1)S(1)}, bf16[2,2,1,96,384]{4,3,1,0,2:T(8,128)(2,1)}, u32[]{:S(2)}, u32[]{:S(2)}) collective-permute-start(bf16[2,2,1,96,384]{4,3,1,0,2:T(8,128)(2,1)S(1)} %bitcast.72), channel_id=1, source_target_pairs={{0,1},{1,2},{2,3},{3,0},{4,5},{5,6},{6,7},{7,4},{8,9},{9,10},{10,1... | collective-permute-start | bytes 884744 | tf_op jit(solution)/shard_map/weights/ppermute | solution.py:303
  46.3 24.5 %collective-permute-start.2 = (bf16[2,2,1,96,384]{4,3,1,0,2:T(8,128)(2,1)S(1)}, bf16[2,2,1,96,384]{4,3,1,0,2:T(8,128)(2,1)}, u32[]{:S(2)}, u32[]{:S(2)}) collective-permute-start(bf16[2,2,1,96,384]{4,3,1,0,2:T(8,128)(2,1)S(1)} %bitcast.73), channel_id=1, source_target_pairs={{0,3},{1,0},{2,1},{3,2},{4,7},{5,4},{6,5},{7,6},{8,11},{9,8},{10,9... | collective-permute-start | bytes 884744 | tf_op jit(solution)/shard_map/weights/ppermute | solution.py:303
  61.7 27.5 %all-to-all-start.1 = ((bf16[128,2,384]{2,1,0:T(2,128)(2,1)}), bf16[128,2,384]{2,1,0:T(2,128)(2,1)S(1)}, u32[]{:S(2)}, u32[]{:S(2)}) async-start(bf16[128,2,384]{2,1,0:T(2,128)(2,1)} %forward_analysis.3), calls=%async_computation.1 | async-start | bytes 393216 | tf_op jit(solution)/shard_map/forward_analysis/all_to_all | solution.py:70
  89.2 52.7 %copy-start.4 = (bf16[4,1024,256]{2,1,0:T(8,128)(2,1)S(1)}, bf16[4,1024,256]{2,1,0:T(8,128)(2,1)}, u32[]{:S(2)}) copy-start(bf16[4,1024,256]{2,1,0:T(8,128)(2,1)} %constant.130.clone.refs_0_) | copy-start | bytes 6291460
  89.9 52.0 %copy-start.8 = (s32[2]{0:T(128)S(1)}, s32[2]{0:T(128)}, u32[]{:S(2)}) copy-start(s32[2]{0:T(128)} %pad_add_fusion.place_ref) | copy-start | bytes 28
  142.9 15.5 %copy-start.13 = (bf16[2,128,384]{2,1,0:T(8,128)(2,1)S(1)}, bf16[2,128,384]{2,1,0:T(8,128)(2,1)}, u32[]{:S(2)}) copy-start(bf16[2,128,384]{2,1,0:T(8,128)(2,1)} %param.11) | copy-start | bytes 589828
  158.5 0.9 copy-start.6
  158.5 1.2 copy-start.14
  160.1 15.1 %copy-start.3 = (bf16[4,256,1024]{2,1,0:T(8,128)(2,1)S(1)}, bf16[4,256,1024]{2,1,0:T(8,128)(2,1)}, u32[]{:S(2)}) copy-start(bf16[4,256,1024]{2,1,0:T(8,128)(2,1)} %constant.132.clone.refs_0_) | copy-start | bytes 6291460
  160.5 16.3 %copy-start.11 = (bf16[256,384]{1,0:T(8,128)(2,1)}, bf16[256,384]{1,0:T(8,128)(2,1)S(1)}, u32[]{:S(2)}) copy-start(bf16[256,384]{1,0:T(8,128)(2,1)S(1)} %fusion.2) | copy-start | bytes 589828
  176.9 25.8 %all-to-all-start.5 = ((bf16[128,2,384]{2,1,0:T(2,128)(2,1)}), bf16[128,2,384]{2,1,0:T(2,128)(2,1)S(1)}, u32[]{:S(2)}, u32[]{:S(2)}) async-start(bf16[128,2,384]{2,1,0:T(2,128)(2,1)} %backward_analysis.2), calls=%async_computation.5 | async-start | bytes 393216 | tf_op jit(solution)/shard_map/backward_analysis/all_to_all | solution.py:70
  184.7 0.9 copy-start.7
  185.6 26.9 %collective-permute-start.3 = (bf16[2,128,576]{2,1,0:T(8,128)(2,1)}, bf16[2,128,576]{2,1,0:T(8,128)(2,1)S(1)}, u32[]{:S(2)}, u32[]{:S(2)}) collective-permute-start(bf16[2,128,576]{2,1,0:T(8,128)(2,1)} %get-tuple-element.30), channel_id=1, source_target_pairs={{0,1},{1,2},{2,3},{3,0},{4,5},{5,6},{6,7},{7,4},{8,9},{9,10},{10,1... | collective-permute-start | bytes 884744 | tf_op jit(solution)/shard_map/pointwise_weights/ppermute | solution.py:343
  187.5 25.0 %collective-permute-start.4 = (bf16[2,128,576]{2,1,0:T(8,128)(2,1)}, bf16[2,128,576]{2,1,0:T(8,128)(2,1)}, u32[]{:S(2)}, u32[]{:S(2)}) collective-permute-start(bf16[2,128,576]{2,1,0:T(8,128)(2,1)} %get-tuple-element.31), channel_id=1, source_target_pairs={{0,2},{1,3},{2,0},{3,1},{4,6},{5,7},{6,4},{7,5},{8,10},{9,11},{10,... | collective-permute-start | bytes 884744 | tf_op jit(solution)/shard_map/pointwise_weights/ppermute | solution.py:343
  191.8 20.8 %collective-permute-start.5 = (bf16[2,128,576]{2,1,0:T(8,128)(2,1)}, bf16[2,128,576]{2,1,0:T(8,128)(2,1)}, u32[]{:S(2)}, u32[]{:S(2)}) collective-permute-start(bf16[2,128,576]{2,1,0:T(8,128)(2,1)} %get-tuple-element.32), channel_id=1, source_target_pairs={{0,3},{1,0},{2,1},{3,2},{4,7},{5,4},{6,5},{7,6},{8,11},{9,8},{10,9... | collective-permute-start | bytes 884744 | tf_op jit(solution)/shard_map/pointwise_weights/ppermute | solution.py:343
  203.6 28.7 %all-to-all-start.6 = ((bf16[128,2,384]{2,1,0:T(2,128)(2,1)}), bf16[128,2,384]{2,1,0:T(2,128)(2,1)S(1)}, u32[]{:S(2)}, u32[]{:S(2)}) async-start(bf16[128,2,384]{2,1,0:T(2,128)(2,1)} %backward_analysis.3), calls=%async_computation.6 | async-start | bytes 393216 | tf_op jit(solution)/shard_map/backward_analysis/all_to_all | solution.py:70
  214.9 18.8 %collective-permute-start.8 = (bf16[2,128,144]{2,1,0:T(8,128)(2,1)}, bf16[2,128,144]{2,1,0:T(8,128)(2,1)S(1)}, u32[]{:S(2)}, u32[]{:S(2)}) collective-permute-start(bf16[2,128,144]{2,1,0:T(8,128)(2,1)} %get-tuple-element.48), channel_id=1, source_target_pairs={{0,24},{4,28},{8,0},{12,4},{16,8},{20,12},{24,16},{28,20},{32,56},... | collective-permute-start | bytes 221192 | tf_op jit(solution)/shard_map/pointwise_weights/ppermute | solution.py:241
  219.5 14.2 %collective-permute-start.7 = (bf16[2,128,144]{2,1,0:T(8,128)(2,1)}, bf16[2,128,144]{2,1,0:T(8,128)(2,1)S(1)}, u32[]{:S(2)}, u32[]{:S(2)}) collective-permute-start(bf16[2,128,144]{2,1,0:T(8,128)(2,1)} %get-tuple-element.49), channel_id=1, source_target_pairs={{0,16},{4,20},{8,24},{12,28},{16,0},{20,4},{24,8},{28,12},{32,48},... | collective-permute-start | bytes 221192 | tf_op jit(solution)/shard_map/pointwise_weights/ppermute | solution.py:241
  222.2 11.4 %collective-permute-start.6 = (bf16[2,128,144]{2,1,0:T(8,128)(2,1)S(1)}, bf16[2,128,144]{2,1,0:T(8,128)(2,1)S(1)}, u32[]{:S(2)}, u32[]{:S(2)}) collective-permute-start(bf16[2,128,144]{2,1,0:T(8,128)(2,1)S(1)} %get-tuple-element.50), channel_id=1, source_target_pairs={{0,8},{4,12},{8,16},{12,20},{16,24},{20,28},{24,0},{28,4},{32,40},... | collective-permute-start | bytes 221192 | tf_op jit(solution)/shard_map/pointwise_weights/ppermute | solution.py:241
  233.7 31.4 %all-to-all-start.7 = ((bf16[128,2,384]{2,1,0:T(2,128)(2,1)}), bf16[128,2,384]{2,1,0:T(2,128)(2,1)S(1)}, u32[]{:S(2)}, u32[]{:S(2)}) async-start(bf16[128,2,384]{2,1,0:T(2,128)(2,1)} %unmix.1), calls=%async_computation.7 | async-start | bytes 393216 | tf_op jit(solution)/shard_map/backward_synthesis/all_to_all | solution.py:70
  245.4 3.1 %collective-permute-start.9 = (bf16[128,144]{1,0:T(8,128)(2,1)S(1)}, bf16[128,144]{1,0:T(8,128)(2,1)S(1)}, u32[]{:S(2)}, u32[]{:S(2)}) collective-permute-start(bf16[128,144]{1,0:T(8,128)(2,1)S(1)} %fusion.14), channel_id=1, source_target_pairs={{0,4},{4,0},{8,12},{12,8},{16,20},{20,16},{24,28},{28,24},{32,36},... | collective-permute-start | bytes 110600 | tf_op jit(solution)/shard_map/pointwise_weights/ppermute | solution.py:364
  266.1 28.8 %all-to-all-start.8 = ((bf16[128,2,512]{2,1,0:T(2,128)(2,1)}), bf16[128,2,512]{2,1,0:T(2,128)(2,1)S(1)}, u32[]{:S(2)}, u32[]{:S(2)}) async-start(bf16[128,2,512]{2,1,0:T(2,128)(2,1)} %backward_synthesis.2), calls=%async_computation.8 | async-start | bytes 524288 | tf_op jit(solution)/shard_map/backward_synthesis/all_to_all | solution.py:70
  273.8 1.4 copy-start.10
  275.3 19.6 %copy-start.2 = (bf16[4,1024,256]{2,1,0:T(8,128)(2,1)S(1)}, bf16[4,1024,256]{2,1,0:T(8,128)(2,1)}, u32[]{:S(2)}) copy-start(bf16[4,1024,256]{2,1,0:T(8,128)(2,1)} %constant.129.clone.matrix_ref) | copy-start | bytes 6291460
  275.4 19.5 %copy-start.9 = (f32[256]{0:T(256)S(1)}, f32[256]{0:T(256)}, u32[]{:S(2)}) copy-start(f32[256]{0:T(256)} %constant.133.clone.quad_ref) | copy-start | bytes 3076
  277.6 24.4 %collective-permute-start.11 = (bf16[2,2,96,384]{3,2,1,0:T(8,128)(2,1)}, bf16[2,2,96,384]{3,2,1,0:T(8,128)(2,1)}, u32[]{:S(2)}, u32[]{:S(2)}) collective-permute-start(bf16[2,2,96,384]{3,2,1,0:T(8,128)(2,1)} %bitcast.58), channel_id=1, source_target_pairs={{0,2},{1,3},{2,0},{3,1},{4,6},{5,7},{6,4},{7,5},{8,10},{9,11},{10,... | collective-permute-start | bytes 884744 | tf_op jit(solution)/shard_map/unmix/ppermute | solution.py:394
  281.6 20.4 %collective-permute-start.12 = (bf16[2,2,96,384]{3,2,1,0:T(8,128)(2,1)}, bf16[2,2,96,384]{3,2,1,0:T(8,128)(2,1)}, u32[]{:S(2)}, u32[]{:S(2)}) collective-permute-start(bf16[2,2,96,384]{3,2,1,0:T(8,128)(2,1)} %bitcast.57), channel_id=1, source_target_pairs={{0,3},{1,0},{2,1},{3,2},{4,7},{5,4},{6,5},{7,6},{8,11},{9,8},{10,9... | collective-permute-start | bytes 884744 | tf_op jit(solution)/shard_map/unmix/ppermute | solution.py:394
  284.4 17.6 %collective-permute-start.10 = (bf16[2,2,96,384]{3,2,1,0:T(8,128)(2,1)}, bf16[2,2,96,384]{3,2,1,0:T(8,128)(2,1)}, u32[]{:S(2)}, u32[]{:S(2)}) collective-permute-start(bf16[2,2,96,384]{3,2,1,0:T(8,128)(2,1)} %bitcast.59), channel_id=1, source_target_pairs={{0,1},{1,2},{2,3},{3,0},{4,5},{5,6},{6,7},{7,4},{8,9},{9,10},{10,1... | collective-permute-start | bytes 884744 | tf_op jit(solution)/shard_map/unmix/ppermute | solution.py:394
  294.8 2.4 copy-start.5
  297.3 3.6 %copy-start.15 = (bf16[768,384]{1,0:T(8,128)(2,1)S(1)}, bf16[768,384]{1,0:T(8,128)(2,1)}, u32[]{:S(2)}) copy-start(bf16[768,384]{1,0:T(8,128)(2,1)} %param.15) | copy-start | bytes 1769476
  297.3 16.5 %all-to-all-start.9 = ((bf16[4,256,384]{2,1,0:T(8,128)(2,1)}), bf16[4,256,384]{2,1,0:T(8,128)(2,1)S(1)}, u32[]{:S(2)}, u32[]{:S(2)}) async-start(bf16[4,256,384]{2,1,0:T(8,128)(2,1)} %backward_synthesis.3), calls=%async_computation.9 | async-start | bytes 1572864 | tf_op jit(solution)/shard_map/backward_synthesis/all_to_all | solution.py:70
  302.0 2.4 slice-start
  302.0 12.7 %copy-start.1 = (bf16[384,768]{1,0:T(8,128)(2,1)S(1)}, bf16[384,768]{1,0:T(8,128)(2,1)}, u32[]{:S(2)}) copy-start(bf16[384,768]{1,0:T(8,128)(2,1)} %param.14) | copy-start | bytes 1769476
  304.3 9.6 %copy-start.12 = (bf16[256,384]{1,0:T(8,128)(2,1)S(1)}, bf16[256,384]{1,0:T(8,128)(2,1)}, u32[]{:S(2)}) copy-start(bf16[256,384]{1,0:T(8,128)(2,1)} %copy-done.11) | copy-start | bytes 589828

commit v9 on v8

--- a/solution.py
+++ b/solution.py
@@ -50,12 +50,9 @@
     doubled = (pair.astype(np.float32) * factor).astype(ml_dtypes.bfloat16)
 
     def arrange(values):
-        values = values.reshape(2, lon_count, nlon // lon_count, lon_count, modes // lon_count)
-        values = values.transpose(3, 0, 4, 1, 2)
-        out = np.zeros(values.shape[:3] + (rows, lon_count, rows, values.shape[4]), values.dtype)
-        for row in range(rows):
-            out[:, :, :, row, :, row] = values
-        return out.reshape(lon_count, 2 * modes // lon_count * rows, nlon * rows)
+        values = values.reshape(2, nlon, lon_count, -1).transpose(2, 0, 3, 1)
+        values = np.repeat(values[:, :, :, None], rows, axis=3)
+        return np.ascontiguousarray(values.reshape(lon_count, -1, nlon))
 
     return arrange(pair), arrange(doubled)
 
@@ -82,21 +79,44 @@
     out_ref[...] = out.astype(jnp.bfloat16).reshape(out_ref.shape)
 
 
-def fourier_kernel(period, place_ref, matrix_ref, quad_ref, values_ref, out_ref):
-    width = out_ref.shape[-1]
+def split_scale(quad_refs, lat_ref, rows, row):
+    return quad_refs[0][rows * lat_ref[0] + row] if quad_refs else 1.0
+
+
+def to_orders_kernel(lon_ref, lat_ref, matrix_ref, values_ref, *refs):
+    *quad_refs, out_ref = refs
+    rows, width = out_ref.shape[1:]
+    period = values_ref.shape[1] // rows
+    total = None
+    for row in range(rows):
+        values = values_ref[:, row * period : (row + 1) * period, :].reshape(-1, width)
+        out = jnp.dot(matrix_ref[0], values, preferred_element_type=jnp.float32)
+        if quad_refs:
+            out = out * split_scale(quad_refs, lat_ref, rows, row)
+        level = lax.broadcasted_iota(jnp.int32, out.shape, 0) & (rows - 1)
+        total = out if row == 0 else jnp.where(level == row, out, total)
+    out_ref[...] = total.astype(jnp.bfloat16).reshape(out_ref.shape)
+
+
+def from_orders_kernel(lon_ref, lat_ref, matrix_ref, values_ref, *refs):
+    *quad_refs, out_ref = refs
+    rows, width = values_ref.shape[1:]
+    count, size, _ = out_ref.shape
+    period = size // rows
     values = values_ref[...].reshape(-1, width)
-    out = lax.dot_general(matrix_ref[0], values, PLAIN, preferred_element_type=jnp.float32)
-    row = lax.broadcasted_iota(jnp.int32, out.shape, 0) & (2 * period - 1)
-    first = quad_ref[2 * place_ref[1]]
-    second = quad_ref[2 * place_ref[1] + 1]
-    out = out * jnp.where(row < period, first, second)
-    out_ref[...] = out.astype(jnp.bfloat16).reshape(out_ref.shape)
-
-
-def gradient_kernel(place_ref, act_ref, back_ref, hidden_ref, pre_grad_ref, *refs):
-    own_ref, *sent_refs, in_ref, out_ref, flat_ref = refs
-    count = len(sent_refs) + 1
-    _, lat_count, chunk = own_ref.shape
+    level = lax.broadcasted_iota(jnp.int32, values.shape, 0) & (rows - 1)
+    for row in range(rows):
+        chosen = jnp.where(level == row, values, jnp.zeros_like(values))
+        out = jnp.dot(matrix_ref[0], chosen, preferred_element_type=jnp.float32)
+        if quad_refs:
+            out = out * split_scale(quad_refs, lat_ref, rows, row)
+        out = out.astype(jnp.bfloat16).reshape(count, period, width)
+        out_ref[:, row * period : (row + 1) * period, :] = out
+
+
+def gradient_kernel(core_ref, act_ref, back_ref, hidden_ref, pre_grad_ref, *refs):
+    keep_ref, give_ref, in_ref, out_ref, flat_ref = refs
+    lat_count = keep_ref.shape[0]
     dims = (((0,), (0,)), ((), ()))
     pairs = ((hidden_ref, pre_grad_ref, in_ref), (act_ref, back_ref, out_ref))
     for part, (left_ref, right_ref, ref) in enumerate(pairs):
@@ -112,15 +132,12 @@
                 lane = i * width + tile * 128
                 rows = ref[pl.ds(tile * size + i, lat_count, stride=step), :]
                 flat_ref[part, :, lane : lane + 128] = rows
-    for place in range(count):
-
-        @pl.when(place_ref[0] == place)
+    for core in range(2):
+
+        @pl.when(core_ref[0] == core)
         def _():
-            own_ref[...] = flat_ref[:, :, place * chunk : (place + 1) * chunk]
-            for shift, ref in enumerate(sent_refs, 1):
-                to = (place + shift) % count
-                block = flat_ref[:, :, to * chunk : (to + 1) * chunk]
-                ref[...] = block.astype(jnp.bfloat16)
+            keep_ref[...] = flat_ref[core]
+            give_ref[...] = flat_ref[1 - core].astype(jnp.bfloat16)
 
 
 def beside_kernel(dims, matrix_ref, values_ref, extra_ref, out_ref):
@@ -152,10 +169,6 @@
     half = values.shape[0] // 2
     out = jnp.concatenate([by_re[:half] - by_im[half:], by_re[half:] + by_im[:half]])
     out_ref[...] = out.astype(jnp.bfloat16).reshape(out_ref.shape)
-
-
-def placed(kernel, place_ref, *refs):
-    kernel(*refs)
 
 
 def whole(shape):
@@ -175,39 +188,34 @@
     )(*operands)
 
 
-def fourier_product(period, place, matrices, quad, values, block, out_shape, grant):
-    kernel = functools.partial(fourier_kernel, period)
+def fourier_product(kernel, places, matrices, quad, values, block, out_shape):
     specs = [
-        pl.BlockSpec((1,) + matrices.shape[1:], lambda i, at: (at[0], 0, 0)),
-        pl.BlockSpec(memory_space=pltpu.SMEM),
+        pl.BlockSpec((1,) + matrices.shape[1:], lambda i, lon, lat: (lon[0], 0, 0)),
         whole(block),
     ]
-    operands = (matrices, quad, values)
-    if quad is None:
-        kernel = functools.partial(placed, functools.partial(product_kernel, PLAIN))
-        specs.pop(1)
-        operands = (matrices, values)
+    operands = (matrices, values)
+    if quad is not None:
+        specs.append(pl.BlockSpec(memory_space=pltpu.SMEM))
+        operands += (quad,)
     moved = 2 * (math.prod(out_shape) + math.prod(block) + math.prod(matrices.shape[1:]))
     return pl.pallas_call(
         kernel,
         grid_spec=pltpu.PrefetchScalarGridSpec(
-            num_scalar_prefetch=1, grid=(1,), in_specs=specs, out_specs=whole(out_shape)
+            num_scalar_prefetch=2, grid=(1,), in_specs=specs, out_specs=whole(out_shape)
         ),
         out_shape=jax.ShapeDtypeStruct(out_shape, jnp.bfloat16),
-        compiler_params=pltpu.CompilerParams(vmem_limit_bytes=grant * MIB),
+        compiler_params=pltpu.CompilerParams(vmem_limit_bytes=20 * MIB),
         cost_estimate=pl.CostEstimate(
-            flops=2 * math.prod(matrices.shape[1:]) * out_shape[-1],
+            flops=4 * math.prod(matrices.shape[1:]) * out_shape[-1],
             bytes_accessed=moved,
             transcendentals=0,
         ),
-    )(place, *operands)
-
-
-def gradient_blocks(lon_index, lon_count, lat_count, act, back, hidden, pre_grad):
-    in_shape = (hidden.shape[1], pre_grad.shape[1])
-    size = math.prod(in_shape)
-    blocks = (2, lat_count, size // (lat_count * lon_count))
-    dtypes = [jnp.float32] + [jnp.bfloat16] * (lon_count - 1)
+    )(*places, *operands)
+
+
+def gradient_rows(core, lat_count, act, back, hidden, pre_grad):
+    size = hidden.shape[1] * pre_grad.shape[1]
+    shape = (lat_count, size // lat_count)
     operands = (act, back, hidden, pre_grad)
     return pl.pallas_call(
         gradient_kernel,
@@ -215,19 +223,22 @@
             num_scalar_prefetch=1,
             grid=(1,),
             in_specs=[whole(operand.shape) for operand in operands],
-            out_specs=[whole(blocks)] * lon_count,
+            out_specs=[whole(shape)] * 2,
             scratch_shapes=[
                 pltpu.VMEM((size // 128, 128), jnp.float32),
                 pltpu.VMEM((size // 128, 128), jnp.float32),
-                pltpu.VMEM((2, lat_count, size // lat_count), jnp.float32),
+                pltpu.VMEM((2,) + shape, jnp.float32),
             ],
         ),
-        out_shape=[jax.ShapeDtypeStruct(blocks, dtype) for dtype in dtypes],
+        out_shape=[
+            jax.ShapeDtypeStruct(shape, jnp.float32),
+            jax.ShapeDtypeStruct(shape, jnp.bfloat16),
+        ],
         compiler_params=pltpu.CompilerParams(vmem_limit_bytes=24 * MIB),
         cost_estimate=pl.CostEstimate(
             flops=4 * size * act.shape[0], bytes_accessed=8 * size, transcendentals=0
         ),
-    )(lon_index.reshape(1).astype(jnp.int32), *operands)
+    )(core.reshape(1).astype(jnp.int32), *operands)
 
 
 def scatter_sum(values, axis, index, count, shifted):
@@ -259,17 +270,19 @@
     quarter = width // lon_count
     half = lat_count // 2
     order = lon_index * half + lat_index % half
-    place = jnp.stack([lon_index, lat_index]).astype(jnp.int32)
+    places = (lon_index.reshape(1).astype(jnp.int32), lat_index.reshape(1).astype(jnp.int32))
     total_lat = rows * lat_count
     spread = (lat_count, rows, width)
     gathered_shape = (lon_count, rows * lon_rows, width)
 
-    def to_orders(values, matrices, scale, grant):
-        return fourier_product(1, place, matrices, scale, values, gathered_shape, spread, grant)
+    def to_orders(values, matrices, scale):
+        return fourier_product(
+            to_orders_kernel, places, matrices, scale, values, gathered_shape, spread
+        )
 
     def from_orders(values, matrices, scale):
         out = fourier_product(
-            lon_rows, place, matrices, scale, values, spread, gathered_shape, 20
+            from_orders_kernel, places, matrices, scale, values, spread, gathered_shape
         )
         return jnp.sum(swap_blocks(out, "lon").astype(jnp.float32), axis=0)
 
@@ -294,7 +307,7 @@
         table = lax.dynamic_slice_in_dim(tables, order, 1)
         own_weight = spectral_weight
         own_weight = own_weight.transpose(0, 1, 3, 2)[:, :, None]
-        four = swap_blocks(to_orders(gathered, plain_t, quad, 60), "lat")
+        four = swap_blocks(to_orders(gathered, plain_t, quad), "lat")
     with jax.named_scope("weights"):
         weights = jnp.zeros((2, rows, lon_count, quarter, width), jnp.bfloat16)
         weights = lax.dynamic_update_slice_in_dim(weights, own_weight, lon_index, 2)
@@ -335,34 +348,34 @@
         gathered, hidden, pre_grad, act = lax.optimization_barrier(
             (gathered, hidden, pre_grad, act)
         )
-        field_grad = swap_blocks(to_orders(gathered, doubled_t, None, 20), "lat")
+        field_grad = swap_blocks(to_orders(gathered, doubled_t, None), "lat")
     with jax.named_scope("pointwise_weights"):
-        parts = [*gradient_blocks(lon_index, lon_count, lat_count, act, back, hidden, pre_grad)]
-        for shift in range(1, lon_count):
-            pairs = [(i, (i + shift) % lon_count) for i in range(lon_count)]
-            parts[shift] = lax.ppermute(parts[shift], "lon", pairs)
+        keep, give = gradient_rows(lat_index & 1, lat_count, act, back, hidden, pre_grad)
+        got = lax.ppermute(give, "lat", [(i, i ^ 1) for i in range(lat_count)])
     with jax.named_scope("backward_analysis"):
         mixed_grad = legendre(PLAIN, field_grad)
+        mixed_grad, keep, got = lax.optimization_barrier((mixed_grad, keep, got))
         mixed_grad = swap_blocks(mixed_grad, "lat")
     with jax.named_scope("pointwise_weights"):
         parts = scatter_sum(
-            add_parts(parts),
-            "lat",
-            (lat_index >> 1) & 3,
-            4,
-            lambda s: [(i, (i & ~6) | ((i + 2 * s) & 6)) for i in range(lat_count)],
+            add_parts([keep, got]),
+            "lon",
+            lon_index,
+            lon_count,
+            lambda s: [(i, (i + s) % lon_count) for i in range(lon_count)],
         )
     with jax.named_scope("unmix"):
         spectrum_grad = complex_product(mixed_grad, True)
-        spectrum_grad, *parts = lax.optimization_barrier((spectrum_grad, *parts))
     with jax.named_scope("backward_synthesis"):
         spectrum_grad = swap_blocks(spectrum_grad, "lat")
     with jax.named_scope("pointwise_weights"):
         sums = add_parts(parts)
-        even = lat_index % 2 == 0
-        give = jnp.where(even, sums[1], sums[0]).astype(jnp.bfloat16)
-        got = lax.ppermute(give, "lat", [(i, i ^ 1) for i in range(lat_count)])
-        parts = [jnp.where(even, sums[0], sums[1]), got]
+        width_half = sums.shape[1] // 2
+        high = (lat_index >> 2) & 1 == 1
+        low_part, high_part = sums[:, :width_half], sums[:, width_half:]
+        give = jnp.where(high, low_part, high_part).astype(jnp.bfloat16)
+        got = lax.ppermute(give, "lat", [(i, i ^ 6) for i in range(lat_count)])
+        parts = [jnp.where(high, high_part, low_part), got]
     with jax.named_scope("backward_synthesis"):
         extra = add_parts(parts).astype(jnp.bfloat16)
         chunk = extra.shape[1]
@@ -394,8 +407,8 @@
             grad_spectral.append(lax.ppermute(block, "lon", pairs))
         grad_spectral = add_parts(grad_spectral)
     with jax.named_scope("pointwise_weights"):
-        sums = four_grad[:, :, width:].reshape(lat_count // 8, 4, 2, room)[..., :chunk]
-        sums = jnp.sum(sums.astype(jnp.float32), axis=0).swapaxes(0, 1).reshape(2, -1)
+        sums = four_grad[:, :, width:].reshape(lat_count // 8, 2, 2, 2, room)[..., :chunk]
+        sums = jnp.sum(sums.astype(jnp.float32), axis=(0, 2)).swapaxes(0, 1).reshape(2, -1)
     return (
         block_output.reshape(grid.shape),
         grad_input.reshape(grid.shape),

time: 316 us -> 308 us (0.975)
  starting transfers between devices: 105 us -> 95.1 us
  waiting for transfers between devices: 73.3 us -> 80.6 us
  blocking collectives: 99 us -> 95.8 us
    all_to_all x7, starting transfers between devices: 63.2 us -> 57.8 us  [swap_blocks(): return lax.all_to_all(values, axis, split_axis=0, concat_axis=0, tiled=True)]
    ppermute x3 -> x1, starting transfers between devices: 9.82 us -> 4.58 us  [body(): got = lax.ppermute(give, 'lat', [(i, i ^ 6) for i in range(lat_count)])]
    all_to_all x7, waiting for transfers between devices: 72.2 us -> 76.7 us  [swap_blocks(): return lax.all_to_all(values, axis, split_axis=0, concat_axis=0, tiled=True)]
    ppermute x3 -> x1, waiting for transfers between devices: 0.01 us -> 3.8 us  [body(): got = lax.ppermute(give, 'lat', [(i, i ^ 6) for i in range(lat_count)])]
    all_gather x1, blocking collectives: 17.3 us -> 14 us  [body(): gathered = lax.all_gather(grid.reshape(-1, width), 'lon', axis=0)]
  transfers between devices with their start and end apart: 20 -> 18, of which waited for: 8 -> 8; matrix products, arithmetic and copies ran while one was open for 5% -> 5% of each run, Pallas kernels for 2% -> 2%
where the time goes in v9:
time: 308 us; the launch traced here: 307 us
  blocking collectives  95.8 us (31%)
  starting transfers between devices  95.1 us (31%)
  waiting for transfers between devices  80.6 us (26%)
  Pallas kernels  12.2 us (4%)
  local copies, waits for them, and re-layouts  10.4 us (3%)
  other arithmetic  7.97 us (3%)
  matrix products  3.83 us (1%)
    all_to_all x7, waiting for transfers between devices, swap_blocks(): return lax.all_to_all(values, axis, split_axis=0, concat_axis=0, tiled=True)  76.7 us
    all_to_all x3, blocking collectives, swap_blocks(): return lax.all_to_all(values, axis, split_axis=0, concat_axis=0, tiled=True)  67.6 us
    all_to_all x7, starting transfers between devices, swap_blocks(): return lax.all_to_all(values, axis, split_axis=0, concat_axis=0, tiled=True)  57.8 us
    all_gather x1, blocking collectives, body(): gathered = lax.all_gather(hidden_grad, 'lon', axis=0)  14.2 us
    all_gather x1, blocking collectives, body(): gathered = lax.all_gather(grid.reshape(-1, width), 'lon', axis=0)  14 us
    ppermute x3, starting transfers between devices, body(): grad_spectral.append(lax.ppermute(block, 'lon', pairs))  11 us
    ppermute x3, starting transfers between devices, body(): moved = lax.ppermute(own_weight, 'lon', pairs)  10.4 us
    ppermute x3, starting transfers between devices, scatter_sum(): parts.append(lax.ppermute(block, axis, shifted(shift)))  9.22 us
  transfers between devices with their start and end apart: 18, of which 8 were waited for; matrix products, arithmetic and copies ran while one was open for 5% of the time, Pallas kernels for 2%

profile of v9, /device:TPU:32, one launch (start us, length us, event | category | flops | bytes accessed | tf_op | source)
XLA Modules:
  0.0 307.1 jit_solution(8905442443186648461)
XLA Ops:
  0.7 14.0 %all_gather.9.values_ref = bf16[4,256,384]{2,1,0:T(8,128)(2,1)S(1)} all-gather(bf16[1,256,384]{2,1,0:T(8,128)(2,1)} %bitcast.65), channel_id=1, replica_groups=mesh['lat'=128,'lon'=4] {'lon'}, dimensions={0}, use_global_device_ids=true | all-gather | bytes 983040 | tf_op jit(solution)/shard_map/forward_analysis/all_gather | solution.py:305
  14.7 0.7 copy-done.9
  15.4 1.7 forward_analysis.2
  17.0 19.2 %all-to-all-start = ((bf16[128,2,384]{2,1,0:T(2,128)(2,1)}), bf16[128,2,384]{2,1,0:T(2,128)(2,1)S(1)}, u32[]{:S(2)}, u32[]{:S(2)}) async-start(bf16[128,2,384]{2,1,0:T(2,128)(2,1)} %forward_analysis.2), calls=%async_computation | async-start | bytes 393216 | tf_op jit(solution)/shard_map/forward_analysis/all_to_all | solution.py:67
  36.2 3.4 %collective-permute-start.1 = (bf16[2,2,1,96,384]{4,3,1,0,2:T(8,128)(2,1)S(1)}, bf16[2,2,1,96,384]{4,3,1,0,2:T(8,128)(2,1)S(1)}, u32[]{:S(2)}, u32[]{:S(2)}) collective-permute-start(bf16[2,2,1,96,384]{4,3,1,0,2:T(8,128)(2,1)S(1)} %bitcast.66), channel_id=1, source_target_pairs={{0,2},{1,3},{2,0},{3,1},{4,6},{5,7},{6,4},{7,5},{8,10},{9,11},{10,... | collective-permute-start | bytes 884744 | tf_op jit(solution)/shard_map/weights/ppermute | solution.py:316
  39.6 4.5 %collective-permute-start = (bf16[2,2,1,96,384]{4,3,1,0,2:T(8,128)(2,1)S(1)}, bf16[2,2,1,96,384]{4,3,1,0,2:T(8,128)(2,1)S(1)}, u32[]{:S(2)}, u32[]{:S(2)}) collective-permute-start(bf16[2,2,1,96,384]{4,3,1,0,2:T(8,128)(2,1)S(1)} %bitcast.67), channel_id=1, source_target_pairs={{0,1},{1,2},{2,3},{3,0},{4,5},{5,6},{6,7},{7,4},{8,9},{9,10},{10,1... | collective-permute-start | bytes 884744 | tf_op jit(solution)/shard_map/weights/ppermute | solution.py:316
  44.1 2.5 collective-permute-start.2
  46.7 0.9 constant_dynamic-slice_fusion.7.matrix_ref
  47.6 8.4 %all-to-all-done.values_ref = bf16[128,2,384]{2,1,0:T(2,128)(2,1)S(1)} async-done(((bf16[128,2,384]{2,1,0:T(2,128)(2,1)}), bf16[128,2,384]{2,1,0:T(2,128)(2,1)S(1)}, u32[]{:S(2)}, u32[]{:S(2)}) %all-to-all-start) | async-done | bytes 196640 | tf_op jit(solution)/shard_map/forward_analysis/all_to_all | solution.py:67
  56.0 0.9 forward_analysis.3
  57.0 7.7 %all-to-all-start.1 = ((bf16[128,2,384]{2,1,0:T(2,128)(2,1)}), bf16[128,2,384]{2,1,0:T(2,128)(2,1)S(1)}, u32[]{:S(2)}, u32[]{:S(2)}) async-start(bf16[128,2,384]{2,1,0:T(2,128)(2,1)} %forward_analysis.3), calls=%async_computation.1 | async-start | bytes 393216 | tf_op jit(solution)/shard_map/forward_analysis/all_to_all | solution.py:67
  65.1 19.4 %all-to-all-done.1.values_ref = bf16[128,2,384]{2,1,0:T(2,128)(2,1)S(1)} async-done(((bf16[128,2,384]{2,1,0:T(2,128)(2,1)}), bf16[128,2,384]{2,1,0:T(2,128)(2,1)S(1)}, u32[]{:S(2)}, u32[]{:S(2)}) %all-to-all-start.1) | async-done | bytes 196640 | tf_op jit(solution)/shard_map/forward_analysis/all_to_all | solution.py:67
  84.5 0.7 mix.1
  85.2 26.0 %all_to_all.50.values_ref = bf16[128,2,384]{2,1,0:T(2,128)(2,1)S(1)} all-to-all(bf16[128,2,384]{2,1,0:T(2,128)(2,1)S(1)} %mix.1), channel_id=1, replica_groups=mesh['lat'=128,'lon'=4] {'lat'}, dimensions={0} | all-to-all | bytes 393216 | tf_op jit(solution)/shard_map/forward_synthesis/all_to_all | solution.py:67
  111.2 0.3 forward_synthesis.2
  111.5 25.8 %all_to_all.51.values_ref = bf16[128,2,384]{2,1,0:T(2,128)(2,1)S(1)} all-to-all(bf16[128,2,384]{2,1,0:T(2,128)(2,1)S(1)} %forward_synthesis.2), channel_id=1, replica_groups=mesh['lat'=128,'lon'=4] {'lat'}, dimensions={0} | all-to-all | bytes 393216 | tf_op jit(solution)/shard_map/forward_synthesis/all_to_all | solution.py:67
  137.3 0.6 forward_synthesis.3
  137.9 15.8 %all_to_all.52 = bf16[4,256,384]{2,1,0:T(8,128)(2,1)S(1)} all-to-all(bf16[4,256,384]{2,1,0:T(8,128)(2,1)S(1)} %forward_synthesis.3), channel_id=1, replica_groups=mesh['lat'=128,'lon'=4] {'lon'}, dimensions={0} | all-to-all | bytes 1572864 | tf_op jit(solution)/shard_map/forward_synthesis/all_to_all | solution.py:67
  153.9 0.4 multiply_convert_fusion
  154.3 0.5 copy-done.7
  155.0 0.4 fusion.pre_grad_ref
  155.5 0.4 fusion.2
  155.9 14.2 %all-gather = bf16[1024,384]{1,0:T(8,128)(2,1)S(1)} all-gather(bf16[256,384]{1,0:T(8,128)(2,1)S(1)} %fusion.2), channel_id=2, replica_groups=mesh['lat'=128,'lon'=4] {'lon'}, dimensions={0}, use_global_device_ids=true | all-gather | bytes 983040 | tf_op jit(solution)/shard_map/backward_analysis/all_gather | solution.py:347
  170.1 1.1 backward_analysis.2
  171.2 5.9 %all-to-all-start.5 = ((bf16[128,2,384]{2,1,0:T(2,128)(2,1)}), bf16[128,2,384]{2,1,0:T(2,128)(2,1)S(1)}, u32[]{:S(2)}, u32[]{:S(2)}) async-start(bf16[128,2,384]{2,1,0:T(2,128)(2,1)} %backward_analysis.2), calls=%async_computation.5 | async-start | bytes 393216 | tf_op jit(solution)/shard_map/backward_analysis/all_to_all | solution.py:67
  177.2 0.9 copy-done.8
  178.1 1.6 pointwise_weights.1
  179.7 2.1 collective-permute-start.3
  181.8 15.2 %all-to-all-done.5.values_ref = bf16[128,2,384]{2,1,0:T(2,128)(2,1)S(1)} async-done(((bf16[128,2,384]{2,1,0:T(2,128)(2,1)}), bf16[128,2,384]{2,1,0:T(2,128)(2,1)S(1)}, u32[]{:S(2)}, u32[]{:S(2)}) %all-to-all-start.5) | async-done | bytes 196640 | tf_op jit(solution)/shard_map/backward_analysis/all_to_all | solution.py:67
  197.0 0.9 backward_analysis.3
  197.9 6.2 %all-to-all-start.6 = ((bf16[128,2,384]{2,1,0:T(2,128)(2,1)}), bf16[128,2,384]{2,1,0:T(2,128)(2,1)S(1)}, u32[]{:S(2)}, u32[]{:S(2)}) async-start(bf16[128,2,384]{2,1,0:T(2,128)(2,1)} %backward_analysis.3), calls=%async_computation.6 | async-start | bytes 393216 | tf_op jit(solution)/shard_map/backward_analysis/all_to_all | solution.py:67
  204.1 2.2 fusion.13
  206.6 1.9 collective-permute-start.4
  208.5 5.1 %collective-permute-start.6 = (bf16[128,576]{1,0:T(8,128)(2,1)S(1)}, bf16[128,576]{1,0:T(8,128)(2,1)S(1)}, u32[]{:S(2)}, u32[]{:S(2)}) collective-permute-start(bf16[128,576]{1,0:T(8,128)(2,1)S(1)} %get-tuple-element.41), channel_id=1, source_target_pairs={{0,3},{1,0},{2,1},{3,2},{4,7},{5,4},{6,5},{7,6},{8,11},{9,8},{10,9... | collective-permute-start | bytes 442376 | tf_op jit(solution)/shard_map/pointwise_weights/ppermute | solution.py:252
  213.7 2.2 collective-permute-start.5
  215.9 8.1 %all-to-all-done.6.values_ref = bf16[128,2,384]{2,1,0:T(2,128)(2,1)S(1)} async-done(((bf16[128,2,384]{2,1,0:T(2,128)(2,1)}), bf16[128,2,384]{2,1,0:T(2,128)(2,1)S(1)}, u32[]{:S(2)}, u32[]{:S(2)}) %all-to-all-start.6) | async-done | bytes 196640 | tf_op jit(solution)/shard_map/backward_analysis/all_to_all | solution.py:67
  224.0 1.3 copy-done.2
  225.2 1.4 unmix.1
  226.6 8.0 %all-to-all-start.7 = ((bf16[128,2,384]{2,1,0:T(2,128)(2,1)}), bf16[128,2,384]{2,1,0:T(2,128)(2,1)S(1)}, u32[]{:S(2)}, u32[]{:S(2)}) async-start(bf16[128,2,384]{2,1,0:T(2,128)(2,1)} %unmix.1), calls=%async_computation.7 | async-start | bytes 393216 | tf_op jit(solution)/shard_map/backward_synthesis/all_to_all | solution.py:67
  234.6 1.2 convert_add_fusion.2
  235.9 4.6 %collective-permute-start.7 = (bf16[128,288]{1,0:T(8,128)(2,1)S(1)}, bf16[128,288]{1,0:T(8,128)(2,1)S(1)}, u32[]{:S(2)}, u32[]{:S(2)}) collective-permute-start(bf16[128,288]{1,0:T(8,128)(2,1)S(1)} %select_convert_fusion), channel_id=1, source_target_pairs={{0,24},{4,28},{8,16},{12,20},{16,8},{20,12},{24,0},{28,4},{32,56},... | collective-permute-start | bytes 221192 | tf_op jit(solution)/shard_map/pointwise_weights/ppermute | solution.py:377
  240.5 3.8 %collective-permute-done.7 = bf16[128,288]{1,0:T(8,128)(2,1)S(1)} collective-permute-done((bf16[128,288]{1,0:T(8,128)(2,1)S(1)}, bf16[128,288]{1,0:T(8,128)(2,1)S(1)}, u32[]{:S(2)}, u32[]{:S(2)}) %collective-permute-start.7) | collective-permute-done | bytes 73760 | tf_op jit(solution)/shard_map/pointwise_weights/ppermute | solution.py:377
  244.5 9.9 %all-to-all-done.7.values_ref = bf16[128,2,384]{2,1,0:T(2,128)(2,1)S(1)} async-done(((bf16[128,2,384]{2,1,0:T(2,128)(2,1)}), bf16[128,2,384]{2,1,0:T(2,128)(2,1)S(1)}, u32[]{:S(2)}, u32[]{:S(2)}) %all-to-all-start.7) | async-done | bytes 196640 | tf_op jit(solution)/shard_map/backward_synthesis/all_to_all | solution.py:67
  254.4 1.0 backward_synthesis.2
  255.4 6.3 %all-to-all-start.8 = ((bf16[128,2,640]{2,1,0:T(2,128)(2,1)}), bf16[128,2,640]{2,1,0:T(2,128)(2,1)S(1)}, u32[]{:S(2)}, u32[]{:S(2)}) async-start(bf16[128,2,640]{2,1,0:T(2,128)(2,1)} %backward_synthesis.2), calls=%async_computation.8 | async-start | bytes 655360 | tf_op jit(solution)/shard_map/backward_synthesis/all_to_all | solution.py:67
  261.8 0.3 maximum_bitcast_fusion
  262.1 0.6 pad_maximum_fusion
  262.7 0.5 fusion.10
  263.3 1.3 copy-done.11
  264.7 0.7 copy.49
  265.5 0.8 copy.47
  266.2 0.8 copy.48
  267.0 5.2 %collective-permute-start.9 = (bf16[2,2,96,384]{3,2,1,0:T(8,128)(2,1)}, bf16[2,2,96,384]{3,2,1,0:T(8,128)(2,1)S(1)}, u32[]{:S(2)}, u32[]{:S(2)}) collective-permute-start(bf16[2,2,96,384]{3,2,1,0:T(8,128)(2,1)} %bitcast.53), channel_id=1, source_target_pairs={{0,2},{1,3},{2,0},{3,1},{4,6},{5,7},{6,4},{7,5},{8,10},{9,11},{10,... | collective-permute-start | bytes 884744 | tf_op jit(solution)/shard_map/unmix/ppermute | solution.py:407
  272.2 1.9 collective-permute-start.10
  274.1 3.9 %collective-permute-start.8 = (bf16[2,2,96,384]{3,2,1,0:T(8,128)(2,1)}, bf16[2,2,96,384]{3,2,1,0:T(8,128)(2,1)}, u32[]{:S(2)}, u32[]{:S(2)}) collective-permute-start(bf16[2,2,96,384]{3,2,1,0:T(8,128)(2,1)} %bitcast.54), channel_id=1, source_target_pairs={{0,1},{1,2},{2,3},{3,0},{4,5},{5,6},{6,7},{7,4},{8,9},{9,10},{10,1... | collective-permute-start | bytes 884744 | tf_op jit(solution)/shard_map/unmix/ppermute | solution.py:407
  278.0 8.8 %all-to-all-done.8.values_ref = bf16[128,2,640]{2,1,0:T(2,128)(2,1)S(1)} async-done(((bf16[128,2,640]{2,1,0:T(2,128)(2,1)}), bf16[128,2,640]{2,1,0:T(2,128)(2,1)S(1)}, u32[]{:S(2)}, u32[]{:S(2)}) %all-to-all-start.8) | async-done | bytes 327712 | tf_op jit(solution)/shard_map/backward_synthesis/all_to_all | solution.py:67
  286.8 2.1 backward_synthesis.3
  288.9 4.5 %all-to-all-start.9 = ((bf16[4,256,384]{2,1,0:T(8,128)(2,1)}), bf16[4,256,384]{2,1,0:T(8,128)(2,1)S(1)}, u32[]{:S(2)}, u32[]{:S(2)}) async-start(bf16[4,256,384]{2,1,0:T(8,128)(2,1)} %backward_synthesis.3), calls=%async_computation.9 | async-start | bytes 1572864 | tf_op jit(solution)/shard_map/backward_synthesis/all_to_all | solution.py:67
  293.4 2.1 fusion.1
  295.5 2.2 fusion.8
  298.0 0.7 squeeze.25
  298.7 0.7 squeeze.24
  299.4 6.9 %all-to-all-done.9 = bf16[4,256,384]{2,1,0:T(8,128)(2,1)S(1)} async-done(((bf16[4,256,384]{2,1,0:T(8,128)(2,1)}), bf16[4,256,384]{2,1,0:T(8,128)(2,1)S(1)}, u32[]{:S(2)}, u32[]{:S(2)}) %all-to-all-start.9) | async-done | bytes 786464 | tf_op jit(solution)/shard_map/backward_synthesis/all_to_all | solution.py:67
  306.4 0.7 add_convert_fusion
  (55 shorter events, 2.1 us)
Async XLA Ops:
  0.6 153.2 %copy-start = (bf16[384,768]{1,0:T(8,128)(2,1)S(1)}, bf16[384,768]{1,0:T(8,128)(2,1)}, u32[]{:S(2)}) copy-start(bf16[384,768]{1,0:T(8,128)(2,1)} %param.14) | copy-start | bytes 1769476
  0.6 14.0 %copy-start.6 = (bf16[4,256,512]{2,1,0:T(8,128)(2,1)S(1)}, bf16[4,256,512]{2,1,0:T(8,128)(2,1)}, u32[]{:S(2)}) copy-start(bf16[4,256,512]{2,1,0:T(8,128)(2,1)} %constant.118.clone.matrix_ref) | copy-start | bytes 3145732
  14.7 0.7 copy-start.9
  15.4 20.9 %copy-start.14 = (bf16[2,2,384,96]{2,3,1,0:T(8,128)(2,1)S(1)}, bf16[2,2,384,96]{2,3,1,0:T(8,128)(2,1)}, u32[]{:S(2)}) copy-start(bf16[2,2,384,96]{2,3,1,0:T(8,128)(2,1)} %param.13) | copy-start | bytes 884740
  17.0 39.0 %all-to-all-start = ((bf16[128,2,384]{2,1,0:T(2,128)(2,1)}), bf16[128,2,384]{2,1,0:T(2,128)(2,1)S(1)}, u32[]{:S(2)}, u32[]{:S(2)}) async-start(bf16[128,2,384]{2,1,0:T(2,128)(2,1)} %forward_analysis.2), calls=%async_computation | async-start | bytes 393216 | tf_op jit(solution)/shard_map/forward_analysis/all_to_all | solution.py:67
  36.2 28.7 %collective-permute-start.1 = (bf16[2,2,1,96,384]{4,3,1,0,2:T(8,128)(2,1)S(1)}, bf16[2,2,1,96,384]{4,3,1,0,2:T(8,128)(2,1)S(1)}, u32[]{:S(2)}, u32[]{:S(2)}) collective-permute-start(bf16[2,2,1,96,384]{4,3,1,0,2:T(8,128)(2,1)S(1)} %bitcast.66), channel_id=1, source_target_pairs={{0,2},{1,3},{2,0},{3,1},{4,6},{5,7},{6,4},{7,5},{8,10},{9,11},{10,... | collective-permute-start | bytes 884744 | tf_op jit(solution)/shard_map/weights/ppermute | solution.py:316
  39.6 25.3 %collective-permute-start = (bf16[2,2,1,96,384]{4,3,1,0,2:T(8,128)(2,1)S(1)}, bf16[2,2,1,96,384]{4,3,1,0,2:T(8,128)(2,1)S(1)}, u32[]{:S(2)}, u32[]{:S(2)}) collective-permute-start(bf16[2,2,1,96,384]{4,3,1,0,2:T(8,128)(2,1)S(1)} %bitcast.67), channel_id=1, source_target_pairs={{0,1},{1,2},{2,3},{3,0},{4,5},{5,6},{6,7},{7,4},{8,9},{9,10},{10,1... | collective-permute-start | bytes 884744 | tf_op jit(solution)/shard_map/weights/ppermute | solution.py:316
  44.1 20.9 %collective-permute-start.2 = (bf16[2,2,1,96,384]{4,3,1,0,2:T(8,128)(2,1)S(1)}, bf16[2,2,1,96,384]{4,3,1,0,2:T(8,128)(2,1)S(1)}, u32[]{:S(2)}, u32[]{:S(2)}) collective-permute-start(bf16[2,2,1,96,384]{4,3,1,0,2:T(8,128)(2,1)S(1)} %bitcast.68), channel_id=1, source_target_pairs={{0,3},{1,0},{2,1},{3,2},{4,7},{5,4},{6,5},{7,6},{8,11},{9,8},{10,9... | collective-permute-start | bytes 884744 | tf_op jit(solution)/shard_map/weights/ppermute | solution.py:316
  57.0 27.5 %all-to-all-start.1 = ((bf16[128,2,384]{2,1,0:T(2,128)(2,1)}), bf16[128,2,384]{2,1,0:T(2,128)(2,1)S(1)}, u32[]{:S(2)}, u32[]{:S(2)}) async-start(bf16[128,2,384]{2,1,0:T(2,128)(2,1)} %forward_analysis.3), calls=%async_computation.1 | async-start | bytes 393216 | tf_op jit(solution)/shard_map/forward_analysis/all_to_all | solution.py:67
  65.1 46.1 %copy-start.1 = (bf16[2,2,4,96,384]{4,3,2,1,0:T(8,128)(2,1)}, bf16[2,2,4,96,384]{4,3,2,1,0:T(8,128)(2,1)S(1)}, u32[]{:S(2)}) copy-start(bf16[2,2,4,96,384]{4,3,2,1,0:T(8,128)(2,1)S(1)} %bitcast_dynamic-update-slice_fusion.1) | copy-start | bytes 3538948
  85.2 52.1 %copy-start.5 = (bf16[4,512,256]{2,1,0:T(8,128)(2,1)S(1)}, bf16[4,512,256]{2,1,0:T(8,128)(2,1)}, u32[]{:S(2)}) copy-start(bf16[4,512,256]{2,1,0:T(8,128)(2,1)} %constant.117.clone.matrix_ref) | copy-start | bytes 3145732
  137.9 15.9 %copy-start.12 = (bf16[2,128,384]{2,1,0:T(8,128)(2,1)S(1)}, bf16[2,128,384]{2,1,0:T(8,128)(2,1)}, u32[]{:S(2)}) copy-start(bf16[2,128,384]{2,1,0:T(8,128)(2,1)} %param.11) | copy-start | bytes 589828
  153.9 0.9 copy-start.7
  153.9 1.2 copy-start.13
  155.5 14.6 %copy-start.4 = (bf16[4,256,512]{2,1,0:T(8,128)(2,1)S(1)}, bf16[4,256,512]{2,1,0:T(8,128)(2,1)}, u32[]{:S(2)}) copy-start(bf16[4,256,512]{2,1,0:T(8,128)(2,1)} %constant.119.clone.matrix_ref) | copy-start | bytes 3145732
  171.2 25.8 %all-to-all-start.5 = ((bf16[128,2,384]{2,1,0:T(2,128)(2,1)}), bf16[128,2,384]{2,1,0:T(2,128)(2,1)S(1)}, u32[]{:S(2)}, u32[]{:S(2)}) async-start(bf16[128,2,384]{2,1,0:T(2,128)(2,1)} %backward_analysis.2), calls=%async_computation.5 | async-start | bytes 393216 | tf_op jit(solution)/shard_map/backward_analysis/all_to_all | solution.py:67
  177.1 0.9 copy-start.8
  179.7 18.2 %collective-permute-start.3 = (bf16[128,2304]{1,0:T(8,128)(2,1)}, bf16[128,2304]{1,0:T(8,128)(2,1)}, u32[]{:S(2)}, u32[]{:S(2)}) collective-permute-start(bf16[128,2304]{1,0:T(8,128)(2,1)} %get-tuple-element.26), channel_id=1, source_target_pairs={{0,4},{4,0},{8,12},{12,8},{16,20},{20,16},{24,28},{28,24},{32,36},... | collective-permute-start | bytes 1769480 | tf_op jit(solution)/shard_map/pointwise_weights/ppermute | solution.py:354
  197.9 26.1 %all-to-all-start.6 = ((bf16[128,2,384]{2,1,0:T(2,128)(2,1)}), bf16[128,2,384]{2,1,0:T(2,128)(2,1)S(1)}, u32[]{:S(2)}, u32[]{:S(2)}) async-start(bf16[128,2,384]{2,1,0:T(2,128)(2,1)} %backward_analysis.3), calls=%async_computation.6 | async-start | bytes 393216 | tf_op jit(solution)/shard_map/backward_analysis/all_to_all | solution.py:67
  206.6 28.0 %collective-permute-start.4 = (bf16[128,576]{1,0:T(8,128)(2,1)S(1)}, bf16[128,576]{1,0:T(8,128)(2,1)S(1)}, u32[]{:S(2)}, u32[]{:S(2)}) collective-permute-start(bf16[128,576]{1,0:T(8,128)(2,1)S(1)} %get-tuple-element.40), channel_id=1, source_target_pairs={{0,1},{1,2},{2,3},{3,0},{4,5},{5,6},{6,7},{7,4},{8,9},{9,10},{10,1... | collective-permute-start | bytes 442376 | tf_op jit(solution)/shard_map/pointwise_weights/ppermute | solution.py:252
  208.5 26.1 %collective-permute-start.6 = (bf16[128,576]{1,0:T(8,128)(2,1)S(1)}, bf16[128,576]{1,0:T(8,128)(2,1)S(1)}, u32[]{:S(2)}, u32[]{:S(2)}) collective-permute-start(bf16[128,576]{1,0:T(8,128)(2,1)S(1)} %get-tuple-element.41), channel_id=1, source_target_pairs={{0,3},{1,0},{2,1},{3,2},{4,7},{5,4},{6,5},{7,6},{8,11},{9,8},{10,9... | collective-permute-start | bytes 442376 | tf_op jit(solution)/shard_map/pointwise_weights/ppermute | solution.py:252
  213.7 21.0 %collective-permute-start.5 = (bf16[128,576]{1,0:T(8,128)(2,1)S(1)}, bf16[128,576]{1,0:T(8,128)(2,1)S(1)}, u32[]{:S(2)}, u32[]{:S(2)}) collective-permute-start(bf16[128,576]{1,0:T(8,128)(2,1)S(1)} %get-tuple-element.42), channel_id=1, source_target_pairs={{0,2},{1,3},{2,0},{3,1},{4,6},{5,7},{6,4},{7,5},{8,10},{9,11},{10,... | collective-permute-start | bytes 442376 | tf_op jit(solution)/shard_map/pointwise_weights/ppermute | solution.py:252
  224.0 1.3 copy-start.2
  226.6 27.8 %all-to-all-start.7 = ((bf16[128,2,384]{2,1,0:T(2,128)(2,1)}), bf16[128,2,384]{2,1,0:T(2,128)(2,1)S(1)}, u32[]{:S(2)}, u32[]{:S(2)}) async-start(bf16[128,2,384]{2,1,0:T(2,128)(2,1)} %unmix.1), calls=%async_computation.7 | async-start | bytes 393216 | tf_op jit(solution)/shard_map/backward_synthesis/all_to_all | solution.py:67
  235.9 8.4 %collective-permute-start.7 = (bf16[128,288]{1,0:T(8,128)(2,1)S(1)}, bf16[128,288]{1,0:T(8,128)(2,1)S(1)}, u32[]{:S(2)}, u32[]{:S(2)}) collective-permute-start(bf16[128,288]{1,0:T(8,128)(2,1)S(1)} %select_convert_fusion), channel_id=1, source_target_pairs={{0,24},{4,28},{8,16},{12,20},{16,8},{20,12},{24,0},{28,4},{32,56},... | collective-permute-start | bytes 221192 | tf_op jit(solution)/shard_map/pointwise_weights/ppermute | solution.py:377
  255.4 31.4 %all-to-all-start.8 = ((bf16[128,2,640]{2,1,0:T(2,128)(2,1)}), bf16[128,2,640]{2,1,0:T(2,128)(2,1)S(1)}, u32[]{:S(2)}, u32[]{:S(2)}) async-start(bf16[128,2,640]{2,1,0:T(2,128)(2,1)} %backward_synthesis.2), calls=%async_computation.8 | async-start | bytes 655360 | tf_op jit(solution)/shard_map/backward_synthesis/all_to_all | solution.py:67
  263.2 1.4 copy-start.11
  264.7 22.1 %copy-start.3 = (bf16[4,512,256]{2,1,0:T(8,128)(2,1)S(1)}, bf16[4,512,256]{2,1,0:T(8,128)(2,1)}, u32[]{:S(2)}) copy-start(bf16[4,512,256]{2,1,0:T(8,128)(2,1)} %constant.116.clone.matrix_ref) | copy-start | bytes 3145732
  264.7 22.1 %copy-start.10 = (f32[256]{0:T(256)S(1)}, f32[256]{0:T(256)}, u32[]{:S(2)}) copy-start(f32[256]{0:T(256)} %constant.120.clone.refs_0_) | copy-start | bytes 3076
  267.0 28.5 %collective-permute-start.9 = (bf16[2,2,96,384]{3,2,1,0:T(8,128)(2,1)}, bf16[2,2,96,384]{3,2,1,0:T(8,128)(2,1)S(1)}, u32[]{:S(2)}, u32[]{:S(2)}) collective-permute-start(bf16[2,2,96,384]{3,2,1,0:T(8,128)(2,1)} %bitcast.53), channel_id=1, source_target_pairs={{0,2},{1,3},{2,0},{3,1},{4,6},{5,7},{6,4},{7,5},{8,10},{9,11},{10,... | collective-permute-start | bytes 884744 | tf_op jit(solution)/shard_map/unmix/ppermute | solution.py:407
  272.2 23.4 %collective-permute-start.10 = (bf16[2,2,96,384]{3,2,1,0:T(8,128)(2,1)}, bf16[2,2,96,384]{3,2,1,0:T(8,128)(2,1)}, u32[]{:S(2)}, u32[]{:S(2)}) collective-permute-start(bf16[2,2,96,384]{3,2,1,0:T(8,128)(2,1)} %bitcast.52), channel_id=1, source_target_pairs={{0,3},{1,0},{2,1},{3,2},{4,7},{5,4},{6,5},{7,6},{8,11},{9,8},{10,9... | collective-permute-start | bytes 884744 | tf_op jit(solution)/shard_map/unmix/ppermute | solution.py:407
  274.1 21.4 %collective-permute-start.8 = (bf16[2,2,96,384]{3,2,1,0:T(8,128)(2,1)}, bf16[2,2,96,384]{3,2,1,0:T(8,128)(2,1)}, u32[]{:S(2)}, u32[]{:S(2)}) collective-permute-start(bf16[2,2,96,384]{3,2,1,0:T(8,128)(2,1)} %bitcast.54), channel_id=1, source_target_pairs={{0,1},{1,2},{2,3},{3,0},{4,5},{5,6},{6,7},{7,4},{8,9},{9,10},{10,1... | collective-permute-start | bytes 884744 | tf_op jit(solution)/shard_map/unmix/ppermute | solution.py:407
  288.9 17.4 %all-to-all-start.9 = ((bf16[4,256,384]{2,1,0:T(8,128)(2,1)}), bf16[4,256,384]{2,1,0:T(8,128)(2,1)S(1)}, u32[]{:S(2)}, u32[]{:S(2)}) async-start(bf16[4,256,384]{2,1,0:T(8,128)(2,1)} %backward_synthesis.3), calls=%async_computation.9 | async-start | bytes 1572864 | tf_op jit(solution)/shard_map/backward_synthesis/all_to_all | solution.py:67

commit v10 on v9

--- a/solution.py
+++ b/solution.py
@@ -79,37 +79,27 @@
     out_ref[...] = out.astype(jnp.bfloat16).reshape(out_ref.shape)
 
 
-def split_scale(quad_refs, lat_ref, rows, row):
-    return quad_refs[0][rows * lat_ref[0] + row] if quad_refs else 1.0
-
-
-def to_orders_kernel(lon_ref, lat_ref, matrix_ref, values_ref, *refs):
-    *quad_refs, out_ref = refs
+def to_orders_kernel(lon_ref, matrix_ref, values_ref, out_ref):
     rows, width = out_ref.shape[1:]
     period = values_ref.shape[1] // rows
     total = None
     for row in range(rows):
         values = values_ref[:, row * period : (row + 1) * period, :].reshape(-1, width)
         out = jnp.dot(matrix_ref[0], values, preferred_element_type=jnp.float32)
-        if quad_refs:
-            out = out * split_scale(quad_refs, lat_ref, rows, row)
         level = lax.broadcasted_iota(jnp.int32, out.shape, 0) & (rows - 1)
         total = out if row == 0 else jnp.where(level == row, out, total)
     out_ref[...] = total.astype(jnp.bfloat16).reshape(out_ref.shape)
 
 
-def from_orders_kernel(lon_ref, lat_ref, matrix_ref, values_ref, *refs):
-    *quad_refs, out_ref = refs
-    rows, width = values_ref.shape[1:]
-    count, size, _ = out_ref.shape
+def from_orders_kernel(lon_ref, matrix_ref, values_ref, out_ref):
+    rows = values_ref.shape[1]
+    count, size, width = out_ref.shape
     period = size // rows
-    values = values_ref[...].reshape(-1, width)
+    values = values_ref[:, :, :width].reshape(-1, width)
     level = lax.broadcasted_iota(jnp.int32, values.shape, 0) & (rows - 1)
     for row in range(rows):
         chosen = jnp.where(level == row, values, jnp.zeros_like(values))
         out = jnp.dot(matrix_ref[0], chosen, preferred_element_type=jnp.float32)
-        if quad_refs:
-            out = out * split_scale(quad_refs, lat_ref, rows, row)
         out = out.astype(jnp.bfloat16).reshape(count, period, width)
         out_ref[:, row * period : (row + 1) * period, :] = out
 
@@ -140,10 +130,19 @@
             give_ref[...] = flat_ref[1 - core].astype(jnp.bfloat16)
 
 
-def beside_kernel(dims, matrix_ref, values_ref, extra_ref, out_ref):
+def weighted_kernel(matrix_ref, quad_ref, values_ref, out_ref):
+    width = out_ref.shape[-1]
+    values = values_ref[...].reshape(-1, width).astype(jnp.float32) * quad_ref[...]
+    values = values.astype(jnp.bfloat16)
+    out = jnp.dot(matrix_ref[0], values, preferred_element_type=jnp.float32)
+    out_ref[...] = out.astype(jnp.bfloat16).reshape(out_ref.shape)
+
+
+def beside_kernel(matrix_ref, quad_ref, values_ref, extra_ref, out_ref):
     width = values_ref.shape[-1]
     values = values_ref[...].reshape(-1, width)
-    out = lax.dot_general(matrix_ref[0], values, dims, preferred_element_type=jnp.float32)
+    out = lax.dot_general(matrix_ref[0], values, TURNED, preferred_element_type=jnp.float32)
+    out = out * quad_ref[...]
     out_ref[:, :, :width] = out.astype(jnp.bfloat16).reshape(values_ref.shape)
     out_ref[:, :, width:] = extra_ref[...]
 
@@ -188,20 +187,16 @@
     )(*operands)
 
 
-def fourier_product(kernel, places, matrices, quad, values, block, out_shape):
+def fourier_product(kernel, place, matrices, values, block, out_shape):
     specs = [
-        pl.BlockSpec((1,) + matrices.shape[1:], lambda i, lon, lat: (lon[0], 0, 0)),
+        pl.BlockSpec((1,) + matrices.shape[1:], lambda i, lon: (lon[0], 0, 0)),
         whole(block),
     ]
-    operands = (matrices, values)
-    if quad is not None:
-        specs.append(pl.BlockSpec(memory_space=pltpu.SMEM))
-        operands += (quad,)
     moved = 2 * (math.prod(out_shape) + math.prod(block) + math.prod(matrices.shape[1:]))
     return pl.pallas_call(
         kernel,
         grid_spec=pltpu.PrefetchScalarGridSpec(
-            num_scalar_prefetch=2, grid=(1,), in_specs=specs, out_specs=whole(out_shape)
+            num_scalar_prefetch=1, grid=(1,), in_specs=specs, out_specs=whole(out_shape)
         ),
         out_shape=jax.ShapeDtypeStruct(out_shape, jnp.bfloat16),
         compiler_params=pltpu.CompilerParams(vmem_limit_bytes=20 * MIB),
@@ -210,7 +205,7 @@
             bytes_accessed=moved,
             transcendentals=0,
         ),
-    )(*places, *operands)
+    )(place.reshape(1).astype(jnp.int32), matrices, values)
 
 
 def gradient_rows(core, lat_count, act, back, hidden, pre_grad):
@@ -270,19 +265,18 @@
     quarter = width // lon_count
     half = lat_count // 2
     order = lon_index * half + lat_index % half
-    places = (lon_index.reshape(1).astype(jnp.int32), lat_index.reshape(1).astype(jnp.int32))
     total_lat = rows * lat_count
     spread = (lat_count, rows, width)
     gathered_shape = (lon_count, rows * lon_rows, width)
 
-    def to_orders(values, matrices, scale):
+    def to_orders(values, matrices):
         return fourier_product(
-            to_orders_kernel, places, matrices, scale, values, gathered_shape, spread
-        )
-
-    def from_orders(values, matrices, scale):
+            to_orders_kernel, lon_index, matrices, values, gathered_shape, spread
+        )
+
+    def from_orders(values, matrices):
         out = fourier_product(
-            from_orders_kernel, places, matrices, scale, values, spread, gathered_shape
+            from_orders_kernel, lon_index, matrices, values, values.shape, gathered_shape
         )
         return jnp.sum(swap_blocks(out, "lon").astype(jnp.float32), axis=0)
 
@@ -307,7 +301,7 @@
         table = lax.dynamic_slice_in_dim(tables, order, 1)
         own_weight = spectral_weight
         own_weight = own_weight.transpose(0, 1, 3, 2)[:, :, None]
-        four = swap_blocks(to_orders(gathered, plain_t, quad), "lat")
+        four = swap_blocks(to_orders(gathered, plain_t), "lat")
     with jax.named_scope("weights"):
         weights = jnp.zeros((2, rows, lon_count, quarter, width), jnp.bfloat16)
         weights = lax.dynamic_update_slice_in_dim(weights, own_weight, lon_index, 2)
@@ -318,12 +312,19 @@
             weights = lax.dynamic_update_slice_in_dim(weights, moved, source, 2)
         weights = weights.reshape(2, rows, width, width)
     with jax.named_scope("forward_analysis"):
-        spectrum = swap_blocks(legendre(PLAIN, four), "lat")
+        spectrum = call_kernel(
+            weighted_kernel,
+            [table, quad, four],
+            [table.shape, quad.shape, spread],
+            spread,
+            2 * total_lat * total_lat * width,
+        )
+        spectrum = swap_blocks(spectrum, "lat")
     with jax.named_scope("mix"):
         mixed = complex_product(spectrum, False)
     with jax.named_scope("forward_synthesis"):
         fields = swap_blocks(legendre(TURNED, swap_blocks(mixed, "lat")), "lat")
-        wave_rows = from_orders(fields, doubled, None)
+        wave_rows = from_orders(fields, doubled)
     with jax.named_scope("pointwise"):
         hidden = (grid.reshape(-1, width).astype(jnp.float32) + wave_rows).astype(jnp.bfloat16)
         back = cotangent.reshape(-1, width)
@@ -348,7 +349,7 @@
         gathered, hidden, pre_grad, act = lax.optimization_barrier(
             (gathered, hidden, pre_grad, act)
         )
-        field_grad = swap_blocks(to_orders(gathered, doubled_t, None), "lat")
+        field_grad = swap_blocks(to_orders(gathered, doubled_t), "lat")
     with jax.named_scope("pointwise_weights"):
         keep, give = gradient_rows(lat_index & 1, lat_count, act, back, hidden, pre_grad)
         got = lax.ppermute(give, "lat", [(i, i ^ 1) for i in range(lat_count)])
@@ -383,15 +384,15 @@
         extra = jnp.pad(extra, ((0, 0), (0, room - chunk)))
         extra = extra.reshape(lat_count, rows, room // rows)
         four_grad = call_kernel(
-            functools.partial(beside_kernel, TURNED),
-            [table, spectrum_grad, extra],
-            [table.shape, spread, extra.shape],
+            beside_kernel,
+            [table, quad, spectrum_grad, extra],
+            [table.shape, quad.shape, spread, extra.shape],
             (lat_count, rows, width + extra.shape[2]),
             2 * total_lat * total_lat * width,
         )
         four_grad, left, right = lax.optimization_barrier((four_grad, spectrum, mixed_grad))
         four_grad = swap_blocks(four_grad, "lat")
-        wave_grad = from_orders(four_grad, plain, quad)
+        wave_grad = from_orders(four_grad, plain)
         grad_input = (hidden_grad.astype(jnp.float32) + wave_grad).astype(jnp.bfloat16)
     with jax.named_scope("unmix"):
         right = jnp.stack([right, jnp.concatenate([right[half:], -right[:half]])])
@@ -435,7 +436,7 @@
         plain_t, doubled_t = fourier_tables(nlon, nlat, mesh.shape["lon"], rows)
         plain = np.ascontiguousarray(plain_t.swapaxes(1, 2))
         doubled = np.ascontiguousarray(doubled_t.swapaxes(1, 2))
-        quad = quadrature(nlat, nlon)
+        quad = quadrature(nlat, nlon)[:, None]
         mapped = jax.shard_map(
             body,
             mesh=mesh,

time: 308 us -> 306 us (level)
  waiting for transfers between devices: 80.6 us -> 83.8 us
    all_to_all x7, waiting for transfers between devices: 76.7 us -> 79.9 us  [swap_blocks(): return lax.all_to_all(values, axis, split_axis=0, concat_axis=0, tiled=True)]
  transfers between devices with their start and end apart: 18 -> 18, of which waited for: 8 -> 8; matrix products, arithmetic and copies ran while one was open for 5% -> 4% of each run, Pallas kernels for 2% -> 2%
where the time goes in v10:
time: 306 us; the launch traced here: 305 us
  blocking collectives  95.7 us (31%)
  starting transfers between devices  94.2 us (31%)
  waiting for transfers between devices  83.8 us (27%)
  Pallas kernels  11.2 us (4%)
  local copies, waits for them, and re-layouts  9.48 us (3%)
  other arithmetic  6.8 us (2%)
    all_to_all x7, waiting for transfers between devices, swap_blocks(): return lax.all_to_all(values, axis, split_axis=0, concat_axis=0, tiled=True)  79.9 us
    all_to_all x3, blocking collectives, swap_blocks(): return lax.all_to_all(values, axis, split_axis=0, concat_axis=0, tiled=True)  67.6 us
    all_to_all x7, starting transfers between devices, swap_blocks(): return lax.all_to_all(values, axis, split_axis=0, concat_axis=0, tiled=True)  56.9 us
    all_gather x1, blocking collectives, body(): gathered = lax.all_gather(hidden_grad, 'lon', axis=0)  14.2 us
    all_gather x1, blocking collectives, body(): gathered = lax.all_gather(grid.reshape(-1, width), 'lon', axis=0)  14 us
    ppermute x3, starting transfers between devices, body(): grad_spectral.append(lax.ppermute(block, 'lon', pairs))  11 us
    ppermute x3, starting transfers between devices, body(): moved = lax.ppermute(own_weight, 'lon', pairs)  10.4 us
    ppermute x3, starting transfers between devices, scatter_sum(): parts.append(lax.ppermute(block, axis, shifted(shift)))  9.22 us
  transfers between devices with their start and end apart: 18, of which 8 were waited for; matrix products, arithmetic and copies ran while one was open for 4% of the time, Pallas kernels for 2%

profile of v10, /device:TPU:32, one launch (start us, length us, event | category | flops | bytes accessed | tf_op | source)
XLA Modules:
  0.0 305.2 jit_solution(6944462502369796196)
XLA Ops:
  0.7 14.0 %all_gather.9.values_ref = bf16[4,256,384]{2,1,0:T(8,128)(2,1)S(1)} all-gather(bf16[1,256,384]{2,1,0:T(8,128)(2,1)} %bitcast.64), channel_id=1, replica_groups=mesh['lat'=128,'lon'=4] {'lon'}, dimensions={0}, use_global_device_ids=true | all-gather | bytes 983040 | tf_op jit(solution)/shard_map/forward_analysis/all_gather | solution.py:299
  14.7 1.1 forward_analysis.2
  15.8 19.2 %all-to-all-start = ((bf16[128,2,384]{2,1,0:T(2,128)(2,1)}), bf16[128,2,384]{2,1,0:T(2,128)(2,1)S(1)}, u32[]{:S(2)}, u32[]{:S(2)}) async-start(bf16[128,2,384]{2,1,0:T(2,128)(2,1)} %forward_analysis.2), calls=%async_computation | async-start | bytes 393216 | tf_op jit(solution)/shard_map/forward_analysis/all_to_all | solution.py:67
  35.0 3.4 %collective-permute-start.1 = (bf16[2,2,1,96,384]{4,3,1,0,2:T(8,128)(2,1)S(1)}, bf16[2,2,1,96,384]{4,3,1,0,2:T(8,128)(2,1)S(1)}, u32[]{:S(2)}, u32[]{:S(2)}) collective-permute-start(bf16[2,2,1,96,384]{4,3,1,0,2:T(8,128)(2,1)S(1)} %bitcast.65), channel_id=1, source_target_pairs={{0,2},{1,3},{2,0},{3,1},{4,6},{5,7},{6,4},{7,5},{8,10},{9,11},{10,... | collective-permute-start | bytes 884744 | tf_op jit(solution)/shard_map/weights/ppermute | solution.py:310
  38.4 4.5 %collective-permute-start = (bf16[2,2,1,96,384]{4,3,1,0,2:T(8,128)(2,1)S(1)}, bf16[2,2,1,96,384]{4,3,1,0,2:T(8,128)(2,1)S(1)}, u32[]{:S(2)}, u32[]{:S(2)}) collective-permute-start(bf16[2,2,1,96,384]{4,3,1,0,2:T(8,128)(2,1)S(1)} %bitcast.66), channel_id=1, source_target_pairs={{0,1},{1,2},{2,3},{3,0},{4,5},{5,6},{6,7},{7,4},{8,9},{9,10},{10,1... | collective-permute-start | bytes 884744 | tf_op jit(solution)/shard_map/weights/ppermute | solution.py:310
  42.9 2.5 collective-permute-start.2
  45.4 0.9 constant_dynamic-slice_fusion.7.matrix_ref
  46.4 8.4 %all-to-all-done.values_ref = bf16[128,2,384]{2,1,0:T(2,128)(2,1)S(1)} async-done(((bf16[128,2,384]{2,1,0:T(2,128)(2,1)}), bf16[128,2,384]{2,1,0:T(2,128)(2,1)S(1)}, u32[]{:S(2)}, u32[]{:S(2)}) %all-to-all-start) | async-done | bytes 196640 | tf_op jit(solution)/shard_map/forward_analysis/all_to_all | solution.py:67
  54.8 1.1 forward_analysis.3
  55.9 7.7 %all-to-all-start.1 = ((bf16[128,2,384]{2,1,0:T(2,128)(2,1)}), bf16[128,2,384]{2,1,0:T(2,128)(2,1)S(1)}, u32[]{:S(2)}, u32[]{:S(2)}) async-start(bf16[128,2,384]{2,1,0:T(2,128)(2,1)} %forward_analysis.3), calls=%async_computation.1 | async-start | bytes 393216 | tf_op jit(solution)/shard_map/forward_analysis/all_to_all | solution.py:67
  64.0 19.4 %all-to-all-done.1.values_ref = bf16[128,2,384]{2,1,0:T(2,128)(2,1)S(1)} async-done(((bf16[128,2,384]{2,1,0:T(2,128)(2,1)}), bf16[128,2,384]{2,1,0:T(2,128)(2,1)S(1)}, u32[]{:S(2)}, u32[]{:S(2)}) %all-to-all-start.1) | async-done | bytes 196640 | tf_op jit(solution)/shard_map/forward_analysis/all_to_all | solution.py:67
  83.4 0.7 mix.1
  84.1 26.0 %all_to_all.50.values_ref = bf16[128,2,384]{2,1,0:T(2,128)(2,1)S(1)} all-to-all(bf16[128,2,384]{2,1,0:T(2,128)(2,1)S(1)} %mix.1), channel_id=1, replica_groups=mesh['lat'=128,'lon'=4] {'lat'}, dimensions={0} | all-to-all | bytes 393216 | tf_op jit(solution)/shard_map/forward_synthesis/all_to_all | solution.py:67
  110.1 0.3 forward_synthesis.2
  110.4 25.8 %all_to_all.51.values_ref = bf16[128,2,384]{2,1,0:T(2,128)(2,1)S(1)} all-to-all(bf16[128,2,384]{2,1,0:T(2,128)(2,1)S(1)} %forward_synthesis.2), channel_id=1, replica_groups=mesh['lat'=128,'lon'=4] {'lat'}, dimensions={0} | all-to-all | bytes 393216 | tf_op jit(solution)/shard_map/forward_synthesis/all_to_all | solution.py:67
  136.2 0.6 forward_synthesis.3
  136.8 15.8 %all_to_all.52 = bf16[4,256,384]{2,1,0:T(8,128)(2,1)S(1)} all-to-all(bf16[4,256,384]{2,1,0:T(8,128)(2,1)S(1)} %forward_synthesis.3), channel_id=1, replica_groups=mesh['lat'=128,'lon'=4] {'lon'}, dimensions={0} | all-to-all | bytes 1572864 | tf_op jit(solution)/shard_map/forward_synthesis/all_to_all | solution.py:67
  152.8 0.4 multiply_convert_fusion
  153.2 0.5 copy-done.8
  153.7 0.2 copy-done.14
  154.0 0.4 fusion.pre_grad_ref
  154.4 0.4 fusion.2
  154.8 0.7 copy-done.11
  155.5 14.2 %all-gather = bf16[1024,384]{1,0:T(8,128)(2,1)S(1)} all-gather(bf16[256,384]{1,0:T(8,128)(2,1)S(1)} %fusion.2), channel_id=2, replica_groups=mesh['lat'=128,'lon'=4] {'lon'}, dimensions={0}, use_global_device_ids=true | all-gather | bytes 983040 | tf_op jit(solution)/shard_map/backward_analysis/all_gather | solution.py:348
  169.7 1.1 backward_analysis.2
  170.8 5.9 %all-to-all-start.5 = ((bf16[128,2,384]{2,1,0:T(2,128)(2,1)}), bf16[128,2,384]{2,1,0:T(2,128)(2,1)S(1)}, u32[]{:S(2)}, u32[]{:S(2)}) async-start(bf16[128,2,384]{2,1,0:T(2,128)(2,1)} %backward_analysis.2), calls=%async_computation.5 | async-start | bytes 393216 | tf_op jit(solution)/shard_map/backward_analysis/all_to_all | solution.py:67
  176.7 1.6 pointwise_weights.1
  178.3 2.1 collective-permute-start.3
  180.4 16.1 %all-to-all-done.5.values_ref = bf16[128,2,384]{2,1,0:T(2,128)(2,1)S(1)} async-done(((bf16[128,2,384]{2,1,0:T(2,128)(2,1)}), bf16[128,2,384]{2,1,0:T(2,128)(2,1)S(1)}, u32[]{:S(2)}, u32[]{:S(2)}) %all-to-all-start.5) | async-done | bytes 196640 | tf_op jit(solution)/shard_map/backward_analysis/all_to_all | solution.py:67
  196.6 0.9 backward_analysis.3
  197.5 6.2 %all-to-all-start.6 = ((bf16[128,2,384]{2,1,0:T(2,128)(2,1)}), bf16[128,2,384]{2,1,0:T(2,128)(2,1)S(1)}, u32[]{:S(2)}, u32[]{:S(2)}) async-start(bf16[128,2,384]{2,1,0:T(2,128)(2,1)} %backward_analysis.3), calls=%async_computation.6 | async-start | bytes 393216 | tf_op jit(solution)/shard_map/backward_analysis/all_to_all | solution.py:67
  203.7 1.2 fusion.13
  205.1 1.9 collective-permute-start.4
  207.1 5.1 %collective-permute-start.6 = (bf16[128,576]{1,0:T(8,128)(2,1)S(1)}, bf16[128,576]{1,0:T(8,128)(2,1)S(1)}, u32[]{:S(2)}, u32[]{:S(2)}) collective-permute-start(bf16[128,576]{1,0:T(8,128)(2,1)S(1)} %get-tuple-element.41), channel_id=1, source_target_pairs={{0,3},{1,0},{2,1},{3,2},{4,7},{5,4},{6,5},{7,6},{8,11},{9,8},{10,9... | collective-permute-start | bytes 442376 | tf_op jit(solution)/shard_map/pointwise_weights/ppermute | solution.py:247
  212.2 2.2 collective-permute-start.5
  214.4 9.2 %all-to-all-done.6.values_ref = bf16[128,2,384]{2,1,0:T(2,128)(2,1)S(1)} async-done(((bf16[128,2,384]{2,1,0:T(2,128)(2,1)}), bf16[128,2,384]{2,1,0:T(2,128)(2,1)S(1)}, u32[]{:S(2)}, u32[]{:S(2)}) %all-to-all-start.6) | async-done | bytes 196640 | tf_op jit(solution)/shard_map/backward_analysis/all_to_all | solution.py:67
  223.6 1.3 copy-done.3
  224.8 1.4 unmix.1
  226.2 6.9 %all-to-all-start.7 = ((bf16[128,2,384]{2,1,0:T(2,128)(2,1)}), bf16[128,2,384]{2,1,0:T(2,128)(2,1)S(1)}, u32[]{:S(2)}, u32[]{:S(2)}) async-start(bf16[128,2,384]{2,1,0:T(2,128)(2,1)} %unmix.1), calls=%async_computation.7 | async-start | bytes 393216 | tf_op jit(solution)/shard_map/backward_synthesis/all_to_all | solution.py:67
  233.2 1.2 convert_add_fusion.2
  234.4 4.6 %collective-permute-start.7 = (bf16[128,288]{1,0:T(8,128)(2,1)S(1)}, bf16[128,288]{1,0:T(8,128)(2,1)S(1)}, u32[]{:S(2)}, u32[]{:S(2)}) collective-permute-start(bf16[128,288]{1,0:T(8,128)(2,1)S(1)} %select_convert_fusion), channel_id=1, source_target_pairs={{0,24},{4,28},{8,16},{12,20},{16,8},{20,12},{24,0},{28,4},{32,56},... | collective-permute-start | bytes 221192 | tf_op jit(solution)/shard_map/pointwise_weights/ppermute | solution.py:378
  239.0 3.8 %collective-permute-done.7 = bf16[128,288]{1,0:T(8,128)(2,1)S(1)} collective-permute-done((bf16[128,288]{1,0:T(8,128)(2,1)S(1)}, bf16[128,288]{1,0:T(8,128)(2,1)S(1)}, u32[]{:S(2)}, u32[]{:S(2)}) %collective-permute-start.7) | collective-permute-done | bytes 73760 | tf_op jit(solution)/shard_map/pointwise_weights/ppermute | solution.py:378
  243.0 9.9 %all-to-all-done.7.values_ref = bf16[128,2,384]{2,1,0:T(2,128)(2,1)S(1)} async-done(((bf16[128,2,384]{2,1,0:T(2,128)(2,1)}), bf16[128,2,384]{2,1,0:T(2,128)(2,1)S(1)}, u32[]{:S(2)}, u32[]{:S(2)}) %all-to-all-start.7) | async-done | bytes 196640 | tf_op jit(solution)/shard_map/backward_synthesis/all_to_all | solution.py:67
  253.0 1.0 backward_synthesis.2
  254.0 6.2 %all-to-all-start.8 = ((bf16[128,2,640]{2,1,0:T(2,128)(2,1)}), bf16[128,2,640]{2,1,0:T(2,128)(2,1)S(1)}, u32[]{:S(2)}, u32[]{:S(2)}) async-start(bf16[128,2,640]{2,1,0:T(2,128)(2,1)} %backward_synthesis.2), calls=%async_computation.8 | async-start | bytes 655360 | tf_op jit(solution)/shard_map/backward_synthesis/all_to_all | solution.py:67
  260.4 0.3 maximum_bitcast_fusion
  260.6 0.6 pad_maximum_fusion
  261.2 0.5 fusion.10
  261.8 1.3 copy-done.10
  263.2 0.7 copy.49
  264.0 0.7 copy.47
  264.7 0.8 copy.48
  265.5 5.2 %collective-permute-start.9 = (bf16[2,2,96,384]{3,2,1,0:T(8,128)(2,1)}, bf16[2,2,96,384]{3,2,1,0:T(8,128)(2,1)S(1)}, u32[]{:S(2)}, u32[]{:S(2)}) collective-permute-start(bf16[2,2,96,384]{3,2,1,0:T(8,128)(2,1)} %bitcast.52), channel_id=1, source_target_pairs={{0,2},{1,3},{2,0},{3,1},{4,6},{5,7},{6,4},{7,5},{8,10},{9,11},{10,... | collective-permute-start | bytes 884744 | tf_op jit(solution)/shard_map/unmix/ppermute | solution.py:408
  270.7 1.9 collective-permute-start.10
  272.6 3.9 %collective-permute-start.8 = (bf16[2,2,96,384]{3,2,1,0:T(8,128)(2,1)}, bf16[2,2,96,384]{3,2,1,0:T(8,128)(2,1)}, u32[]{:S(2)}, u32[]{:S(2)}) collective-permute-start(bf16[2,2,96,384]{3,2,1,0:T(8,128)(2,1)} %bitcast.53), channel_id=1, source_target_pairs={{0,1},{1,2},{2,3},{3,0},{4,5},{5,6},{6,7},{7,4},{8,9},{9,10},{10,1... | collective-permute-start | bytes 884744 | tf_op jit(solution)/shard_map/unmix/ppermute | solution.py:408
  276.5 8.8 %all-to-all-done.8.values_ref = bf16[128,2,640]{2,1,0:T(2,128)(2,1)S(1)} async-done(((bf16[128,2,640]{2,1,0:T(2,128)(2,1)}), bf16[128,2,640]{2,1,0:T(2,128)(2,1)S(1)}, u32[]{:S(2)}, u32[]{:S(2)}) %all-to-all-start.8) | async-done | bytes 327712 | tf_op jit(solution)/shard_map/backward_synthesis/all_to_all | solution.py:67
  285.3 1.5 backward_synthesis.3
  286.8 4.7 %all-to-all-start.9 = ((bf16[4,256,384]{2,1,0:T(8,128)(2,1)}), bf16[4,256,384]{2,1,0:T(8,128)(2,1)S(1)}, u32[]{:S(2)}, u32[]{:S(2)}) async-start(bf16[4,256,384]{2,1,0:T(8,128)(2,1)} %backward_synthesis.3), calls=%async_computation.9 | async-start | bytes 1572864 | tf_op jit(solution)/shard_map/backward_synthesis/all_to_all | solution.py:67
  291.5 1.0 fusion.1
  292.5 2.1 fusion.8
  295.0 0.7 squeeze.25
  295.6 0.7 squeeze.24
  296.3 8.1 %all-to-all-done.9 = bf16[4,256,384]{2,1,0:T(8,128)(2,1)S(1)} async-done(((bf16[4,256,384]{2,1,0:T(8,128)(2,1)}), bf16[4,256,384]{2,1,0:T(8,128)(2,1)S(1)}, u32[]{:S(2)}, u32[]{:S(2)}) %all-to-all-start.9) | async-done | bytes 786464 | tf_op jit(solution)/shard_map/backward_synthesis/all_to_all | solution.py:67
  304.5 0.7 add_convert_fusion
  (59 shorter events, 1.9 us)
Async XLA Ops:
  0.6 152.1 %copy-start = (bf16[384,768]{1,0:T(8,128)(2,1)S(1)}, bf16[384,768]{1,0:T(8,128)(2,1)}, u32[]{:S(2)}) copy-start(bf16[384,768]{1,0:T(8,128)(2,1)} %param.14) | copy-start | bytes 1769476
  0.6 14.0 %copy-start.7 = (bf16[4,256,512]{2,1,0:T(8,128)(2,1)S(1)}, bf16[4,256,512]{2,1,0:T(8,128)(2,1)}, u32[]{:S(2)}) copy-start(bf16[4,256,512]{2,1,0:T(8,128)(2,1)} %constant.118.clone.matrix_ref) | copy-start | bytes 3145732
  14.7 20.3 %copy-start.16 = (bf16[2,2,384,96]{2,3,1,0:T(8,128)(2,1)S(1)}, bf16[2,2,384,96]{2,3,1,0:T(8,128)(2,1)}, u32[]{:S(2)}) copy-start(bf16[2,2,384,96]{2,3,1,0:T(8,128)(2,1)} %param.13) | copy-start | bytes 884740
  14.7 40.1 %copy-start.9 = (f32[256,1]{1,0:T(8,128)S(1)}, f32[256,1]{1,0:T(8,128)}, u32[]{:S(2)}) copy-start(f32[256,1]{1,0:T(8,128)} %constant.120.clone.quad_ref) | copy-start | bytes 3076
  15.8 39.0 %all-to-all-start = ((bf16[128,2,384]{2,1,0:T(2,128)(2,1)}), bf16[128,2,384]{2,1,0:T(2,128)(2,1)S(1)}, u32[]{:S(2)}, u32[]{:S(2)}) async-start(bf16[128,2,384]{2,1,0:T(2,128)(2,1)} %forward_analysis.2), calls=%async_computation | async-start | bytes 393216 | tf_op jit(solution)/shard_map/forward_analysis/all_to_all | solution.py:67
  35.0 28.9 %collective-permute-start.1 = (bf16[2,2,1,96,384]{4,3,1,0,2:T(8,128)(2,1)S(1)}, bf16[2,2,1,96,384]{4,3,1,0,2:T(8,128)(2,1)S(1)}, u32[]{:S(2)}, u32[]{:S(2)}) collective-permute-start(bf16[2,2,1,96,384]{4,3,1,0,2:T(8,128)(2,1)S(1)} %bitcast.65), channel_id=1, source_target_pairs={{0,2},{1,3},{2,0},{3,1},{4,6},{5,7},{6,4},{7,5},{8,10},{9,11},{10,... | collective-permute-start | bytes 884744 | tf_op jit(solution)/shard_map/weights/ppermute | solution.py:310
  38.4 25.4 %collective-permute-start = (bf16[2,2,1,96,384]{4,3,1,0,2:T(8,128)(2,1)S(1)}, bf16[2,2,1,96,384]{4,3,1,0,2:T(8,128)(2,1)S(1)}, u32[]{:S(2)}, u32[]{:S(2)}) collective-permute-start(bf16[2,2,1,96,384]{4,3,1,0,2:T(8,128)(2,1)S(1)} %bitcast.66), channel_id=1, source_target_pairs={{0,1},{1,2},{2,3},{3,0},{4,5},{5,6},{6,7},{7,4},{8,9},{9,10},{10,1... | collective-permute-start | bytes 884744 | tf_op jit(solution)/shard_map/weights/ppermute | solution.py:310
  42.9 21.1 %collective-permute-start.2 = (bf16[2,2,1,96,384]{4,3,1,0,2:T(8,128)(2,1)S(1)}, bf16[2,2,1,96,384]{4,3,1,0,2:T(8,128)(2,1)S(1)}, u32[]{:S(2)}, u32[]{:S(2)}) collective-permute-start(bf16[2,2,1,96,384]{4,3,1,0,2:T(8,128)(2,1)S(1)} %bitcast.67), channel_id=1, source_target_pairs={{0,3},{1,0},{2,1},{3,2},{4,7},{5,4},{6,5},{7,6},{8,11},{9,8},{10,9... | collective-permute-start | bytes 884744 | tf_op jit(solution)/shard_map/weights/ppermute | solution.py:310
  55.9 27.5 %all-to-all-start.1 = ((bf16[128,2,384]{2,1,0:T(2,128)(2,1)}), bf16[128,2,384]{2,1,0:T(2,128)(2,1)S(1)}, u32[]{:S(2)}, u32[]{:S(2)}) async-start(bf16[128,2,384]{2,1,0:T(2,128)(2,1)} %forward_analysis.3), calls=%async_computation.1 | async-start | bytes 393216 | tf_op jit(solution)/shard_map/forward_analysis/all_to_all | solution.py:67
  64.0 46.1 %copy-start.2 = (bf16[2,2,4,96,384]{4,3,2,1,0:T(8,128)(2,1)}, bf16[2,2,4,96,384]{4,3,2,1,0:T(8,128)(2,1)S(1)}, u32[]{:S(2)}) copy-start(bf16[2,2,4,96,384]{4,3,2,1,0:T(8,128)(2,1)S(1)} %bitcast_dynamic-update-slice_fusion.1) | copy-start | bytes 3538948
  84.1 52.1 %copy-start.6 = (bf16[4,512,256]{2,1,0:T(8,128)(2,1)S(1)}, bf16[4,512,256]{2,1,0:T(8,128)(2,1)}, u32[]{:S(2)}) copy-start(bf16[4,512,256]{2,1,0:T(8,128)(2,1)} %constant.117.clone.matrix_ref) | copy-start | bytes 3145732
  136.8 15.9 %copy-start.13 = (bf16[2,128,384]{2,1,0:T(8,128)(2,1)S(1)}, bf16[2,128,384]{2,1,0:T(8,128)(2,1)}, u32[]{:S(2)}) copy-start(bf16[2,128,384]{2,1,0:T(8,128)(2,1)} %param.11) | copy-start | bytes 589828
  152.8 0.9 copy-start.8
  152.8 1.2 copy-start.14
  154.4 15.3 %copy-start.5 = (bf16[4,256,512]{2,1,0:T(8,128)(2,1)S(1)}, bf16[4,256,512]{2,1,0:T(8,128)(2,1)}, u32[]{:S(2)}) copy-start(bf16[4,256,512]{2,1,0:T(8,128)(2,1)} %constant.119.clone.matrix_ref) | copy-start | bytes 3145732
  154.8 0.7 copy-start.11
  170.8 25.8 %all-to-all-start.5 = ((bf16[128,2,384]{2,1,0:T(2,128)(2,1)}), bf16[128,2,384]{2,1,0:T(2,128)(2,1)S(1)}, u32[]{:S(2)}, u32[]{:S(2)}) async-start(bf16[128,2,384]{2,1,0:T(2,128)(2,1)} %backward_analysis.2), calls=%async_computation.5 | async-start | bytes 393216 | tf_op jit(solution)/shard_map/backward_analysis/all_to_all | solution.py:67
  178.3 19.1 %collective-permute-start.3 = (bf16[128,2304]{1,0:T(8,128)(2,1)}, bf16[128,2304]{1,0:T(8,128)(2,1)S(1)}, u32[]{:S(2)}, u32[]{:S(2)}) collective-permute-start(bf16[128,2304]{1,0:T(8,128)(2,1)} %get-tuple-element.26), channel_id=1, source_target_pairs={{0,4},{4,0},{8,12},{12,8},{16,20},{20,16},{24,28},{28,24},{32,36},... | collective-permute-start | bytes 1769480 | tf_op jit(solution)/shard_map/pointwise_weights/ppermute | solution.py:355
  197.5 26.1 %all-to-all-start.6 = ((bf16[128,2,384]{2,1,0:T(2,128)(2,1)}), bf16[128,2,384]{2,1,0:T(2,128)(2,1)S(1)}, u32[]{:S(2)}, u32[]{:S(2)}) async-start(bf16[128,2,384]{2,1,0:T(2,128)(2,1)} %backward_analysis.3), calls=%async_computation.6 | async-start | bytes 393216 | tf_op jit(solution)/shard_map/backward_analysis/all_to_all | solution.py:67
  205.1 28.0 %collective-permute-start.4 = (bf16[128,576]{1,0:T(8,128)(2,1)S(1)}, bf16[128,576]{1,0:T(8,128)(2,1)S(1)}, u32[]{:S(2)}, u32[]{:S(2)}) collective-permute-start(bf16[128,576]{1,0:T(8,128)(2,1)S(1)} %get-tuple-element.40), channel_id=1, source_target_pairs={{0,1},{1,2},{2,3},{3,0},{4,5},{5,6},{6,7},{7,4},{8,9},{9,10},{10,1... | collective-permute-start | bytes 442376 | tf_op jit(solution)/shard_map/pointwise_weights/ppermute | solution.py:247
  207.1 26.1 %collective-permute-start.6 = (bf16[128,576]{1,0:T(8,128)(2,1)S(1)}, bf16[128,576]{1,0:T(8,128)(2,1)S(1)}, u32[]{:S(2)}, u32[]{:S(2)}) collective-permute-start(bf16[128,576]{1,0:T(8,128)(2,1)S(1)} %get-tuple-element.41), channel_id=1, source_target_pairs={{0,3},{1,0},{2,1},{3,2},{4,7},{5,4},{6,5},{7,6},{8,11},{9,8},{10,9... | collective-permute-start | bytes 442376 | tf_op jit(solution)/shard_map/pointwise_weights/ppermute | solution.py:247
  212.2 21.0 %collective-permute-start.5 = (bf16[128,576]{1,0:T(8,128)(2,1)S(1)}, bf16[128,576]{1,0:T(8,128)(2,1)S(1)}, u32[]{:S(2)}, u32[]{:S(2)}) collective-permute-start(bf16[128,576]{1,0:T(8,128)(2,1)S(1)} %get-tuple-element.42), channel_id=1, source_target_pairs={{0,2},{1,3},{2,0},{3,1},{4,6},{5,7},{6,4},{7,5},{8,10},{9,11},{10,... | collective-permute-start | bytes 442376 | tf_op jit(solution)/shard_map/pointwise_weights/ppermute | solution.py:247
  223.6 1.3 copy-start.3
  226.2 26.8 %all-to-all-start.7 = ((bf16[128,2,384]{2,1,0:T(2,128)(2,1)}), bf16[128,2,384]{2,1,0:T(2,128)(2,1)S(1)}, u32[]{:S(2)}, u32[]{:S(2)}) async-start(bf16[128,2,384]{2,1,0:T(2,128)(2,1)} %unmix.1), calls=%async_computation.7 | async-start | bytes 393216 | tf_op jit(solution)/shard_map/backward_synthesis/all_to_all | solution.py:67
  234.4 8.4 %collective-permute-start.7 = (bf16[128,288]{1,0:T(8,128)(2,1)S(1)}, bf16[128,288]{1,0:T(8,128)(2,1)S(1)}, u32[]{:S(2)}, u32[]{:S(2)}) collective-permute-start(bf16[128,288]{1,0:T(8,128)(2,1)S(1)} %select_convert_fusion), channel_id=1, source_target_pairs={{0,24},{4,28},{8,16},{12,20},{16,8},{20,12},{24,0},{28,4},{32,56},... | collective-permute-start | bytes 221192 | tf_op jit(solution)/shard_map/pointwise_weights/ppermute | solution.py:378
  254.0 31.4 %all-to-all-start.8 = ((bf16[128,2,640]{2,1,0:T(2,128)(2,1)}), bf16[128,2,640]{2,1,0:T(2,128)(2,1)S(1)}, u32[]{:S(2)}, u32[]{:S(2)}) async-start(bf16[128,2,640]{2,1,0:T(2,128)(2,1)} %backward_synthesis.2), calls=%async_computation.8 | async-start | bytes 655360 | tf_op jit(solution)/shard_map/backward_synthesis/all_to_all | solution.py:67
  261.7 1.4 copy-start.10
  263.2 22.1 %copy-start.4 = (bf16[4,512,256]{2,1,0:T(8,128)(2,1)S(1)}, bf16[4,512,256]{2,1,0:T(8,128)(2,1)}, u32[]{:S(2)}) copy-start(bf16[4,512,256]{2,1,0:T(8,128)(2,1)} %constant.116.clone.matrix_ref) | copy-start | bytes 3145732
  265.5 27.0 %collective-permute-start.9 = (bf16[2,2,96,384]{3,2,1,0:T(8,128)(2,1)}, bf16[2,2,96,384]{3,2,1,0:T(8,128)(2,1)S(1)}, u32[]{:S(2)}, u32[]{:S(2)}) collective-permute-start(bf16[2,2,96,384]{3,2,1,0:T(8,128)(2,1)} %bitcast.52), channel_id=1, source_target_pairs={{0,2},{1,3},{2,0},{3,1},{4,6},{5,7},{6,4},{7,5},{8,10},{9,11},{10,... | collective-permute-start | bytes 884744 | tf_op jit(solution)/shard_map/unmix/ppermute | solution.py:408
  270.7 21.9 %collective-permute-start.10 = (bf16[2,2,96,384]{3,2,1,0:T(8,128)(2,1)}, bf16[2,2,96,384]{3,2,1,0:T(8,128)(2,1)S(1)}, u32[]{:S(2)}, u32[]{:S(2)}) collective-permute-start(bf16[2,2,96,384]{3,2,1,0:T(8,128)(2,1)} %bitcast.51), channel_id=1, source_target_pairs={{0,3},{1,0},{2,1},{3,2},{4,7},{5,4},{6,5},{7,6},{8,11},{9,8},{10,9... | collective-permute-start | bytes 884744 | tf_op jit(solution)/shard_map/unmix/ppermute | solution.py:408
  272.6 19.9 %collective-permute-start.8 = (bf16[2,2,96,384]{3,2,1,0:T(8,128)(2,1)}, bf16[2,2,96,384]{3,2,1,0:T(8,128)(2,1)}, u32[]{:S(2)}, u32[]{:S(2)}) collective-permute-start(bf16[2,2,96,384]{3,2,1,0:T(8,128)(2,1)} %bitcast.53), channel_id=1, source_target_pairs={{0,1},{1,2},{2,3},{3,0},{4,5},{5,6},{6,7},{7,4},{8,9},{9,10},{10,1... | collective-permute-start | bytes 884744 | tf_op jit(solution)/shard_map/unmix/ppermute | solution.py:408
  286.8 4.7 %copy-start.15 = (bf16[768,384]{1,0:T(8,128)(2,1)S(1)}, bf16[768,384]{1,0:T(8,128)(2,1)}, u32[]{:S(2)}) copy-start(bf16[768,384]{1,0:T(8,128)(2,1)} %param.15) | copy-start | bytes 1769476
  286.8 17.6 %all-to-all-start.9 = ((bf16[4,256,384]{2,1,0:T(8,128)(2,1)}), bf16[4,256,384]{2,1,0:T(8,128)(2,1)S(1)}, u32[]{:S(2)}, u32[]{:S(2)}) async-start(bf16[4,256,384]{2,1,0:T(8,128)(2,1)} %backward_synthesis.3), calls=%async_computation.9 | async-start | bytes 1572864 | tf_op jit(solution)/shard_map/backward_synthesis/all_to_all | solution.py:67
  294.6 9.8 %copy-start.12 = (bf16[256,384]{1,0:T(8,128)(2,1)S(1)}, bf16[256,384]{1,0:T(8,128)(2,1)}, u32[]{:S(2)}) copy-start(bf16[256,384]{1,0:T(8,128)(2,1)} %copy-done.11) | copy-start | bytes 589828
  294.6 10.6 %copy-start.1 = (bf16[384,768]{1,0:T(8,128)(2,1)S(1)}, bf16[384,768]{1,0:T(8,128)(2,1)}, u32[]{:S(2)}) copy-start(bf16[384,768]{1,0:T(8,128)(2,1)} %param.14) | copy-start | bytes 1769476

commit v11 on v10

--- a/solution.py
+++ b/solution.py
@@ -163,8 +163,6 @@
         return total
 
     by_re, by_im = product(0), product(1)
-    if conjugate:
-        by_im = -by_im
     half = values.shape[0] // 2
     out = jnp.concatenate([by_re[:half] - by_im[half:], by_re[half:] + by_im[:half]])
     out_ref[...] = out.astype(jnp.bfloat16).reshape(out_ref.shape)
@@ -286,7 +284,7 @@
         blocks = [table.shape, spread]
         return call_kernel(kernel, [table, values], blocks, spread, flops)
 
-    def complex_product(values, conjugate):
+    def complex_product(values, weights, conjugate):
         return call_kernel(
             functools.partial(mix_kernel, conjugate),
             [weights, values],
@@ -321,7 +319,7 @@
         )
         spectrum = swap_blocks(spectrum, "lat")
     with jax.named_scope("mix"):
-        mixed = complex_product(spectrum, False)
+        mixed = complex_product(spectrum, weights, False)
     with jax.named_scope("forward_synthesis"):
         fields = swap_blocks(legendre(TURNED, swap_blocks(mixed, "lat")), "lat")
         wave_rows = from_orders(fields, doubled)
@@ -355,7 +353,7 @@
         got = lax.ppermute(give, "lat", [(i, i ^ 1) for i in range(lat_count)])
     with jax.named_scope("backward_analysis"):
         mixed_grad = legendre(PLAIN, field_grad)
-        mixed_grad, keep, got = lax.optimization_barrier((mixed_grad, keep, got))
+        mixed_grad, keep, got, late = lax.optimization_barrier((mixed_grad, keep, got, weights))
         mixed_grad = swap_blocks(mixed_grad, "lat")
     with jax.named_scope("pointwise_weights"):
         parts = scatter_sum(
@@ -366,7 +364,8 @@
             lambda s: [(i, (i + s) % lon_count) for i in range(lon_count)],
         )
     with jax.named_scope("unmix"):
-        spectrum_grad = complex_product(mixed_grad, True)
+        conjugate = jnp.stack([late[0], -late[1]])
+        spectrum_grad = complex_product(mixed_grad, conjugate, True)
     with jax.named_scope("backward_synthesis"):
         spectrum_grad = swap_blocks(spectrum_grad, "lat")
     with jax.named_scope("pointwise_weights"):

time: 306 us -> 306 us (level)
  transfers between devices with their start and end apart: 18 -> 18, of which waited for: 8 -> 8; matrix products, arithmetic and copies ran while one was open for 4% -> 5% of each run, Pallas kernels for 2% -> 2%
where the time goes in v11:
time: 306 us; the launch traced here: 305 us
  starting transfers between devices  95.9 us (31%)
  blocking collectives  95.8 us (31%)
  waiting for transfers between devices  81 us (26%)
  Pallas kernels  11.2 us (4%)
  other arithmetic  8.83 us (3%)
  local copies, waits for them, and re-layouts  8.26 us (3%)
    all_to_all x7, waiting for transfers between devices, swap_blocks(): return lax.all_to_all(values, axis, split_axis=0, concat_axis=0, tiled=True)  77.1 us
    all_to_all x3, blocking collectives, swap_blocks(): return lax.all_to_all(values, axis, split_axis=0, concat_axis=0, tiled=True)  67.6 us
    all_to_all x7, starting transfers between devices, swap_blocks(): return lax.all_to_all(values, axis, split_axis=0, concat_axis=0, tiled=True)  58.6 us
    all_gather x1, blocking collectives, body(): gathered = lax.all_gather(hidden_grad, 'lon', axis=0)  14.2 us
    all_gather x1, blocking collectives, body(): gathered = lax.all_gather(grid.reshape(-1, width), 'lon', axis=0)  14 us
    ppermute x3, starting transfers between devices, body(): grad_spectral.append(lax.ppermute(block, 'lon', pairs))  11 us
    ppermute x3, starting transfers between devices, body(): moved = lax.ppermute(own_weight, 'lon', pairs)  10.4 us
    ppermute x3, starting transfers between devices, scatter_sum(): parts.append(lax.ppermute(block, axis, shifted(shift)))  9.22 us
  transfers between devices with their start and end apart: 18, of which 8 were waited for; matrix products, arithmetic and copies ran while one was open for 5% of the time, Pallas kernels for 2%

profile of v11, /device:TPU:32, one launch (start us, length us, event | category | flops | bytes accessed | tf_op | source)
XLA Modules:
  0.0 305.0 jit_solution(8422472162683887677)
XLA Ops:
  0.7 14.0 %all_gather.9.values_ref = bf16[4,256,384]{2,1,0:T(8,128)(2,1)S(1)} all-gather(bf16[1,256,384]{2,1,0:T(8,128)(2,1)} %bitcast.64), channel_id=1, replica_groups=mesh['lat'=128,'lon'=4] {'lon'}, dimensions={0}, use_global_device_ids=true | all-gather | bytes 983040 | tf_op jit(solution)/shard_map/forward_analysis/all_gather | solution.py:297
  14.7 1.1 forward_analysis.2
  15.8 19.2 %all-to-all-start = ((bf16[128,2,384]{2,1,0:T(2,128)(2,1)}), bf16[128,2,384]{2,1,0:T(2,128)(2,1)S(1)}, u32[]{:S(2)}, u32[]{:S(2)}) async-start(bf16[128,2,384]{2,1,0:T(2,128)(2,1)} %forward_analysis.2), calls=%async_computation | async-start | bytes 393216 | tf_op jit(solution)/shard_map/forward_analysis/all_to_all | solution.py:67
  35.0 3.4 %collective-permute-start.1 = (bf16[2,2,1,96,384]{4,3,1,0,2:T(8,128)(2,1)S(1)}, bf16[2,2,1,96,384]{4,3,1,0,2:T(8,128)(2,1)S(1)}, u32[]{:S(2)}, u32[]{:S(2)}) collective-permute-start(bf16[2,2,1,96,384]{4,3,1,0,2:T(8,128)(2,1)S(1)} %bitcast.65), channel_id=1, source_target_pairs={{0,2},{1,3},{2,0},{3,1},{4,6},{5,7},{6,4},{7,5},{8,10},{9,11},{10,... | collective-permute-start | bytes 884744 | tf_op jit(solution)/shard_map/weights/ppermute | solution.py:308
  38.4 4.5 %collective-permute-start = (bf16[2,2,1,96,384]{4,3,1,0,2:T(8,128)(2,1)S(1)}, bf16[2,2,1,96,384]{4,3,1,0,2:T(8,128)(2,1)}, u32[]{:S(2)}, u32[]{:S(2)}) collective-permute-start(bf16[2,2,1,96,384]{4,3,1,0,2:T(8,128)(2,1)S(1)} %bitcast.66), channel_id=1, source_target_pairs={{0,1},{1,2},{2,3},{3,0},{4,5},{5,6},{6,7},{7,4},{8,9},{9,10},{10,1... | collective-permute-start | bytes 884744 | tf_op jit(solution)/shard_map/weights/ppermute | solution.py:308
  42.9 2.5 collective-permute-start.2
  45.4 0.9 constant_dynamic-slice_fusion.7.matrix_ref
  46.4 8.4 %all-to-all-done.values_ref = bf16[128,2,384]{2,1,0:T(2,128)(2,1)S(1)} async-done(((bf16[128,2,384]{2,1,0:T(2,128)(2,1)}), bf16[128,2,384]{2,1,0:T(2,128)(2,1)S(1)}, u32[]{:S(2)}, u32[]{:S(2)}) %all-to-all-start) | async-done | bytes 196640 | tf_op jit(solution)/shard_map/forward_analysis/all_to_all | solution.py:67
  54.8 1.1 forward_analysis.3
  55.9 7.7 %all-to-all-start.1 = ((bf16[128,2,384]{2,1,0:T(2,128)(2,1)}), bf16[128,2,384]{2,1,0:T(2,128)(2,1)S(1)}, u32[]{:S(2)}, u32[]{:S(2)}) async-start(bf16[128,2,384]{2,1,0:T(2,128)(2,1)} %forward_analysis.3), calls=%async_computation.1 | async-start | bytes 393216 | tf_op jit(solution)/shard_map/forward_analysis/all_to_all | solution.py:67
  63.8 1.0 bitcast_dynamic-update-slice_fusion.3
  65.0 18.4 %all-to-all-done.1.values_ref = bf16[128,2,384]{2,1,0:T(2,128)(2,1)S(1)} async-done(((bf16[128,2,384]{2,1,0:T(2,128)(2,1)}), bf16[128,2,384]{2,1,0:T(2,128)(2,1)S(1)}, u32[]{:S(2)}, u32[]{:S(2)}) %all-to-all-start.1) | async-done | bytes 196640 | tf_op jit(solution)/shard_map/forward_analysis/all_to_all | solution.py:67
  83.4 0.7 mix.1
  84.1 26.0 %all_to_all.50.values_ref = bf16[128,2,384]{2,1,0:T(2,128)(2,1)S(1)} all-to-all(bf16[128,2,384]{2,1,0:T(2,128)(2,1)S(1)} %mix.1), channel_id=1, replica_groups=mesh['lat'=128,'lon'=4] {'lat'}, dimensions={0} | all-to-all | bytes 393216 | tf_op jit(solution)/shard_map/forward_synthesis/all_to_all | solution.py:67
  110.1 0.3 forward_synthesis.2
  110.4 25.8 %all_to_all.51.values_ref = bf16[128,2,384]{2,1,0:T(2,128)(2,1)S(1)} all-to-all(bf16[128,2,384]{2,1,0:T(2,128)(2,1)S(1)} %forward_synthesis.2), channel_id=1, replica_groups=mesh['lat'=128,'lon'=4] {'lat'}, dimensions={0} | all-to-all | bytes 393216 | tf_op jit(solution)/shard_map/forward_synthesis/all_to_all | solution.py:67
  136.2 0.6 forward_synthesis.3
  136.8 15.8 %all_to_all.52 = bf16[4,256,384]{2,1,0:T(8,128)(2,1)S(1)} all-to-all(bf16[4,256,384]{2,1,0:T(8,128)(2,1)S(1)} %forward_synthesis.3), channel_id=1, replica_groups=mesh['lat'=128,'lon'=4] {'lon'}, dimensions={0} | all-to-all | bytes 1572864 | tf_op jit(solution)/shard_map/forward_synthesis/all_to_all | solution.py:67
  152.8 0.4 multiply_convert_fusion
  153.2 0.5 copy-done.7
  153.7 0.2 copy-done.14
  154.0 0.5 fusion.pre_grad_ref
  154.4 0.4 fusion.2
  154.8 14.2 %all-gather = bf16[1024,384]{1,0:T(8,128)(2,1)S(1)} all-gather(bf16[256,384]{1,0:T(8,128)(2,1)S(1)} %fusion.2), channel_id=2, replica_groups=mesh['lat'=128,'lon'=4] {'lon'}, dimensions={0}, use_global_device_ids=true | all-gather | bytes 983040 | tf_op jit(solution)/shard_map/backward_analysis/all_gather | solution.py:346
  169.0 1.1 backward_analysis.2
  170.1 5.9 %all-to-all-start.5 = ((bf16[128,2,384]{2,1,0:T(2,128)(2,1)}), bf16[128,2,384]{2,1,0:T(2,128)(2,1)S(1)}, u32[]{:S(2)}, u32[]{:S(2)}) async-start(bf16[128,2,384]{2,1,0:T(2,128)(2,1)} %backward_analysis.2), calls=%async_computation.5 | async-start | bytes 393216 | tf_op jit(solution)/shard_map/backward_analysis/all_to_all | solution.py:67
  176.1 1.6 pointwise_weights.1
  177.7 1.0 copy-done.2
  178.7 2.0 collective-permute-start.3
  180.8 15.1 %all-to-all-done.5.values_ref = bf16[128,2,384]{2,1,0:T(2,128)(2,1)S(1)} async-done(((bf16[128,2,384]{2,1,0:T(2,128)(2,1)}), bf16[128,2,384]{2,1,0:T(2,128)(2,1)S(1)}, u32[]{:S(2)}, u32[]{:S(2)}) %all-to-all-start.5) | async-done | bytes 196640 | tf_op jit(solution)/shard_map/backward_analysis/all_to_all | solution.py:67
  195.9 0.9 backward_analysis.3
  196.8 6.2 %all-to-all-start.6 = ((bf16[128,2,384]{2,1,0:T(2,128)(2,1)}), bf16[128,2,384]{2,1,0:T(2,128)(2,1)S(1)}, u32[]{:S(2)}, u32[]{:S(2)}) async-start(bf16[128,2,384]{2,1,0:T(2,128)(2,1)} %backward_analysis.3), calls=%async_computation.6 | async-start | bytes 393216 | tf_op jit(solution)/shard_map/backward_analysis/all_to_all | solution.py:67
  203.1 2.6 fusion.13
  205.6 0.2 constant_dynamic-slice_fusion.6
  205.9 1.9 collective-permute-start.4
  207.8 5.1 %collective-permute-start.6 = (bf16[128,576]{1,0:T(8,128)(2,1)S(1)}, bf16[128,576]{1,0:T(8,128)(2,1)}, u32[]{:S(2)}, u32[]{:S(2)}) collective-permute-start(bf16[128,576]{1,0:T(8,128)(2,1)S(1)} %get-tuple-element.45), channel_id=1, source_target_pairs={{0,3},{1,0},{2,1},{3,2},{4,7},{5,4},{6,5},{7,6},{8,11},{9,8},{10,9... | collective-permute-start | bytes 442376 | tf_op jit(solution)/shard_map/pointwise_weights/ppermute | solution.py:245
  212.9 2.2 collective-permute-start.5
  215.4 7.5 %all-to-all-done.6.values_ref = bf16[128,2,384]{2,1,0:T(2,128)(2,1)S(1)} async-done(((bf16[128,2,384]{2,1,0:T(2,128)(2,1)}), bf16[128,2,384]{2,1,0:T(2,128)(2,1)S(1)}, u32[]{:S(2)}, u32[]{:S(2)}) %all-to-all-start.6) | async-done | bytes 196640 | tf_op jit(solution)/shard_map/backward_analysis/all_to_all | solution.py:67
  222.9 1.4 unmix.1
  224.2 8.6 %all-to-all-start.7 = ((bf16[128,2,384]{2,1,0:T(2,128)(2,1)}), bf16[128,2,384]{2,1,0:T(2,128)(2,1)S(1)}, u32[]{:S(2)}, u32[]{:S(2)}) async-start(bf16[128,2,384]{2,1,0:T(2,128)(2,1)} %unmix.1), calls=%async_computation.7 | async-start | bytes 393216 | tf_op jit(solution)/shard_map/backward_synthesis/all_to_all | solution.py:67
  232.9 1.4 convert_add_fusion.2
  234.4 4.6 %collective-permute-start.7 = (bf16[128,288]{1,0:T(8,128)(2,1)S(1)}, bf16[128,288]{1,0:T(8,128)(2,1)S(1)}, u32[]{:S(2)}, u32[]{:S(2)}) collective-permute-start(bf16[128,288]{1,0:T(8,128)(2,1)S(1)} %select_convert_fusion), channel_id=1, source_target_pairs={{0,24},{4,28},{8,16},{12,20},{16,8},{20,12},{24,0},{28,4},{32,56},... | collective-permute-start | bytes 221192 | tf_op jit(solution)/shard_map/pointwise_weights/ppermute | solution.py:377
  238.9 3.8 %collective-permute-done.7 = bf16[128,288]{1,0:T(8,128)(2,1)S(1)} collective-permute-done((bf16[128,288]{1,0:T(8,128)(2,1)S(1)}, bf16[128,288]{1,0:T(8,128)(2,1)S(1)}, u32[]{:S(2)}, u32[]{:S(2)}) %collective-permute-start.7) | collective-permute-done | bytes 73760 | tf_op jit(solution)/shard_map/pointwise_weights/ppermute | solution.py:377
  242.9 9.7 %all-to-all-done.7.values_ref = bf16[128,2,384]{2,1,0:T(2,128)(2,1)S(1)} async-done(((bf16[128,2,384]{2,1,0:T(2,128)(2,1)}), bf16[128,2,384]{2,1,0:T(2,128)(2,1)S(1)}, u32[]{:S(2)}, u32[]{:S(2)}) %all-to-all-start.7) | async-done | bytes 196640 | tf_op jit(solution)/shard_map/backward_synthesis/all_to_all | solution.py:67
  252.7 1.0 backward_synthesis.2
  253.7 6.3 %all-to-all-start.8 = ((bf16[128,2,640]{2,1,0:T(2,128)(2,1)}), bf16[128,2,640]{2,1,0:T(2,128)(2,1)S(1)}, u32[]{:S(2)}, u32[]{:S(2)}) async-start(bf16[128,2,640]{2,1,0:T(2,128)(2,1)} %backward_synthesis.2), calls=%async_computation.8 | async-start | bytes 655360 | tf_op jit(solution)/shard_map/backward_synthesis/all_to_all | solution.py:67
  260.1 0.3 maximum_bitcast_fusion
  260.4 0.6 pad_maximum_fusion.1
  261.0 0.5 fusion.10
  261.7 0.7 copy.49
  262.5 0.8 copy.47
  263.2 0.8 copy.48
  264.0 5.2 %collective-permute-start.9 = (bf16[2,2,96,384]{3,2,1,0:T(8,128)(2,1)}, bf16[2,2,96,384]{3,2,1,0:T(8,128)(2,1)}, u32[]{:S(2)}, u32[]{:S(2)}) collective-permute-start(bf16[2,2,96,384]{3,2,1,0:T(8,128)(2,1)} %bitcast.52), channel_id=1, source_target_pairs={{0,2},{1,3},{2,0},{3,1},{4,6},{5,7},{6,4},{7,5},{8,10},{9,11},{10,... | collective-permute-start | bytes 884744 | tf_op jit(solution)/shard_map/unmix/ppermute | solution.py:407
  269.2 1.9 collective-permute-start.10
  271.1 3.9 %collective-permute-start.8 = (bf16[2,2,96,384]{3,2,1,0:T(8,128)(2,1)}, bf16[2,2,96,384]{3,2,1,0:T(8,128)(2,1)}, u32[]{:S(2)}, u32[]{:S(2)}) collective-permute-start(bf16[2,2,96,384]{3,2,1,0:T(8,128)(2,1)} %bitcast.53), channel_id=1, source_target_pairs={{0,1},{1,2},{2,3},{3,0},{4,5},{5,6},{6,7},{7,4},{8,9},{9,10},{10,1... | collective-permute-start | bytes 884744 | tf_op jit(solution)/shard_map/unmix/ppermute | solution.py:407
  275.0 10.0 %all-to-all-done.8.values_ref = bf16[128,2,640]{2,1,0:T(2,128)(2,1)S(1)} async-done(((bf16[128,2,640]{2,1,0:T(2,128)(2,1)}), bf16[128,2,640]{2,1,0:T(2,128)(2,1)S(1)}, u32[]{:S(2)}, u32[]{:S(2)}) %all-to-all-start.8) | async-done | bytes 327712 | tf_op jit(solution)/shard_map/backward_synthesis/all_to_all | solution.py:67
  285.1 1.5 backward_synthesis.3
  286.6 4.7 %all-to-all-start.9 = ((bf16[4,256,384]{2,1,0:T(8,128)(2,1)}), bf16[4,256,384]{2,1,0:T(8,128)(2,1)S(1)}, u32[]{:S(2)}, u32[]{:S(2)}) async-start(bf16[4,256,384]{2,1,0:T(8,128)(2,1)} %backward_synthesis.3), calls=%async_computation.9 | async-start | bytes 1572864 | tf_op jit(solution)/shard_map/backward_synthesis/all_to_all | solution.py:67
  291.2 1.0 fusion.1
  292.3 2.3 fusion.8
  294.9 0.7 squeeze.26
  295.6 0.7 squeeze.25
  296.2 7.9 %all-to-all-done.9 = bf16[4,256,384]{2,1,0:T(8,128)(2,1)S(1)} async-done(((bf16[4,256,384]{2,1,0:T(8,128)(2,1)}), bf16[4,256,384]{2,1,0:T(8,128)(2,1)S(1)}, u32[]{:S(2)}, u32[]{:S(2)}) %all-to-all-start.9) | async-done | bytes 786464 | tf_op jit(solution)/shard_map/backward_synthesis/all_to_all | solution.py:67
  304.2 0.7 add_convert_fusion
  (61 shorter events, 1.9 us)
Async XLA Ops:
  0.6 152.1 %copy-start = (bf16[384,768]{1,0:T(8,128)(2,1)S(1)}, bf16[384,768]{1,0:T(8,128)(2,1)}, u32[]{:S(2)}) copy-start(bf16[384,768]{1,0:T(8,128)(2,1)} %param.14) | copy-start | bytes 1769476
  0.6 14.0 %copy-start.6 = (bf16[4,256,512]{2,1,0:T(8,128)(2,1)S(1)}, bf16[4,256,512]{2,1,0:T(8,128)(2,1)}, u32[]{:S(2)}) copy-start(bf16[4,256,512]{2,1,0:T(8,128)(2,1)} %constant.118.clone.matrix_ref) | copy-start | bytes 3145732
  14.7 20.3 %copy-start.16 = (bf16[2,2,384,96]{2,3,1,0:T(8,128)(2,1)S(1)}, bf16[2,2,384,96]{2,3,1,0:T(8,128)(2,1)}, u32[]{:S(2)}) copy-start(bf16[2,2,384,96]{2,3,1,0:T(8,128)(2,1)} %param.13) | copy-start | bytes 884740
  14.7 40.1 %copy-start.8 = (f32[256,1]{1,0:T(8,128)S(1)}, f32[256,1]{1,0:T(8,128)}, u32[]{:S(2)}) copy-start(f32[256,1]{1,0:T(8,128)} %constant.120.clone.quad_ref) | copy-start | bytes 3076
  15.8 39.0 %all-to-all-start = ((bf16[128,2,384]{2,1,0:T(2,128)(2,1)}), bf16[128,2,384]{2,1,0:T(2,128)(2,1)S(1)}, u32[]{:S(2)}, u32[]{:S(2)}) async-start(bf16[128,2,384]{2,1,0:T(2,128)(2,1)} %forward_analysis.2), calls=%async_computation | async-start | bytes 393216 | tf_op jit(solution)/shard_map/forward_analysis/all_to_all | solution.py:67
  35.0 29.8 %collective-permute-start.1 = (bf16[2,2,1,96,384]{4,3,1,0,2:T(8,128)(2,1)S(1)}, bf16[2,2,1,96,384]{4,3,1,0,2:T(8,128)(2,1)S(1)}, u32[]{:S(2)}, u32[]{:S(2)}) collective-permute-start(bf16[2,2,1,96,384]{4,3,1,0,2:T(8,128)(2,1)S(1)} %bitcast.65), channel_id=1, source_target_pairs={{0,2},{1,3},{2,0},{3,1},{4,6},{5,7},{6,4},{7,5},{8,10},{9,11},{10,... | collective-permute-start | bytes 884744 | tf_op jit(solution)/shard_map/weights/ppermute | solution.py:308
  38.4 25.4 %collective-permute-start = (bf16[2,2,1,96,384]{4,3,1,0,2:T(8,128)(2,1)S(1)}, bf16[2,2,1,96,384]{4,3,1,0,2:T(8,128)(2,1)}, u32[]{:S(2)}, u32[]{:S(2)}) collective-permute-start(bf16[2,2,1,96,384]{4,3,1,0,2:T(8,128)(2,1)S(1)} %bitcast.66), channel_id=1, source_target_pairs={{0,1},{1,2},{2,3},{3,0},{4,5},{5,6},{6,7},{7,4},{8,9},{9,10},{10,1... | collective-permute-start | bytes 884744 | tf_op jit(solution)/shard_map/weights/ppermute | solution.py:308
  42.9 22.0 %collective-permute-start.2 = (bf16[2,2,1,96,384]{4,3,1,0,2:T(8,128)(2,1)S(1)}, bf16[2,2,1,96,384]{4,3,1,0,2:T(8,128)(2,1)S(1)}, u32[]{:S(2)}, u32[]{:S(2)}) collective-permute-start(bf16[2,2,1,96,384]{4,3,1,0,2:T(8,128)(2,1)S(1)} %bitcast.67), channel_id=1, source_target_pairs={{0,3},{1,0},{2,1},{3,2},{4,7},{5,4},{6,5},{7,6},{8,11},{9,8},{10,9... | collective-permute-start | bytes 884744 | tf_op jit(solution)/shard_map/weights/ppermute | solution.py:308
  55.9 27.5 %all-to-all-start.1 = ((bf16[128,2,384]{2,1,0:T(2,128)(2,1)}), bf16[128,2,384]{2,1,0:T(2,128)(2,1)S(1)}, u32[]{:S(2)}, u32[]{:S(2)}) async-start(bf16[128,2,384]{2,1,0:T(2,128)(2,1)} %forward_analysis.3), calls=%async_computation.1 | async-start | bytes 393216 | tf_op jit(solution)/shard_map/forward_analysis/all_to_all | solution.py:67
  84.1 52.1 %copy-start.5 = (bf16[4,512,256]{2,1,0:T(8,128)(2,1)S(1)}, bf16[4,512,256]{2,1,0:T(8,128)(2,1)}, u32[]{:S(2)}) copy-start(bf16[4,512,256]{2,1,0:T(8,128)(2,1)} %constant.117.clone.matrix_ref) | copy-start | bytes 3145732
  136.8 15.9 %copy-start.13 = (bf16[2,128,384]{2,1,0:T(8,128)(2,1)S(1)}, bf16[2,128,384]{2,1,0:T(8,128)(2,1)}, u32[]{:S(2)}) copy-start(bf16[2,128,384]{2,1,0:T(8,128)(2,1)} %param.11) | copy-start | bytes 589828
  152.8 0.9 copy-start.7
  152.8 1.2 copy-start.14
  154.4 14.6 %copy-start.4 = (bf16[4,256,512]{2,1,0:T(8,128)(2,1)S(1)}, bf16[4,256,512]{2,1,0:T(8,128)(2,1)}, u32[]{:S(2)}) copy-start(bf16[4,256,512]{2,1,0:T(8,128)(2,1)} %constant.119.clone.matrix_ref) | copy-start | bytes 3145732
  154.8 15.3 %copy-start.11 = (bf16[256,384]{1,0:T(8,128)(2,1)}, bf16[256,384]{1,0:T(8,128)(2,1)S(1)}, u32[]{:S(2)}) copy-start(bf16[256,384]{1,0:T(8,128)(2,1)S(1)} %fusion.2) | copy-start | bytes 589828
  170.1 25.8 %all-to-all-start.5 = ((bf16[128,2,384]{2,1,0:T(2,128)(2,1)}), bf16[128,2,384]{2,1,0:T(2,128)(2,1)S(1)}, u32[]{:S(2)}, u32[]{:S(2)}) async-start(bf16[128,2,384]{2,1,0:T(2,128)(2,1)} %backward_analysis.2), calls=%async_computation.5 | async-start | bytes 393216 | tf_op jit(solution)/shard_map/backward_analysis/all_to_all | solution.py:67
  177.7 1.0 copy-start.2
  178.7 18.1 %collective-permute-start.3 = (bf16[128,2304]{1,0:T(8,128)(2,1)}, bf16[128,2304]{1,0:T(8,128)(2,1)}, u32[]{:S(2)}, u32[]{:S(2)}) collective-permute-start(bf16[128,2304]{1,0:T(8,128)(2,1)} %get-tuple-element.27), channel_id=1, source_target_pairs={{0,4},{4,0},{8,12},{12,8},{16,20},{20,16},{24,28},{28,24},{32,36},... | collective-permute-start | bytes 1769480 | tf_op jit(solution)/shard_map/pointwise_weights/ppermute | solution.py:353
  196.8 26.1 %all-to-all-start.6 = ((bf16[128,2,384]{2,1,0:T(2,128)(2,1)}), bf16[128,2,384]{2,1,0:T(2,128)(2,1)S(1)}, u32[]{:S(2)}, u32[]{:S(2)}) async-start(bf16[128,2,384]{2,1,0:T(2,128)(2,1)} %backward_analysis.3), calls=%async_computation.6 | async-start | bytes 393216 | tf_op jit(solution)/shard_map/backward_analysis/all_to_all | solution.py:67
  205.9 27.0 %collective-permute-start.4 = (bf16[128,576]{1,0:T(8,128)(2,1)S(1)}, bf16[128,576]{1,0:T(8,128)(2,1)S(1)}, u32[]{:S(2)}, u32[]{:S(2)}) collective-permute-start(bf16[128,576]{1,0:T(8,128)(2,1)S(1)} %get-tuple-element.44), channel_id=1, source_target_pairs={{0,1},{1,2},{2,3},{3,0},{4,5},{5,6},{6,7},{7,4},{8,9},{9,10},{10,1... | collective-permute-start | bytes 442376 | tf_op jit(solution)/shard_map/pointwise_weights/ppermute | solution.py:245
  207.8 25.1 %collective-permute-start.6 = (bf16[128,576]{1,0:T(8,128)(2,1)S(1)}, bf16[128,576]{1,0:T(8,128)(2,1)}, u32[]{:S(2)}, u32[]{:S(2)}) collective-permute-start(bf16[128,576]{1,0:T(8,128)(2,1)S(1)} %get-tuple-element.45), channel_id=1, source_target_pairs={{0,3},{1,0},{2,1},{3,2},{4,7},{5,4},{6,5},{7,6},{8,11},{9,8},{10,9... | collective-permute-start | bytes 442376 | tf_op jit(solution)/shard_map/pointwise_weights/ppermute | solution.py:245
  212.9 19.9 %collective-permute-start.5 = (bf16[128,576]{1,0:T(8,128)(2,1)S(1)}, bf16[128,576]{1,0:T(8,128)(2,1)}, u32[]{:S(2)}, u32[]{:S(2)}) collective-permute-start(bf16[128,576]{1,0:T(8,128)(2,1)S(1)} %get-tuple-element.46), channel_id=1, source_target_pairs={{0,2},{1,3},{2,0},{3,1},{4,6},{5,7},{6,4},{7,5},{8,10},{9,11},{10,... | collective-permute-start | bytes 442376 | tf_op jit(solution)/shard_map/pointwise_weights/ppermute | solution.py:245
  224.2 28.4 %all-to-all-start.7 = ((bf16[128,2,384]{2,1,0:T(2,128)(2,1)}), bf16[128,2,384]{2,1,0:T(2,128)(2,1)S(1)}, u32[]{:S(2)}, u32[]{:S(2)}) async-start(bf16[128,2,384]{2,1,0:T(2,128)(2,1)} %unmix.1), calls=%async_computation.7 | async-start | bytes 393216 | tf_op jit(solution)/shard_map/backward_synthesis/all_to_all | solution.py:67
  232.9 19.8 %copy-start.9 = (f32[256,1]{1,0:T(8,128)S(1)}, f32[256,1]{1,0:T(8,128)}, u32[]{:S(2)}) copy-start(f32[256,1]{1,0:T(8,128)} %constant.120.clone.quad_ref) | copy-start | bytes 3076
  234.4 8.4 %collective-permute-start.7 = (bf16[128,288]{1,0:T(8,128)(2,1)S(1)}, bf16[128,288]{1,0:T(8,128)(2,1)S(1)}, u32[]{:S(2)}, u32[]{:S(2)}) collective-permute-start(bf16[128,288]{1,0:T(8,128)(2,1)S(1)} %select_convert_fusion), channel_id=1, source_target_pairs={{0,24},{4,28},{8,16},{12,20},{16,8},{20,12},{24,0},{28,4},{32,56},... | collective-permute-start | bytes 221192 | tf_op jit(solution)/shard_map/pointwise_weights/ppermute | solution.py:377
  253.7 31.4 %all-to-all-start.8 = ((bf16[128,2,640]{2,1,0:T(2,128)(2,1)}), bf16[128,2,640]{2,1,0:T(2,128)(2,1)S(1)}, u32[]{:S(2)}, u32[]{:S(2)}) async-start(bf16[128,2,640]{2,1,0:T(2,128)(2,1)} %backward_synthesis.2), calls=%async_computation.8 | async-start | bytes 655360 | tf_op jit(solution)/shard_map/backward_synthesis/all_to_all | solution.py:67
  261.4 2.5 copy-start.10
  261.7 23.3 %copy-start.3 = (bf16[4,512,256]{2,1,0:T(8,128)(2,1)S(1)}, bf16[4,512,256]{2,1,0:T(8,128)(2,1)}, u32[]{:S(2)}) copy-start(bf16[4,512,256]{2,1,0:T(8,128)(2,1)} %constant.116.clone.matrix_ref) | copy-start | bytes 3145732
  264.0 28.3 %collective-permute-start.9 = (bf16[2,2,96,384]{3,2,1,0:T(8,128)(2,1)}, bf16[2,2,96,384]{3,2,1,0:T(8,128)(2,1)}, u32[]{:S(2)}, u32[]{:S(2)}) collective-permute-start(bf16[2,2,96,384]{3,2,1,0:T(8,128)(2,1)} %bitcast.52), channel_id=1, source_target_pairs={{0,2},{1,3},{2,0},{3,1},{4,6},{5,7},{6,4},{7,5},{8,10},{9,11},{10,... | collective-permute-start | bytes 884744 | tf_op jit(solution)/shard_map/unmix/ppermute | solution.py:407
  269.2 23.1 %collective-permute-start.10 = (bf16[2,2,96,384]{3,2,1,0:T(8,128)(2,1)}, bf16[2,2,96,384]{3,2,1,0:T(8,128)(2,1)}, u32[]{:S(2)}, u32[]{:S(2)}) collective-permute-start(bf16[2,2,96,384]{3,2,1,0:T(8,128)(2,1)} %bitcast.51), channel_id=1, source_target_pairs={{0,3},{1,0},{2,1},{3,2},{4,7},{5,4},{6,5},{7,6},{8,11},{9,8},{10,9... | collective-permute-start | bytes 884744 | tf_op jit(solution)/shard_map/unmix/ppermute | solution.py:407
  271.1 21.2 %collective-permute-start.8 = (bf16[2,2,96,384]{3,2,1,0:T(8,128)(2,1)}, bf16[2,2,96,384]{3,2,1,0:T(8,128)(2,1)}, u32[]{:S(2)}, u32[]{:S(2)}) collective-permute-start(bf16[2,2,96,384]{3,2,1,0:T(8,128)(2,1)} %bitcast.53), channel_id=1, source_target_pairs={{0,1},{1,2},{2,3},{3,0},{4,5},{5,6},{6,7},{7,4},{8,9},{9,10},{10,1... | collective-permute-start | bytes 884744 | tf_op jit(solution)/shard_map/unmix/ppermute | solution.py:407
  286.5 4.7 %copy-start.15 = (bf16[768,384]{1,0:T(8,128)(2,1)S(1)}, bf16[768,384]{1,0:T(8,128)(2,1)}, u32[]{:S(2)}) copy-start(bf16[768,384]{1,0:T(8,128)(2,1)} %param.15) | copy-start | bytes 1769476
  286.6 17.6 %all-to-all-start.9 = ((bf16[4,256,384]{2,1,0:T(8,128)(2,1)}), bf16[4,256,384]{2,1,0:T(8,128)(2,1)S(1)}, u32[]{:S(2)}, u32[]{:S(2)}) async-start(bf16[4,256,384]{2,1,0:T(8,128)(2,1)} %backward_synthesis.3), calls=%async_computation.9 | async-start | bytes 1572864 | tf_op jit(solution)/shard_map/backward_synthesis/all_to_all | solution.py:67
  294.6 9.7 %copy-start.12 = (bf16[256,384]{1,0:T(8,128)(2,1)S(1)}, bf16[256,384]{1,0:T(8,128)(2,1)}, u32[]{:S(2)}) copy-start(bf16[256,384]{1,0:T(8,128)(2,1)} %copy-done.11) | copy-start | bytes 589828
  294.6 10.4 %copy-start.1 = (bf16[384,768]{1,0:T(8,128)(2,1)S(1)}, bf16[384,768]{1,0:T(8,128)(2,1)}, u32[]{:S(2)}) copy-start(bf16[384,768]{1,0:T(8,128)(2,1)} %param.14) | copy-start | bytes 1769476
